TPU v7x, 256 devices: a whole 4x4x8 slice. The times are simulated.
256 devices in a mesh: dp: 8 (over x, core), fsdp: 32 (over y, z).
Axes of the slice: x: 4, y: 4, z: 8, core: 2. Of those that a mesh axis runs over, the one named last changes fastest.
Arguments:
- tokens: bfloat16 [1024, 4096], P(('dp', 'fsdp')), may hold values from -6 to 6
- cotangent: bfloat16 [1024, 4096], P(('dp', 'fsdp')), may hold values from -6 to 6
- gate_blocks: bfloat16 [7168, 4096], P('fsdp'), may hold values from -0.125 to 0.125
- up_blocks: bfloat16 [7168, 4096], P('fsdp'), may hold values from -0.125 to 0.125
- down_blocks: bfloat16 [7168, 4096], P('fsdp'), may hold values from -0.0625 to 0.0625
- block_index: int32 [3, 7168], P(None, 'fsdp'), may hold values from 0 to 63, as said below
Outputs:
- layer_out: bfloat16 [1024, 4096], P(('dp', 'fsdp'))
- input_grad: bfloat16 [1024, 4096], P(('dp', 'fsdp'))
- gate_grad: bfloat16 [7168, 4096], P('fsdp', 'dp')
- up_grad: bfloat16 [7168, 4096], P('fsdp', 'dp')
- down_grad: bfloat16 [7168, 4096], P('fsdp', 'dp')
Inputs may be any that keep to these rules, and one draw needn't show every extreme that they name: `block_index`: slot q of each matrix lies in hidden block-column q // 32; the 32 slots of one hidden block-column name distinct feature blocks.
All inputs are finite; a program needn't handle non-finite values.
Results may differ from a plain program's by a relative error of at most 0.022.
Values may be sent and summed in bfloat16 or wider, within the bound.
No kernel may reach another device: no remote copies, remote signals or barrier semaphores. Data moves between devices by JAX's collectives and lax.ppermute only.
A program may use at most 128 MiB of HBM per device.

v0:
```python
import jax
import jax.numpy as jnp
import numpy as np
from jax import lax
from jax.experimental import pallas as pl
from jax.experimental.pallas import tpu as pltpu
from jax.sharding import PartitionSpec as P

D = 4096
BLK = 64
KEEP = 32
COLS = 7
SLOT = COLS * KEEP
TOK = 128
HALF = 32
FEAT = 64 * HALF
WIDE = COLS * 128
NX, NC, NY, NZ = 4, 2, 4, 8
BF = jnp.bfloat16
F32 = jnp.float32


def swap_matrix():
    m = np.zeros((256, 256), np.float32)
    for a in range(16):
        for b in range(16):
            m[a * 16 + b, b * 16 + a] = 1
    return m


def feature_split():
    m = np.zeros((256, 256), np.float32)
    for i in range(4):
        for p in range(2):
            for k in range(HALF):
                m[i * 64 + 2 * k + p, p * 128 + i * 32 + k] = 1
    return m


def hidden_split():
    m = np.zeros((512, 256), np.float32)
    for j in range(4):
        for p in range(2):
            for k in range(HALF):
                m[j * 128 + 2 * k + p, p * 128 + j * 32 + k] = 1
    return m


def hidden_join():
    m = np.zeros((256, 512), np.float32)
    for j in range(4):
        for p in range(2):
            for k in range(HALF):
                for h in range(2):
                    m[p * 128 + j * 32 + k, j * 128 + h * 64 + 2 * k + p] = 1
    return m


SWAP = swap_matrix()
FSPLIT = feature_split()
HSPLIT = hidden_split()
HJOIN = hidden_join()


def mm(a, b):
    return jnp.dot(a, b, preferred_element_type=F32)


def mm_nt(a, b):
    return lax.dot_general(a, b, (((1,), (1,)), ((), ())), preferred_element_type=F32)


def low_half(shape):
    return lax.broadcasted_iota(jnp.int32, shape, 1) < 64


def prep_kernel(idx, g_ref, u_ref, d_ref, swap, pg, pu, pd, scr):
    j = pl.program_id(0)
    pd[...] = jnp.zeros_like(pd)

    @pl.when(j < COLS)
    def _():
        pg[...] = jnp.zeros_like(pg)
        pu[...] = jnp.zeros_like(pu)
        for m, src in enumerate((g_ref, u_ref, d_ref)):
            for qh in range(2):
                rows = slice(qh * 16, qh * 16 + 16)
                halves = [
                    jnp.concatenate(
                        [src[rows, (kh * 16 + k) * 128:(kh * 16 + k + 1) * 128] for k in range(16)], axis=0
                    )
                    for kh in range(2)
                ]
                tiles = scr.at[2 * m + qh]
                tiles[...] = mm(swap[...], jnp.concatenate(halves, axis=1)).astype(BF)
                for q in range(16):
                    i = idx[m, j * KEEP + qh * 16 + q]
                    for kh in range(2):
                        tile = tiles[q * 16:q * 16 + 16, kh * 128:kh * 128 + 128]
                        if m == 2:
                            pd[kh * 16:kh * 16 + 16, pl.ds(pl.multiple_of(i * 128, 128), 128)] = tile
                        else:
                            dst = pg if m == 0 else pu
                            dst[pl.ds(pl.multiple_of(i * 32 + kh * 16, 16), 16), :] = tile


def prep(idx, gate, up, down):
    blocks = pl.BlockSpec((KEEP, D), lambda j, s: (jnp.minimum(j, COLS - 1), 0))
    panel = pl.BlockSpec((FEAT, 128), lambda j, s: (0, jnp.minimum(j, COLS - 1)))
    return pl.pallas_call(
        prep_kernel,
        grid_spec=pltpu.PrefetchScalarGridSpec(
            num_scalar_prefetch=1,
            grid=(COLS + 1,),
            in_specs=[blocks, blocks, blocks, pl.BlockSpec((256, 256), lambda j, s: (0, 0))],
            out_specs=[panel, panel, pl.BlockSpec((KEEP, 2 * D), lambda j, s: (j, 0))],
            scratch_shapes=[pltpu.VMEM((6, 256, 256), BF)],
        ),
        out_shape=[
            jax.ShapeDtypeStruct((FEAT, WIDE), BF),
            jax.ShapeDtypeStruct((FEAT, WIDE), BF),
            jax.ShapeDtypeStruct((256, 2 * D), BF),
        ],
        compiler_params=pltpu.CompilerParams(vmem_limit_bytes=40 << 20),
        cost_estimate=pl.CostEstimate(flops=3_000_000_000, bytes_accessed=17_000_000, transcendentals=0),
        name="prep",
    )(idx, gate, up, down, jnp.asarray(SWAP, BF))


def forward_kernel(t0, t1, t2, t3, pg, pu, pd, fsplit, fsplit_t, hsplit, hsplit_t,
                   xxt, gl2, ul2, hht, o0, o1, o2, o3, tok, xx, hid, hh):
    for n, piece in enumerate((t0, t1, t2, t3)):
        tok[n * 32:n * 32 + 32, :] = piece[...]
    for c in range(16):
        chunk = tok[:, c * 256:c * 256 + 256]
        split = mm(chunk, fsplit[...]).astype(BF)
        turned = mm_nt(fsplit_t[...], chunk).astype(BF)
        for p in range(2):
            xx[p * 128:p * 128 + 128, c * 128:c * 128 + 128] = split[:, p * 128:p * 128 + 128]
            xxt[c * 128:c * 128 + 128, p * 128:p * 128 + 128] = turned[p * 128:p * 128 + 128, :]
    low = low_half((TOK, 128))
    hid[:, WIDE:] = jnp.zeros((TOK, 128), BF)
    for n in range(0, WIDE, 256):
        width = min(256, WIDE - n)
        gate = mm(xx[...], pg[:, n:n + width])
        up = mm(xx[...], pu[:, n:n + width])
        for s in range(0, width, 128):
            cols = slice(n + s, n + s + 128)
            gl = jnp.where(low, gate[:TOK, s:s + 128], gate[TOK:, s:s + 128])
            gl = gl + pltpu.roll(gl, 64, 1)
            ul = jnp.where(low, up[:TOK, s:s + 128], up[TOK:, s:s + 128])
            ul = ul + pltpu.roll(ul, 64, 1)
            gl2[:, cols] = gl
            ul2[:, cols] = ul
            hid[:, cols] = (gl * (1.0 / (1.0 + jnp.exp(-gl))) * ul).astype(BF)
    for g in range(2):
        group = hid[:, g * 512:g * 512 + 512]
        split = mm(group, hsplit[...]).astype(BF)
        turned = mm_nt(hsplit_t[...], group).astype(BF)
        for p in range(2):
            hh[p * 128:p * 128 + 128, g * 128:g * 128 + 128] = split[:, p * 128:p * 128 + 128]
            hht[g * 128:g * 128 + 128, p * 128:p * 128 + 128] = turned[p * 128:p * 128 + 128, :]

    def step(n, carry):
        out = mm(hh[...], pd[:, pl.ds(pl.multiple_of(n * 1024, 1024), 1024)])
        parts = []
        for m in range(4):
            a0, a1 = out[:TOK, m * 256:m * 256 + 128], out[TOK:, m * 256:m * 256 + 128]
            b0, b1 = out[:TOK, m * 256 + 128:m * 256 + 256], out[TOK:, m * 256 + 128:m * 256 + 256]
            parts.append(jnp.where(low, a0, b1) + pltpu.roll(jnp.where(low, b0, a1), 64, 1))
        whole = jnp.concatenate(parts, axis=1).astype(BF)
        for r, dst in enumerate((o0, o1, o2, o3)):
            dst[:, pl.ds(pl.multiple_of(n * 512, 512), 512)] = whole[r * 32:r * 32 + 32, :]
        return carry

    lax.fori_loop(0, 8, step, 0)


def vm(n):
    return [pl.BlockSpec(memory_space=pltpu.VMEM)] * n


def forward(pieces, pg, pu, pd):
    piece = jax.ShapeDtypeStruct((32, D), BF)
    lin = jax.ShapeDtypeStruct((TOK, WIDE), F32)
    return pl.pallas_call(
        forward_kernel,
        in_specs=vm(11),
        out_specs=vm(8),
        out_shape=[jax.ShapeDtypeStruct((FEAT, 256), BF), lin, lin, jax.ShapeDtypeStruct((256, 256), BF)] + [piece] * 4,
        scratch_shapes=[
            pltpu.VMEM((TOK, D), BF),
            pltpu.VMEM((256, FEAT), BF),
            pltpu.VMEM((TOK, 1024), BF),
            pltpu.VMEM((256, 256), BF),
        ],
        compiler_params=pltpu.CompilerParams(vmem_limit_bytes=50 << 20),
        cost_estimate=pl.CostEstimate(flops=4_000_000_000, bytes_accessed=17_000_000, transcendentals=200_000),
        name="forward",
    )(*pieces, pg, pu, pd, jnp.asarray(FSPLIT, BF), jnp.asarray(FSPLIT.T, BF), jnp.asarray(HSPLIT, BF),
      jnp.asarray(HSPLIT.T, BF))


def emit(place, swap, tiles, swapped, own, sib, group):
    swapped[...] = mm(swap[...], tiles[...]).astype(BF)
    rows = pl.ds(pl.multiple_of(group * 16, 16), 16)
    for rel, dst in enumerate((own, sib)):
        for dx in range(NX):
            r = 2 * lax.rem(place[1] + dx, NX) + (place[0] + rel) % 2
            top = lax.rem(r, 4) * 64
            lanes = pl.ds(pl.multiple_of((r // 4) * 128, 128), 128)
            for k in range(4):
                dst[dx, rows, k * 128:k * 128 + 128] = swapped[pl.ds(pl.multiple_of(top + k * 16, 16), 16), lanes]


def down_kernel(idx, place, c0, c1, c2, c3, hht, swap, cx, own, sib, part, tiles, swapped):
    low = low_half((32, 128))
    for n, piece in enumerate((c0, c1, c2, c3)):
        for m in range(32):
            c = piece[:, m * 128:m * 128 + 128].astype(F32)
            rolled = pltpu.roll(c, 64, 1)
            zero = jnp.zeros_like(c)
            first = slice(2 * m * 128, 2 * m * 128 + 128)
            second = slice(2 * m * 128 + 128, 2 * m * 128 + 256)
            top = slice(n * 32, n * 32 + 32)
            bottom = slice(TOK + n * 32, TOK + n * 32 + 32)
            cx[top, first] = jnp.where(low, c, zero).astype(BF)
            cx[bottom, first] = jnp.where(low, zero, rolled).astype(BF)
            cx[top, second] = jnp.where(low, rolled, zero).astype(BF)
            cx[bottom, second] = jnp.where(low, zero, c).astype(BF)

    def product(n, carry):
        lanes = pl.ds(pl.multiple_of(n * 512, 512), 512)
        part[:, lanes] = mm(hht[...], cx[:, lanes]).astype(BF)
        return carry

    lax.fori_loop(0, 16, product, 0)

    def pick(group, carry):
        row = (group // 2) * 32
        for q in range(16):
            i = idx[2, group * 16 + q]
            for kh in range(2):
                tiles[q * 16:q * 16 + 16, kh * 128:kh * 128 + 128] = part[
                    pl.ds(pl.multiple_of(row + kh * 16, 16), 16), pl.ds(pl.multiple_of(i * 128, 128), 128)
                ]
        emit(place, swap, tiles, swapped, own, sib, group)
        return carry

    lax.fori_loop(0, 2 * COLS, pick, 0)


def smem(n):
    return [pl.BlockSpec(memory_space=pltpu.SMEM)] * n


WIRE = jax.ShapeDtypeStruct((NX, SLOT, 512), BF)


def down_grads(idx, place, pieces, hht):
    return pl.pallas_call(
        down_kernel,
        in_specs=smem(2) + vm(6),
        out_specs=vm(3),
        out_shape=[jax.ShapeDtypeStruct((256, 2 * D), BF), WIRE, WIRE],
        scratch_shapes=[pltpu.VMEM((256, 2 * D), BF), pltpu.VMEM((256, 256), BF), pltpu.VMEM((256, 256), BF)],
        compiler_params=pltpu.CompilerParams(vmem_limit_bytes=50 << 20),
        cost_estimate=pl.CostEstimate(flops=1_700_000_000, bytes_accessed=7_000_000, transcendentals=0),
        name="down_grads",
    )(idx, place, *pieces, hht, jnp.asarray(SWAP, BF))


def delta_kernel(cx, pd, gl2, ul2, pg, pu, hjoin, fjoin, gdx, udx, i0, i1, i2, i3):
    def product(n, acc):
        lanes = pl.ds(pl.multiple_of(n * 1024, 1024), 1024)
        return acc + mm_nt(cx[:, lanes], pd[:, lanes])

    hd = lax.fori_loop(0, 8, product, jnp.zeros((256, 256), F32))
    high = hd.astype(BF)
    rest = (hd - high.astype(F32)).astype(BF)
    low = low_half((TOK, 128))
    for g in range(2):
        cols = slice(g * 128, g * 128 + 128)
        joined = sum(
            mm(jnp.concatenate([part[:TOK, cols], part[TOK:, cols]], axis=1), hjoin[...]) for part in (high, rest)
        )
        for jl in range(4):
            j = g * 4 + jl
            if j < COLS:
                lanes = slice(j * 128, j * 128 + 128)
                delta = joined[:, jl * 128:jl * 128 + 128]
                gl, ul = gl2[:, lanes], ul2[:, lanes]
                sig = 1.0 / (1.0 + jnp.exp(-gl))
                gd = delta * ul * sig * (1.0 + gl * (1.0 - sig))
                ud = delta * gl * sig
                for dst, val in ((gdx, gd), (udx, ud)):
                    dst[:TOK, lanes] = jnp.where(low, val, 0.0).astype(BF)
                    dst[TOK:, lanes] = jnp.where(low, 0.0, val).astype(BF)

    def back(n, carry):
        rows = pl.ds(pl.multiple_of(n * 256, 256), 256)
        acc = (mm_nt(gdx[...], pg[rows, :]) + mm_nt(udx[...], pu[rows, :])).astype(BF)
        for c in range(2):
            cols = slice(c * 128, c * 128 + 128)
            pair = jnp.concatenate([acc[:TOK, cols], acc[TOK:, cols]], axis=1)
            whole = mm(pair, fjoin[...]).astype(BF)
            lanes = pl.ds(pl.multiple_of(n * 512 + c * 256, 256), 256)
            for r, dst in enumerate((i0, i1, i2, i3)):
                dst[:, lanes] = whole[r * 32:r * 32 + 32, :]
        return carry

    lax.fori_loop(0, 8, back, 0)


def deltas(cx, pd, gl2, ul2, pg, pu):
    piece = jax.ShapeDtypeStruct((32, D), BF)
    wide = jax.ShapeDtypeStruct((256, WIDE), BF)
    return pl.pallas_call(
        delta_kernel,
        in_specs=vm(8),
        out_specs=vm(6),
        out_shape=[wide, wide] + [piece] * 4,
        compiler_params=pltpu.CompilerParams(vmem_limit_bytes=50 << 20),
        cost_estimate=pl.CostEstimate(flops=3_500_000_000, bytes_accessed=18_000_000, transcendentals=200_000),
        name="deltas",
    )(cx, pd, gl2, ul2, pg, pu, jnp.asarray(HJOIN, BF), jnp.asarray(FSPLIT.T, BF))


def inward_kernel(idx, place, xxt, gdx, udx, swap, own_g, sib_g, own_u, sib_u, part, tiles, swapped):
    for m, (delta, own, sib) in enumerate(((gdx, own_g, sib_g), (udx, own_u, sib_u))):
        def product(n, carry):
            rows = pl.ds(pl.multiple_of(n * 256, 256), 256)
            part[rows, :] = mm(xxt[rows, :], delta[...]).astype(BF)
            return carry

        lax.fori_loop(0, 8, product, 0)
        for j in range(COLS):
            def pick(half, carry):
                for q in range(16):
                    i = idx[m, j * KEEP + half * 16 + q]
                    for kh in range(2):
                        tiles[q * 16:q * 16 + 16, kh * 128:kh * 128 + 128] = part[
                            pl.ds(pl.multiple_of(i * 32 + kh * 16, 16), 16), j * 128:j * 128 + 128
                        ]
                emit(place, swap, tiles, swapped, own, sib, 2 * j + half)
                return carry

            lax.fori_loop(0, 2, pick, 0)


def inward_grads(idx, place, xxt, gdx, udx):
    return pl.pallas_call(
        inward_kernel,
        in_specs=smem(2) + vm(4),
        out_specs=vm(4),
        out_shape=[WIRE] * 4,
        scratch_shapes=[pltpu.VMEM((FEAT, WIDE), BF), pltpu.VMEM((256, 256), BF), pltpu.VMEM((256, 256), BF)],
        compiler_params=pltpu.CompilerParams(vmem_limit_bytes=50 << 20),
        cost_estimate=pl.CostEstimate(flops=3_000_000_000, bytes_accessed=10_000_000, transcendentals=0),
        name="inward_grads",
    )(idx, place, xxt, gdx, udx, jnp.asarray(SWAP, BF))


def from_z(value, step):
    pairs = [(y * NZ + (z + step) % NZ, y * NZ + z) for y in range(NY) for z in range(NZ)]
    return lax.ppermute(value, "fsdp", pairs)


def from_y(value, step):
    pairs = [((y + step) % NY * NZ + z, y * NZ + z) for y in range(NY) for z in range(NZ)]
    return lax.ppermute(value, "fsdp", pairs)


def from_x(value, step):
    pairs = [((x + step) % NX * NC + c, x * NC + c) for x in range(NX) for c in range(NC)]
    return lax.ppermute(value, "dp", pairs)


def from_core(value):
    pairs = [(x * NC + 1 - c, x * NC + c) for x in range(NX) for c in range(NC)]
    return lax.ppermute(value, "dp", pairs)


def gather_z(value):
    up, down = [value], [value]
    for step in range(4):
        up.append(from_z(up[-1], 1))
        if step < 3:
            down.append(from_z(down[-1], -1))
    return up + down[:0:-1]


def reduce_grads(own, sib):
    other = from_core(sib)
    parts = [(own[d].astype(F32) + other[d].astype(F32)).astype(BF) for d in range(NX)]
    got = [from_x(parts[d], -d) for d in range(1, NX)]
    total = sum((g.astype(F32) for g in got), parts[0].astype(F32))
    return (total * (1.0 / (NX * NC))).astype(BF)


def reduce_y(pieces):
    got = [from_y(pieces[d], -d) for d in range(1, NY)]
    return sum((g.astype(F32) for g in got), pieces[0].astype(F32)).astype(BF)


def body(tokens, cotangent, gate_blocks, up_blocks, down_blocks, block_index):
    rows = tokens.shape[0]
    at = lax.axis_index("fsdp")
    here = lax.axis_index("dp")
    place = jnp.stack([here % NC, here // NC]).astype(jnp.int32)

    pg, pu, pd = prep(block_index, gate_blocks, up_blocks, down_blocks)

    ring = jnp.stack(gather_z(jnp.concatenate([tokens, cotangent], axis=0)))
    ring = jnp.roll(ring, at % NZ, axis=0)
    tok_z = ring[:, :rows].reshape(NZ * rows, D)
    cot_z = ring[:, rows:].reshape(NZ * rows, D)
    tok = [tok_z] + [from_y(tok_z, s) for s in range(1, NY)]
    cot = [cot_z] + [from_y(cot_z, s) for s in range(1, NY)]

    xxt, gl2, ul2, hht, *out_parts = forward(tok, pg, pu, pd)
    out_y = reduce_y(out_parts)
    cx, own_d, sib_d = down_grads(block_index, place, cot, hht)
    down_grad = reduce_grads(own_d, sib_d)
    gdx, udx, *in_parts = deltas(cx, pd, gl2, ul2, pg, pu)
    in_y = reduce_y(in_parts)
    own_g, sib_g, own_u, sib_u = inward_grads(block_index, place, xxt, gdx, udx)
    gate_grad = reduce_grads(own_g, sib_g)
    up_grad = reduce_grads(own_u, sib_u)

    both = jnp.concatenate([out_y.reshape(NZ, rows, D), in_y.reshape(NZ, rows, D)], axis=1)
    groups = [[y * NZ + z for z in range(NZ)] for y in range(NY)]
    got = lax.all_to_all(both, "fsdp", 0, 0, axis_index_groups=groups, tiled=True)
    total = got.astype(F32).sum(axis=0).astype(BF)
    return (total[:rows], total[rows:], gate_grad, up_grad, down_grad)


def solution(mesh):
    return jax.shard_map(
        body,
        mesh=mesh,
        in_specs=(
            P(("dp", "fsdp"), None),
            P(("dp", "fsdp"), None),
            P("fsdp", None),
            P("fsdp", None),
            P("fsdp", None),
            P(None, "fsdp"),
        ),
        out_specs=(
            P(("dp", "fsdp"), None),
            P(("dp", "fsdp"), None),
            P("fsdp", "dp"),
            P("fsdp", "dp"),
            P("fsdp", "dp"),
        ),
        check_vma=False,
    )
```

profile of v0, /device:TPU:8, one launch (start us, length us, event | category | flops | bytes accessed | tf_op | source)
XLA Modules:
  0.0 172.2 jit_solution(1756431790466902073)
XLA Ops:
  0.7 1.0 pad_maximum_fusion.1
  1.6 5.9 %collective-permute-start = (bf16[8,4096]{1,0:T(8,128)(2,1)S(1)}, bf16[8,4096]{1,0:T(8,128)(2,1)S(1)}, u32[]{:S(2)}, u32[]{:S(2)}) collective-permute-start(bf16[8,4096]{1,0:T(8,128)(2,1)S(1)} %pad_maximum_fusion.1), channel_id=1, source_target_pairs={{1,0},{2,1},{3,2},{4,3},{5,4},{6,5},{7,6},{0,7},{9,8},{10,9},{11,1... | collective-permute-start | bytes 196616 | tf_op jit(solution)/shard_map/ppermute | solution.py:366
  7.6 1.4 bitcast_dynamic-update-slice_fusion.14
  9.5 3.6 %collective-permute-start.1 = (bf16[8,4096]{1,0:T(8,128)(2,1)S(1)}, bf16[8,4096]{1,0:T(8,128)(2,1)S(1)}, u32[]{:S(2)}, u32[]{:S(2)}) collective-permute-start(bf16[8,4096]{1,0:T(8,128)(2,1)S(1)} %collective-permute-done), channel_id=1, source_target_pairs={{1,0},{2,1},{3,2},{4,3},{5,4},{6,5},{7,6},{0,7},{9,8},{10,9},{11,1... | collective-permute-start | bytes 196616 | tf_op jit(solution)/shard_map/ppermute | solution.py:366
  13.0 0.6 bitcast_dynamic-update-slice_fusion.12
  13.7 1.3 collective-permute-done.1
  14.9 3.6 %collective-permute-start.2 = (bf16[8,4096]{1,0:T(8,128)(2,1)S(1)}, bf16[8,4096]{1,0:T(8,128)(2,1)S(1)}, u32[]{:S(2)}, u32[]{:S(2)}) collective-permute-start(bf16[8,4096]{1,0:T(8,128)(2,1)S(1)} %collective-permute-done.1), channel_id=1, source_target_pairs={{1,0},{2,1},{3,2},{4,3},{5,4},{6,5},{7,6},{0,7},{9,8},{10,9},{11,1... | collective-permute-start | bytes 196616 | tf_op jit(solution)/shard_map/ppermute | solution.py:366
  19.1 1.3 collective-permute-done.2
  20.4 3.6 %collective-permute-start.3 = (bf16[8,4096]{1,0:T(8,128)(2,1)S(1)}, bf16[8,4096]{1,0:T(8,128)(2,1)S(1)}, u32[]{:S(2)}, u32[]{:S(2)}) collective-permute-start(bf16[8,4096]{1,0:T(8,128)(2,1)S(1)} %collective-permute-done.2), channel_id=1, source_target_pairs={{1,0},{2,1},{3,2},{4,3},{5,4},{6,5},{7,6},{0,7},{9,8},{10,9},{11,1... | collective-permute-start | bytes 196616 | tf_op jit(solution)/shard_map/ppermute | solution.py:366
  24.0 0.6 bitcast_dynamic-update-slice_fusion.8
  24.6 1.3 collective-permute-done.3
  25.9 0.6 bitcast_dynamic-update-slice_fusion.6
  27.1 0.6 bitcast_dynamic-update-slice_fusion.2
  28.4 1.4 bitcast_dynamic-update-slice_fusion.15
  30.4 0.6 bitcast_dynamic-update-slice_fusion.11
  31.7 0.6 bitcast_dynamic-update-slice_fusion.7
  32.3 0.6 bitcast_dynamic-update-slice_fusion.5
  32.9 0.6 bitcast_dynamic-update-slice_fusion.3
  34.2 2.1 %constant_dynamic-slice_fusion = (bf16[8,4,4096]{2,1,0:T(4,128)(2,1)S(1)}, bf16[8,4,4096]{2,1,0:T(4,128)(2,1)}) fusion(bf16[16,8,4096]{2,1,0:T(8,128)(2,1)} %bitcast_dynamic-update-slice_fusion.1, s32[]{:T(128)S(6)} %select_n.29, s32[]{:T(128)S(6)} %add.143), kind=kLoop, calls=%fused_computation.60 | loop fusion | bytes 1048584 | tf_op jit(solution)/shard_map/slice | solution.py:416
  36.4 1.7 collective-permute-start.9
  38.0 0.9 collective-permute-start.8
  39.0 2.4 %collective-permute-start.7 = (bf16[32,4096]{1,0:T(8,128)(2,1)S(1)}, bf16[32,4096]{1,0:T(8,128)(2,1)S(1)}, u32[]{:S(2)}, u32[]{:S(2)}) collective-permute-start(bf16[32,4096]{1,0:T(8,128)(2,1)S(1)} %reshape.76.t0), channel_id=1, source_target_pairs={{8,0},{9,1},{10,2},{11,3},{12,4},{13,5},{14,6},{15,7},{16,8},{17,9... | collective-permute-start | bytes 786440 | tf_op jit(solution)/shard_map/ppermute | solution.py:371
  41.4 1.5 copy-done.5
  42.9 1.5 copy-done.6
  44.4 8.0 %prep.1 = (bf16[2048,896]{1,0:T(8,128)(2,1)S(1)}, bf16[2048,896]{1,0:T(8,128)(2,1)S(1)}, bf16[256,8192]{1,0:T(8,128)(2,1)}) custom-call(s32[3,224]{1,0:T(4,128)S(1)} %copy-done.7, bf16[224,4096]{1,0:T(8,128)(2,1)S(1)} %copy-done.4, bf16[224,4096]{1,0:T(8,128)(2,1)S(1)} %copy-done.5, bf16[224,4096]{1,0:T(8,128)(2,1)S(1)} %copy-done.6, ...), custom_call_target="tpu_custom_call" | custom-call | flops 3000000000 | bytes 17000000 | tf_op jit(solution)/shard_map/prep/pallas_call | solution.py:110
  52.4 1.8 %copy-done = bf16[2048,896]{1,0:T(8,128)(2,1)} copy-done((bf16[2048,896]{1,0:T(8,128)(2,1)}, bf16[2048,896]{1,0:T(8,128)(2,1)S(1)}, u32[]{:S(2)}) %copy-start) | copy-done | bytes 3670040
  54.2 1.8 %copy-done.1 = bf16[2048,896]{1,0:T(8,128)(2,1)} copy-done((bf16[2048,896]{1,0:T(8,128)(2,1)}, bf16[2048,896]{1,0:T(8,128)(2,1)S(1)}, u32[]{:S(2)}) %copy-start.1) | copy-done | bytes 3670040
  56.0 1.0 reshape.78.c0
  57.1 3.4 %collective-permute-start.14 = (bf16[32,4096]{1,0:T(8,128)(2,1)S(1)}, bf16[32,4096]{1,0:T(8,128)(2,1)S(1)}, u32[]{:S(2)}, u32[]{:S(2)}) collective-permute-start(bf16[32,4096]{1,0:T(8,128)(2,1)S(1)} %reshape.78.c0), channel_id=1, source_target_pairs={{16,0},{17,1},{18,2},{19,3},{20,4},{21,5},{22,6},{23,7},{24,8},{25... | collective-permute-start | bytes 786440 | tf_op jit(solution)/shard_map/ppermute | solution.py:371
  60.6 0.9 copy-done.9
  61.5 0.9 copy-done.12
  62.4 11.6 %forward.1 = (bf16[2048,256]{1,0:T(8,128)(2,1)}, f32[128,896]{1,0:T(8,128)S(1)}, f32[128,896]{1,0:T(8,128)S(1)}, bf16[256,256]{1,0:T(8,128)(2,1)S(1)}, bf16[32,4...) custom-call(bf16[32,4096]{1,0:T(8,128)(2,1)S(1)} %reshape.76.t0, ...), custom_call_target="tpu_custom_call" | custom-call | flops 4000000000 | bytes 17000000 | tf_op jit(solution)/shard_map/forward/pallas_call | solution.py:186
  74.0 2.0 %collective-permute-start.10 = (bf16[32,4096]{1,0:T(8,128)(2,1)S(1)}, bf16[32,4096]{1,0:T(8,128)(2,1)S(1)}, u32[]{:S(2)}, u32[]{:S(2)}) collective-permute-start(bf16[32,4096]{1,0:T(8,128)(2,1)S(1)} %get-tuple-element.33), channel_id=1, source_target_pairs={{24,0},{25,1},{26,2},{27,3},{28,4},{29,5},{30,6},{31,7},{0,8},{1,9... | collective-permute-start | bytes 786440 | tf_op jit(solution)/shard_map/ppermute | solution.py:371
  76.1 1.4 collective-permute-start.11
  77.5 0.7 collective-permute-start.12
  78.2 11.8 %down_grads.1 = (bf16[256,8192]{1,0:T(8,128)(2,1)}, bf16[4,224,512]{2,1,0:T(8,128)(2,1)S(1)}, bf16[4,224,512]{2,1,0:T(8,128)(2,1)}) custom-call(s32[3,224]{1,0:T(4,128)S(1)} %copy-done.7, s32[2]{0:T(128)S(1)} %pad_add_fusion.place, bf16[32,4096]{1,0:T(8,128)(2,1)S(1)} %reshape.78.c0, bf16[32,4096]{1,0:T(8,128)(2,1)S(1)} %collective-permute-done.13.c1, ...), custom_call_target="tpu_custom_call" | custom-call | flops 1700000000 | bytes 7000000 | tf_op jit(solution)/shard_map/down_grads/pallas_call | solution.py:261
  90.0 14.0 %deltas.1 = (bf16[256,896]{1,0:T(8,128)(2,1)S(1)}, bf16[256,896]{1,0:T(8,128)(2,1)S(1)}, bf16[32,4096]{1,0:T(8,128)(2,1)S(1)}, bf16[32,4096]{1,0:T(8,128)(2,1)S(...) custom-call(bf16[256,8192]{1,0:T(8,128)(2,1)} %get-tuple-element.37.cx, ...), custom_call_target="tpu_custom_call" | custom-call | flops 3500000000 | bytes 18000000 | tf_op jit(solution)/shard_map/deltas/pallas_call | solution.py:318
  104.0 1.4 collective-permute-start.16
  105.4 3.3 %collective-permute-start.17 = (bf16[32,4096]{1,0:T(8,128)(2,1)S(1)}, bf16[32,4096]{1,0:T(8,128)(2,1)S(1)}, u32[]{:S(2)}, u32[]{:S(2)}) collective-permute-start(bf16[32,4096]{1,0:T(8,128)(2,1)S(1)} %get-tuple-element.42), channel_id=1, source_target_pairs={{16,0},{17,1},{18,2},{19,3},{20,4},{21,5},{22,6},{23,7},{24,8},{25... | collective-permute-start | bytes 786440 | tf_op jit(solution)/shard_map/ppermute | solution.py:371
  108.8 16.0 %inward_grads.1 = (bf16[4,224,512]{2,1,0:T(8,128)(2,1)S(1)}, bf16[4,224,512]{2,1,0:T(8,128)(2,1)}, bf16[4,224,512]{2,1,0:T(8,128)(2,1)S(1)}, bf16[4,224,512]{2,1,0:T(8,128)(2,1)}) custom-call(s32[3,224]{1,0:T(4,128)S(1)} %copy-done.7, s32[2]{0:T(128)S(1)} %pad_add_fusion.place, bf16[2048,256]{1,0:T(8,128)(2,1)} %get-tuple-element.44.xxt, ...), custom_call_target="tpu_custom_call" | custom-call | flops 3000000000 | bytes 10000000 | tf_op jit(solution)/shard_map/inward_grads/pallas_call | solution.py:352
  125.8 5.4 %collective-permute-done.18 = bf16[32,4096]{1,0:T(8,128)(2,1)S(1)} collective-permute-done((bf16[32,4096]{1,0:T(8,128)(2,1)S(1)}, bf16[32,4096]{1,0:T(8,128)(2,1)S(1)}, u32[]{:S(2)}, u32[]{:S(2)}) %collective-permute-start.18) | collective-permute-done | bytes 262176 | tf_op jit(solution)/shard_map/ppermute | solution.py:371
  131.3 0.8 reshape.77
  132.2 2.0 %pad_maximum_fusion = bf16[8,8,4096]{2,1,0:T(8,128)(2,1)} fusion(bf16[8,4,4096]{2,1,0:T(4,128)(2,1)S(1)} %reshape.79, bf16[8,4,4096]{2,1,0:T(4,128)(2,1)} %reshape.77), kind=kLoop, calls=%fused_computation | loop fusion | flops 1048576 | bytes 1048576 | tf_op jit(solution)/shard_map/concatenate | solution.py:431
  134.3 4.8 %all-to-all-start = ((bf16[8,8,4096]{2,1,0:T(8,128)(2,1)}), bf16[8,8,4096]{2,1,0:T(8,128)(2,1)S(1)}, u32[]{:S(2)}, u32[]{:S(2)}) async-start(bf16[8,8,4096]{2,1,0:T(8,128)(2,1)} %pad_maximum_fusion), calls=%async_computation | async-start | bytes 1048576 | tf_op jit(solution)/shard_map/all_to_all | solution.py:433
  139.1 1.4 fusion.21
  140.5 1.6 collective-permute-start.28
  142.1 1.7 %collective-permute-start.30 = (bf16[224,512]{1,0:T(8,128)(2,1)S(1)}, bf16[224,512]{1,0:T(8,128)(2,1)S(1)}, u32[]{:S(2)}, u32[]{:S(2)}) collective-permute-start(bf16[224,512]{1,0:T(8,128)(2,1)S(1)} %get-tuple-element.54), channel_id=1, source_target_pairs={{64,0},{96,32},{128,64},{160,96},{192,128},{224,160},{0,192},{32,2... | collective-permute-start | bytes 688136 | tf_op jit(solution)/shard_map/ppermute | solution.py:376
  143.8 1.8 %collective-permute-start.29 = (bf16[224,512]{1,0:T(8,128)(2,1)S(1)}, bf16[224,512]{1,0:T(8,128)(2,1)S(1)}, u32[]{:S(2)}, u32[]{:S(2)}) collective-permute-start(bf16[224,512]{1,0:T(8,128)(2,1)S(1)} %get-tuple-element.55), channel_id=1, source_target_pairs={{128,0},{160,32},{192,64},{224,96},{0,128},{32,160},{64,192},{96,2... | collective-permute-start | bytes 688136 | tf_op jit(solution)/shard_map/ppermute | solution.py:376
  145.6 1.3 fusion.13
  147.0 0.7 collective-permute-start.20
  147.6 2.6 %collective-permute-start.22 = (bf16[224,512]{1,0:T(8,128)(2,1)S(1)}, bf16[224,512]{1,0:T(8,128)(2,1)S(1)}, u32[]{:S(2)}, u32[]{:S(2)}) collective-permute-start(bf16[224,512]{1,0:T(8,128)(2,1)S(1)} %get-tuple-element.60), channel_id=1, source_target_pairs={{64,0},{96,32},{128,64},{160,96},{192,128},{224,160},{0,192},{32,2... | collective-permute-start | bytes 688136 | tf_op jit(solution)/shard_map/ppermute | solution.py:376
  150.3 1.4 fusion.17
  151.6 3.0 %collective-permute-done.28 = bf16[224,512]{1,0:T(8,128)(2,1)S(1)} collective-permute-done((bf16[224,512]{1,0:T(8,128)(2,1)S(1)}, bf16[224,512]{1,0:T(8,128)(2,1)S(1)}, u32[]{:S(2)}, u32[]{:S(2)}) %collective-permute-start.28) | collective-permute-done | bytes 229408 | tf_op jit(solution)/shard_map/ppermute | solution.py:376
  154.7 1.7 collective-permute-start.21
  156.3 3.2 %collective-permute-start.26 = (bf16[224,512]{1,0:T(8,128)(2,1)S(1)}, bf16[224,512]{1,0:T(8,128)(2,1)S(1)}, u32[]{:S(2)}, u32[]{:S(2)}) collective-permute-start(bf16[224,512]{1,0:T(8,128)(2,1)S(1)} %get-tuple-element.57), channel_id=1, source_target_pairs={{64,0},{96,32},{128,64},{160,96},{192,128},{224,160},{0,192},{32,2... | collective-permute-start | bytes 688136 | tf_op jit(solution)/shard_map/ppermute | solution.py:376
  159.6 1.8 %fusion.3 = bf16[224,512]{1,0:T(8,128)(2,1)} fusion(bf16[224,512]{1,0:T(8,128)(2,1)S(1)} %collective-permute-done.30, bf16[224,512]{1,0:T(8,128)(2,1)S(1)} %collective-permute-done.29, bf16[224,512]{1,0:T(8,128)(2,1)S(1)} %collective-permute-done.28, bf16[4,224,512]{2,1,0:T(8,128)(2,1)} %collective-permute-done.27, bf16[4,224,512]{2,1,0:T(8,128)(2,1)S(1)} %get-tuple-element.51), kind=kLoop, calls=%fused_computation.7 | loop fusion | flops 1490944 | bytes 1376256 | tf_op jit(solution)/shard_map/convert_element_type | solution.py:398
  161.4 0.7 collective-permute-start.25
  162.0 1.6 collective-permute-done.22
  163.7 1.1 collective-permute-done.21
  164.8 1.8 %fusion.11 = bf16[224,512]{1,0:T(8,128)(2,1)} fusion(bf16[224,512]{1,0:T(8,128)(2,1)S(1)} %collective-permute-done.22, bf16[224,512]{1,0:T(8,128)(2,1)S(1)} %collective-permute-done.21, bf16[224,512]{1,0:T(8,128)(2,1)S(1)} %collective-permute-done.20, bf16[4,224,512]{2,1,0:T(8,128)(2,1)} %collective-permute-done.19, ...), kind=kLoop, calls=%fused_computation.17 | loop fusion | flops 1490944 | bytes 1376256 | tf_op jit(solution)/shard_map/convert_element_type | solution.py:398
  167.2 1.4 collective-permute-done.26
  168.6 1.1 collective-permute-done.25
  169.7 1.8 %fusion.7 = bf16[224,512]{1,0:T(8,128)(2,1)} fusion(bf16[224,512]{1,0:T(8,128)(2,1)S(1)} %collective-permute-done.26, bf16[224,512]{1,0:T(8,128)(2,1)S(1)} %collective-permute-done.25, bf16[224,512]{1,0:T(8,128)(2,1)S(1)} %collective-permute-done.24, bf16[4,224,512]{2,1,0:T(8,128)(2,1)} %collective-permute-done.23, bf16[4,224,512]{2,1,0:T(8,128)(2,1)S(1)} %get-tuple-element.49), kind=kLoop, calls=%fused_computation.12 | loop fusion | flops 1490944 | bytes 1376256 | tf_op jit(solution)/shard_map/convert_element_type | solution.py:398
  171.5 0.7 fusion.24
  (65 shorter events, 6.2 us)
Async XLA Ops:
  0.6 40.8 %copy-start.10 = (bf16[256,256]{1,0:T(8,128)(2,1)S(1)}, bf16[256,256]{1,0:T(8,128)(2,1)}, u32[]{:S(2)}) copy-start(bf16[256,256]{1,0:T(8,128)(2,1)} %constant.76.clone.swap) | copy-start | bytes 393220
  0.6 40.8 %copy-start.7 = (s32[3,224]{1,0:T(4,128)S(1)}, s32[3,224]{1,0:T(4,128)}, u32[]{:S(2)}) copy-start(s32[3,224]{1,0:T(4,128)} %idx.5) | copy-start | bytes 8068
  0.7 40.7 %copy-start.4 = (bf16[224,4096]{1,0:T(8,128)(2,1)S(1)}, bf16[224,4096]{1,0:T(8,128)(2,1)}, u32[]{:S(2)}) copy-start(bf16[224,4096]{1,0:T(8,128)(2,1)} %g_ref.1) | copy-start | bytes 5505028
  1.6 7.8 %collective-permute-start = (bf16[8,4096]{1,0:T(8,128)(2,1)S(1)}, bf16[8,4096]{1,0:T(8,128)(2,1)S(1)}, u32[]{:S(2)}, u32[]{:S(2)}) collective-permute-start(bf16[8,4096]{1,0:T(8,128)(2,1)S(1)} %pad_maximum_fusion.1), channel_id=1, source_target_pairs={{1,0},{2,1},{3,2},{4,3},{5,4},{6,5},{7,6},{0,7},{9,8},{10,9},{11,1... | collective-permute-start | bytes 196616 | tf_op jit(solution)/shard_map/ppermute | solution.py:366
  7.6 5.5 %collective-permute-start.4 = (bf16[8,4096]{1,0:T(8,128)(2,1)S(1)}, bf16[8,4096]{1,0:T(8,128)(2,1)S(1)}, u32[]{:S(2)}, u32[]{:S(2)}) collective-permute-start(bf16[8,4096]{1,0:T(8,128)(2,1)S(1)} %pad_maximum_fusion.1), channel_id=1, source_target_pairs={{7,0},{0,1},{1,2},{2,3},{3,4},{4,5},{5,6},{6,7},{15,8},{8,9},{9,10... | collective-permute-start | bytes 196616 | tf_op jit(solution)/shard_map/ppermute | solution.py:366
  9.5 5.5 %collective-permute-start.1 = (bf16[8,4096]{1,0:T(8,128)(2,1)S(1)}, bf16[8,4096]{1,0:T(8,128)(2,1)S(1)}, u32[]{:S(2)}, u32[]{:S(2)}) collective-permute-start(bf16[8,4096]{1,0:T(8,128)(2,1)S(1)} %collective-permute-done), channel_id=1, source_target_pairs={{1,0},{2,1},{3,2},{4,3},{5,4},{6,5},{7,6},{0,7},{9,8},{10,9},{11,1... | collective-permute-start | bytes 196616 | tf_op jit(solution)/shard_map/ppermute | solution.py:366
  13.0 5.5 %collective-permute-start.5 = (bf16[8,4096]{1,0:T(8,128)(2,1)S(1)}, bf16[8,4096]{1,0:T(8,128)(2,1)S(1)}, u32[]{:S(2)}, u32[]{:S(2)}) collective-permute-start(bf16[8,4096]{1,0:T(8,128)(2,1)S(1)} %collective-permute-done.4), channel_id=1, source_target_pairs={{7,0},{0,1},{1,2},{2,3},{3,4},{4,5},{5,6},{6,7},{15,8},{8,9},{9,10... | collective-permute-start | bytes 196616 | tf_op jit(solution)/shard_map/ppermute | solution.py:366
  14.9 5.5 %collective-permute-start.2 = (bf16[8,4096]{1,0:T(8,128)(2,1)S(1)}, bf16[8,4096]{1,0:T(8,128)(2,1)S(1)}, u32[]{:S(2)}, u32[]{:S(2)}) collective-permute-start(bf16[8,4096]{1,0:T(8,128)(2,1)S(1)} %collective-permute-done.1), channel_id=1, source_target_pairs={{1,0},{2,1},{3,2},{4,3},{5,4},{6,5},{7,6},{0,7},{9,8},{10,9},{11,1... | collective-permute-start | bytes 196616 | tf_op jit(solution)/shard_map/ppermute | solution.py:366
  18.5 8.0 %collective-permute-start.6 = (bf16[8,4096]{1,0:T(8,128)(2,1)S(1)}, bf16[8,4096]{1,0:T(8,128)(2,1)S(1)}, u32[]{:S(2)}, u32[]{:S(2)}) collective-permute-start(bf16[8,4096]{1,0:T(8,128)(2,1)S(1)} %collective-permute-done.5), channel_id=1, source_target_pairs={{7,0},{0,1},{1,2},{2,3},{3,4},{4,5},{5,6},{6,7},{15,8},{8,9},{9,10... | collective-permute-start | bytes 196616 | tf_op jit(solution)/shard_map/ppermute | solution.py:366
  20.4 5.5 %collective-permute-start.3 = (bf16[8,4096]{1,0:T(8,128)(2,1)S(1)}, bf16[8,4096]{1,0:T(8,128)(2,1)S(1)}, u32[]{:S(2)}, u32[]{:S(2)}) collective-permute-start(bf16[8,4096]{1,0:T(8,128)(2,1)S(1)} %collective-permute-done.2), channel_id=1, source_target_pairs={{1,0},{2,1},{3,2},{4,3},{5,4},{6,5},{7,6},{0,7},{9,8},{10,9},{11,1... | collective-permute-start | bytes 196616 | tf_op jit(solution)/shard_map/ppermute | solution.py:366
  36.3 24.2 %copy-start.8 = (bf16[256,512]{1,0:T(8,128)(2,1)S(1)}, bf16[256,512]{1,0:T(8,128)(2,1)}, u32[]{:S(2)}) copy-start(bf16[256,512]{1,0:T(8,128)(2,1)} %constant.80.clone.hsplit_t) | copy-start | bytes 786436
  36.4 24.2 %copy-start.3 = (bf16[256,256]{1,0:T(8,128)(2,1)S(1)}, bf16[256,256]{1,0:T(8,128)(2,1)}, u32[]{:S(2)}) copy-start(bf16[256,256]{1,0:T(8,128)(2,1)} %constant.78.clone.fsplit_t.fjoin) | copy-start | bytes 393220
  36.4 24.1 %collective-permute-start.9 = (bf16[32,4096]{1,0:T(8,128)(2,1)S(1)}, bf16[32,4096]{1,0:T(8,128)(2,1)S(1)}, u32[]{:S(2)}, u32[]{:S(2)}) collective-permute-start(bf16[32,4096]{1,0:T(8,128)(2,1)S(1)} %reshape.76.t0), channel_id=1, source_target_pairs={{24,0},{25,1},{26,2},{27,3},{28,4},{29,5},{30,6},{31,7},{0,8},{1,9... | collective-permute-start | bytes 786440 | tf_op jit(solution)/shard_map/ppermute | solution.py:371
  38.0 22.5 %collective-permute-start.8 = (bf16[32,4096]{1,0:T(8,128)(2,1)S(1)}, bf16[32,4096]{1,0:T(8,128)(2,1)S(1)}, u32[]{:S(2)}, u32[]{:S(2)}) collective-permute-start(bf16[32,4096]{1,0:T(8,128)(2,1)S(1)} %reshape.76.t0), channel_id=1, source_target_pairs={{16,0},{17,1},{18,2},{19,3},{20,4},{21,5},{22,6},{23,7},{24,8},{25... | collective-permute-start | bytes 786440 | tf_op jit(solution)/shard_map/ppermute | solution.py:371
  39.0 21.5 %collective-permute-start.7 = (bf16[32,4096]{1,0:T(8,128)(2,1)S(1)}, bf16[32,4096]{1,0:T(8,128)(2,1)S(1)}, u32[]{:S(2)}, u32[]{:S(2)}) collective-permute-start(bf16[32,4096]{1,0:T(8,128)(2,1)S(1)} %reshape.76.t0), channel_id=1, source_target_pairs={{8,0},{9,1},{10,2},{11,3},{12,4},{13,5},{14,6},{15,7},{16,8},{17,9... | collective-permute-start | bytes 786440 | tf_op jit(solution)/shard_map/ppermute | solution.py:371
  41.4 1.5 copy-start.5
  42.9 1.5 copy-start.6
  52.4 1.8 %copy-start = (bf16[2048,896]{1,0:T(8,128)(2,1)}, bf16[2048,896]{1,0:T(8,128)(2,1)S(1)}, u32[]{:S(2)}) copy-start(bf16[2048,896]{1,0:T(8,128)(2,1)S(1)} %get-tuple-element.29.pg) | copy-start | bytes 11010052
  54.2 1.8 %copy-start.1 = (bf16[2048,896]{1,0:T(8,128)(2,1)}, bf16[2048,896]{1,0:T(8,128)(2,1)S(1)}, u32[]{:S(2)}) copy-start(bf16[2048,896]{1,0:T(8,128)(2,1)S(1)} %get-tuple-element.30.pu) | copy-start | bytes 11010052
  57.0 20.5 %collective-permute-start.15 = (bf16[32,4096]{1,0:T(8,128)(2,1)S(1)}, bf16[32,4096]{1,0:T(8,128)(2,1)S(1)}, u32[]{:S(2)}, u32[]{:S(2)}) collective-permute-start(bf16[32,4096]{1,0:T(8,128)(2,1)S(1)} %reshape.78.c0), channel_id=1, source_target_pairs={{24,0},{25,1},{26,2},{27,3},{28,4},{29,5},{30,6},{31,7},{0,8},{1,9... | collective-permute-start | bytes 786440 | tf_op jit(solution)/shard_map/ppermute | solution.py:371
  57.1 21.1 %collective-permute-start.14 = (bf16[32,4096]{1,0:T(8,128)(2,1)S(1)}, bf16[32,4096]{1,0:T(8,128)(2,1)S(1)}, u32[]{:S(2)}, u32[]{:S(2)}) collective-permute-start(bf16[32,4096]{1,0:T(8,128)(2,1)S(1)} %reshape.78.c0), channel_id=1, source_target_pairs={{16,0},{17,1},{18,2},{19,3},{20,4},{21,5},{22,6},{23,7},{24,8},{25... | collective-permute-start | bytes 786440 | tf_op jit(solution)/shard_map/ppermute | solution.py:371
  60.5 17.7 %collective-permute-start.13 = (bf16[32,4096]{1,0:T(8,128)(2,1)S(1)}, bf16[32,4096]{1,0:T(8,128)(2,1)S(1)}, u32[]{:S(2)}, u32[]{:S(2)}) collective-permute-start(bf16[32,4096]{1,0:T(8,128)(2,1)S(1)} %reshape.78.c0), channel_id=1, source_target_pairs={{8,0},{9,1},{10,2},{11,3},{12,4},{13,5},{14,6},{15,7},{16,8},{17,9... | collective-permute-start | bytes 786440 | tf_op jit(solution)/shard_map/ppermute | solution.py:371
  60.5 1.0 copy-start.9
  61.5 0.9 copy-start.12
  62.4 15.8 %copy-start.11 = (bf16[256,256]{1,0:T(8,128)(2,1)S(1)}, bf16[256,256]{1,0:T(8,128)(2,1)}, u32[]{:S(2)}) copy-start(bf16[256,256]{1,0:T(8,128)(2,1)} %constant.76.clone.swap) | copy-start | bytes 393220
  74.0 16.0 %copy-start.2 = (bf16[256,512]{1,0:T(8,128)(2,1)S(1)}, bf16[256,512]{1,0:T(8,128)(2,1)}, u32[]{:S(2)}) copy-start(bf16[256,512]{1,0:T(8,128)(2,1)} %constant.81.clone.hjoin) | copy-start | bytes 786436
  74.0 50.8 %collective-permute-start.10 = (bf16[32,4096]{1,0:T(8,128)(2,1)S(1)}, bf16[32,4096]{1,0:T(8,128)(2,1)S(1)}, u32[]{:S(2)}, u32[]{:S(2)}) collective-permute-start(bf16[32,4096]{1,0:T(8,128)(2,1)S(1)} %get-tuple-element.33), channel_id=1, source_target_pairs={{24,0},{25,1},{26,2},{27,3},{28,4},{29,5},{30,6},{31,7},{0,8},{1,9... | collective-permute-start | bytes 786440 | tf_op jit(solution)/shard_map/ppermute | solution.py:371
  76.1 48.8 %collective-permute-start.11 = (bf16[32,4096]{1,0:T(8,128)(2,1)S(1)}, bf16[32,4096]{1,0:T(8,128)(2,1)S(1)}, u32[]{:S(2)}, u32[]{:S(2)}) collective-permute-start(bf16[32,4096]{1,0:T(8,128)(2,1)S(1)} %get-tuple-element.34), channel_id=1, source_target_pairs={{16,0},{17,1},{18,2},{19,3},{20,4},{21,5},{22,6},{23,7},{24,8},{25... | collective-permute-start | bytes 786440 | tf_op jit(solution)/shard_map/ppermute | solution.py:371
  77.5 47.4 %collective-permute-start.12 = (bf16[32,4096]{1,0:T(8,128)(2,1)S(1)}, bf16[32,4096]{1,0:T(8,128)(2,1)S(1)}, u32[]{:S(2)}, u32[]{:S(2)}) collective-permute-start(bf16[32,4096]{1,0:T(8,128)(2,1)S(1)} %get-tuple-element.35), channel_id=1, source_target_pairs={{8,0},{9,1},{10,2},{11,3},{12,4},{13,5},{14,6},{15,7},{16,8},{17,9... | collective-permute-start | bytes 786440 | tf_op jit(solution)/shard_map/ppermute | solution.py:371
  104.0 21.5 %collective-permute-start.16 = (bf16[32,4096]{1,0:T(8,128)(2,1)S(1)}, bf16[32,4096]{1,0:T(8,128)(2,1)S(1)}, u32[]{:S(2)}, u32[]{:S(2)}) collective-permute-start(bf16[32,4096]{1,0:T(8,128)(2,1)S(1)} %get-tuple-element.41), channel_id=1, source_target_pairs={{24,0},{25,1},{26,2},{27,3},{28,4},{29,5},{30,6},{31,7},{0,8},{1,9... | collective-permute-start | bytes 786440 | tf_op jit(solution)/shard_map/ppermute | solution.py:371
  105.4 20.3 %collective-permute-start.17 = (bf16[32,4096]{1,0:T(8,128)(2,1)S(1)}, bf16[32,4096]{1,0:T(8,128)(2,1)S(1)}, u32[]{:S(2)}, u32[]{:S(2)}) collective-permute-start(bf16[32,4096]{1,0:T(8,128)(2,1)S(1)} %get-tuple-element.42), channel_id=1, source_target_pairs={{16,0},{17,1},{18,2},{19,3},{20,4},{21,5},{22,6},{23,7},{24,8},{25... | collective-permute-start | bytes 786440 | tf_op jit(solution)/shard_map/ppermute | solution.py:371
  124.8 6.4 %collective-permute-start.18 = (bf16[32,4096]{1,0:T(8,128)(2,1)S(1)}, bf16[32,4096]{1,0:T(8,128)(2,1)S(1)}, u32[]{:S(2)}, u32[]{:S(2)}) collective-permute-start(bf16[32,4096]{1,0:T(8,128)(2,1)S(1)} %get-tuple-element.43), channel_id=1, source_target_pairs={{8,0},{9,1},{10,2},{11,3},{12,4},{13,5},{14,6},{15,7},{16,8},{17,9... | collective-permute-start | bytes 786440 | tf_op jit(solution)/shard_map/ppermute | solution.py:371
  124.8 14.3 %collective-permute-start.27 = (bf16[4,224,512]{2,1,0:T(8,128)(2,1)}, bf16[4,224,512]{2,1,0:T(8,128)(2,1)}, u32[]{:S(2)}, u32[]{:S(2)}) collective-permute-start(bf16[4,224,512]{2,1,0:T(8,128)(2,1)} %get-tuple-element.52), channel_id=1, source_target_pairs={{32,0},{0,32},{96,64},{64,96},{160,128},{128,160},{224,192},{192,2... | collective-permute-start | bytes 2752520 | tf_op jit(solution)/shard_map/ppermute | solution.py:381
  124.9 20.7 %collective-permute-start.19 = (bf16[4,224,512]{2,1,0:T(8,128)(2,1)}, bf16[4,224,512]{2,1,0:T(8,128)(2,1)}, u32[]{:S(2)}, u32[]{:S(2)}) collective-permute-start(bf16[4,224,512]{2,1,0:T(8,128)(2,1)} %get-tuple-element.48), channel_id=1, source_target_pairs={{32,0},{0,32},{96,64},{64,96},{160,128},{128,160},{224,192},{192,2... | collective-permute-start | bytes 2752520 | tf_op jit(solution)/shard_map/ppermute | solution.py:381
  125.6 22.1 %collective-permute-start.23 = (bf16[4,224,512]{2,1,0:T(8,128)(2,1)}, bf16[4,224,512]{2,1,0:T(8,128)(2,1)}, u32[]{:S(2)}, u32[]{:S(2)}) collective-permute-start(bf16[4,224,512]{2,1,0:T(8,128)(2,1)} %get-tuple-element.50), channel_id=1, source_target_pairs={{32,0},{0,32},{96,64},{64,96},{160,128},{128,160},{224,192},{192,2... | collective-permute-start | bytes 2752520 | tf_op jit(solution)/shard_map/ppermute | solution.py:381
  134.3 37.2 %all-to-all-start = ((bf16[8,8,4096]{2,1,0:T(8,128)(2,1)}), bf16[8,8,4096]{2,1,0:T(8,128)(2,1)S(1)}, u32[]{:S(2)}, u32[]{:S(2)}) async-start(bf16[8,8,4096]{2,1,0:T(8,128)(2,1)} %pad_maximum_fusion), calls=%async_computation | async-start | bytes 1048576 | tf_op jit(solution)/shard_map/all_to_all | solution.py:433
  140.5 14.2 %collective-permute-start.28 = (bf16[224,512]{1,0:T(8,128)(2,1)S(1)}, bf16[224,512]{1,0:T(8,128)(2,1)S(1)}, u32[]{:S(2)}, u32[]{:S(2)}) collective-permute-start(bf16[224,512]{1,0:T(8,128)(2,1)S(1)} %get-tuple-element.53), channel_id=1, source_target_pairs={{192,0},{224,32},{0,64},{32,96},{64,128},{96,160},{128,192},{160,2... | collective-permute-start | bytes 688136 | tf_op jit(solution)/shard_map/ppermute | solution.py:376
  142.1 14.3 %collective-permute-start.30 = (bf16[224,512]{1,0:T(8,128)(2,1)S(1)}, bf16[224,512]{1,0:T(8,128)(2,1)S(1)}, u32[]{:S(2)}, u32[]{:S(2)}) collective-permute-start(bf16[224,512]{1,0:T(8,128)(2,1)S(1)} %get-tuple-element.54), channel_id=1, source_target_pairs={{64,0},{96,32},{128,64},{160,96},{192,128},{224,160},{0,192},{32,2... | collective-permute-start | bytes 688136 | tf_op jit(solution)/shard_map/ppermute | solution.py:376
  143.8 12.5 %collective-permute-start.29 = (bf16[224,512]{1,0:T(8,128)(2,1)S(1)}, bf16[224,512]{1,0:T(8,128)(2,1)S(1)}, u32[]{:S(2)}, u32[]{:S(2)}) collective-permute-start(bf16[224,512]{1,0:T(8,128)(2,1)S(1)} %get-tuple-element.55), channel_id=1, source_target_pairs={{128,0},{160,32},{192,64},{224,96},{0,128},{32,160},{64,192},{96,2... | collective-permute-start | bytes 688136 | tf_op jit(solution)/shard_map/ppermute | solution.py:376
  147.0 14.4 %collective-permute-start.20 = (bf16[224,512]{1,0:T(8,128)(2,1)S(1)}, bf16[224,512]{1,0:T(8,128)(2,1)S(1)}, u32[]{:S(2)}, u32[]{:S(2)}) collective-permute-start(bf16[224,512]{1,0:T(8,128)(2,1)S(1)} %get-tuple-element.59), channel_id=1, source_target_pairs={{192,0},{224,32},{0,64},{32,96},{64,128},{96,160},{128,192},{160,2... | collective-permute-start | bytes 688136 | tf_op jit(solution)/shard_map/ppermute | solution.py:376
  147.6 16.0 %collective-permute-start.22 = (bf16[224,512]{1,0:T(8,128)(2,1)S(1)}, bf16[224,512]{1,0:T(8,128)(2,1)S(1)}, u32[]{:S(2)}, u32[]{:S(2)}) collective-permute-start(bf16[224,512]{1,0:T(8,128)(2,1)S(1)} %get-tuple-element.60), channel_id=1, source_target_pairs={{64,0},{96,32},{128,64},{160,96},{192,128},{224,160},{0,192},{32,2... | collective-permute-start | bytes 688136 | tf_op jit(solution)/shard_map/ppermute | solution.py:376
  154.7 10.1 %collective-permute-start.21 = (bf16[224,512]{1,0:T(8,128)(2,1)S(1)}, bf16[224,512]{1,0:T(8,128)(2,1)S(1)}, u32[]{:S(2)}, u32[]{:S(2)}) collective-permute-start(bf16[224,512]{1,0:T(8,128)(2,1)S(1)} %get-tuple-element.61), channel_id=1, source_target_pairs={{128,0},{160,32},{192,64},{224,96},{0,128},{32,160},{64,192},{96,2... | collective-permute-start | bytes 688136 | tf_op jit(solution)/shard_map/ppermute | solution.py:376
  156.3 10.8 %collective-permute-start.24 = (bf16[224,512]{1,0:T(8,128)(2,1)S(1)}, bf16[224,512]{1,0:T(8,128)(2,1)S(1)}, u32[]{:S(2)}, u32[]{:S(2)}) collective-permute-start(bf16[224,512]{1,0:T(8,128)(2,1)S(1)} %get-tuple-element.56), channel_id=1, source_target_pairs={{192,0},{224,32},{0,64},{32,96},{64,128},{96,160},{128,192},{160,2... | collective-permute-start | bytes 688136 | tf_op jit(solution)/shard_map/ppermute | solution.py:376
  156.3 12.2 %collective-permute-start.26 = (bf16[224,512]{1,0:T(8,128)(2,1)S(1)}, bf16[224,512]{1,0:T(8,128)(2,1)S(1)}, u32[]{:S(2)}, u32[]{:S(2)}) collective-permute-start(bf16[224,512]{1,0:T(8,128)(2,1)S(1)} %get-tuple-element.57), channel_id=1, source_target_pairs={{64,0},{96,32},{128,64},{160,96},{192,128},{224,160},{0,192},{32,2... | collective-permute-start | bytes 688136 | tf_op jit(solution)/shard_map/ppermute | solution.py:376
  161.4 8.3 %collective-permute-start.25 = (bf16[224,512]{1,0:T(8,128)(2,1)S(1)}, bf16[224,512]{1,0:T(8,128)(2,1)S(1)}, u32[]{:S(2)}, u32[]{:S(2)}) collective-permute-start(bf16[224,512]{1,0:T(8,128)(2,1)S(1)} %get-tuple-element.58), channel_id=1, source_target_pairs={{128,0},{160,32},{192,64},{224,96},{0,128},{32,160},{64,192},{96,2... | collective-permute-start | bytes 688136 | tf_op jit(solution)/shard_map/ppermute | solution.py:376
where the time goes:
time: 174 us; the launch traced here: 172 us
  Pallas kernels  61.5 us (35%)
  starting transfers between devices  53.6 us (31%)
  local copies, waits for them, and re-layouts  22 us (13%)
  waiting for transfers between devices  18.5 us (11%)
  other arithmetic  15.8 us (9%)
    ppermute x12, starting transfers between devices, from_y(): return lax.ppermute(value, 'fsdp', pairs)  17.4 us
    ppermute x7, starting transfers between devices, from_z(): return lax.ppermute(value, 'fsdp', pairs)  16.7 us
    unnamed x39, local copies, waits for them, and re-layouts  16.6 us
    pallas_call x1, Pallas kernels, inward_grads(): pl.pallas_call(inward_kernel, in_specs=smem(2) + vm(4), out_specs=vm(4),...  16 us
    pallas_call x1, Pallas kernels, deltas(): pl.pallas_call(delta_kernel, in_specs=vm(8), out_specs=vm(6), out_shape=[...  14 us
    ppermute x9, starting transfers between devices, from_x(): return lax.ppermute(value, 'dp', pairs)  14 us
    pallas_call x1, Pallas kernels, down_grads(): pl.pallas_call(down_kernel, in_specs=smem(2) + vm(6), out_specs=vm(3), ou...  11.8 us
    pallas_call x1, Pallas kernels, forward(): pl.pallas_call(forward_kernel, in_specs=vm(11), out_specs=vm(8), out_shap...  11.6 us
  transfers between devices with their start and end apart: 32, of which 11 were waited for; matrix products, arithmetic and copies ran while one was open for 10% of the time, Pallas kernels for 36%

commit v1 on v0

v1 whole, which is shorter than its diff:
```python
import functools

import jax
import jax.numpy as jnp
import numpy as np
from jax import lax
from jax.experimental import pallas as pl
from jax.experimental.pallas import tpu as pltpu
from jax.sharding import PartitionSpec as P

D = 4096
BLK = 64
KEEP = 32
COLS = 7
SLOT = COLS * KEEP
TOK = 128
FEAT = 2048
WIDE = COLS * 128
NX, NC, NY, NZ = 4, 2, 4, 8
BF = jnp.bfloat16
F32 = jnp.float32

TILE_ROWS = [[8 * x + 4 * c + k4 for x in range(NX) for k4 in range(4)] for c in range(NC)]
ORDER = TILE_ROWS[0] + TILE_ROWS[1]


def swap_matrix():
    m = np.zeros((256, 256), np.float32)
    for a in range(16):
        for b in range(16):
            m[a * 16 + b, b * 16 + a] = 1
    return m


def feature_split():
    m = np.zeros((256, 256), np.float32)
    for i in range(4):
        for p in range(2):
            for n, k in enumerate(ORDER):
                m[i * 64 + 2 * k + p, p * 128 + i * 32 + n] = 1
    return m


def feature_turn(core):
    m = np.zeros((256, 256), np.float32)
    for rel in range(2):
        for p in range(2):
            for i in range(4):
                for n, k in enumerate(TILE_ROWS[core ^ rel]):
                    m[rel * 128 + p * 64 + i * 16 + n, i * 64 + 2 * k + p] = 1
    return m


def hidden_split():
    m = np.zeros((512, 256), np.float32)
    for j in range(4):
        for p in range(2):
            for n, k in enumerate(ORDER):
                m[j * 128 + 2 * k + p, p * 128 + j * 32 + n] = 1
    return m


def hidden_turn(core):
    m = np.zeros((256, 512), np.float32)
    for rel in range(2):
        for p in range(2):
            for j in range(4):
                for n, k in enumerate(TILE_ROWS[core ^ rel]):
                    m[rel * 128 + p * 64 + j * 16 + n, j * 128 + 2 * k + p] = 1
    return m


def hidden_join():
    m = np.zeros((256, 512), np.float32)
    for j in range(4):
        for p in range(2):
            for n, k in enumerate(ORDER):
                for h in range(2):
                    m[p * 128 + j * 32 + n, j * 128 + h * 64 + 2 * k + p] = 1
    return m


def wire_swap(x):
    m = np.zeros((256, 256), np.float32)
    for rel in range(NX):
        for k4 in range(4):
            for q in range(16):
                m[rel * 64 + k4 * 16 + q, q * 16 + (rel ^ x) * 4 + k4] = 1
    return m


SWAP = swap_matrix()
FSPLIT = feature_split()
FTURN = np.stack([feature_turn(0), feature_turn(1)])
HSPLIT = hidden_split()
HTURN = np.stack([hidden_turn(0), hidden_turn(1)])
HJOIN = hidden_join()
WSWAP = np.stack([wire_swap(x) for x in range(NX)])


def mm(a, b):
    return jnp.dot(a, b, preferred_element_type=F32)


def mm_nt(a, b):
    return lax.dot_general(a, b, (((1,), (1,)), ((), ())), preferred_element_type=F32)


def low_half(shape):
    return lax.broadcasted_iota(jnp.int32, shape, 1) < 64


def vm(n):
    return [pl.BlockSpec(memory_space=pltpu.VMEM)] * n


def smem(n):
    return [pl.BlockSpec(memory_space=pltpu.SMEM)] * n


def params(mib):
    return pltpu.CompilerParams(vmem_limit_bytes=mib << 20)


def cost(us):
    return pl.CostEstimate(flops=us * 100_000_000, bytes_accessed=us * 100_000, transcendentals=0)


def shape(*dims, dtype=BF):
    return jax.ShapeDtypeStruct(dims, dtype)


def prep_kernel(idx, g_ref, u_ref, d_ref, swap, pg, pu, pd, scr):
    j = pl.program_id(0)
    pd[...] = jnp.zeros_like(pd)

    @pl.when(j < COLS)
    def _():
        pg[...] = jnp.zeros_like(pg)
        pu[...] = jnp.zeros_like(pu)
        for m, src in enumerate((g_ref, u_ref, d_ref)):
            for qh in range(2):
                rows = slice(qh * 16, qh * 16 + 16)
                halves = [
                    jnp.concatenate([src[rows, k * 128:k * 128 + 128] for k in TILE_ROWS[c]], axis=0)
                    for c in range(2)
                ]
                tiles = scr.at[2 * m + qh]
                tiles[...] = mm(swap[...], jnp.concatenate(halves, axis=1)).astype(BF)
                for q in range(16):
                    i = idx[m, j * KEEP + qh * 16 + q]
                    for c in range(2):
                        tile = tiles[q * 16:q * 16 + 16, c * 128:c * 128 + 128]
                        if m == 2:
                            pd[c * 16:c * 16 + 16, pl.ds(pl.multiple_of(i * 128, 128), 128)] = tile
                        else:
                            dst = pg if m == 0 else pu
                            dst[pl.ds(pl.multiple_of(i * 32 + c * 16, 16), 16), :] = tile


def prep(idx, gate, up, down):
    blocks = pl.BlockSpec((KEEP, D), lambda j, s: (jnp.minimum(j, COLS - 1), 0))
    panel = pl.BlockSpec((FEAT, 128), lambda j, s: (0, jnp.minimum(j, COLS - 1)))
    return pl.pallas_call(
        prep_kernel,
        grid_spec=pltpu.PrefetchScalarGridSpec(
            num_scalar_prefetch=1,
            grid=(COLS + 1,),
            in_specs=[blocks, blocks, blocks, pl.BlockSpec((256, 256), lambda j, s: (0, 0))],
            out_specs=[panel, panel, pl.BlockSpec((KEEP, 2 * D), lambda j, s: (j, 0))],
            scratch_shapes=[pltpu.VMEM((6, 256, 256), BF)],
        ),
        out_shape=[shape(FEAT, WIDE), shape(FEAT, WIDE), shape(256, 2 * D)],
        compiler_params=params(12),
        cost_estimate=cost(2),
        name="prep",
    )(idx, gate, up, down, jnp.asarray(SWAP, BF))


def forward_kernel(t0, t1, t2, t3, pg, pu, pd, fsplit, fturn, hsplit, hturn,
                   xt_own, xt_sib, ht_own, ht_sib, gl2, ul2, o0, o1, o2, o3, tok, xx, hid, hh):
    for n, piece in enumerate((t0, t1, t2, t3)):
        tok[n * 32:n * 32 + 32, :] = piece[...]
    for c in range(16):
        chunk = tok[:, c * 256:c * 256 + 256]
        split = mm(chunk, fsplit[...]).astype(BF)
        turned = mm_nt(fturn[...], chunk).astype(BF)
        for p in range(2):
            xx[p * 128:p * 128 + 128, c * 128:c * 128 + 128] = split[:, p * 128:p * 128 + 128]
            at = p * 1024 + c * 64
            xt_own[at:at + 64, :] = turned[p * 64:p * 64 + 64, :]
            xt_sib[at:at + 64, :] = turned[128 + p * 64:128 + p * 64 + 64, :]
    low = low_half((TOK, 128))
    hid[:, WIDE:] = jnp.zeros((TOK, 128), BF)
    for n in range(0, WIDE, 256):
        width = min(256, WIDE - n)
        gate = mm(xx[...], pg[:, n:n + width])
        up = mm(xx[...], pu[:, n:n + width])
        for s in range(0, width, 128):
            cols = slice(n + s, n + s + 128)
            gl = jnp.where(low, gate[:TOK, s:s + 128], gate[TOK:, s:s + 128])
            gl = gl + pltpu.roll(gl, 64, 1)
            ul = jnp.where(low, up[:TOK, s:s + 128], up[TOK:, s:s + 128])
            ul = ul + pltpu.roll(ul, 64, 1)
            gl2[:, cols] = gl
            ul2[:, cols] = ul
            hid[:, cols] = (gl * (1.0 / (1.0 + jnp.exp(-gl))) * ul).astype(BF)
    for g in range(2):
        group = hid[:, g * 512:g * 512 + 512]
        split = mm(group, hsplit[...]).astype(BF)
        turned = mm_nt(hturn[...], group).astype(BF)
        for p in range(2):
            hh[p * 128:p * 128 + 128, g * 128:g * 128 + 128] = split[:, p * 128:p * 128 + 128]
            at = p * 128 + g * 64
            ht_own[at:at + 64, :] = turned[p * 64:p * 64 + 64, :]
            ht_sib[at:at + 64, :] = turned[128 + p * 64:128 + p * 64 + 64, :]

    def step(n, carry):
        out = mm(hh[...], pd[:, pl.ds(pl.multiple_of(n * 1024, 1024), 1024)])
        parts = []
        for m in range(4):
            a0, a1 = out[:TOK, m * 256:m * 256 + 128], out[TOK:, m * 256:m * 256 + 128]
            b0, b1 = out[:TOK, m * 256 + 128:m * 256 + 256], out[TOK:, m * 256 + 128:m * 256 + 256]
            parts.append(jnp.where(low, a0, b1) + pltpu.roll(jnp.where(low, b0, a1), 64, 1))
        whole = jnp.concatenate(parts, axis=1).astype(BF)
        for r, dst in enumerate((o0, o1, o2, o3)):
            dst[:, pl.ds(pl.multiple_of(n * 512, 512), 512)] = whole[r * 32:r * 32 + 32, :]
        return carry

    lax.fori_loop(0, 8, step, 0)


def forward(pieces, pg, pu, pd, fturn, hturn):
    lin = shape(TOK, WIDE, dtype=F32)
    return pl.pallas_call(
        forward_kernel,
        in_specs=vm(11),
        out_specs=vm(10),
        out_shape=[shape(FEAT, TOK)] * 2 + [shape(256, TOK)] * 2 + [lin, lin] + [shape(32, D)] * 4,
        scratch_shapes=[
            pltpu.VMEM((TOK, D), BF),
            pltpu.VMEM((256, FEAT), BF),
            pltpu.VMEM((TOK, 1024), BF),
            pltpu.VMEM((256, 256), BF),
        ],
        compiler_params=params(24),
        cost_estimate=cost(3),
        name="forward",
    )(*pieces, pg, pu, pd, jnp.asarray(FSPLIT, BF), fturn, jnp.asarray(HSPLIT, BF), hturn)


def emit(wswap, tiles, parts, j):
    turned = mm(wswap[...], tiles[...]).astype(BF)
    for rel, dst in enumerate(parts):
        for k in range(4):
            top = (rel * 4 + k) * 16
            for half in range(2):
                dst[j * KEEP + half * 16:j * KEEP + half * 16 + 16, k * 128:k * 128 + 128] = turned[
                    top:top + 16, half * 128:half * 128 + 128
                ]


def down_kernel(idx, c0, c1, c2, c3, d0, d1, d2, d3, ht_own, ht_oth, wswap, w0, w1, w2, w3, both, part, tiles):
    for n, piece in enumerate((c0, c1, c2, c3, d0, d1, d2, d3)):
        both[n * 32:n * 32 + 32, :] = piece[...]

    def product(n, carry):
        lanes = pl.ds(pl.multiple_of(n * 512, 512), 512)
        hidden = jnp.concatenate([ht_own[...], ht_oth[...]], axis=1)
        part[:, lanes] = mm(hidden, both[:, lanes]).astype(BF)
        return carry

    lax.fori_loop(0, 8, product, 0)
    side = lax.broadcasted_iota(jnp.int32, (16, 128), 1) // 64
    for j in range(COLS):
        for q in range(KEEP):
            i = idx[2, j * KEEP + q]
            odd = lax.rem(i, 2)
            lanes = pl.ds(pl.multiple_of((i // 2) * 128, 128), 128)
            near = part[pl.ds(pl.multiple_of(odd * 128 + j * 16, 16), 16), lanes].astype(F32)
            far = part[pl.ds(pl.multiple_of((1 - odd) * 128 + j * 16, 16), 16), lanes].astype(F32)
            tile = jnp.where(side == odd, near, pltpu.roll(far, 64, 1)).astype(BF)
            tiles[(q % 16) * 16:(q % 16) * 16 + 16, (q // 16) * 128:(q // 16) * 128 + 128] = tile
        emit(wswap, tiles, (w0, w1, w2, w3), j)


def down_grads(idx, pieces, others, ht_own, ht_oth, wswap):
    return pl.pallas_call(
        down_kernel,
        in_specs=smem(1) + vm(11),
        out_specs=vm(4),
        out_shape=[shape(SLOT, 512)] * 4,
        scratch_shapes=[pltpu.VMEM((256, D), BF), pltpu.VMEM((256, D), BF), pltpu.VMEM((256, 256), BF)],
        compiler_params=params(14),
        cost_estimate=cost(2),
        name="down_grads",
    )(idx, *pieces, *others, ht_own, ht_oth, wswap)


def delta_kernel(c0, c1, c2, c3, pd, gl2, ul2, hjoin, gd_own, ud_own, gdx, udx, cx):
    low = low_half((32, 128))
    for n, piece in enumerate((c0, c1, c2, c3)):
        top = slice(n * 32, n * 32 + 32)
        bottom = slice(TOK + n * 32, TOK + n * 32 + 32)
        for m in range(32):
            c = piece[:, m * 128:m * 128 + 128].astype(F32)
            rolled = pltpu.roll(c, 64, 1)
            zero = jnp.zeros_like(c)
            first = slice(2 * m * 128, 2 * m * 128 + 128)
            second = slice(2 * m * 128 + 128, 2 * m * 128 + 256)
            cx[top, first] = jnp.where(low, c, zero).astype(BF)
            cx[bottom, first] = jnp.where(low, zero, rolled).astype(BF)
            cx[top, second] = jnp.where(low, rolled, zero).astype(BF)
            cx[bottom, second] = jnp.where(low, zero, c).astype(BF)

    def product(n, acc):
        lanes = pl.ds(pl.multiple_of(n * 1024, 1024), 1024)
        return acc + mm_nt(cx[:, lanes], pd[:, lanes])

    hd = lax.fori_loop(0, 8, product, jnp.zeros((256, 256), F32))
    high = hd.astype(BF)
    rest = (hd - high.astype(F32)).astype(BF)
    low = low_half((TOK, 128))
    gd_own[:, 384:] = jnp.zeros((TOK, 128), BF)
    ud_own[:, 384:] = jnp.zeros((TOK, 128), BF)
    for g in range(2):
        cols = slice(g * 128, g * 128 + 128)
        joined = sum(
            mm(jnp.concatenate([part[:TOK, cols], part[TOK:, cols]], axis=1), hjoin[...]) for part in (high, rest)
        )
        before = None
        for jl in range(4):
            j = g * 4 + jl
            if j == COLS:
                break
            lanes = slice(j * 128, j * 128 + 128)
            delta = joined[:, jl * 128:jl * 128 + 128]
            gl, ul = gl2[:, lanes], ul2[:, lanes]
            sig = 1.0 / (1.0 + jnp.exp(-gl))
            gd = delta * ul * sig * (1.0 + gl * (1.0 - sig))
            ud = delta * gl * sig
            for dst, val in ((gdx, gd), (udx, ud)):
                dst[:TOK, lanes] = jnp.where(low, val, 0.0).astype(BF)
                dst[TOK:, lanes] = jnp.where(low, 0.0, val).astype(BF)
            pair = slice((j // 2) * 128, (j // 2) * 128 + 128)
            if j % 2:
                gd_own[:, pair] = jnp.where(low, before[0], gd).astype(BF)
                ud_own[:, pair] = jnp.where(low, before[1], ud).astype(BF)
            elif j == COLS - 1:
                gd_own[:, pair] = jnp.where(low, gd, 0.0).astype(BF)
                ud_own[:, pair] = jnp.where(low, ud, 0.0).astype(BF)
            before = (gd, ud)


def deltas(pieces, pd, gl2, ul2):
    return pl.pallas_call(
        delta_kernel,
        in_specs=vm(8),
        out_specs=vm(4),
        out_shape=[shape(TOK, 512)] * 2 + [shape(256, WIDE)] * 2,
        scratch_shapes=[pltpu.VMEM((256, 2 * D), BF)],
        compiler_params=params(18),
        cost_estimate=cost(2),
        name="deltas",
    )(*pieces, pd, gl2, ul2, jnp.asarray(HJOIN, BF))


def back_kernel(gdx, udx, pg, pu, fjoin, i0, i1, i2, i3):
    def back(n, carry):
        rows = pl.ds(pl.multiple_of(n * 256, 256), 256)
        acc = (mm_nt(gdx[...], pg[rows, :]) + mm_nt(udx[...], pu[rows, :])).astype(BF)
        for c in range(2):
            cols = slice(c * 128, c * 128 + 128)
            pair = jnp.concatenate([acc[:TOK, cols], acc[TOK:, cols]], axis=1)
            whole = mm(pair, fjoin[...]).astype(BF)
            lanes = pl.ds(pl.multiple_of(n * 512 + c * 256, 256), 256)
            for r, dst in enumerate((i0, i1, i2, i3)):
                dst[:, lanes] = whole[r * 32:r * 32 + 32, :]
        return carry

    lax.fori_loop(0, 8, back, 0)


def input_parts(gdx, udx, pg, pu):
    return pl.pallas_call(
        back_kernel,
        in_specs=vm(5),
        out_specs=vm(4),
        out_shape=[shape(32, D)] * 4,
        compiler_params=params(18),
        cost_estimate=cost(2),
        name="input_parts",
    )(gdx, udx, pg, pu, jnp.asarray(FSPLIT.T, BF))


def inward_kernel(m, idx, xt_own, xt_oth, d_own, d_oth, wswap, w0, w1, w2, w3, part, tiles):
    delta = jnp.concatenate([d_own[...], d_oth[...]], axis=0)

    def product(n, carry):
        rows = pl.ds(pl.multiple_of(n * 256, 256), 256)
        part[rows, :] = mm(jnp.concatenate([xt_own[rows, :], xt_oth[rows, :]], axis=1), delta).astype(BF)
        return carry

    lax.fori_loop(0, 8, product, 0)
    low = low_half((16, 128))
    for j in range(COLS):
        odd = j % 2
        lanes = slice((j // 2) * 128, (j // 2) * 128 + 128)
        for q in range(KEEP):
            i = idx[m, j * KEEP + q]
            first = part[pl.ds(pl.multiple_of(i * 16, 16), 16), lanes].astype(F32)
            second = part[pl.ds(pl.multiple_of(1024 + i * 16, 16), 16), lanes].astype(F32)
            if odd:
                first = pltpu.roll(first, 64, 1)
            else:
                second = pltpu.roll(second, 64, 1)
            tile = jnp.where(low, first, second).astype(BF)
            tiles[(q % 16) * 16:(q % 16) * 16 + 16, (q // 16) * 128:(q // 16) * 128 + 128] = tile
        emit(wswap, tiles, (w0, w1, w2, w3), j)


def inward_grads(m, idx, xt_own, xt_oth, d_own, d_oth, wswap):
    return pl.pallas_call(
        functools.partial(inward_kernel, m),
        in_specs=smem(1) + vm(5),
        out_specs=vm(4),
        out_shape=[shape(SLOT, 512)] * 4,
        scratch_shapes=[pltpu.VMEM((FEAT, 512), BF), pltpu.VMEM((256, 256), BF)],
        compiler_params=params(14),
        cost_estimate=cost(2),
        name=("gate_grads", "up_grads")[m],
    )(idx, xt_own, xt_oth, d_own, d_oth, wswap)


def from_y(value, step):
    pairs = [((y + step) % NY * NZ + z, y * NZ + z) for y in range(NY) for z in range(NZ)]
    return lax.ppermute(value, "fsdp", pairs)


def from_x(value, other):
    pairs = [((x ^ other) * NC + c, x * NC + c) for x in range(NX) for c in range(NC)]
    return lax.ppermute(value, "dp", pairs)


def from_core(value):
    pairs = [(x * NC + 1 - c, x * NC + c) for x in range(NX) for c in range(NC)]
    return lax.ppermute(value, "dp", pairs)


def over_z(value):
    groups = [[y * NZ + z for z in range(NZ)] for y in range(NY)]
    return lax.all_to_all(value, "fsdp", 0, 0, axis_index_groups=groups, tiled=True)


def total_of(first, others):
    return sum((o.astype(F32) for o in others), first.astype(F32))


def reduce_x(parts):
    total = total_of(parts[0], [from_x(parts[d], d) for d in range(1, NX)])
    return (total * (1.0 / (NX * NC))).astype(BF)


def reduce_yz(pieces):
    rows = pieces[0].shape[0] // NZ
    total = total_of(pieces[0], [from_y(pieces[d], -d) for d in range(1, NY)])
    return over_z(total.astype(BF).reshape(NZ, rows, D)).astype(F32).sum(axis=0).astype(BF)


def body(tokens, cotangent, gate_blocks, up_blocks, down_blocks, block_index):
    rows = tokens.shape[0]
    here = lax.axis_index("dp")
    core, x = here % NC, here // NC
    fturn = jnp.where(core == 0, jnp.asarray(FTURN[0], BF), jnp.asarray(FTURN[1], BF))
    hturn = jnp.where(core == 0, jnp.asarray(HTURN[0], BF), jnp.asarray(HTURN[1], BF))
    wswap = lax.dynamic_index_in_dim(jnp.asarray(WSWAP, BF), x, 0, keepdims=False)

    own = jnp.concatenate([tokens, cotangent], axis=0)
    ring = over_z(jnp.broadcast_to(own[None], (NZ,) + own.shape))
    pg, pu, pd = prep(block_index, gate_blocks, up_blocks, down_blocks)
    tok_z = ring[:, :rows].reshape(NZ * rows, D)
    cot_z = ring[:, rows:].reshape(NZ * rows, D)
    tok = [tok_z] + [from_y(tok_z, s) for s in range(1, NY)]
    cot = [cot_z] + [from_y(cot_z, s) for s in range(1, NY)]
    cot_oth = [from_core(c) for c in cot]

    xt_own, xt_sib, ht_own, ht_sib, gl2, ul2, *out_parts = forward(tok, pg, pu, pd, fturn, hturn)
    xt_oth, ht_oth = from_core(xt_sib), from_core(ht_sib)
    layer_out = reduce_yz(out_parts)
    down_grad = reduce_x(down_grads(block_index, cot, cot_oth, ht_own, ht_oth, wswap))
    gd, ud, gdx, udx = deltas(cot, pd, gl2, ul2)
    gd_oth, ud_oth = from_core(gd), from_core(ud)
    input_grad = reduce_yz(input_parts(gdx, udx, pg, pu))
    gate_grad = reduce_x(inward_grads(0, block_index, xt_own, xt_oth, gd, gd_oth, wswap))
    up_grad = reduce_x(inward_grads(1, block_index, xt_own, xt_oth, ud, ud_oth, wswap))
    return (layer_out, input_grad, gate_grad, up_grad, down_grad)


def solution(mesh):
    return jax.shard_map(
        body,
        mesh=mesh,
        in_specs=(
            P(("dp", "fsdp"), None),
            P(("dp", "fsdp"), None),
            P("fsdp", None),
            P("fsdp", None),
            P("fsdp", None),
            P(None, "fsdp"),
        ),
        out_specs=(
            P(("dp", "fsdp"), None),
            P(("dp", "fsdp"), None),
            P("fsdp", "dp"),
            P("fsdp", "dp"),
            P("fsdp", "dp"),
        ),
        check_vma=False,
    )
```

time: 174 us -> 157 us (0.902)
  blocking collectives: 0 us -> 25.8 us
  Pallas kernels: 61.5 us -> 39.2 us
  starting transfers between devices: 53.6 us -> 43.4 us
  waiting for transfers between devices: 18.5 us -> 13.8 us
  other arithmetic: 15.8 us -> 13.1 us
    all_to_all x0 -> x1, blocking collectives: none -> 25.8 us  [over_z(): lax.all_to_all(value, 'fsdp', 0, 0, axis_index_groups=groups, tiled=True)]
    pallas_call x4 -> x6, Pallas kernels: 53.5 us -> 32 us  [the longest x1 8.88 us: forward(): pl.pallas_call(forward_kernel, in_specs=vm(11), out_specs=vm(10), out_sha...]
    ppermute x7 -> x0, starting transfers between devices: 16.7 us -> none  [from_z(): return lax.ppermute(value, 'fsdp', pairs)]
    all_to_all x1 -> x2, starting transfers between devices: 4.82 us -> 11 us  [over_z(): lax.all_to_all(value, 'fsdp', 0, 0, axis_index_groups=groups, tiled=True)]
    ppermute x7 -> x0, waiting for transfers between devices: 4.21 us -> none  [from_z(): return lax.ppermute(value, 'fsdp', pairs)]
    reduce_sum x1 -> x2, other arithmetic: 0.07 us -> 3.38 us  [reduce_yz(): over_z(total.astype(BF).reshape(NZ, rows, D)).astype(F32).sum(axis=0)]
    convert_element_type x8 -> x5, other arithmetic: 9.75 us -> 6.82 us  [the longest x3 3.62 us: reduce_x(): return (total * (1.0 / (NX * NC))).astype(BF)]
    unnamed x2 -> x0, other arithmetic: 2.86 us -> none
  transfers between devices with their start and end apart: 32 -> 31, of which waited for: 11 -> 5; matrix products, arithmetic and copies ran while one was open for 10% -> 10% of each run, Pallas kernels for 36% -> 25%
where the time goes in v1:
time: 157 us; the launch traced here: 156 us
  starting transfers between devices  43.4 us (28%)
  Pallas kernels  39.2 us (25%)
  blocking collectives  25.8 us (16%)
  local copies, waits for them, and re-layouts  20.3 us (13%)
  waiting for transfers between devices  13.8 us (9%)
  other arithmetic  13.1 us (8%)
    all_to_all x1, blocking collectives, over_z(): lax.all_to_all(value, 'fsdp', 0, 0, axis_index_groups=groups, tiled=True)  25.8 us
    ppermute x12, starting transfers between devices, from_y(): return lax.ppermute(value, 'fsdp', pairs)  18.2 us
    unnamed x56, local copies, waits for them, and re-layouts  14.7 us
    ppermute x9, starting transfers between devices, from_x(): return lax.ppermute(value, 'dp', pairs)  12.5 us
    all_to_all x2, starting transfers between devices, over_z(): lax.all_to_all(value, 'fsdp', 0, 0, axis_index_groups=groups, tiled=True)  11 us
    pallas_call x1, Pallas kernels, forward(): pl.pallas_call(forward_kernel, in_specs=vm(11), out_specs=vm(10), out_sha...  8.88 us
    pallas_call x1, Pallas kernels, prep(): pl.pallas_call(prep_kernel, grid_spec=pltpu.PrefetchScalarGridSpec(num_sc...  7.14 us
    pallas_call x2, Pallas kernels, inward_grads(): pl.pallas_call(functools.partial(inward_kernel, m), in_specs=smem(1) + vm...  6.79 us
  transfers between devices with their start and end apart: 31, of which 5 were waited for; matrix products, arithmetic and copies ran while one was open for 10% of the time, Pallas kernels for 25%

profile of v1, /device:TPU:8, one launch (start us, length us, event | category | flops | bytes accessed | tf_op | source)
XLA Modules:
  0.0 156.4 jit_solution(12613539389677334574)
XLA Ops:
  0.7 0.9 pad_maximum_fusion
  1.6 25.8 %all_to_all.15 = bf16[8,8,4096]{2,1,0:T(8,128)(2,1)S(1)} all-to-all(bf16[8,8,4096]{2,1,0:T(8,128)(2,1)S(1)} %broadcast_in_dim.2), channel_id=1, replica_groups={{0,1,2,3,4,5,6,7},{8,9,10,11,12,13,14,15},{16,17,18,19,20,21,22,23},{24..., dimensions={0} | all-to-all | bytes 1048576 | tf_op jit(solution)/shard_map/all_to_all | solution.py:452
  27.4 1.0 fusion
  28.4 0.5 collective-permute-start
  29.0 2.6 %collective-permute-start.1 = (bf16[32,4096]{1,0:T(8,128)(2,1)S(1)}, bf16[32,4096]{1,0:T(8,128)(2,1)}, u32[]{:S(2)}, u32[]{:S(2)}) collective-permute-start(bf16[32,4096]{1,0:T(8,128)(2,1)S(1)} %reshape.23.t0), channel_id=1, source_target_pairs={{16,0},{17,1},{18,2},{19,3},{20,4},{21,5},{22,6},{23,7},{24,8},{25... | collective-permute-start | bytes 786440 | tf_op jit(solution)/shard_map/ppermute | solution.py:437
  31.5 1.9 %collective-permute-start.2 = (bf16[32,4096]{1,0:T(8,128)(2,1)S(1)}, bf16[32,4096]{1,0:T(8,128)(2,1)}, u32[]{:S(2)}, u32[]{:S(2)}) collective-permute-start(bf16[32,4096]{1,0:T(8,128)(2,1)S(1)} %reshape.23.t0), channel_id=1, source_target_pairs={{24,0},{25,1},{26,2},{27,3},{28,4},{29,5},{30,6},{31,7},{0,8},{1,9... | collective-permute-start | bytes 786440 | tf_op jit(solution)/shard_map/ppermute | solution.py:437
  33.4 1.0 broadcast_select_fusion.hturn
  34.4 1.0 reshape.25.c0
  35.7 1.4 collective-permute-start.7
  37.0 1.4 collective-permute-done.t1
  38.4 0.7 copy-done.13
  39.1 1.0 collective-permute-start.8
  40.1 4.4 %collective-permute-done.1.t2 = bf16[32,4096]{1,0:T(8,128)(2,1)} collective-permute-done((bf16[32,4096]{1,0:T(8,128)(2,1)S(1)}, bf16[32,4096]{1,0:T(8,128)(2,1)}, u32[]{:S(2)}, u32[]{:S(2)}) %collective-permute-start.1) | collective-permute-done | bytes 262176 | tf_op jit(solution)/shard_map/ppermute | solution.py:437
  44.5 0.9 broadcast_select_fusion.1.fturn
  45.5 1.5 copy-done.7
  47.0 1.5 copy-done.8
  48.5 0.9 copy-done.19
  49.4 7.1 %prep.1 = (bf16[2048,896]{1,0:T(8,128)(2,1)S(1)}, bf16[2048,896]{1,0:T(8,128)(2,1)S(1)}, bf16[256,8192]{1,0:T(8,128)(2,1)S(1)}) custom-call(s32[3,224]{1,0:T(4,128)S(1)} %copy-done.22, bf16[224,4096]{1,0:T(8,128)(2,1)S(1)} %copy-done.6, bf16[224,4096]{1,0:T(8,128)(2,1)S(1)} %copy-done.7, bf16[224,4096]{1,0:T(8,128)(2,1)S(1)} %copy-done.8, ...), custom_call_target="tpu_custom_call" | custom-call | flops 200000000 | bytes 200000 | tf_op jit(solution)/shard_map/prep/pallas_call | solution.py:164
  56.6 1.1 copy-done.12
  57.7 8.9 %forward.1 = (bf16[2048,128]{1,0:T(8,128)(2,1)S(1)}, bf16[2048,128]{1,0:T(8,128)(2,1)S(1)}, bf16[256,128]{1,0:T(8,128)(2,1)S(1)}, bf16[256,128]{1,0:T(8,128)(2,1...) custom-call(bf16[32,4096]{1,0:T(8,128)(2,1)S(1)} %reshape.23.t0, ...), custom_call_target="tpu_custom_call" | custom-call | flops 300000000 | bytes 300000 | tf_op jit(solution)/shard_map/forward/pallas_call | solution.py:235
  66.6 0.7 copy-done.10
  67.3 0.6 copy-done.23
  68.2 5.0 %collective-permute-start.4 = (bf16[32,4096]{1,0:T(8,128)(2,1)}, bf16[32,4096]{1,0:T(8,128)(2,1)}, u32[]{:S(2)}, u32[]{:S(2)}) collective-permute-start(bf16[32,4096]{1,0:T(8,128)(2,1)} %get-tuple-element.43), channel_id=1, source_target_pairs={{16,0},{17,1},{18,2},{19,3},{20,4},{21,5},{22,6},{23,7},{24,8},{25... | collective-permute-start | bytes 786440 | tf_op jit(solution)/shard_map/ppermute | solution.py:437
  73.2 0.7 collective-permute-start.3
  73.9 0.5 collective-permute-start.25
  74.4 0.9 dynamic-slice_bitcast_fusion.wswap
  75.3 2.2 %copy-done.1 = bf16[256,8192]{1,0:T(8,128)(2,1)S(1)} copy-done((bf16[256,8192]{1,0:T(8,128)(2,1)S(1)}, bf16[256,8192]{1,0:T(8,128)(2,1)}, u32[]{:S(2)}) %copy-start.1) | copy-done | bytes 4194328
  77.5 0.9 copy-done.9
  78.4 4.0 %deltas.1 = (bf16[128,512]{1,0:T(8,128)(2,1)S(1)}, bf16[128,512]{1,0:T(8,128)(2,1)S(1)}, bf16[256,896]{1,0:T(8,128)(2,1)S(1)}, bf16[256,896]{1,0:T(8,128)(2,1)S(1)}) custom-call(bf16[32,4096]{1,0:T(8,128)(2,1)S(1)} %reshape.25.c0, bf16[32,4096]{1,0:T(8,128)(2,1)S(1)} %collective-permute-done.6.c1, bf16[32,4096]{1,0:T(8,128)(2,1)S(1)} %collective-permute-done.7.c2, ...), custom_call_target="tpu_custom_call" | custom-call | flops 200000000 | bytes 200000 | tf_op jit(solution)/shard_map/deltas/pallas_call | solution.py:356
  82.5 2.1 %copy-done.5 = bf16[2048,896]{1,0:T(8,128)(2,1)S(1)} copy-done((bf16[2048,896]{1,0:T(8,128)(2,1)S(1)}, bf16[2048,896]{1,0:T(8,128)(2,1)}, u32[]{:S(2)}) %copy-start.5) | copy-done | bytes 3670040
  84.6 6.1 %input_parts.1 = (bf16[32,4096]{1,0:T(8,128)(2,1)S(1)}, bf16[32,4096]{1,0:T(8,128)(2,1)}, bf16[32,4096]{1,0:T(8,128)(2,1)}, bf16[32,4096]{1,0:T(8,128)(2,1)}) custom-call(bf16[256,896]{1,0:T(8,128)(2,1)S(1)} %get-tuple-element.47.gdx, bf16[256,896]{1,0:T(8,128)(2,1)S(1)} %get-tuple-element.48.udx, bf16[2048,896]{1,0:T(8,128)(2,1)S(1)} %copy-done.3, ...), custom_call_target="tpu_custom_call" | custom-call | flops 200000000 | bytes 200000 | tf_op jit(solution)/shard_map/input_parts/pallas_call | solution.py:385
  90.7 1.4 collective-permute-start.11
  92.1 0.9 collective-permute-start.10
  93.0 2.5 %collective-permute-start.9 = (bf16[32,4096]{1,0:T(8,128)(2,1)}, bf16[32,4096]{1,0:T(8,128)(2,1)}, u32[]{:S(2)}, u32[]{:S(2)}) collective-permute-start(bf16[32,4096]{1,0:T(8,128)(2,1)} %get-tuple-element.50), channel_id=1, source_target_pairs={{24,0},{25,1},{26,2},{27,3},{28,4},{29,5},{30,6},{31,7},{0,8},{1,9... | collective-permute-start | bytes 786440 | tf_op jit(solution)/shard_map/ppermute | solution.py:437
  95.5 0.5 collective-permute-start.24
  96.0 2.0 %add_convert_fusion.1 = bf16[32,4096]{1,0:T(8,128)(2,1)} fusion(bf16[32,4096]{1,0:T(8,128)(2,1)} %collective-permute-done.5, bf16[32,4096]{1,0:T(8,128)(2,1)} %collective-permute-done.4, bf16[32,4096]{1,0:T(8,128)(2,1)} %collective-permute-done.3, bf16[32,4096]{1,0:T(8,128)(2,1)S(1)} %copy-done.11), kind=kLoop, calls=%fused_computation.1 | loop fusion | flops 1048576 | bytes 1310720 | tf_op jit(solution)/shard_map/convert_element_type | solution.py:467
  98.0 1.8 %reshape.24 = bf16[8,4,4096]{2,1,0:T(4,128)(2,1)} reshape(bf16[32,4096]{1,0:T(8,128)(2,1)} %add_convert_fusion.1) | data formatting | bytes 524288 | tf_op jit(solution)/shard_map/reshape | solution.py:467
  99.8 4.0 %all-to-all-start.1 = ((bf16[8,4,4096]{2,1,0:T(4,128)(2,1)}), bf16[8,4,4096]{2,1,0:T(4,128)(2,1)}, u32[]{:S(2)}, u32[]{:S(2)}) async-start(bf16[8,4,4096]{2,1,0:T(4,128)(2,1)} %reshape.24), calls=%async_computation.1 | async-start | bytes 524288 | tf_op jit(solution)/shard_map/all_to_all | solution.py:452
  104.0 0.8 copy-done.24
  104.8 0.8 copy-done.26
  105.7 6.2 %down_grads.1 = (bf16[224,512]{1,0:T(8,128)(2,1)S(1)}, bf16[224,512]{1,0:T(8,128)(2,1)}, bf16[224,512]{1,0:T(8,128)(2,1)}, bf16[224,512]{1,0:T(8,128)(2,1)}) custom-call(s32[3,224]{1,0:T(4,128)S(1)} %copy-done.22, bf16[32,4096]{1,0:T(8,128)(2,1)S(1)} %reshape.25.c0, bf16[32,4096]{1,0:T(8,128)(2,1)S(1)} %collective-permute-done.6.c1, ...), custom_call_target="tpu_custom_call" | custom-call | flops 200000000 | bytes 200000 | tf_op jit(solution)/shard_map/down_grads/pallas_call | solution.py:288
  111.9 0.7 copy-done.15
  112.6 2.8 %collective-permute-start.28 = (bf16[224,512]{1,0:T(8,128)(2,1)}, bf16[224,512]{1,0:T(8,128)(2,1)S(1)}, u32[]{:S(2)}, u32[]{:S(2)}) collective-permute-start(bf16[224,512]{1,0:T(8,128)(2,1)} %get-tuple-element.70), channel_id=1, source_target_pairs={{192,0},{224,32},{128,64},{160,96},{64,128},{96,160},{0,192},{32,2... | collective-permute-start | bytes 688136 | tf_op jit(solution)/shard_map/ppermute | solution.py:442
  115.4 0.8 collective-permute-start.27
  116.2 0.5 collective-permute-start.26
  116.7 1.2 add_convert_fusion
  118.0 0.8 reshape.26
  118.8 7.0 %all-to-all-start.2 = ((bf16[8,4,4096]{2,1,0:T(4,128)(2,1)}), bf16[8,4,4096]{2,1,0:T(4,128)(2,1)}, u32[]{:S(2)}, u32[]{:S(2)}) async-start(bf16[8,4,4096]{2,1,0:T(4,128)(2,1)} %reshape.26), calls=%async_computation.2 | async-start | bytes 524288 | tf_op jit(solution)/shard_map/all_to_all | solution.py:452
  126.1 1.3 collective-permute-done.13.d_oth
  127.6 3.4 %gate_grads.1 = (bf16[224,512]{1,0:T(8,128)(2,1)S(1)}, bf16[224,512]{1,0:T(8,128)(2,1)S(1)}, bf16[224,512]{1,0:T(8,128)(2,1)S(1)}, bf16[224,512]{1,0:T(8,128)(2,1)S(1)}) custom-call(s32[3,224]{1,0:T(4,128)S(1)} %copy-done.22, bf16[2048,128]{1,0:T(8,128)(2,1)S(1)} %get-tuple-element.53.xt_own, bf16[2048,128]{1,0:T(8,128)(2,1)S(1)} %collective-permute-done.12.xt_oth, ...), custom_call_target="tpu_custom_call" | custom-call | flops 200000000 | bytes 200000 | tf_op jit(solution)/shard_map/gate_grads/pallas_call | solution.py:423
  131.0 2.9 %collective-permute-start.16 = (bf16[224,512]{1,0:T(8,128)(2,1)S(1)}, bf16[224,512]{1,0:T(8,128)(2,1)}, u32[]{:S(2)}, u32[]{:S(2)}) collective-permute-start(bf16[224,512]{1,0:T(8,128)(2,1)S(1)} %get-tuple-element.59), channel_id=1, source_target_pairs={{192,0},{224,32},{128,64},{160,96},{64,128},{96,160},{0,192},{32,2... | collective-permute-start | bytes 688136 | tf_op jit(solution)/shard_map/ppermute | solution.py:442
  133.9 0.8 collective-permute-start.15
  134.7 0.5 collective-permute-start.14
  135.2 0.8 multiply_convert_fusion
  136.1 3.4 %up_grads.1 = (bf16[224,512]{1,0:T(8,128)(2,1)S(1)}, bf16[224,512]{1,0:T(8,128)(2,1)S(1)}, bf16[224,512]{1,0:T(8,128)(2,1)S(1)}, bf16[224,512]{1,0:T(8,128)(2,1)S(1)}) custom-call(s32[3,224]{1,0:T(4,128)S(1)} %copy-done.22, bf16[2048,128]{1,0:T(8,128)(2,1)S(1)} %get-tuple-element.53.xt_own, bf16[2048,128]{1,0:T(8,128)(2,1)S(1)} %collective-permute-done.12.xt_oth, ...), custom_call_target="tpu_custom_call" | custom-call | flops 200000000 | bytes 200000 | tf_op jit(solution)/shard_map/up_grads/pallas_call | solution.py:423
  139.5 2.8 %collective-permute-start.20 = (bf16[224,512]{1,0:T(8,128)(2,1)S(1)}, bf16[224,512]{1,0:T(8,128)(2,1)S(1)}, u32[]{:S(2)}, u32[]{:S(2)}) collective-permute-start(bf16[224,512]{1,0:T(8,128)(2,1)S(1)} %get-tuple-element.64), channel_id=1, source_target_pairs={{192,0},{224,32},{128,64},{160,96},{64,128},{96,160},{0,192},{32,2... | collective-permute-start | bytes 688136 | tf_op jit(solution)/shard_map/ppermute | solution.py:442
  142.3 0.8 collective-permute-start.19
  143.1 1.7 %reduce_sum.24 = bf16[4,4096]{1,0:T(4,128)(2,1)} reduce(bf16[8,4,4096]{2,1,0:T(4,128)(2,1)} %all-to-all-done.1, bf16[]{:T(256)} %constant.58.clone.1), dimensions={0}, to_apply=%region_0.1 | reduce | flops 114688 | bytes 294914 | tf_op jit(solution)/shard_map/reduce_sum | solution.py:467
  144.8 1.7 %reduce_sum.25 = bf16[4,4096]{1,0:T(4,128)(2,1)} reduce(bf16[8,4,4096]{2,1,0:T(4,128)(2,1)} %all-to-all-done.2, bf16[]{:T(256)} %constant.58.clone.1), dimensions={0}, to_apply=%region_1.2 | reduce | flops 114688 | bytes 294914 | tf_op jit(solution)/shard_map/reduce_sum | solution.py:467
  146.5 0.5 collective-permute-start.18
  147.0 2.0 %multiply_convert_fusion.2 = bf16[224,512]{1,0:T(8,128)(2,1)} fusion(bf16[224,512]{1,0:T(8,128)(2,1)} %collective-permute-done.16, bf16[224,512]{1,0:T(8,128)(2,1)} %collective-permute-done.15, bf16[224,512]{1,0:T(8,128)(2,1)} %collective-permute-done.14, bf16[224,512]{1,0:T(8,128)(2,1)S(1)} %get-tuple-element.56), kind=kLoop, calls=%fused_computation.4 | loop fusion | flops 1032192 | bytes 1146880 | tf_op jit(solution)/shard_map/convert_element_type | solution.py:461
  149.0 5.9 %collective-permute-done.20 = bf16[224,512]{1,0:T(8,128)(2,1)S(1)} collective-permute-done((bf16[224,512]{1,0:T(8,128)(2,1)S(1)}, bf16[224,512]{1,0:T(8,128)(2,1)S(1)}, u32[]{:S(2)}, u32[]{:S(2)}) %collective-permute-start.20) | collective-permute-done | bytes 229408 | tf_op jit(solution)/shard_map/ppermute | solution.py:442
  155.0 0.7 collective-permute-done.18
  155.6 0.8 multiply_convert_fusion.1
  (79 shorter events, 1.3 us)
Async XLA Ops:
  0.6 44.8 %copy-start.22 = (s32[3,224]{1,0:T(4,128)S(1)}, s32[3,224]{1,0:T(4,128)}, u32[]{:S(2)}) copy-start(s32[3,224]{1,0:T(4,128)} %idx.7) | copy-start | bytes 8068
  0.6 44.8 %copy-start.6 = (bf16[224,4096]{1,0:T(8,128)(2,1)S(1)}, bf16[224,4096]{1,0:T(8,128)(2,1)}, u32[]{:S(2)}) copy-start(bf16[224,4096]{1,0:T(8,128)(2,1)} %g_ref.1) | copy-start | bytes 5505028
  28.4 10.0 %collective-permute-start = (bf16[32,4096]{1,0:T(8,128)(2,1)S(1)}, bf16[32,4096]{1,0:T(8,128)(2,1)S(1)}, u32[]{:S(2)}, u32[]{:S(2)}) collective-permute-start(bf16[32,4096]{1,0:T(8,128)(2,1)S(1)} %reshape.23.t0), channel_id=1, source_target_pairs={{8,0},{9,1},{10,2},{11,3},{12,4},{13,5},{14,6},{15,7},{16,8},{17,9... | collective-permute-start | bytes 786440 | tf_op jit(solution)/shard_map/ppermute | solution.py:437
  29.0 15.6 %collective-permute-start.1 = (bf16[32,4096]{1,0:T(8,128)(2,1)S(1)}, bf16[32,4096]{1,0:T(8,128)(2,1)}, u32[]{:S(2)}, u32[]{:S(2)}) collective-permute-start(bf16[32,4096]{1,0:T(8,128)(2,1)S(1)} %reshape.23.t0), channel_id=1, source_target_pairs={{16,0},{17,1},{18,2},{19,3},{20,4},{21,5},{22,6},{23,7},{24,8},{25... | collective-permute-start | bytes 786440 | tf_op jit(solution)/shard_map/ppermute | solution.py:437
  31.5 25.0 %copy-start.18 = (bf16[256,256]{1,0:T(8,128)(2,1)S(1)}, bf16[256,256]{1,0:T(8,128)(2,1)}, u32[]{:S(2)}) copy-start(bf16[256,256]{1,0:T(8,128)(2,1)} %constant.68.clone.fsplit) | copy-start | bytes 393220
  31.5 25.0 %collective-permute-start.2 = (bf16[32,4096]{1,0:T(8,128)(2,1)S(1)}, bf16[32,4096]{1,0:T(8,128)(2,1)}, u32[]{:S(2)}, u32[]{:S(2)}) collective-permute-start(bf16[32,4096]{1,0:T(8,128)(2,1)S(1)} %reshape.23.t0), channel_id=1, source_target_pairs={{24,0},{25,1},{26,2},{27,3},{28,4},{29,5},{30,6},{31,7},{0,8},{1,9... | collective-permute-start | bytes 786440 | tf_op jit(solution)/shard_map/ppermute | solution.py:437
  35.4 32.8 %collective-permute-start.6 = (bf16[32,4096]{1,0:T(8,128)(2,1)S(1)}, bf16[32,4096]{1,0:T(8,128)(2,1)S(1)}, u32[]{:S(2)}, u32[]{:S(2)}) collective-permute-start(bf16[32,4096]{1,0:T(8,128)(2,1)S(1)} %reshape.25.c0), channel_id=1, source_target_pairs={{8,0},{9,1},{10,2},{11,3},{12,4},{13,5},{14,6},{15,7},{16,8},{17,9... | collective-permute-start | bytes 786440 | tf_op jit(solution)/shard_map/ppermute | solution.py:437
  35.7 37.5 %collective-permute-start.7 = (bf16[32,4096]{1,0:T(8,128)(2,1)S(1)}, bf16[32,4096]{1,0:T(8,128)(2,1)S(1)}, u32[]{:S(2)}, u32[]{:S(2)}) collective-permute-start(bf16[32,4096]{1,0:T(8,128)(2,1)S(1)} %reshape.25.c0), channel_id=1, source_target_pairs={{16,0},{17,1},{18,2},{19,3},{20,4},{21,5},{22,6},{23,7},{24,8},{25... | collective-permute-start | bytes 786440 | tf_op jit(solution)/shard_map/ppermute | solution.py:437
  38.4 0.7 copy-start.13
  39.1 34.7 %collective-permute-start.8 = (bf16[32,4096]{1,0:T(8,128)(2,1)S(1)}, bf16[32,4096]{1,0:T(8,128)(2,1)S(1)}, u32[]{:S(2)}, u32[]{:S(2)}) collective-permute-start(bf16[32,4096]{1,0:T(8,128)(2,1)S(1)} %reshape.25.c0), channel_id=1, source_target_pairs={{24,0},{25,1},{26,2},{27,3},{28,4},{29,5},{30,6},{31,7},{0,8},{1,9... | collective-permute-start | bytes 786440 | tf_op jit(solution)/shard_map/ppermute | solution.py:437
  40.1 16.5 %copy-start.14 = (bf16[32,4096]{1,0:T(8,128)(2,1)S(1)}, bf16[32,4096]{1,0:T(8,128)(2,1)}, u32[]{:S(2)}) copy-start(bf16[32,4096]{1,0:T(8,128)(2,1)} %copy-done.13) | copy-start | bytes 786436
  44.5 29.4 %collective-permute-start.21 = (bf16[32,4096]{1,0:T(8,128)(2,1)S(1)}, bf16[32,4096]{1,0:T(8,128)(2,1)}, u32[]{:S(2)}, u32[]{:S(2)}) collective-permute-start(bf16[32,4096]{1,0:T(8,128)(2,1)S(1)} %reshape.25.c0), channel_id=1, source_target_pairs={{32,0},{0,32},{96,64},{64,96},{160,128},{128,160},{224,192},{192,2... | collective-permute-start | bytes 786440 | tf_op jit(solution)/shard_map/ppermute | solution.py:447
  45.5 1.5 copy-start.7
  47.0 1.5 copy-start.8
  48.5 0.9 copy-start.19
  56.5 10.1 %copy-start = (bf16[256,8192]{1,0:T(8,128)(2,1)}, bf16[256,8192]{1,0:T(8,128)(2,1)S(1)}, u32[]{:S(2)}) copy-start(bf16[256,8192]{1,0:T(8,128)(2,1)S(1)} %get-tuple-element.40.pd) | copy-start | bytes 12582916
  56.5 10.1 %copy-start.2 = (bf16[2048,896]{1,0:T(8,128)(2,1)}, bf16[2048,896]{1,0:T(8,128)(2,1)S(1)}, u32[]{:S(2)}) copy-start(bf16[2048,896]{1,0:T(8,128)(2,1)S(1)} %get-tuple-element.38.pg) | copy-start | bytes 11010052
  56.5 10.1 %copy-start.4 = (bf16[2048,896]{1,0:T(8,128)(2,1)}, bf16[2048,896]{1,0:T(8,128)(2,1)S(1)}, u32[]{:S(2)}) copy-start(bf16[2048,896]{1,0:T(8,128)(2,1)S(1)} %get-tuple-element.39.pu) | copy-start | bytes 11010052
  56.6 1.1 copy-start.12
  66.6 0.7 copy-start.10
  67.3 0.6 copy-start.23
  68.0 5.9 %copy-start.27 = (bf16[2048,128]{1,0:T(8,128)(2,1)}, bf16[2048,128]{1,0:T(8,128)(2,1)S(1)}, u32[]{:S(2)}) copy-start(bf16[2048,128]{1,0:T(8,128)(2,1)S(1)} %get-tuple-element.54) | copy-start | bytes 1572868
  68.0 14.5 %copy-start.17 = (bf16[256,256]{1,0:T(8,128)(2,1)S(1)}, bf16[256,256]{1,0:T(8,128)(2,1)}, u32[]{:S(2)}) copy-start(bf16[256,256]{1,0:T(8,128)(2,1)} %constant.71.clone.fjoin) | copy-start | bytes 393220
  68.0 24.1 %collective-permute-start.5 = (bf16[32,4096]{1,0:T(8,128)(2,1)}, bf16[32,4096]{1,0:T(8,128)(2,1)}, u32[]{:S(2)}, u32[]{:S(2)}) collective-permute-start(bf16[32,4096]{1,0:T(8,128)(2,1)} %get-tuple-element.44), channel_id=1, source_target_pairs={{8,0},{9,1},{10,2},{11,3},{12,4},{13,5},{14,6},{15,7},{16,8},{17,9... | collective-permute-start | bytes 786440 | tf_op jit(solution)/shard_map/ppermute | solution.py:437
  68.2 24.8 %collective-permute-start.4 = (bf16[32,4096]{1,0:T(8,128)(2,1)}, bf16[32,4096]{1,0:T(8,128)(2,1)}, u32[]{:S(2)}, u32[]{:S(2)}) collective-permute-start(bf16[32,4096]{1,0:T(8,128)(2,1)} %get-tuple-element.43), channel_id=1, source_target_pairs={{16,0},{17,1},{18,2},{19,3},{20,4},{21,5},{22,6},{23,7},{24,8},{25... | collective-permute-start | bytes 786440 | tf_op jit(solution)/shard_map/ppermute | solution.py:437
  73.2 22.3 %collective-permute-start.3 = (bf16[32,4096]{1,0:T(8,128)(2,1)}, bf16[32,4096]{1,0:T(8,128)(2,1)}, u32[]{:S(2)}, u32[]{:S(2)}) collective-permute-start(bf16[32,4096]{1,0:T(8,128)(2,1)} %get-tuple-element.42), channel_id=1, source_target_pairs={{24,0},{25,1},{26,2},{27,3},{28,4},{29,5},{30,6},{31,7},{0,8},{1,9... | collective-permute-start | bytes 786440 | tf_op jit(solution)/shard_map/ppermute | solution.py:437
  73.9 21.7 %collective-permute-start.22 = (bf16[32,4096]{1,0:T(8,128)(2,1)S(1)}, bf16[32,4096]{1,0:T(8,128)(2,1)S(1)}, u32[]{:S(2)}, u32[]{:S(2)}) collective-permute-start(bf16[32,4096]{1,0:T(8,128)(2,1)S(1)} %collective-permute-done.6.c1), channel_id=1, source_target_pairs={{32,0},{0,32},{96,64},{64,96},{160,128},{128,160},{224,192},{192,2... | collective-permute-start | bytes 786440 | tf_op jit(solution)/shard_map/ppermute | solution.py:447
  73.9 16.8 %collective-permute-start.25 = (bf16[256,128]{1,0:T(8,128)(2,1)S(1)}, bf16[256,128]{1,0:T(8,128)(2,1)S(1)}, u32[]{:S(2)}, u32[]{:S(2)}) collective-permute-start(bf16[256,128]{1,0:T(8,128)(2,1)S(1)} %get-tuple-element.66), channel_id=1, source_target_pairs={{32,0},{0,32},{96,64},{64,96},{160,128},{128,160},{224,192},{192,2... | collective-permute-start | bytes 196616 | tf_op jit(solution)/shard_map/ppermute | solution.py:447
  75.3 2.2 %copy-start.1 = (bf16[256,8192]{1,0:T(8,128)(2,1)S(1)}, bf16[256,8192]{1,0:T(8,128)(2,1)}, u32[]{:S(2)}) copy-start(bf16[256,8192]{1,0:T(8,128)(2,1)} %copy-done) | copy-start | bytes 12582916
  77.5 0.9 copy-start.9
  78.4 4.0 %copy-start.3 = (bf16[2048,896]{1,0:T(8,128)(2,1)S(1)}, bf16[2048,896]{1,0:T(8,128)(2,1)}, u32[]{:S(2)}) copy-start(bf16[2048,896]{1,0:T(8,128)(2,1)} %copy-done.2) | copy-start | bytes 11010052
  82.4 8.2 %copy-start.20 = (bf16[128,512]{1,0:T(8,128)(2,1)}, bf16[128,512]{1,0:T(8,128)(2,1)S(1)}, u32[]{:S(2)}) copy-start(bf16[128,512]{1,0:T(8,128)(2,1)S(1)} %get-tuple-element.55.d_own) | copy-start | bytes 393220
  82.5 2.1 %copy-start.5 = (bf16[2048,896]{1,0:T(8,128)(2,1)S(1)}, bf16[2048,896]{1,0:T(8,128)(2,1)}, u32[]{:S(2)}) copy-start(bf16[2048,896]{1,0:T(8,128)(2,1)} %copy-done.4) | copy-start | bytes 11010052
  84.6 11.5 %copy-start.11 = (bf16[32,4096]{1,0:T(8,128)(2,1)S(1)}, bf16[32,4096]{1,0:T(8,128)(2,1)}, u32[]{:S(2)}) copy-start(bf16[32,4096]{1,0:T(8,128)(2,1)} %copy-done.10) | copy-start | bytes 786436
  90.7 13.1 %copy-start.25 = (bf16[256,128]{1,0:T(8,128)(2,1)}, bf16[256,128]{1,0:T(8,128)(2,1)S(1)}, u32[]{:S(2)}) copy-start(bf16[256,128]{1,0:T(8,128)(2,1)S(1)} %collective-permute-done.25.ht_oth) | copy-start | bytes 196612
  90.7 35.1 %copy-start.21 = (bf16[128,512]{1,0:T(8,128)(2,1)S(1)}, bf16[128,512]{1,0:T(8,128)(2,1)}, u32[]{:S(2)}) copy-start(bf16[128,512]{1,0:T(8,128)(2,1)} %copy-done.20) | copy-start | bytes 393220
  90.7 24.7 %collective-permute-start.11 = (bf16[32,4096]{1,0:T(8,128)(2,1)}, bf16[32,4096]{1,0:T(8,128)(2,1)}, u32[]{:S(2)}, u32[]{:S(2)}) collective-permute-start(bf16[32,4096]{1,0:T(8,128)(2,1)} %get-tuple-element.52), channel_id=1, source_target_pairs={{8,0},{9,1},{10,2},{11,3},{12,4},{13,5},{14,6},{15,7},{16,8},{17,9... | collective-permute-start | bytes 786440 | tf_op jit(solution)/shard_map/ppermute | solution.py:437
  92.1 24.1 %collective-permute-start.10 = (bf16[32,4096]{1,0:T(8,128)(2,1)}, bf16[32,4096]{1,0:T(8,128)(2,1)}, u32[]{:S(2)}, u32[]{:S(2)}) collective-permute-start(bf16[32,4096]{1,0:T(8,128)(2,1)} %get-tuple-element.51), channel_id=1, source_target_pairs={{16,0},{17,1},{18,2},{19,3},{20,4},{21,5},{22,6},{23,7},{24,8},{25... | collective-permute-start | bytes 786440 | tf_op jit(solution)/shard_map/ppermute | solution.py:437
  93.0 23.7 %collective-permute-start.9 = (bf16[32,4096]{1,0:T(8,128)(2,1)}, bf16[32,4096]{1,0:T(8,128)(2,1)}, u32[]{:S(2)}, u32[]{:S(2)}) collective-permute-start(bf16[32,4096]{1,0:T(8,128)(2,1)} %get-tuple-element.50), channel_id=1, source_target_pairs={{24,0},{25,1},{26,2},{27,3},{28,4},{29,5},{30,6},{31,7},{0,8},{1,9... | collective-permute-start | bytes 786440 | tf_op jit(solution)/shard_map/ppermute | solution.py:437
  95.5 8.3 %collective-permute-start.23 = (bf16[32,4096]{1,0:T(8,128)(2,1)S(1)}, bf16[32,4096]{1,0:T(8,128)(2,1)S(1)}, u32[]{:S(2)}, u32[]{:S(2)}) collective-permute-start(bf16[32,4096]{1,0:T(8,128)(2,1)S(1)} %collective-permute-done.7.c2), channel_id=1, source_target_pairs={{32,0},{0,32},{96,64},{64,96},{160,128},{128,160},{224,192},{192,2... | collective-permute-start | bytes 786440 | tf_op jit(solution)/shard_map/ppermute | solution.py:447
  95.5 8.5 %collective-permute-start.24 = (bf16[32,4096]{1,0:T(8,128)(2,1)S(1)}, bf16[32,4096]{1,0:T(8,128)(2,1)S(1)}, u32[]{:S(2)}, u32[]{:S(2)}) collective-permute-start(bf16[32,4096]{1,0:T(8,128)(2,1)S(1)} %collective-permute-done.8.c3), channel_id=1, source_target_pairs={{32,0},{0,32},{96,64},{64,96},{160,128},{128,160},{224,192},{192,2... | collective-permute-start | bytes 786440 | tf_op jit(solution)/shard_map/ppermute | solution.py:447
  99.8 19.0 %all-to-all-start.1 = ((bf16[8,4,4096]{2,1,0:T(4,128)(2,1)}), bf16[8,4,4096]{2,1,0:T(4,128)(2,1)}, u32[]{:S(2)}, u32[]{:S(2)}) async-start(bf16[8,4,4096]{2,1,0:T(4,128)(2,1)} %reshape.24), calls=%async_computation.1 | async-start | bytes 524288 | tf_op jit(solution)/shard_map/all_to_all | solution.py:452
  103.8 23.8 %collective-permute-start.12 = (bf16[2048,128]{1,0:T(8,128)(2,1)}, bf16[2048,128]{1,0:T(8,128)(2,1)S(1)}, u32[]{:S(2)}, u32[]{:S(2)}) collective-permute-start(bf16[2048,128]{1,0:T(8,128)(2,1)} %copy-done.27), channel_id=1, source_target_pairs={{32,0},{0,32},{96,64},{64,96},{160,128},{128,160},{224,192},{192,2... | collective-permute-start | bytes 1572872 | tf_op jit(solution)/shard_map/ppermute | solution.py:447
  104.0 0.8 copy-start.24
  104.8 0.8 copy-start.26
  111.9 0.7 copy-start.15
  112.6 22.6 %copy-start.16 = (bf16[224,512]{1,0:T(8,128)(2,1)S(1)}, bf16[224,512]{1,0:T(8,128)(2,1)}, u32[]{:S(2)}) copy-start(bf16[224,512]{1,0:T(8,128)(2,1)} %copy-done.15) | copy-start | bytes 688132
  112.6 21.3 %collective-permute-start.28 = (bf16[224,512]{1,0:T(8,128)(2,1)}, bf16[224,512]{1,0:T(8,128)(2,1)S(1)}, u32[]{:S(2)}, u32[]{:S(2)}) collective-permute-start(bf16[224,512]{1,0:T(8,128)(2,1)} %get-tuple-element.70), channel_id=1, source_target_pairs={{192,0},{224,32},{128,64},{160,96},{64,128},{96,160},{0,192},{32,2... | collective-permute-start | bytes 688136 | tf_op jit(solution)/shard_map/ppermute | solution.py:442
  115.4 19.3 %collective-permute-start.27 = (bf16[224,512]{1,0:T(8,128)(2,1)}, bf16[224,512]{1,0:T(8,128)(2,1)S(1)}, u32[]{:S(2)}, u32[]{:S(2)}) collective-permute-start(bf16[224,512]{1,0:T(8,128)(2,1)} %get-tuple-element.69), channel_id=1, source_target_pairs={{128,0},{160,32},{192,64},{224,96},{0,128},{32,160},{64,192},{96,2... | collective-permute-start | bytes 688136 | tf_op jit(solution)/shard_map/ppermute | solution.py:442
  116.2 19.0 %collective-permute-start.26 = (bf16[224,512]{1,0:T(8,128)(2,1)}, bf16[224,512]{1,0:T(8,128)(2,1)S(1)}, u32[]{:S(2)}, u32[]{:S(2)}) collective-permute-start(bf16[224,512]{1,0:T(8,128)(2,1)} %get-tuple-element.68), channel_id=1, source_target_pairs={{64,0},{96,32},{0,64},{32,96},{192,128},{224,160},{128,192},{160,2... | collective-permute-start | bytes 688136 | tf_op jit(solution)/shard_map/ppermute | solution.py:442
  118.8 26.0 %all-to-all-start.2 = ((bf16[8,4,4096]{2,1,0:T(4,128)(2,1)}), bf16[8,4,4096]{2,1,0:T(4,128)(2,1)}, u32[]{:S(2)}, u32[]{:S(2)}) async-start(bf16[8,4,4096]{2,1,0:T(4,128)(2,1)} %reshape.26), calls=%async_computation.2 | async-start | bytes 524288 | tf_op jit(solution)/shard_map/all_to_all | solution.py:452
  125.8 1.7 %collective-permute-start.13 = (bf16[128,512]{1,0:T(8,128)(2,1)S(1)}, bf16[128,512]{1,0:T(8,128)(2,1)S(1)}, u32[]{:S(2)}, u32[]{:S(2)}) collective-permute-start(bf16[128,512]{1,0:T(8,128)(2,1)S(1)} %copy-done.21), channel_id=1, source_target_pairs={{32,0},{0,32},{96,64},{64,96},{160,128},{128,160},{224,192},{192,2... | collective-permute-start | bytes 393224 | tf_op jit(solution)/shard_map/ppermute | solution.py:447
  127.5 8.6 %collective-permute-start.17 = (bf16[128,512]{1,0:T(8,128)(2,1)S(1)}, bf16[128,512]{1,0:T(8,128)(2,1)S(1)}, u32[]{:S(2)}, u32[]{:S(2)}) collective-permute-start(bf16[128,512]{1,0:T(8,128)(2,1)S(1)} %get-tuple-element.60.d_own), channel_id=1, source_target_pairs={{32,0},{0,32},{96,64},{64,96},{160,128},{128,160},{224,192},{192,2... | collective-permute-start | bytes 393224 | tf_op jit(solution)/shard_map/ppermute | solution.py:447
  131.0 15.5 %collective-permute-start.16 = (bf16[224,512]{1,0:T(8,128)(2,1)S(1)}, bf16[224,512]{1,0:T(8,128)(2,1)}, u32[]{:S(2)}, u32[]{:S(2)}) collective-permute-start(bf16[224,512]{1,0:T(8,128)(2,1)S(1)} %get-tuple-element.59), channel_id=1, source_target_pairs={{192,0},{224,32},{128,64},{160,96},{64,128},{96,160},{0,192},{32,2... | collective-permute-start | bytes 688136 | tf_op jit(solution)/shard_map/ppermute | solution.py:442
  133.9 13.2 %collective-permute-start.15 = (bf16[224,512]{1,0:T(8,128)(2,1)S(1)}, bf16[224,512]{1,0:T(8,128)(2,1)}, u32[]{:S(2)}, u32[]{:S(2)}) collective-permute-start(bf16[224,512]{1,0:T(8,128)(2,1)S(1)} %get-tuple-element.58), channel_id=1, source_target_pairs={{128,0},{160,32},{192,64},{224,96},{0,128},{32,160},{64,192},{96,2... | collective-permute-start | bytes 688136 | tf_op jit(solution)/shard_map/ppermute | solution.py:442
  134.7 12.4 %collective-permute-start.14 = (bf16[224,512]{1,0:T(8,128)(2,1)S(1)}, bf16[224,512]{1,0:T(8,128)(2,1)}, u32[]{:S(2)}, u32[]{:S(2)}) collective-permute-start(bf16[224,512]{1,0:T(8,128)(2,1)S(1)} %get-tuple-element.57), channel_id=1, source_target_pairs={{64,0},{96,32},{0,64},{32,96},{192,128},{224,160},{128,192},{160,2... | collective-permute-start | bytes 688136 | tf_op jit(solution)/shard_map/ppermute | solution.py:442
  139.5 15.5 %collective-permute-start.20 = (bf16[224,512]{1,0:T(8,128)(2,1)S(1)}, bf16[224,512]{1,0:T(8,128)(2,1)S(1)}, u32[]{:S(2)}, u32[]{:S(2)}) collective-permute-start(bf16[224,512]{1,0:T(8,128)(2,1)S(1)} %get-tuple-element.64), channel_id=1, source_target_pairs={{192,0},{224,32},{128,64},{160,96},{64,128},{96,160},{0,192},{32,2... | collective-permute-start | bytes 688136 | tf_op jit(solution)/shard_map/ppermute | solution.py:442
  142.3 12.6 %collective-permute-start.19 = (bf16[224,512]{1,0:T(8,128)(2,1)S(1)}, bf16[224,512]{1,0:T(8,128)(2,1)S(1)}, u32[]{:S(2)}, u32[]{:S(2)}) collective-permute-start(bf16[224,512]{1,0:T(8,128)(2,1)S(1)} %get-tuple-element.63), channel_id=1, source_target_pairs={{128,0},{160,32},{192,64},{224,96},{0,128},{32,160},{64,192},{96,2... | collective-permute-start | bytes 688136 | tf_op jit(solution)/shard_map/ppermute | solution.py:442
  146.5 9.1 %collective-permute-start.18 = (bf16[224,512]{1,0:T(8,128)(2,1)S(1)}, bf16[224,512]{1,0:T(8,128)(2,1)S(1)}, u32[]{:S(2)}, u32[]{:S(2)}) collective-permute-start(bf16[224,512]{1,0:T(8,128)(2,1)S(1)} %get-tuple-element.62), channel_id=1, source_target_pairs={{64,0},{96,32},{0,64},{32,96},{192,128},{224,160},{128,192},{160,2... | collective-permute-start | bytes 688136 | tf_op jit(solution)/shard_map/ppermute | solution.py:442

commit v2 on v1

--- a/solution.py
+++ b/solution.py
@@ -2,7 +2,6 @@
 
 import jax
 import jax.numpy as jnp
-import numpy as np
 from jax import lax
 from jax.experimental import pallas as pl
 from jax.experimental.pallas import tpu as pltpu
@@ -21,81 +20,43 @@
 F32 = jnp.float32
 
 TILE_ROWS = [[8 * x + 4 * c + k4 for x in range(NX) for k4 in range(4)] for c in range(NC)]
-ORDER = TILE_ROWS[0] + TILE_ROWS[1]
+
+
+def rows_of(n):
+    return lax.broadcasted_iota(jnp.int32, (n, 1), 0)
+
+
+def cols_of(n):
+    return lax.broadcasted_iota(jnp.int32, (1, n), 1)
+
+
+def one_hot(left, right):
+    return jnp.where(left == right, 1.0, 0.0).astype(BF)
+
+
+def split_index(at, stride):
+    k = 8 * ((at >> 2) & 3) + 4 * ((at >> 4) & 1) + (at & 3)
+    return ((at >> 5) & 3) * stride + 2 * k + (at >> 7)
+
+
+def turn_index(at, core, stride):
+    k = 8 * ((at >> 2) & 3) + 4 * (core ^ (at >> 7)) + (at & 3)
+    return ((at >> 4) & 3) * stride + 2 * k + ((at >> 6) & 1)
 
 
 def swap_matrix():
-    m = np.zeros((256, 256), np.float32)
-    for a in range(16):
-        for b in range(16):
-            m[a * 16 + b, b * 16 + a] = 1
-    return m
-
-
-def feature_split():
-    m = np.zeros((256, 256), np.float32)
-    for i in range(4):
-        for p in range(2):
-            for n, k in enumerate(ORDER):
-                m[i * 64 + 2 * k + p, p * 128 + i * 32 + n] = 1
-    return m
-
-
-def feature_turn(core):
-    m = np.zeros((256, 256), np.float32)
-    for rel in range(2):
-        for p in range(2):
-            for i in range(4):
-                for n, k in enumerate(TILE_ROWS[core ^ rel]):
-                    m[rel * 128 + p * 64 + i * 16 + n, i * 64 + 2 * k + p] = 1
-    return m
-
-
-def hidden_split():
-    m = np.zeros((512, 256), np.float32)
-    for j in range(4):
-        for p in range(2):
-            for n, k in enumerate(ORDER):
-                m[j * 128 + 2 * k + p, p * 128 + j * 32 + n] = 1
-    return m
-
-
-def hidden_turn(core):
-    m = np.zeros((256, 512), np.float32)
-    for rel in range(2):
-        for p in range(2):
-            for j in range(4):
-                for n, k in enumerate(TILE_ROWS[core ^ rel]):
-                    m[rel * 128 + p * 64 + j * 16 + n, j * 128 + 2 * k + p] = 1
-    return m
-
-
-def hidden_join():
-    m = np.zeros((256, 512), np.float32)
-    for j in range(4):
-        for p in range(2):
-            for n, k in enumerate(ORDER):
-                for h in range(2):
-                    m[p * 128 + j * 32 + n, j * 128 + h * 64 + 2 * k + p] = 1
-    return m
+    at = cols_of(256)
+    return one_hot(rows_of(256), (at & 15) * 16 + (at >> 4))
 
 
 def wire_swap(x):
-    m = np.zeros((256, 256), np.float32)
-    for rel in range(NX):
-        for k4 in range(4):
-            for q in range(16):
-                m[rel * 64 + k4 * 16 + q, q * 16 + (rel ^ x) * 4 + k4] = 1
-    return m
-
-
-SWAP = swap_matrix()
-FSPLIT = feature_split()
-FTURN = np.stack([feature_turn(0), feature_turn(1)])
-HSPLIT = hidden_split()
-HTURN = np.stack([hidden_turn(0), hidden_turn(1)])
-HJOIN = hidden_join()
-WSWAP = np.stack([wire_swap(x) for x in range(NX)])
+    at = rows_of(256)
+    return one_hot((at & 15) * 16 + ((at >> 6) ^ x) * 4 + ((at >> 4) & 3), cols_of(256))
+
+
+def place():
+    dp, fsdp = lax.axis_index("dp"), lax.axis_index("fsdp")
+    return lax.rem(dp, NC), dp // NC, fsdp // NZ
 
 
 def mm(a, b):
@@ -130,7 +91,7 @@
     return jax.ShapeDtypeStruct(dims, dtype)
 
 
-def prep_kernel(idx, g_ref, u_ref, d_ref, swap, pg, pu, pd, scr):
+def prep_kernel(idx, g_ref, u_ref, d_ref, pg, pu, pd, scr):
     j = pl.program_id(0)
     pd[...] = jnp.zeros_like(pd)
 
@@ -138,6 +99,7 @@
     def _():
         pg[...] = jnp.zeros_like(pg)
         pu[...] = jnp.zeros_like(pu)
+        swap = swap_matrix()
         for m, src in enumerate((g_ref, u_ref, d_ref)):
             for qh in range(2):
                 rows = slice(qh * 16, qh * 16 + 16)
@@ -146,7 +108,7 @@
                     for c in range(2)
                 ]
                 tiles = scr.at[2 * m + qh]
-                tiles[...] = mm(swap[...], jnp.concatenate(halves, axis=1)).astype(BF)
+                tiles[...] = mm(swap, jnp.concatenate(halves, axis=1)).astype(BF)
                 for q in range(16):
                     i = idx[m, j * KEEP + qh * 16 + q]
                     for c in range(2):
@@ -166,25 +128,29 @@
         grid_spec=pltpu.PrefetchScalarGridSpec(
             num_scalar_prefetch=1,
             grid=(COLS + 1,),
-            in_specs=[blocks, blocks, blocks, pl.BlockSpec((256, 256), lambda j, s: (0, 0))],
+            in_specs=[blocks, blocks, blocks],
             out_specs=[panel, panel, pl.BlockSpec((KEEP, 2 * D), lambda j, s: (j, 0))],
             scratch_shapes=[pltpu.VMEM((6, 256, 256), BF)],
         ),
-        out_shape=[shape(FEAT, WIDE), shape(FEAT, WIDE), shape(256, 2 * D)],
+        out_shape=[pltpu.VMEM((FEAT, WIDE), BF), pltpu.VMEM((FEAT, WIDE), BF), pltpu.VMEM((256, 2 * D), BF)],
         compiler_params=params(12),
         cost_estimate=cost(2),
         name="prep",
-    )(idx, gate, up, down, jnp.asarray(SWAP, BF))
-
-
-def forward_kernel(t0, t1, t2, t3, pg, pu, pd, fsplit, fturn, hsplit, hturn,
-                   xt_own, xt_sib, ht_own, ht_sib, gl2, ul2, o0, o1, o2, o3, tok, xx, hid, hh):
+    )(idx, *(pltpu.with_memory_space_constraint(b, pltpu.HBM) for b in (gate, up, down)))
+
+
+def forward_kernel(t0, t1, t2, t3, pg, pu, pd, xt_own, xt_sib, ht_own, ht_sib, gl2, ul2, out_parts, tok, xx, hid, hh):
+    core, _, y = place()
+    fsplit = one_hot(rows_of(256), split_index(cols_of(256), 64))
+    fturn = one_hot(turn_index(rows_of(256), core, 64), cols_of(256))
+    hsplit = one_hot(rows_of(512), split_index(cols_of(256), 128))
+    hturn = one_hot(turn_index(rows_of(256), core, 128), cols_of(512))
     for n, piece in enumerate((t0, t1, t2, t3)):
         tok[n * 32:n * 32 + 32, :] = piece[...]
     for c in range(16):
         chunk = tok[:, c * 256:c * 256 + 256]
-        split = mm(chunk, fsplit[...]).astype(BF)
-        turned = mm_nt(fturn[...], chunk).astype(BF)
+        split = mm(chunk, fsplit).astype(BF)
+        turned = mm_nt(fturn, chunk).astype(BF)
         for p in range(2):
             xx[p * 128:p * 128 + 128, c * 128:c * 128 + 128] = split[:, p * 128:p * 128 + 128]
             at = p * 1024 + c * 64
@@ -207,8 +173,8 @@
             hid[:, cols] = (gl * (1.0 / (1.0 + jnp.exp(-gl))) * ul).astype(BF)
     for g in range(2):
         group = hid[:, g * 512:g * 512 + 512]
-        split = mm(group, hsplit[...]).astype(BF)
-        turned = mm_nt(hturn[...], group).astype(BF)
+        split = mm(group, hsplit).astype(BF)
+        turned = mm_nt(hturn, group).astype(BF)
         for p in range(2):
             hh[p * 128:p * 128 + 128, g * 128:g * 128 + 128] = split[:, p * 128:p * 128 + 128]
             at = p * 128 + g * 64
@@ -223,20 +189,20 @@
             b0, b1 = out[:TOK, m * 256 + 128:m * 256 + 256], out[TOK:, m * 256 + 128:m * 256 + 256]
             parts.append(jnp.where(low, a0, b1) + pltpu.roll(jnp.where(low, b0, a1), 64, 1))
         whole = jnp.concatenate(parts, axis=1).astype(BF)
-        for r, dst in enumerate((o0, o1, o2, o3)):
-            dst[:, pl.ds(pl.multiple_of(n * 512, 512), 512)] = whole[r * 32:r * 32 + 32, :]
+        for r in range(NY):
+            out_parts[lax.rem(y + r, NY), :, pl.ds(pl.multiple_of(n * 512, 512), 512)] = whole[r * 32:r * 32 + 32, :]
         return carry
 
     lax.fori_loop(0, 8, step, 0)
 
 
-def forward(pieces, pg, pu, pd, fturn, hturn):
-    lin = shape(TOK, WIDE, dtype=F32)
+def forward(pieces, pg, pu, pd):
+    lin = pltpu.VMEM((TOK, WIDE), F32)
     return pl.pallas_call(
         forward_kernel,
-        in_specs=vm(11),
-        out_specs=vm(10),
-        out_shape=[shape(FEAT, TOK)] * 2 + [shape(256, TOK)] * 2 + [lin, lin] + [shape(32, D)] * 4,
+        in_specs=vm(7),
+        out_specs=vm(7),
+        out_shape=[shape(FEAT, TOK)] * 2 + [shape(256, TOK)] * 2 + [lin, lin, shape(NY, 32, D)],
         scratch_shapes=[
             pltpu.VMEM((TOK, D), BF),
             pltpu.VMEM((256, FEAT), BF),
@@ -246,11 +212,11 @@
         compiler_params=params(24),
         cost_estimate=cost(3),
         name="forward",
-    )(*pieces, pg, pu, pd, jnp.asarray(FSPLIT, BF), fturn, jnp.asarray(HSPLIT, BF), hturn)
+    )(*pieces, pg, pu, pd)
 
 
 def emit(wswap, tiles, parts, j):
-    turned = mm(wswap[...], tiles[...]).astype(BF)
+    turned = mm(wswap, tiles[...]).astype(BF)
     for rel, dst in enumerate(parts):
         for k in range(4):
             top = (rel * 4 + k) * 16
@@ -260,7 +226,8 @@
                 ]
 
 
-def down_kernel(idx, c0, c1, c2, c3, d0, d1, d2, d3, ht_own, ht_oth, wswap, w0, w1, w2, w3, both, part, tiles):
+def down_kernel(idx, c0, c1, c2, c3, d0, d1, d2, d3, ht_own, ht_oth, w0, w1, w2, w3, both, part, tiles):
+    wswap = wire_swap(place()[1])
     for n, piece in enumerate((c0, c1, c2, c3, d0, d1, d2, d3)):
         both[n * 32:n * 32 + 32, :] = piece[...]
 
@@ -284,20 +251,22 @@
         emit(wswap, tiles, (w0, w1, w2, w3), j)
 
 
-def down_grads(idx, pieces, others, ht_own, ht_oth, wswap):
+def down_grads(idx, pieces, others, ht_own, ht_oth):
     return pl.pallas_call(
         down_kernel,
-        in_specs=smem(1) + vm(11),
+        in_specs=smem(1) + vm(10),
         out_specs=vm(4),
         out_shape=[shape(SLOT, 512)] * 4,
         scratch_shapes=[pltpu.VMEM((256, D), BF), pltpu.VMEM((256, D), BF), pltpu.VMEM((256, 256), BF)],
         compiler_params=params(14),
         cost_estimate=cost(2),
         name="down_grads",
-    )(idx, *pieces, *others, ht_own, ht_oth, wswap)
-
-
-def delta_kernel(c0, c1, c2, c3, pd, gl2, ul2, hjoin, gd_own, ud_own, gdx, udx, cx):
+    )(idx, *pieces, *others, ht_own, ht_oth)
+
+
+def delta_kernel(c0, c1, c2, c3, pd, gl2, ul2, gd_own, ud_own, gdx, udx, cx):
+    at = cols_of(512)
+    hjoin = one_hot(split_index(rows_of(256), 128), (at >> 7) * 128 + (at & 63))
     low = low_half((32, 128))
     for n, piece in enumerate((c0, c1, c2, c3)):
         top = slice(n * 32, n * 32 + 32)
@@ -326,7 +295,7 @@
     for g in range(2):
         cols = slice(g * 128, g * 128 + 128)
         joined = sum(
-            mm(jnp.concatenate([part[:TOK, cols], part[TOK:, cols]], axis=1), hjoin[...]) for part in (high, rest)
+            mm(jnp.concatenate([part[:TOK, cols], part[TOK:, cols]], axis=1), hjoin) for part in (high, rest)
         )
         before = None
         for jl in range(4):
@@ -355,24 +324,26 @@
 def deltas(pieces, pd, gl2, ul2):
     return pl.pallas_call(
         delta_kernel,
-        in_specs=vm(8),
+        in_specs=vm(7),
         out_specs=vm(4),
-        out_shape=[shape(TOK, 512)] * 2 + [shape(256, WIDE)] * 2,
+        out_shape=[shape(TOK, 512)] * 2 + [pltpu.VMEM((256, WIDE), BF)] * 2,
         scratch_shapes=[pltpu.VMEM((256, 2 * D), BF)],
         compiler_params=params(18),
         cost_estimate=cost(2),
         name="deltas",
-    )(*pieces, pd, gl2, ul2, jnp.asarray(HJOIN, BF))
-
-
-def back_kernel(gdx, udx, pg, pu, fjoin, i0, i1, i2, i3):
+    )(*pieces, pd, gl2, ul2)
+
+
+def back_kernel(gdx, udx, pg, pu, i0, i1, i2, i3):
+    fjoin = one_hot(split_index(rows_of(256), 64), cols_of(256))
+
     def back(n, carry):
         rows = pl.ds(pl.multiple_of(n * 256, 256), 256)
         acc = (mm_nt(gdx[...], pg[rows, :]) + mm_nt(udx[...], pu[rows, :])).astype(BF)
         for c in range(2):
             cols = slice(c * 128, c * 128 + 128)
             pair = jnp.concatenate([acc[:TOK, cols], acc[TOK:, cols]], axis=1)
-            whole = mm(pair, fjoin[...]).astype(BF)
+            whole = mm(pair, fjoin).astype(BF)
             lanes = pl.ds(pl.multiple_of(n * 512 + c * 256, 256), 256)
             for r, dst in enumerate((i0, i1, i2, i3)):
                 dst[:, lanes] = whole[r * 32:r * 32 + 32, :]
@@ -384,16 +355,17 @@
 def input_parts(gdx, udx, pg, pu):
     return pl.pallas_call(
         back_kernel,
-        in_specs=vm(5),
+        in_specs=vm(4),
         out_specs=vm(4),
         out_shape=[shape(32, D)] * 4,
         compiler_params=params(18),
         cost_estimate=cost(2),
         name="input_parts",
-    )(gdx, udx, pg, pu, jnp.asarray(FSPLIT.T, BF))
-
-
-def inward_kernel(m, idx, xt_own, xt_oth, d_own, d_oth, wswap, w0, w1, w2, w3, part, tiles):
+    )(gdx, udx, pg, pu)
+
+
+def inward_kernel(m, idx, xt_own, xt_oth, d_own, d_oth, w0, w1, w2, w3, part, tiles):
+    wswap = wire_swap(place()[1])
     delta = jnp.concatenate([d_own[...], d_oth[...]], axis=0)
 
     def product(n, carry):
@@ -419,17 +391,17 @@
         emit(wswap, tiles, (w0, w1, w2, w3), j)
 
 
-def inward_grads(m, idx, xt_own, xt_oth, d_own, d_oth, wswap):
+def inward_grads(m, idx, xt_own, xt_oth, d_own, d_oth):
     return pl.pallas_call(
         functools.partial(inward_kernel, m),
-        in_specs=smem(1) + vm(5),
+        in_specs=smem(1) + vm(4),
         out_specs=vm(4),
         out_shape=[shape(SLOT, 512)] * 4,
         scratch_shapes=[pltpu.VMEM((FEAT, 512), BF), pltpu.VMEM((256, 256), BF)],
         compiler_params=params(14),
         cost_estimate=cost(2),
         name=("gate_grads", "up_grads")[m],
-    )(idx, xt_own, xt_oth, d_own, d_oth, wswap)
+    )(idx, xt_own, xt_oth, d_own, d_oth)
 
 
 def from_y(value, step):
@@ -447,9 +419,20 @@
     return lax.ppermute(value, "dp", pairs)
 
 
+def z_groups():
+    return [[y * NZ + z for z in range(NZ)] for y in range(NY)]
+
+
 def over_z(value):
-    groups = [[y * NZ + z for z in range(NZ)] for y in range(NY)]
-    return lax.all_to_all(value, "fsdp", 0, 0, axis_index_groups=groups, tiled=True)
+    return lax.all_to_all(value, "fsdp", 0, 0, axis_index_groups=z_groups(), tiled=True)
+
+
+def copies_over_z(value):
+    return over_z(jnp.broadcast_to(value[None], (NZ,) + value.shape)).reshape(-1, D)
+
+
+def after(value, *others):
+    return lax.optimization_barrier((value,) + others)[0]
 
 
 def total_of(first, others):
@@ -467,32 +450,36 @@
     return over_z(total.astype(BF).reshape(NZ, rows, D)).astype(F32).sum(axis=0).astype(BF)
 
 
+def scatter_yz(parts):
+    rows = parts.shape[1] // NZ
+    columns = [[y * NZ + z for y in range(NY)] for z in range(NZ)]
+    mine = lax.psum_scatter(parts, "fsdp", scatter_dimension=0, axis_index_groups=columns)
+    mine = mine.reshape(NZ, 4 * rows, D // 4)
+    return lax.psum_scatter(mine, "fsdp", scatter_dimension=0, axis_index_groups=z_groups()).reshape(rows, D)
+
+
 def body(tokens, cotangent, gate_blocks, up_blocks, down_blocks, block_index):
-    rows = tokens.shape[0]
-    here = lax.axis_index("dp")
-    core, x = here % NC, here // NC
-    fturn = jnp.where(core == 0, jnp.asarray(FTURN[0], BF), jnp.asarray(FTURN[1], BF))
-    hturn = jnp.where(core == 0, jnp.asarray(HTURN[0], BF), jnp.asarray(HTURN[1], BF))
-    wswap = lax.dynamic_index_in_dim(jnp.asarray(WSWAP, BF), x, 0, keepdims=False)
-
-    own = jnp.concatenate([tokens, cotangent], axis=0)
-    ring = over_z(jnp.broadcast_to(own[None], (NZ,) + own.shape))
-    pg, pu, pd = prep(block_index, gate_blocks, up_blocks, down_blocks)
-    tok_z = ring[:, :rows].reshape(NZ * rows, D)
-    cot_z = ring[:, rows:].reshape(NZ * rows, D)
+    tok_z = copies_over_z(tokens)
+    cot_z = copies_over_z(cotangent)
     tok = [tok_z] + [from_y(tok_z, s) for s in range(1, NY)]
+    pg, pu, pd = prep(after(block_index, tok_z), gate_blocks, up_blocks, down_blocks)
+    cot_z = after(cot_z, pd)
     cot = [cot_z] + [from_y(cot_z, s) for s in range(1, NY)]
     cot_oth = [from_core(c) for c in cot]
 
-    xt_own, xt_sib, ht_own, ht_sib, gl2, ul2, *out_parts = forward(tok, pg, pu, pd, fturn, hturn)
+    xt_own, xt_sib, ht_own, ht_sib, gl2, ul2, out_parts = forward(tok, pg, pu, pd)
     xt_oth, ht_oth = from_core(xt_sib), from_core(ht_sib)
-    layer_out = reduce_yz(out_parts)
-    down_grad = reduce_x(down_grads(block_index, cot, cot_oth, ht_own, ht_oth, wswap))
-    gd, ud, gdx, udx = deltas(cot, pd, gl2, ul2)
+    layer_out = scatter_yz(out_parts)
+    wire = down_grads(block_index, cot, cot_oth, ht_own, ht_oth)
+    down_grad = reduce_x(wire)
+    gd, ud, gdx, udx = deltas(cot, pd, after(gl2, wire[0]), ul2)
     gd_oth, ud_oth = from_core(gd), from_core(ud)
-    input_grad = reduce_yz(input_parts(gdx, udx, pg, pu))
-    gate_grad = reduce_x(inward_grads(0, block_index, xt_own, xt_oth, gd, gd_oth, wswap))
-    up_grad = reduce_x(inward_grads(1, block_index, xt_own, xt_oth, ud, ud_oth, wswap))
+    in_parts = input_parts(gdx, udx, pg, pu)
+    input_grad = reduce_yz(in_parts)
+    wire = inward_grads(0, block_index, xt_own, xt_oth, after(gd, in_parts[0]), gd_oth)
+    gate_grad = reduce_x(wire)
+    wire = inward_grads(1, block_index, xt_own, xt_oth, after(ud, wire[0]), ud_oth)
+    up_grad = reduce_x(wire)
     return (layer_out, input_grad, gate_grad, up_grad, down_grad)
 
 

time: 157 us -> 172 us (1.096)
  waiting for transfers between devices: 13.8 us -> 33 us
  between operations: 0.97 us -> 14.3 us
  local copies, waits for them, and re-layouts: 20.3 us -> 9.99 us
  starting transfers between devices: 43.4 us -> 35.6 us
  other arithmetic: 13.1 us -> 5.41 us
  blocking collectives: 25.8 us -> 33.1 us
    reduce_scatter x0 -> x2, waiting for transfers between devices: none -> 11.9 us  [the longest x1 11.9 us: scatter_yz(): lax.psum_scatter(mine, 'fsdp', scatter_dimension=0, axis_index_groups=z_g...]
    unnamed x56 -> x18, local copies, waits for them, and re-layouts: 14.7 us -> 4.93 us
    all_to_all x1 -> x2, blocking collectives: 25.8 us -> 33.1 us  [over_z(): lax.all_to_all(value, 'fsdp', 0, 0, axis_index_groups=z_groups(), tiled=T...]
    ppermute x12 -> x9, waiting for transfers between devices: 5.86 us -> 11.6 us  [from_y(): return lax.ppermute(value, 'fsdp', pairs)]
    all_to_all x2 -> x1, starting transfers between devices: 11 us -> 6.18 us  [over_z(): lax.all_to_all(value, 'fsdp', 0, 0, axis_index_groups=z_groups(), tiled=T...]
    all_to_all x2 -> x1, waiting for transfers between devices: 0.01 us -> 4.47 us  [over_z(): lax.all_to_all(value, 'fsdp', 0, 0, axis_index_groups=z_groups(), tiled=T...]
    another operation x0 -> x2, local copies, waits for them, and re-layouts: none -> 3.23 us  [the longest x1 1.82 us: scatter_yz(): mine = mine.reshape(NZ, 4 * rows, D // 4)]
    pallas_call x4, Pallas kernels: 25.2 us -> 22.4 us  [the longest x1 7.76 us: forward(): pl.pallas_call(forward_kernel, in_specs=vm(7), out_specs=vm(7), out_shape...]
  transfers between devices with their start and end apart: 31 -> 29, of which waited for: 5 -> 8; matrix products, arithmetic and copies ran while one was open for 10% -> 5% of each run, Pallas kernels for 25% -> 18%
where the time goes in v2:
time: 172 us; the launch traced here: 170 us
  Pallas kernels  38.8 us (23%)
  starting transfers between devices  35.6 us (21%)
  blocking collectives  33.1 us (19%)
  waiting for transfers between devices  33 us (19%)
  between operations  14.3 us (8%)
  local copies, waits for them, and re-layouts  9.99 us (6%)
  other arithmetic  5.41 us (3%)
    all_to_all x2, blocking collectives, over_z(): lax.all_to_all(value, 'fsdp', 0, 0, axis_index_groups=z_groups(), tiled=T...  33.1 us
    ppermute x9, starting transfers between devices, from_y(): return lax.ppermute(value, 'fsdp', pairs)  15.8 us
    ppermute x9, starting transfers between devices, from_x(): return lax.ppermute(value, 'dp', pairs)  12.5 us
    reduce_scatter x1, waiting for transfers between devices, scatter_yz(): lax.psum_scatter(mine, 'fsdp', scatter_dimension=0, axis_index_groups=z_g...  11.9 us
    ppermute x9, waiting for transfers between devices, from_y(): return lax.ppermute(value, 'fsdp', pairs)  11.6 us
    pallas_call x1, Pallas kernels, prep(): pl.pallas_call(prep_kernel, grid_spec=pltpu.PrefetchScalarGridSpec(num_sc...  8.84 us
    pallas_call x1, Pallas kernels, forward(): pl.pallas_call(forward_kernel, in_specs=vm(7), out_specs=vm(7), out_shape...  7.76 us
    pallas_call x2, Pallas kernels, inward_grads(): pl.pallas_call(functools.partial(inward_kernel, m), in_specs=smem(1) + vm...  7.6 us
  transfers between devices with their start and end apart: 29, of which 8 were waited for; matrix products, arithmetic and copies ran while one was open for 5% of the time, Pallas kernels for 18%

profile of v2, /device:TPU:8, one launch (start us, length us, event | category | flops | bytes accessed | tf_op | source)
XLA Modules:
  0.0 170.2 jit_solution(5035244368363809094)
XLA Ops:
  7.2 0.0 reduce-scatter.3.cloned.1.call-start
  7.2 0.8 broadcast_in_dim.4
  8.0 20.1 %all_to_all.15 = bf16[8,4,4096]{2,1,0:T(4,128)(2,1)S(1)} all-to-all(bf16[8,4,4096]{2,1,0:T(4,128)(2,1)S(1)} %broadcast_in_dim.4), channel_id=1, replica_groups={{0,1,2,3,4,5,6,7},{8,9,10,11,12,13,14,15},{16,17,18,19,20,21,22,23},{24..., dimensions={0} | all-to-all | bytes 524288 | tf_op jit(solution)/shard_map/all_to_all | solution.py:427
  28.2 0.1 reshape.21.t0
  28.3 0.5 collective-permute-start
  28.8 2.6 %collective-permute-start.1 = (bf16[32,4096]{1,0:T(8,128)(2,1)S(1)}, bf16[32,4096]{1,0:T(8,128)(2,1)S(1)}, u32[]{:S(2)}, u32[]{:S(2)}) collective-permute-start(bf16[32,4096]{1,0:T(8,128)(2,1)S(1)} %reshape.21.t0), channel_id=1, source_target_pairs={{16,0},{17,1},{18,2},{19,3},{20,4},{21,5},{22,6},{23,7},{24,8},{25... | collective-permute-start | bytes 786440 | tf_op jit(solution)/shard_map/ppermute | solution.py:409
  31.4 1.9 %collective-permute-start.2 = (bf16[32,4096]{1,0:T(8,128)(2,1)S(1)}, bf16[32,4096]{1,0:T(8,128)(2,1)S(1)}, u32[]{:S(2)}, u32[]{:S(2)}) collective-permute-start(bf16[32,4096]{1,0:T(8,128)(2,1)S(1)} %reshape.21.t0), channel_id=1, source_target_pairs={{24,0},{25,1},{26,2},{27,3},{28,4},{29,5},{30,6},{31,7},{0,8},{1,9... | collective-permute-start | bytes 786440 | tf_op jit(solution)/shard_map/ppermute | solution.py:409
  33.3 0.7 copy-done.6
  33.9 8.8 %prep.1 = (bf16[2048,896]{1,0:T(8,128)(2,1)S(1)}, bf16[2048,896]{1,0:T(8,128)(2,1)S(1)}, bf16[256,8192]{1,0:T(8,128)(2,1)S(1)}) custom-call(s32[3,224]{1,0:T(4,128)S(1)} %copy-done.6, bf16[224,4096]{1,0:T(8,128)(2,1)} %g_ref.1, bf16[224,4096]{1,0:T(8,128)(2,1)} %u_ref.1, bf16[224,4096]{1,0:T(8,128)(2,1)} %d_ref.1), custom_call_target="tpu_custom_call" | custom-call | flops 200000000 | bytes 200000 | tf_op jit(solution)/shard_map/prep/pallas_call | solution.py:126
  42.8 0.0 collective-permute-done.t1
  42.8 0.0 collective-permute-done.1.t2
  42.9 0.0 copy-start.8
  42.9 0.0 copy-start.7
  42.9 7.8 %forward.1 = (bf16[2048,128]{1,0:T(8,128)(2,1)S(1)}, bf16[2048,128]{1,0:T(8,128)(2,1)S(1)}, bf16[256,128]{1,0:T(8,128)(2,1)S(1)}, bf16[256,128]{1,0:T(8,128)(2,1...) custom-call(bf16[32,4096]{1,0:T(8,128)(2,1)S(1)} %reshape.21.t0, ...), custom_call_target="tpu_custom_call" | custom-call | flops 300000000 | bytes 300000 | tf_op jit(solution)/shard_map/forward/pallas_call | solution.py:201
  50.6 0.0 reduce-scatter.3.cloned.1.call-update
  50.7 0.0 reduce-scatter.5.cloned.1.call-start
  50.7 0.1 broadcast_in_dim.5
  50.8 13.0 %all_to_all.16 = bf16[8,4,4096]{2,1,0:T(4,128)(2,1)S(1)} all-to-all(bf16[8,4,4096]{2,1,0:T(4,128)(2,1)S(1)} %broadcast_in_dim.5), channel_id=1, replica_groups={{0,1,2,3,4,5,6,7},{8,9,10,11,12,13,14,15},{16,17,18,19,20,21,22,23},{24..., dimensions={0} | all-to-all | bytes 524288 | tf_op jit(solution)/shard_map/all_to_all | solution.py:427
  63.8 0.1 reshape.22.c0
  63.9 4.0 %collective-permute-start.3 = (bf16[32,4096]{1,0:T(8,128)(2,1)S(1)}, bf16[32,4096]{1,0:T(8,128)(2,1)S(1)}, u32[]{:S(2)}, u32[]{:S(2)}) collective-permute-start(bf16[32,4096]{1,0:T(8,128)(2,1)S(1)} %reshape.22.c0), channel_id=1, source_target_pairs={{8,0},{9,1},{10,2},{11,3},{12,4},{13,5},{14,6},{15,7},{16,8},{17,9... | collective-permute-start | bytes 786440 | tf_op jit(solution)/shard_map/ppermute | solution.py:409
  67.9 0.0 collective-permute-start.4
  67.9 1.5 collective-permute-start.5
  69.4 6.2 %collective-permute-done.3.c1 = bf16[32,4096]{1,0:T(8,128)(2,1)S(1)} collective-permute-done((bf16[32,4096]{1,0:T(8,128)(2,1)S(1)}, bf16[32,4096]{1,0:T(8,128)(2,1)S(1)}, u32[]{:S(2)}, u32[]{:S(2)}) %collective-permute-start.3) | collective-permute-done | bytes 262176 | tf_op jit(solution)/shard_map/ppermute | solution.py:409
  75.7 5.2 %collective-permute-done.4.c2 = bf16[32,4096]{1,0:T(8,128)(2,1)S(1)} collective-permute-done((bf16[32,4096]{1,0:T(8,128)(2,1)S(1)}, bf16[32,4096]{1,0:T(8,128)(2,1)S(1)}, u32[]{:S(2)}, u32[]{:S(2)}) %collective-permute-start.4) | collective-permute-done | bytes 262176 | tf_op jit(solution)/shard_map/ppermute | solution.py:409
  80.9 0.1 collective-permute-done.5.c3
  81.0 0.4 collective-permute-start.9
  81.5 0.1 collective-permute-start.10
  81.5 0.4 collective-permute-start.14
  82.0 1.0 collective-permute-done.10.ht_oth
  83.0 5.1 %down_grads.1 = (bf16[224,512]{1,0:T(8,128)(2,1)S(1)}, bf16[224,512]{1,0:T(8,128)(2,1)S(1)}, bf16[224,512]{1,0:T(8,128)(2,1)S(1)}, bf16[224,512]{1,0:T(8,128)(2,1)S(1)}) custom-call(s32[3,224]{1,0:T(4,128)S(1)} %copy-done.7, bf16[32,4096]{1,0:T(8,128)(2,1)S(1)} %reshape.22.c0, bf16[32,4096]{1,0:T(8,128)(2,1)S(1)} %collective-permute-done.3.c1, ...), custom_call_target="tpu_custom_call" | custom-call | flops 200000000 | bytes 200000 | tf_op jit(solution)/shard_map/down_grads/pallas_call | solution.py:255
  88.1 2.8 %collective-permute-start.25 = (bf16[224,512]{1,0:T(8,128)(2,1)S(1)}, bf16[224,512]{1,0:T(8,128)(2,1)S(1)}, u32[]{:S(2)}, u32[]{:S(2)}) collective-permute-start(bf16[224,512]{1,0:T(8,128)(2,1)S(1)} %get-tuple-element.74), channel_id=1, source_target_pairs={{192,0},{224,32},{128,64},{160,96},{64,128},{96,160},{0,192},{32,2... | collective-permute-start | bytes 688136 | tf_op jit(solution)/shard_map/ppermute | solution.py:414
  90.9 0.8 collective-permute-start.24
  91.7 0.6 collective-permute-start.23
  92.3 2.2 %copy-done.1 = bf16[256,8192]{1,0:T(8,128)(2,1)S(1)} copy-done((bf16[256,8192]{1,0:T(8,128)(2,1)S(1)}, bf16[256,8192]{1,0:T(8,128)(2,1)}, u32[]{:S(2)}) %copy-start.1) | copy-done | bytes 4194328
  94.5 4.2 %deltas.1 = (bf16[128,512]{1,0:T(8,128)(2,1)S(1)}, bf16[128,512]{1,0:T(8,128)(2,1)S(1)}, bf16[256,896]{1,0:T(8,128)(2,1)S(1)}, bf16[256,896]{1,0:T(8,128)(2,1)S(1)}) custom-call(bf16[32,4096]{1,0:T(8,128)(2,1)S(1)} %reshape.22.c0, bf16[32,4096]{1,0:T(8,128)(2,1)S(1)} %collective-permute-done.3.c1, bf16[32,4096]{1,0:T(8,128)(2,1)S(1)} %collective-permute-done.4.c2, ...), custom_call_target="tpu_custom_call" | custom-call | flops 200000000 | bytes 200000 | tf_op jit(solution)/shard_map/deltas/pallas_call | solution.py:325
  98.6 0.1 collective-permute-start.15
  98.8 2.0 %copy-done.5 = bf16[2048,896]{1,0:T(8,128)(2,1)S(1)} copy-done((bf16[2048,896]{1,0:T(8,128)(2,1)S(1)}, bf16[2048,896]{1,0:T(8,128)(2,1)}, u32[]{:S(2)}) %copy-start.5) | copy-done | bytes 3670040
  100.8 5.4 %input_parts.1 = (bf16[32,4096]{1,0:T(8,128)(2,1)S(1)}, bf16[32,4096]{1,0:T(8,128)(2,1)S(1)}, bf16[32,4096]{1,0:T(8,128)(2,1)S(1)}, bf16[32,4096]{1,0:T(8,128)(2,1)S(1)}) custom-call(bf16[256,896]{1,0:T(8,128)(2,1)S(1)} %get-tuple-element.52.gdx, bf16[256,896]{1,0:T(8,128)(2,1)S(1)} %get-tuple-element.53.udx, bf16[2048,896]{1,0:T(8,128)(2,1)S(1)} %copy-done.3, ...), custom_call_target="tpu_custom_call" | custom-call | flops 200000000 | bytes 200000 | tf_op jit(solution)/shard_map/input_parts/pallas_call | solution.py:356
  106.2 2.0 %collective-permute-start.13 = (bf16[32,4096]{1,0:T(8,128)(2,1)S(1)}, bf16[32,4096]{1,0:T(8,128)(2,1)}, u32[]{:S(2)}, u32[]{:S(2)}) collective-permute-start(bf16[32,4096]{1,0:T(8,128)(2,1)S(1)} %get-tuple-element.57), channel_id=1, source_target_pairs={{8,0},{9,1},{10,2},{11,3},{12,4},{13,5},{14,6},{15,7},{16,8},{17,9... | collective-permute-start | bytes 786440 | tf_op jit(solution)/shard_map/ppermute | solution.py:409
  108.2 0.7 collective-permute-start.12
  108.9 2.5 %collective-permute-start.11 = (bf16[32,4096]{1,0:T(8,128)(2,1)S(1)}, bf16[32,4096]{1,0:T(8,128)(2,1)}, u32[]{:S(2)}, u32[]{:S(2)}) collective-permute-start(bf16[32,4096]{1,0:T(8,128)(2,1)S(1)} %get-tuple-element.55), channel_id=1, source_target_pairs={{24,0},{25,1},{26,2},{27,3},{28,4},{29,5},{30,6},{31,7},{0,8},{1,9... | collective-permute-start | bytes 786440 | tf_op jit(solution)/shard_map/ppermute | solution.py:409
  111.4 0.8 multiply_convert_fusion
  112.2 4.2 %gate_grads.1 = (bf16[224,512]{1,0:T(8,128)(2,1)S(1)}, bf16[224,512]{1,0:T(8,128)(2,1)S(1)}, bf16[224,512]{1,0:T(8,128)(2,1)S(1)}, bf16[224,512]{1,0:T(8,128)(2,1)}) custom-call(s32[3,224]{1,0:T(4,128)S(1)} %copy-done.7, bf16[2048,128]{1,0:T(8,128)(2,1)S(1)} %get-tuple-element.58.xt_own, bf16[2048,128]{1,0:T(8,128)(2,1)S(1)} %collective-permute-done.14.xt_oth, ...), custom_call_target="tpu_custom_call" | custom-call | flops 200000000 | bytes 200000 | tf_op jit(solution)/shard_map/gate_grads/pallas_call | solution.py:395
  116.4 2.6 %collective-permute-start.18 = (bf16[224,512]{1,0:T(8,128)(2,1)}, bf16[224,512]{1,0:T(8,128)(2,1)S(1)}, u32[]{:S(2)}, u32[]{:S(2)}) collective-permute-start(bf16[224,512]{1,0:T(8,128)(2,1)} %get-tuple-element.65), channel_id=1, source_target_pairs={{192,0},{224,32},{128,64},{160,96},{64,128},{96,160},{0,192},{32,2... | collective-permute-start | bytes 688136 | tf_op jit(solution)/shard_map/ppermute | solution.py:414
  119.0 0.9 collective-permute-start.17
  119.9 3.4 %up_grads.1 = (bf16[224,512]{1,0:T(8,128)(2,1)S(1)}, bf16[224,512]{1,0:T(8,128)(2,1)S(1)}, bf16[224,512]{1,0:T(8,128)(2,1)S(1)}, bf16[224,512]{1,0:T(8,128)(2,1)S(1)}) custom-call(s32[3,224]{1,0:T(4,128)S(1)} %copy-done.7, bf16[2048,128]{1,0:T(8,128)(2,1)S(1)} %get-tuple-element.58.xt_own, bf16[2048,128]{1,0:T(8,128)(2,1)S(1)} %collective-permute-done.14.xt_oth, ...), custom_call_target="tpu_custom_call" | custom-call | flops 200000000 | bytes 200000 | tf_op jit(solution)/shard_map/up_grads/pallas_call | solution.py:395
  123.4 0.0 reduce-scatter.3.cloned.1.call-done
  123.4 1.8 %reshape_reduce_scatter.6 = bf16[8,16,1024]{2,1,0:T(8,128)(2,1)} reshape(bf16[1,32,4096]{2,1,0:T(8,128)(2,1)} %reduce-scatter.3.cloned.1.call-done) | data formatting | bytes 524288 | tf_op jit(solution)/shard_map/reshape;reduce_scatter | solution.py:457
  125.2 0.0 reduce-scatter.5.cloned.1.call-update
  125.2 0.7 collective-permute-start.16
  125.9 2.6 %collective-permute-start.22 = (bf16[224,512]{1,0:T(8,128)(2,1)S(1)}, bf16[224,512]{1,0:T(8,128)(2,1)S(1)}, u32[]{:S(2)}, u32[]{:S(2)}) collective-permute-start(bf16[224,512]{1,0:T(8,128)(2,1)S(1)} %get-tuple-element.71), channel_id=1, source_target_pairs={{192,0},{224,32},{128,64},{160,96},{64,128},{96,160},{0,192},{32,2... | collective-permute-start | bytes 688136 | tf_op jit(solution)/shard_map/ppermute | solution.py:414
  128.5 0.9 collective-permute-start.21
  129.4 1.3 add_convert_fusion
  130.7 0.8 reshape.23
  131.5 6.2 %all-to-all-start.2 = ((bf16[8,4,4096]{2,1,0:T(4,128)(2,1)}), bf16[8,4,4096]{2,1,0:T(4,128)(2,1)S(1)}, u32[]{:S(2)}, u32[]{:S(2)}) async-start(bf16[8,4,4096]{2,1,0:T(4,128)(2,1)} %reshape.23), calls=%async_computation.4 | async-start | bytes 524288 | tf_op jit(solution)/shard_map/all_to_all | solution.py:427
  137.7 0.6 collective-permute-start.20
  138.3 1.8 %multiply_convert_fusion.2 = bf16[224,512]{1,0:T(8,128)(2,1)} fusion(bf16[224,512]{1,0:T(8,128)(2,1)S(1)} %collective-permute-done.18, bf16[224,512]{1,0:T(8,128)(2,1)} %collective-permute-done.17, bf16[224,512]{1,0:T(8,128)(2,1)S(1)} %collective-permute-done.16, bf16[224,512]{1,0:T(8,128)(2,1)S(1)} %get-tuple-element.62), kind=kLoop, calls=%fused_computation.3 | loop fusion | flops 1032192 | bytes 1146880 | tf_op jit(solution)/shard_map/convert_element_type | solution.py:444
  140.1 0.4 collective-permute-done.22
  140.5 3.6 %collective-permute-done.20 = bf16[224,512]{1,0:T(8,128)(2,1)S(1)} collective-permute-done((bf16[224,512]{1,0:T(8,128)(2,1)S(1)}, bf16[224,512]{1,0:T(8,128)(2,1)S(1)}, u32[]{:S(2)}, u32[]{:S(2)}) %collective-permute-start.20) | collective-permute-done | bytes 229408 | tf_op jit(solution)/shard_map/ppermute | solution.py:414
  144.1 0.8 multiply_convert_fusion.1
  144.9 4.5 %all-to-all-done.2 = bf16[8,4,4096]{2,1,0:T(4,128)(2,1)S(1)} async-done(((bf16[8,4,4096]{2,1,0:T(4,128)(2,1)}), bf16[8,4,4096]{2,1,0:T(4,128)(2,1)S(1)}, u32[]{:S(2)}, u32[]{:S(2)}) %all-to-all-start.2) | async-done | bytes 262176 | tf_op jit(solution)/shard_map/all_to_all | solution.py:427
  149.4 0.7 reduce_sum.12
  150.1 11.9 %reduce-scatter.5.cloned.1.call-done = bf16[1,16,1024]{2,1,0:T(8,128)(2,1)} async-done(((bf16[8,16,1024]{2,1,0:T(8,128)(2,1)}), bf16[1,16,1024]{2,1,0:T(8,128)(2,1)}) %reduce-scatter.5.cloned.1.call-update) | async-done | bytes 32784 | tf_op jit(solution)/shard_map/reduce_scatter | solution.py:458
  162.0 1.4 reshape_reduce_scatter.7
  (35 shorter events, 0.1 us)
Async XLA Ops:
  7.2 116.2 %reduce-scatter.3.cloned.1.call-start = ((), (), s32[]{:S(2)}) async-start(), calls=%async_computation.5 | async-start | bytes 1310720 | tf_op jit(solution)/shard_map/reduce_scatter | solution.py:456
  28.3 14.6 %collective-permute-start = (bf16[32,4096]{1,0:T(8,128)(2,1)S(1)}, bf16[32,4096]{1,0:T(8,128)(2,1)S(1)}, u32[]{:S(2)}, u32[]{:S(2)}) collective-permute-start(bf16[32,4096]{1,0:T(8,128)(2,1)S(1)} %reshape.21.t0), channel_id=1, source_target_pairs={{8,0},{9,1},{10,2},{11,3},{12,4},{13,5},{14,6},{15,7},{16,8},{17,9... | collective-permute-start | bytes 786440 | tf_op jit(solution)/shard_map/ppermute | solution.py:409
  28.8 14.1 %collective-permute-start.1 = (bf16[32,4096]{1,0:T(8,128)(2,1)S(1)}, bf16[32,4096]{1,0:T(8,128)(2,1)S(1)}, u32[]{:S(2)}, u32[]{:S(2)}) collective-permute-start(bf16[32,4096]{1,0:T(8,128)(2,1)S(1)} %reshape.21.t0), channel_id=1, source_target_pairs={{16,0},{17,1},{18,2},{19,3},{20,4},{21,5},{22,6},{23,7},{24,8},{25... | collective-permute-start | bytes 786440 | tf_op jit(solution)/shard_map/ppermute | solution.py:409
  31.4 11.5 %collective-permute-start.2 = (bf16[32,4096]{1,0:T(8,128)(2,1)S(1)}, bf16[32,4096]{1,0:T(8,128)(2,1)S(1)}, u32[]{:S(2)}, u32[]{:S(2)}) collective-permute-start(bf16[32,4096]{1,0:T(8,128)(2,1)S(1)} %reshape.21.t0), channel_id=1, source_target_pairs={{24,0},{25,1},{26,2},{27,3},{28,4},{29,5},{30,6},{31,7},{0,8},{1,9... | collective-permute-start | bytes 786440 | tf_op jit(solution)/shard_map/ppermute | solution.py:409
  33.3 0.7 copy-start.6
  42.8 7.8 %copy-start = (bf16[256,8192]{1,0:T(8,128)(2,1)}, bf16[256,8192]{1,0:T(8,128)(2,1)S(1)}, u32[]{:S(2)}) copy-start(bf16[256,8192]{1,0:T(8,128)(2,1)S(1)} %get-tuple-element.43.pd) | copy-start | bytes 12582916
  42.8 7.8 %copy-start.2 = (bf16[2048,896]{1,0:T(8,128)(2,1)}, bf16[2048,896]{1,0:T(8,128)(2,1)S(1)}, u32[]{:S(2)}) copy-start(bf16[2048,896]{1,0:T(8,128)(2,1)S(1)} %get-tuple-element.41.pg) | copy-start | bytes 11010052
  42.8 7.8 %copy-start.4 = (bf16[2048,896]{1,0:T(8,128)(2,1)}, bf16[2048,896]{1,0:T(8,128)(2,1)S(1)}, u32[]{:S(2)}) copy-start(bf16[2048,896]{1,0:T(8,128)(2,1)S(1)} %get-tuple-element.42.pu) | copy-start | bytes 11010052
  42.9 7.9 %copy-start.8 = (bf16[4,4096]{1,0:T(4,128)(2,1)S(1)}, bf16[4,4096]{1,0:T(4,128)(2,1)}, u32[]{:S(2)}) copy-start(bf16[4,4096]{1,0:T(4,128)(2,1)} %param.7) | copy-start | bytes 98308
  42.9 40.1 %copy-start.7 = (s32[3,224]{1,0:T(4,128)S(1)}, s32[3,224]{1,0:T(4,128)}, u32[]{:S(2)}) copy-start(s32[3,224]{1,0:T(4,128)} %idx.6) | copy-start | bytes 8068
  50.7 111.3 %reduce-scatter.5.cloned.1.call-start = ((), (), s32[]{:S(2)}) async-start(), calls=%async_computation.6 | async-start | bytes 294912 | tf_op jit(solution)/shard_map/reduce_scatter | solution.py:458
  63.9 11.8 %collective-permute-start.3 = (bf16[32,4096]{1,0:T(8,128)(2,1)S(1)}, bf16[32,4096]{1,0:T(8,128)(2,1)S(1)}, u32[]{:S(2)}, u32[]{:S(2)}) collective-permute-start(bf16[32,4096]{1,0:T(8,128)(2,1)S(1)} %reshape.22.c0), channel_id=1, source_target_pairs={{8,0},{9,1},{10,2},{11,3},{12,4},{13,5},{14,6},{15,7},{16,8},{17,9... | collective-permute-start | bytes 786440 | tf_op jit(solution)/shard_map/ppermute | solution.py:409
  67.9 13.1 %collective-permute-start.4 = (bf16[32,4096]{1,0:T(8,128)(2,1)S(1)}, bf16[32,4096]{1,0:T(8,128)(2,1)S(1)}, u32[]{:S(2)}, u32[]{:S(2)}) collective-permute-start(bf16[32,4096]{1,0:T(8,128)(2,1)S(1)} %reshape.22.c0), channel_id=1, source_target_pairs={{16,0},{17,1},{18,2},{19,3},{20,4},{21,5},{22,6},{23,7},{24,8},{25... | collective-permute-start | bytes 786440 | tf_op jit(solution)/shard_map/ppermute | solution.py:409
  67.9 13.1 %collective-permute-start.5 = (bf16[32,4096]{1,0:T(8,128)(2,1)S(1)}, bf16[32,4096]{1,0:T(8,128)(2,1)S(1)}, u32[]{:S(2)}, u32[]{:S(2)}) collective-permute-start(bf16[32,4096]{1,0:T(8,128)(2,1)S(1)} %reshape.22.c0), channel_id=1, source_target_pairs={{24,0},{25,1},{26,2},{27,3},{28,4},{29,5},{30,6},{31,7},{0,8},{1,9... | collective-permute-start | bytes 786440 | tf_op jit(solution)/shard_map/ppermute | solution.py:409
  69.4 12.1 %collective-permute-start.6 = (bf16[32,4096]{1,0:T(8,128)(2,1)S(1)}, bf16[32,4096]{1,0:T(8,128)(2,1)S(1)}, u32[]{:S(2)}, u32[]{:S(2)}) collective-permute-start(bf16[32,4096]{1,0:T(8,128)(2,1)S(1)} %reshape.22.c0), channel_id=1, source_target_pairs={{32,0},{0,32},{96,64},{64,96},{160,128},{128,160},{224,192},{192,2... | collective-permute-start | bytes 786440 | tf_op jit(solution)/shard_map/ppermute | solution.py:419
  75.7 7.3 %collective-permute-start.7 = (bf16[32,4096]{1,0:T(8,128)(2,1)S(1)}, bf16[32,4096]{1,0:T(8,128)(2,1)S(1)}, u32[]{:S(2)}, u32[]{:S(2)}) collective-permute-start(bf16[32,4096]{1,0:T(8,128)(2,1)S(1)} %collective-permute-done.3.c1), channel_id=1, source_target_pairs={{32,0},{0,32},{96,64},{64,96},{160,128},{128,160},{224,192},{192,2... | collective-permute-start | bytes 786440 | tf_op jit(solution)/shard_map/ppermute | solution.py:419
  80.9 2.0 %collective-permute-start.8 = (bf16[32,4096]{1,0:T(8,128)(2,1)S(1)}, bf16[32,4096]{1,0:T(8,128)(2,1)S(1)}, u32[]{:S(2)}, u32[]{:S(2)}) collective-permute-start(bf16[32,4096]{1,0:T(8,128)(2,1)S(1)} %collective-permute-done.4.c2), channel_id=1, source_target_pairs={{32,0},{0,32},{96,64},{64,96},{160,128},{128,160},{224,192},{192,2... | collective-permute-start | bytes 786440 | tf_op jit(solution)/shard_map/ppermute | solution.py:419
  81.0 1.9 %collective-permute-start.9 = (bf16[32,4096]{1,0:T(8,128)(2,1)S(1)}, bf16[32,4096]{1,0:T(8,128)(2,1)S(1)}, u32[]{:S(2)}, u32[]{:S(2)}) collective-permute-start(bf16[32,4096]{1,0:T(8,128)(2,1)S(1)} %collective-permute-done.5.c3), channel_id=1, source_target_pairs={{32,0},{0,32},{96,64},{64,96},{160,128},{128,160},{224,192},{192,2... | collective-permute-start | bytes 786440 | tf_op jit(solution)/shard_map/ppermute | solution.py:419
  81.5 1.5 collective-permute-start.10
  81.5 30.7 %collective-permute-start.14 = (bf16[2048,128]{1,0:T(8,128)(2,1)S(1)}, bf16[2048,128]{1,0:T(8,128)(2,1)S(1)}, u32[]{:S(2)}, u32[]{:S(2)}) collective-permute-start(bf16[2048,128]{1,0:T(8,128)(2,1)S(1)} %get-tuple-element.59), channel_id=1, source_target_pairs={{32,0},{0,32},{96,64},{64,96},{160,128},{128,160},{224,192},{192,2... | collective-permute-start | bytes 1572872 | tf_op jit(solution)/shard_map/ppermute | solution.py:419
  88.1 20.1 %collective-permute-start.25 = (bf16[224,512]{1,0:T(8,128)(2,1)S(1)}, bf16[224,512]{1,0:T(8,128)(2,1)S(1)}, u32[]{:S(2)}, u32[]{:S(2)}) collective-permute-start(bf16[224,512]{1,0:T(8,128)(2,1)S(1)} %get-tuple-element.74), channel_id=1, source_target_pairs={{192,0},{224,32},{128,64},{160,96},{64,128},{96,160},{0,192},{32,2... | collective-permute-start | bytes 688136 | tf_op jit(solution)/shard_map/ppermute | solution.py:414
  90.9 17.9 %collective-permute-start.24 = (bf16[224,512]{1,0:T(8,128)(2,1)S(1)}, bf16[224,512]{1,0:T(8,128)(2,1)S(1)}, u32[]{:S(2)}, u32[]{:S(2)}) collective-permute-start(bf16[224,512]{1,0:T(8,128)(2,1)S(1)} %get-tuple-element.73), channel_id=1, source_target_pairs={{128,0},{160,32},{192,64},{224,96},{0,128},{32,160},{64,192},{96,2... | collective-permute-start | bytes 688136 | tf_op jit(solution)/shard_map/ppermute | solution.py:414
  91.7 19.7 %collective-permute-start.23 = (bf16[224,512]{1,0:T(8,128)(2,1)S(1)}, bf16[224,512]{1,0:T(8,128)(2,1)S(1)}, u32[]{:S(2)}, u32[]{:S(2)}) collective-permute-start(bf16[224,512]{1,0:T(8,128)(2,1)S(1)} %get-tuple-element.72), channel_id=1, source_target_pairs={{64,0},{96,32},{0,64},{32,96},{192,128},{224,160},{128,192},{160,2... | collective-permute-start | bytes 688136 | tf_op jit(solution)/shard_map/ppermute | solution.py:414
  92.3 2.2 %copy-start.1 = (bf16[256,8192]{1,0:T(8,128)(2,1)S(1)}, bf16[256,8192]{1,0:T(8,128)(2,1)}, u32[]{:S(2)}) copy-start(bf16[256,8192]{1,0:T(8,128)(2,1)} %copy-done) | copy-start | bytes 12582916
  94.5 4.3 %copy-start.3 = (bf16[2048,896]{1,0:T(8,128)(2,1)S(1)}, bf16[2048,896]{1,0:T(8,128)(2,1)}, u32[]{:S(2)}) copy-start(bf16[2048,896]{1,0:T(8,128)(2,1)} %copy-done.2) | copy-start | bytes 11010052
  98.6 7.5 %collective-permute-start.15 = (bf16[128,512]{1,0:T(8,128)(2,1)S(1)}, bf16[128,512]{1,0:T(8,128)(2,1)S(1)}, u32[]{:S(2)}, u32[]{:S(2)}) collective-permute-start(bf16[128,512]{1,0:T(8,128)(2,1)S(1)} %get-tuple-element.61.d_own), channel_id=1, source_target_pairs={{32,0},{0,32},{96,64},{64,96},{160,128},{128,160},{224,192},{192,2... | collective-permute-start | bytes 393224 | tf_op jit(solution)/shard_map/ppermute | solution.py:419
  98.8 2.0 %copy-start.5 = (bf16[2048,896]{1,0:T(8,128)(2,1)S(1)}, bf16[2048,896]{1,0:T(8,128)(2,1)}, u32[]{:S(2)}) copy-start(bf16[2048,896]{1,0:T(8,128)(2,1)} %copy-done.4) | copy-start | bytes 11010052
  106.2 19.1 %collective-permute-start.13 = (bf16[32,4096]{1,0:T(8,128)(2,1)S(1)}, bf16[32,4096]{1,0:T(8,128)(2,1)}, u32[]{:S(2)}, u32[]{:S(2)}) collective-permute-start(bf16[32,4096]{1,0:T(8,128)(2,1)S(1)} %get-tuple-element.57), channel_id=1, source_target_pairs={{8,0},{9,1},{10,2},{11,3},{12,4},{13,5},{14,6},{15,7},{16,8},{17,9... | collective-permute-start | bytes 786440 | tf_op jit(solution)/shard_map/ppermute | solution.py:409
  108.2 17.7 %collective-permute-start.12 = (bf16[32,4096]{1,0:T(8,128)(2,1)S(1)}, bf16[32,4096]{1,0:T(8,128)(2,1)}, u32[]{:S(2)}, u32[]{:S(2)}) collective-permute-start(bf16[32,4096]{1,0:T(8,128)(2,1)S(1)} %get-tuple-element.56), channel_id=1, source_target_pairs={{16,0},{17,1},{18,2},{19,3},{20,4},{21,5},{22,6},{23,7},{24,8},{25... | collective-permute-start | bytes 786440 | tf_op jit(solution)/shard_map/ppermute | solution.py:409
  108.9 19.7 %collective-permute-start.11 = (bf16[32,4096]{1,0:T(8,128)(2,1)S(1)}, bf16[32,4096]{1,0:T(8,128)(2,1)}, u32[]{:S(2)}, u32[]{:S(2)}) collective-permute-start(bf16[32,4096]{1,0:T(8,128)(2,1)S(1)} %get-tuple-element.55), channel_id=1, source_target_pairs={{24,0},{25,1},{26,2},{27,3},{28,4},{29,5},{30,6},{31,7},{0,8},{1,9... | collective-permute-start | bytes 786440 | tf_op jit(solution)/shard_map/ppermute | solution.py:409
  111.4 7.6 %collective-permute-start.19 = (bf16[128,512]{1,0:T(8,128)(2,1)S(1)}, bf16[128,512]{1,0:T(8,128)(2,1)S(1)}, u32[]{:S(2)}, u32[]{:S(2)}) collective-permute-start(bf16[128,512]{1,0:T(8,128)(2,1)S(1)} %get-tuple-element.67.d_own), channel_id=1, source_target_pairs={{32,0},{0,32},{96,64},{64,96},{160,128},{128,160},{224,192},{192,2... | collective-permute-start | bytes 393224 | tf_op jit(solution)/shard_map/ppermute | solution.py:419
  116.4 21.3 %collective-permute-start.18 = (bf16[224,512]{1,0:T(8,128)(2,1)}, bf16[224,512]{1,0:T(8,128)(2,1)S(1)}, u32[]{:S(2)}, u32[]{:S(2)}) collective-permute-start(bf16[224,512]{1,0:T(8,128)(2,1)} %get-tuple-element.65), channel_id=1, source_target_pairs={{192,0},{224,32},{128,64},{160,96},{64,128},{96,160},{0,192},{32,2... | collective-permute-start | bytes 688136 | tf_op jit(solution)/shard_map/ppermute | solution.py:414
  119.0 19.3 %collective-permute-start.17 = (bf16[224,512]{1,0:T(8,128)(2,1)S(1)}, bf16[224,512]{1,0:T(8,128)(2,1)}, u32[]{:S(2)}, u32[]{:S(2)}) collective-permute-start(bf16[224,512]{1,0:T(8,128)(2,1)S(1)} %get-tuple-element.64), channel_id=1, source_target_pairs={{128,0},{160,32},{192,64},{224,96},{0,128},{32,160},{64,192},{96,2... | collective-permute-start | bytes 688136 | tf_op jit(solution)/shard_map/ppermute | solution.py:414
  125.2 13.1 %collective-permute-start.16 = (bf16[224,512]{1,0:T(8,128)(2,1)S(1)}, bf16[224,512]{1,0:T(8,128)(2,1)S(1)}, u32[]{:S(2)}, u32[]{:S(2)}) collective-permute-start(bf16[224,512]{1,0:T(8,128)(2,1)S(1)} %get-tuple-element.63), channel_id=1, source_target_pairs={{64,0},{96,32},{0,64},{32,96},{192,128},{224,160},{128,192},{160,2... | collective-permute-start | bytes 688136 | tf_op jit(solution)/shard_map/ppermute | solution.py:414
  125.9 14.6 %collective-permute-start.22 = (bf16[224,512]{1,0:T(8,128)(2,1)S(1)}, bf16[224,512]{1,0:T(8,128)(2,1)S(1)}, u32[]{:S(2)}, u32[]{:S(2)}) collective-permute-start(bf16[224,512]{1,0:T(8,128)(2,1)S(1)} %get-tuple-element.71), channel_id=1, source_target_pairs={{192,0},{224,32},{128,64},{160,96},{64,128},{96,160},{0,192},{32,2... | collective-permute-start | bytes 688136 | tf_op jit(solution)/shard_map/ppermute | solution.py:414
  128.5 12.0 %collective-permute-start.21 = (bf16[224,512]{1,0:T(8,128)(2,1)S(1)}, bf16[224,512]{1,0:T(8,128)(2,1)S(1)}, u32[]{:S(2)}, u32[]{:S(2)}) collective-permute-start(bf16[224,512]{1,0:T(8,128)(2,1)S(1)} %get-tuple-element.70), channel_id=1, source_target_pairs={{128,0},{160,32},{192,64},{224,96},{0,128},{32,160},{64,192},{96,2... | collective-permute-start | bytes 688136 | tf_op jit(solution)/shard_map/ppermute | solution.py:414
  131.5 17.9 %all-to-all-start.2 = ((bf16[8,4,4096]{2,1,0:T(4,128)(2,1)}), bf16[8,4,4096]{2,1,0:T(4,128)(2,1)S(1)}, u32[]{:S(2)}, u32[]{:S(2)}) async-start(bf16[8,4,4096]{2,1,0:T(4,128)(2,1)} %reshape.23), calls=%async_computation.4 | async-start | bytes 524288 | tf_op jit(solution)/shard_map/all_to_all | solution.py:427
  137.7 6.4 %collective-permute-start.20 = (bf16[224,512]{1,0:T(8,128)(2,1)S(1)}, bf16[224,512]{1,0:T(8,128)(2,1)S(1)}, u32[]{:S(2)}, u32[]{:S(2)}) collective-permute-start(bf16[224,512]{1,0:T(8,128)(2,1)S(1)} %get-tuple-element.69), channel_id=1, source_target_pairs={{64,0},{96,32},{0,64},{32,96},{192,128},{224,160},{128,192},{160,2... | collective-permute-start | bytes 688136 | tf_op jit(solution)/shard_map/ppermute | solution.py:414
Sparse Core Ops, SparseCore 0:
  50.8 24.3 reduce-scatter.2
  125.4 36.5 reduce-scatter.4

commit v3 on v2

v3 whole, which is shorter than its diff:
```python
import functools

import jax
import jax.numpy as jnp
from jax import lax
from jax.experimental import pallas as pl
from jax.experimental.pallas import tpu as pltpu
from jax.sharding import PartitionSpec as P

D = 4096
BLK = 64
KEEP = 32
COLS = 7
SLOT = COLS * KEEP
TOK = 128
FEAT = 2048
WIDE = COLS * 128
NX, NC, NY, NZ = 4, 2, 4, 8
BF = jnp.bfloat16
F32 = jnp.float32

TILE_ROWS = [[8 * x + 4 * c + k4 for x in range(NX) for k4 in range(4)] for c in range(NC)]


def rows_of(n):
    return lax.broadcasted_iota(jnp.int32, (n, 1), 0)


def cols_of(n):
    return lax.broadcasted_iota(jnp.int32, (1, n), 1)


def one_hot(left, right):
    return jnp.where(left == right, 1.0, 0.0).astype(BF)


def split_index(at, stride):
    k = 8 * ((at >> 2) & 3) + 4 * ((at >> 4) & 1) + (at & 3)
    return ((at >> 5) & 3) * stride + 2 * k + (at >> 7)


def turn_index(at, core, stride):
    k = 8 * ((at >> 2) & 3) + 4 * (core ^ (at >> 7)) + (at & 3)
    return ((at >> 4) & 3) * stride + 2 * k + ((at >> 6) & 1)


def swap_matrix():
    at = cols_of(256)
    return one_hot(rows_of(256), (at & 15) * 16 + (at >> 4))


def wire_swap(x):
    at = rows_of(256)
    return one_hot((at & 15) * 16 + ((at >> 6) ^ x) * 4 + ((at >> 4) & 3), cols_of(256))


def place():
    dp, fsdp = lax.axis_index("dp"), lax.axis_index("fsdp")
    return lax.rem(dp, NC), dp // NC, fsdp // NZ


def mm(a, b):
    return jnp.dot(a, b, preferred_element_type=F32)


def mm_nt(a, b):
    return lax.dot_general(a, b, (((1,), (1,)), ((), ())), preferred_element_type=F32)


def low_half(shape):
    return lax.broadcasted_iota(jnp.int32, shape, 1) < 64


def vm(n):
    return [pl.BlockSpec(memory_space=pltpu.VMEM)] * n


def smem(n):
    return [pl.BlockSpec(memory_space=pltpu.SMEM)] * n


def params(mib):
    return pltpu.CompilerParams(vmem_limit_bytes=mib << 20)


def cost(us):
    return pl.CostEstimate(flops=int(us * 1_000_000_000), bytes_accessed=1000, transcendentals=0)


def shape(*dims, dtype=BF):
    return jax.ShapeDtypeStruct(dims, dtype)


def unfold(src, qh, swap):
    rows = slice(qh * 16, qh * 16 + 16)
    halves = [jnp.concatenate([src[rows, k * 128:k * 128 + 128] for k in TILE_ROWS[c]], axis=0) for c in range(2)]
    return mm(swap, jnp.concatenate(halves, axis=1)).astype(BF)


def inward_panels_kernel(idx, g_ref, u_ref, pg, pu, scr):
    j = pl.program_id(0)
    pg[...] = jnp.zeros_like(pg)
    pu[...] = jnp.zeros_like(pu)
    swap = swap_matrix()
    for m, (src, dst) in enumerate(((g_ref, pg), (u_ref, pu))):
        for qh in range(2):
            tiles = scr.at[2 * m + qh]
            tiles[...] = unfold(src, qh, swap)
            for q in range(16):
                i = idx[m, j * KEEP + qh * 16 + q]
                for c in range(2):
                    dst[pl.ds(pl.multiple_of(i * 32 + c * 16, 16), 16), :] = tiles[
                        q * 16:q * 16 + 16, c * 128:c * 128 + 128
                    ]


def outward_panel_kernel(idx, d_ref, pd, scr):
    j = pl.program_id(0)
    pd[...] = jnp.zeros_like(pd)

    @pl.when(j < COLS)
    def _():
        swap = swap_matrix()
        for qh in range(2):
            tiles = scr.at[qh]
            tiles[...] = unfold(d_ref, qh, swap)
            for q in range(16):
                i = idx[2, j * KEEP + qh * 16 + q]
                for c in range(2):
                    pd[c * 16:c * 16 + 16, pl.ds(pl.multiple_of(i * 128, 128), 128)] = tiles[
                        q * 16:q * 16 + 16, c * 128:c * 128 + 128
                    ]


def hbm(value):
    return pltpu.with_memory_space_constraint(value, pltpu.HBM)


def inward_panels(idx, gate, up):
    blocks = pl.BlockSpec((KEEP, D), lambda j, s: (j, 0))
    panel = pl.BlockSpec((FEAT, 128), lambda j, s: (0, j))
    return pl.pallas_call(
        inward_panels_kernel,
        grid_spec=pltpu.PrefetchScalarGridSpec(
            num_scalar_prefetch=1,
            grid=(COLS,),
            in_specs=[blocks, blocks],
            out_specs=[panel, panel],
            scratch_shapes=[pltpu.VMEM((4, 256, 256), BF)],
        ),
        out_shape=[pltpu.VMEM((FEAT, WIDE), BF), pltpu.VMEM((FEAT, WIDE), BF)],
        compiler_params=params(10),
        cost_estimate=cost(6),
        name="inward_panels",
    )(idx, hbm(gate), hbm(up))


def outward_panel(idx, down):
    return pl.pallas_call(
        outward_panel_kernel,
        grid_spec=pltpu.PrefetchScalarGridSpec(
            num_scalar_prefetch=1,
            grid=(COLS + 1,),
            in_specs=[pl.BlockSpec((KEEP, D), lambda j, s: (jnp.minimum(j, COLS - 1), 0))],
            out_specs=pl.BlockSpec((KEEP, 2 * D), lambda j, s: (j, 0)),
            scratch_shapes=[pltpu.VMEM((2, 256, 256), BF)],
        ),
        out_shape=pltpu.VMEM((256, 2 * D), BF),
        compiler_params=params(10),
        cost_estimate=cost(3),
        name="outward_panel",
    )(idx, hbm(down))


def forward_kernel(t0, t1, t2, t3, pg, pu, pd, xt_own, ht_own, sib, gl2, ul2, out_parts, tok, xx, hid, hh):
    core, _, y = place()
    fsplit = one_hot(rows_of(256), split_index(cols_of(256), 64))
    fturn = one_hot(turn_index(rows_of(256), core, 64), cols_of(256))
    hsplit = one_hot(rows_of(512), split_index(cols_of(256), 128))
    hturn = one_hot(turn_index(rows_of(256), core, 128), cols_of(512))
    for n, piece in enumerate((t0, t1, t2, t3)):
        tok[n * 32:n * 32 + 32, :] = piece[...]
    for c in range(16):
        chunk = tok[:, c * 256:c * 256 + 256]
        split = mm(chunk, fsplit).astype(BF)
        turned = mm_nt(fturn, chunk).astype(BF)
        for p in range(2):
            xx[p * 128:p * 128 + 128, c * 128:c * 128 + 128] = split[:, p * 128:p * 128 + 128]
            at = p * 1024 + c * 64
            xt_own[at:at + 64, :] = turned[p * 64:p * 64 + 64, :]
            sib[at:at + 64, :] = turned[128 + p * 64:128 + p * 64 + 64, :]
    low = low_half((TOK, 128))
    hid[:, WIDE:] = jnp.zeros((TOK, 128), BF)
    for n in range(0, WIDE, 256):
        width = min(256, WIDE - n)
        gate = mm(xx[...], pg[:, n:n + width])
        up = mm(xx[...], pu[:, n:n + width])
        for s in range(0, width, 128):
            cols = slice(n + s, n + s + 128)
            gl = jnp.where(low, gate[:TOK, s:s + 128], gate[TOK:, s:s + 128])
            gl = gl + pltpu.roll(gl, 64, 1)
            ul = jnp.where(low, up[:TOK, s:s + 128], up[TOK:, s:s + 128])
            ul = ul + pltpu.roll(ul, 64, 1)
            gl2[:, cols] = gl
            ul2[:, cols] = ul
            hid[:, cols] = (gl * (1.0 / (1.0 + jnp.exp(-gl))) * ul).astype(BF)
    for g in range(2):
        group = hid[:, g * 512:g * 512 + 512]
        split = mm(group, hsplit).astype(BF)
        turned = mm_nt(hturn, group).astype(BF)
        for p in range(2):
            hh[p * 128:p * 128 + 128, g * 128:g * 128 + 128] = split[:, p * 128:p * 128 + 128]
            at = p * 128 + g * 64
            ht_own[at:at + 64, :] = turned[p * 64:p * 64 + 64, :]
            sib[FEAT + at:FEAT + at + 64, :] = turned[128 + p * 64:128 + p * 64 + 64, :]

    def step(n, carry):
        out = mm(hh[...], pd[:, pl.ds(pl.multiple_of(n * 1024, 1024), 1024)])
        parts = []
        for m in range(4):
            a0, a1 = out[:TOK, m * 256:m * 256 + 128], out[TOK:, m * 256:m * 256 + 128]
            b0, b1 = out[:TOK, m * 256 + 128:m * 256 + 256], out[TOK:, m * 256 + 128:m * 256 + 256]
            parts.append(jnp.where(low, a0, b1) + pltpu.roll(jnp.where(low, b0, a1), 64, 1))
        whole = jnp.concatenate(parts, axis=1).astype(BF)
        for r in range(NY):
            out_parts[lax.rem(y + r, NY), :, pl.ds(pl.multiple_of(n * 512, 512), 512)] = whole[r * 32:r * 32 + 32, :]
        return carry

    lax.fori_loop(0, 8, step, 0)


def forward(pieces, pg, pu, pd):
    lin = pltpu.VMEM((TOK, WIDE), F32)
    return pl.pallas_call(
        forward_kernel,
        in_specs=vm(7),
        out_specs=vm(6),
        out_shape=[
            shape(FEAT, TOK), shape(256, TOK), shape(FEAT + 256, TOK), lin, lin, shape(NY, 32, D)
        ],
        scratch_shapes=[
            pltpu.VMEM((TOK, D), BF),
            pltpu.VMEM((256, FEAT), BF),
            pltpu.VMEM((TOK, 1024), BF),
            pltpu.VMEM((256, 256), BF),
        ],
        compiler_params=params(24),
        cost_estimate=cost(8),
        name="forward",
    )(*pieces, pg, pu, pd)


def emit(wswap, tiles, parts, row):
    turned = mm(wswap, tiles[...]).astype(BF)
    for rel, dst in enumerate(parts):
        for k in range(4):
            top = (rel * 4 + k) * 16
            for half in range(2):
                dst[row + half * 16:row + half * 16 + 16, k * 128:k * 128 + 128] = turned[
                    top:top + 16, half * 128:half * 128 + 128
                ]


def down_kernel(idx, cot_own, cot_oth, ht_own, sib_oth, w0, w1, w2, w3, both, part, tiles):
    wswap = wire_swap(place()[1])
    both[:TOK, :] = cot_own[...]
    both[TOK:, :] = cot_oth[...]

    def product(n, carry):
        lanes = pl.ds(pl.multiple_of(n * 512, 512), 512)
        hidden = jnp.concatenate([ht_own[...], sib_oth[FEAT:, :]], axis=1)
        part[:, lanes] = mm(hidden, both[:, lanes]).astype(BF)
        return carry

    lax.fori_loop(0, 8, product, 0)
    side = lax.broadcasted_iota(jnp.int32, (16, 128), 1) // 64
    for j in range(COLS):
        for q in range(KEEP):
            i = idx[2, j * KEEP + q]
            odd = lax.rem(i, 2)
            lanes = pl.ds(pl.multiple_of((i // 2) * 128, 128), 128)
            near = part[pl.ds(pl.multiple_of(odd * 128 + j * 16, 16), 16), lanes].astype(F32)
            far = part[pl.ds(pl.multiple_of((1 - odd) * 128 + j * 16, 16), 16), lanes].astype(F32)
            tile = jnp.where(side == odd, near, pltpu.roll(far, 64, 1)).astype(BF)
            tiles[(q % 16) * 16:(q % 16) * 16 + 16, (q // 16) * 128:(q // 16) * 128 + 128] = tile
        emit(wswap, tiles, (w0, w1, w2, w3), j * KEEP)


def down_grads(idx, cot_own, cot_oth, ht_own, sib_oth):
    return pl.pallas_call(
        down_kernel,
        in_specs=smem(1) + vm(4),
        out_specs=vm(4),
        out_shape=[shape(SLOT, 512)] * 4,
        scratch_shapes=[pltpu.VMEM((256, D), BF), pltpu.VMEM((256, D), BF), pltpu.VMEM((256, 256), BF)],
        compiler_params=params(14),
        cost_estimate=cost(0.2),
        name="down_grads",
    )(idx, cot_own, cot_oth, ht_own, sib_oth)


def delta_kernel(c0, c1, c2, c3, pd_far, gl2, ul2, own, cot, gdx, udx, cx, pd, sem):
    fetch = pltpu.make_async_copy(pd_far, pd, sem)
    fetch.start()
    at = cols_of(512)
    hjoin = one_hot(split_index(rows_of(256), 128), (at >> 7) * 128 + (at & 63))
    low = low_half((32, 128))
    for n, piece in enumerate((c0, c1, c2, c3)):
        top = slice(n * 32, n * 32 + 32)
        bottom = slice(TOK + n * 32, TOK + n * 32 + 32)
        cot[top, :] = piece[...]
        for m in range(32):
            c = piece[:, m * 128:m * 128 + 128].astype(F32)
            rolled = pltpu.roll(c, 64, 1)
            zero = jnp.zeros_like(c)
            first = slice(2 * m * 128, 2 * m * 128 + 128)
            second = slice(2 * m * 128 + 128, 2 * m * 128 + 256)
            cx[top, first] = jnp.where(low, c, zero).astype(BF)
            cx[bottom, first] = jnp.where(low, zero, rolled).astype(BF)
            cx[top, second] = jnp.where(low, rolled, zero).astype(BF)
            cx[bottom, second] = jnp.where(low, zero, c).astype(BF)

    fetch.wait()

    def product(n, acc):
        lanes = pl.ds(pl.multiple_of(n * 1024, 1024), 1024)
        return acc + mm_nt(cx[:, lanes], pd[:, lanes])

    hd = lax.fori_loop(0, 8, product, jnp.zeros((256, 256), F32))
    high = hd.astype(BF)
    rest = (hd - high.astype(F32)).astype(BF)
    low = low_half((TOK, 128))
    for g in range(2):
        cols = slice(g * 128, g * 128 + 128)
        joined = sum(
            mm(jnp.concatenate([part[:TOK, cols], part[TOK:, cols]], axis=1), hjoin) for part in (high, rest)
        )
        before = None
        for jl in range(4):
            j = g * 4 + jl
            if j == COLS:
                break
            lanes = slice(j * 128, j * 128 + 128)
            delta = joined[:, jl * 128:jl * 128 + 128]
            gl, ul = gl2[:, lanes], ul2[:, lanes]
            sig = 1.0 / (1.0 + jnp.exp(-gl))
            gd = delta * ul * sig * (1.0 + gl * (1.0 - sig))
            ud = delta * gl * sig
            for dst, val in ((gdx, gd), (udx, ud)):
                dst[:TOK, lanes] = jnp.where(low, val, 0.0).astype(BF)
                dst[TOK:, lanes] = jnp.where(low, 0.0, val).astype(BF)
            pair = slice((j // 2) * 128, (j // 2) * 128 + 128)
            if j % 2:
                own[:TOK, pair] = jnp.where(low, before[0], gd).astype(BF)
                own[TOK:, pair] = jnp.where(low, before[1], ud).astype(BF)
            elif j == COLS - 1:
                own[:TOK, pair] = jnp.where(low, gd, 0.0).astype(BF)
                own[TOK:, pair] = jnp.where(low, ud, 0.0).astype(BF)
            before = (gd, ud)


def deltas(pieces, pd, gl2, ul2):
    return pl.pallas_call(
        delta_kernel,
        in_specs=vm(4) + [pl.BlockSpec(memory_space=pl.ANY)] + vm(2),
        out_specs=vm(4),
        out_shape=[shape(256, 512), shape(TOK, D)] + [pltpu.VMEM((256, WIDE), BF)] * 2,
        scratch_shapes=[
            pltpu.VMEM((256, 2 * D), BF),
            pltpu.VMEM((256, 2 * D), BF),
            pltpu.SemaphoreType.DMA,
        ],
        compiler_params=params(18),
        cost_estimate=cost(0.2),
        name="deltas",
    )(*pieces, hbm(pd), gl2, ul2)


def back_kernel(gdx, udx, pg, pu, parts):
    y = place()[2]
    fjoin = one_hot(split_index(rows_of(256), 64), cols_of(256))
    n = pl.program_id(0)
    acc = (mm_nt(gdx[...], pg[...]) + mm_nt(udx[...], pu[...])).astype(BF)
    for c in range(2):
        cols = slice(c * 128, c * 128 + 128)
        pair = jnp.concatenate([acc[:TOK, cols], acc[TOK:, cols]], axis=1)
        whole = mm(pair, fjoin).astype(BF)
        lanes = pl.ds(pl.multiple_of(n * 512 + c * 256, 256), 256)
        for r in range(NY):
            parts[lax.rem(y + r, NY), :, lanes] = whole[r * 32:r * 32 + 32, :]


def input_parts(gdx, udx, pg, pu):
    whole = pl.BlockSpec((256, WIDE), lambda n: (0, 0))
    panel = pl.BlockSpec((256, WIDE), lambda n: (n, 0))
    return pl.pallas_call(
        back_kernel,
        grid=(FEAT // 256,),
        in_specs=[whole, whole, panel, panel],
        out_specs=pl.BlockSpec((NY, 32, D), lambda n: (0, 0, 0)),
        out_shape=shape(NY, 32, D),
        compiler_params=params(10),
        cost_estimate=cost(0.2),
        name="input_parts",
    )(gdx, udx, hbm(pg), hbm(pu))


def inward_kernel(m, idx, xt_own, sib_oth, d_own, d_oth, w0, w1, w2, w3, part, tiles):
    wswap = wire_swap(place()[1])
    low = low_half((16, 128))
    delta = jnp.concatenate([d[m * TOK:m * TOK + TOK, :] for d in (d_own, d_oth)], axis=0)

    def product(n, carry):
        rows = pl.ds(pl.multiple_of(n * 256, 256), 256)
        tokens = jnp.concatenate([xt_own[rows, :], sib_oth[rows, :]], axis=1)
        part[rows, :] = mm(tokens, delta).astype(BF)
        return carry

    lax.fori_loop(0, 8, product, 0)
    for j in range(COLS):
        odd = j % 2
        lanes = slice((j // 2) * 128, (j // 2) * 128 + 128)
        for q in range(KEEP):
            i = idx[m, j * KEEP + q]
            first = part[pl.ds(pl.multiple_of(i * 16, 16), 16), lanes].astype(F32)
            second = part[pl.ds(pl.multiple_of(1024 + i * 16, 16), 16), lanes].astype(F32)
            if odd:
                first = pltpu.roll(first, 64, 1)
            else:
                second = pltpu.roll(second, 64, 1)
            tile = jnp.where(low, first, second).astype(BF)
            tiles[(q % 16) * 16:(q % 16) * 16 + 16, (q // 16) * 128:(q // 16) * 128 + 128] = tile
        emit(wswap, tiles, (w0, w1, w2, w3), j * KEEP)


def inward_grads(m, idx, xt_own, sib_oth, d_own, d_oth):
    return pl.pallas_call(
        functools.partial(inward_kernel, m),
        in_specs=smem(1) + vm(4),
        out_specs=vm(4),
        out_shape=[shape(SLOT, 512)] * 4,
        scratch_shapes=[pltpu.VMEM((FEAT, 512), BF), pltpu.VMEM((256, 256), BF)],
        compiler_params=params(14),
        cost_estimate=cost(0.2),
        name=("gate_grads", "up_grads")[m],
    )(idx, xt_own, sib_oth, d_own, d_oth)


def from_y(value, step):
    pairs = [((y + step) % NY * NZ + z, y * NZ + z) for y in range(NY) for z in range(NZ)]
    return lax.ppermute(value, "fsdp", pairs)


def from_x(value, other):
    pairs = [((x ^ other) * NC + c, x * NC + c) for x in range(NX) for c in range(NC)]
    return lax.ppermute(value, "dp", pairs)


def from_core(value):
    pairs = [(x * NC + 1 - c, x * NC + c) for x in range(NX) for c in range(NC)]
    return lax.ppermute(value, "dp", pairs)


def z_groups():
    return [[y * NZ + z for z in range(NZ)] for y in range(NY)]


def y_groups():
    return [[y * NZ + z for y in range(NY)] for z in range(NZ)]


def over_z(value):
    return lax.all_to_all(value, "fsdp", 0, 0, axis_index_groups=z_groups(), tiled=True)


def over_y(value):
    return lax.all_to_all(value, "fsdp", 0, 0, axis_index_groups=y_groups(), tiled=True)


def copies_over_z(value):
    return over_z(jnp.broadcast_to(value[None], (NZ,) + value.shape))


def after(value, *others):
    return lax.optimization_barrier((value,) + others)[0]


def exchange_x(parts):
    return [parts[0]] + [from_x(parts[d], d) for d in range(1, NX)]


def mean_of(parts):
    total = sum((p.astype(F32) for p in parts[1:]), parts[0].astype(F32))
    return (total * (1.0 / (NX * NC))).astype(BF)


def body(tokens, cotangent, gate_blocks, up_blocks, down_blocks, block_index):
    rows = tokens.shape[0]
    ring = copies_over_z(jnp.concatenate([tokens, cotangent], axis=0))
    tok_z = ring[:, :rows].reshape(NZ * rows, D)
    cot_z = ring[:, rows:].reshape(NZ * rows, D)
    tok = [tok_z] + [from_y(tok_z, s) for s in range(1, NY)]
    idx = after(block_index, tok_z)
    pg, pu = inward_panels(idx, gate_blocks, up_blocks)
    cot_z = after(cot_z, pg)
    pd = outward_panel(idx, down_blocks)
    cot = [cot_z] + [from_y(cot_z, s) for s in range(1, NY)]

    xt_own, ht_own, sib, gl2, ul2, out_parts = forward(tok, pg, pu, pd)
    sib_oth = from_core(sib)
    out_y = lax.psum_scatter(
        after(out_parts, *cot), "fsdp", scatter_dimension=0, axis_index_groups=y_groups()
    )
    own, cot_own, gdx, udx = deltas(cot, pd, gl2, ul2)
    oth, cot_oth = from_core(own), from_core(cot_own)
    gate_wire = inward_grads(0, block_index, xt_own, sib_oth, own, oth)
    gate_got = exchange_x(gate_wire)
    in_parts = input_parts(after(gdx, gate_wire[0]), udx, pg, pu)
    in_got = over_y(in_parts)
    down_wire = down_grads(block_index, cot_own, cot_oth, after(ht_own, in_parts), sib_oth)
    down_got = exchange_x(down_wire)
    up_wire = inward_grads(1, block_index, xt_own, sib_oth, after(own, down_wire[0], *gate_got[1:]), oth)
    up_got = exchange_x(up_wire)
    in_y = after(in_got, up_wire[0], *down_got[1:]).astype(F32).sum(axis=0).astype(BF)
    gate_grad, up_grad, down_grad = (mean_of(g) for g in (gate_got, up_got, down_got))

    both = jnp.concatenate([part.reshape(NZ, rows, D) for part in (out_y, in_y)], axis=1)
    total = over_z(both).astype(F32).sum(axis=0).astype(BF)
    return (total[:rows], total[rows:], gate_grad, up_grad, down_grad)


def solution(mesh):
    return jax.shard_map(
        body,
        mesh=mesh,
        in_specs=(
            P(("dp", "fsdp"), None),
            P(("dp", "fsdp"), None),
            P("fsdp", None),
            P("fsdp", None),
            P("fsdp", None),
            P(None, "fsdp"),
        ),
        out_specs=(
            P(("dp", "fsdp"), None),
            P(("dp", "fsdp"), None),
            P("fsdp", "dp"),
            P("fsdp", "dp"),
            P("fsdp", "dp"),
        ),
        check_vma=False,
    )
```

time: 172 us -> 157 us (0.913)
  waiting for transfers between devices: 33 us -> 19 us
  Pallas kernels: 38.8 us -> 50 us
  blocking collectives: 33.1 us -> 25.8 us
  local copies, waits for them, and re-layouts: 9.99 us -> 6.7 us
  starting transfers between devices: 35.6 us -> 32.8 us
    reduce_scatter x2 -> x1, waiting for transfers between devices: 11.9 us -> 0.02 us  [body(): lax.psum_scatter(after(out_parts, *cot), 'fsdp', scatter_dimension=0, axi...]
    ppermute x9 -> x6, waiting for transfers between devices: 11.6 us -> 0.02 us  [from_y(): return lax.ppermute(value, 'fsdp', pairs)]
    ppermute x9, waiting for transfers between devices: 4.02 us -> 15.1 us  [from_x(): return lax.ppermute(value, 'dp', pairs)]
    pallas_call x5 -> x6, Pallas kernels: 31.2 us -> 42.2 us  [the longest x1 9.14 us: input_parts(): pl.pallas_call(back_kernel, grid=(FEAT // 256,), in_specs=[whole, whole,...]
    all_to_all x2 -> x1, blocking collectives: 33.1 us -> 25.8 us  [over_z(): lax.all_to_all(value, 'fsdp', 0, 0, axis_index_groups=z_groups(), tiled=T...]
    ppermute x9 -> x6, starting transfers between devices: 15.8 us -> 8.57 us  [from_y(): return lax.ppermute(value, 'fsdp', pairs)]
    all_to_all x0 -> x1, starting transfers between devices: none -> 5.55 us  [over_y(): lax.all_to_all(value, 'fsdp', 0, 0, axis_index_groups=y_groups(), tiled=T...]
    all_to_all x1, waiting for transfers between devices: 4.47 us -> 1.36 us  [over_z(): lax.all_to_all(value, 'fsdp', 0, 0, axis_index_groups=z_groups(), tiled=T...]
  transfers between devices with their start and end apart: 29 -> 21, of which waited for: 8 -> 8; matrix products, arithmetic and copies ran while one was open for 5% -> 3% of each run, Pallas kernels for 18% -> 32%
where the time goes in v3:
time: 157 us; the launch traced here: 156 us
  Pallas kernels  50 us (32%)
  starting transfers between devices  32.8 us (21%)
  blocking collectives  25.8 us (16%)
  waiting for transfers between devices  19 us (12%)
  between operations  14.4 us (9%)
  other arithmetic  6.93 us (4%)
  local copies, waits for them, and re-layouts  6.7 us (4%)
    all_to_all x1, blocking collectives, over_z(): lax.all_to_all(value, 'fsdp', 0, 0, axis_index_groups=z_groups(), tiled=T...  25.8 us
    ppermute x9, waiting for transfers between devices, from_x(): return lax.ppermute(value, 'dp', pairs)  15.1 us
    ppermute x9, starting transfers between devices, from_x(): return lax.ppermute(value, 'dp', pairs)  14.2 us
    pallas_call x1, Pallas kernels, input_parts(): pl.pallas_call(back_kernel, grid=(FEAT // 256,), in_specs=[whole, whole,...  9.14 us
    ppermute x6, starting transfers between devices, from_y(): return lax.ppermute(value, 'fsdp', pairs)  8.57 us
    pallas_call x2, Pallas kernels, inward_grads(): pl.pallas_call(functools.partial(inward_kernel, m), in_specs=smem(1) + vm...  7.77 us
    pallas_call x1, Pallas kernels, inward_panels(): pl.pallas_call(inward_panels_kernel, grid_spec=pltpu.PrefetchScalarGridSp...  7.72 us
    pallas_call x1, Pallas kernels, forward(): pl.pallas_call(forward_kernel, in_specs=vm(7), out_specs=vm(6), out_shape...  7.67 us
  transfers between devices with their start and end apart: 21, of which 8 were waited for; matrix products, arithmetic and copies ran while one was open for 3% of the time, Pallas kernels for 32%

profile of v3, /device:TPU:8, one launch (start us, length us, event | category | flops | bytes accessed | tf_op | source)
XLA Modules:
  0.0 155.6 jit_solution(14842645812235627690)
XLA Ops:
  7.2 0.0 reduce-scatter.2.cloned.1.call-start
  7.2 0.8 pad_maximum_fusion.1
  8.1 25.8 %all_to_all.15 = bf16[8,8,4096]{2,1,0:T(8,128)(2,1)S(1)} all-to-all(bf16[8,8,4096]{2,1,0:T(8,128)(2,1)S(1)} %broadcast_in_dim.2), channel_id=1, replica_groups={{0,1,2,3,4,5,6,7},{8,9,10,11,12,13,14,15},{16,17,18,19,20,21,22,23},{24..., dimensions={0} | all-to-all | bytes 1048576 | tf_op jit(solution)/shard_map/all_to_all | solution.py:473
  33.8 0.2 fusion
  34.1 0.1 reshape.20.t0
  34.1 1.7 %collective-permute-start.2 = (bf16[32,4096]{1,0:T(8,128)(2,1)S(1)}, bf16[32,4096]{1,0:T(8,128)(2,1)S(1)}, u32[]{:S(2)}, u32[]{:S(2)}) collective-permute-start(bf16[32,4096]{1,0:T(8,128)(2,1)S(1)} %reshape.20.t0), channel_id=1, source_target_pairs={{24,0},{25,1},{26,2},{27,3},{28,4},{29,5},{30,6},{31,7},{0,8},{1,9... | collective-permute-start | bytes 786440 | tf_op jit(solution)/shard_map/ppermute | solution.py:451
  35.8 0.9 collective-permute-start.1
  36.7 2.4 %collective-permute-start = (bf16[32,4096]{1,0:T(8,128)(2,1)S(1)}, bf16[32,4096]{1,0:T(8,128)(2,1)S(1)}, u32[]{:S(2)}, u32[]{:S(2)}) collective-permute-start(bf16[32,4096]{1,0:T(8,128)(2,1)S(1)} %reshape.20.t0), channel_id=1, source_target_pairs={{8,0},{9,1},{10,2},{11,3},{12,4},{13,5},{14,6},{15,7},{16,8},{17,9... | collective-permute-start | bytes 786440 | tf_op jit(solution)/shard_map/ppermute | solution.py:451
  39.2 0.1 reshape.21.c0
  39.2 7.7 %inward_panels.1 = (bf16[2048,896]{1,0:T(8,128)(2,1)S(1)}, bf16[2048,896]{1,0:T(8,128)(2,1)S(1)}) custom-call(s32[3,224]{1,0:T(4,128)S(1)} %copy-done.9, bf16[224,4096]{1,0:T(8,128)(2,1)} %g_ref.1, bf16[224,4096]{1,0:T(8,128)(2,1)} %u_ref.1), custom_call_target="tpu_custom_call" | custom-call | flops 6000000000 | bytes 1000 | tf_op jit(solution)/shard_map/inward_panels/pallas_call | solution.py:142
  47.0 0.1 collective-permute-start.5
  47.1 3.4 %collective-permute-start.4 = (bf16[32,4096]{1,0:T(8,128)(2,1)S(1)}, bf16[32,4096]{1,0:T(8,128)(2,1)S(1)}, u32[]{:S(2)}, u32[]{:S(2)}) collective-permute-start(bf16[32,4096]{1,0:T(8,128)(2,1)S(1)} %reshape.21.c0), channel_id=1, source_target_pairs={{16,0},{17,1},{18,2},{19,3},{20,4},{21,5},{22,6},{23,7},{24,8},{25... | collective-permute-start | bytes 786440 | tf_op jit(solution)/shard_map/ppermute | solution.py:451
  50.5 5.8 %outward_panel.1.pd.pd_far = bf16[256,8192]{1,0:T(8,128)(2,1)S(1)} custom-call(s32[3,224]{1,0:T(4,128)S(1)} %copy-done.9, bf16[224,4096]{1,0:T(8,128)(2,1)} %d_ref.1), custom_call_target="tpu_custom_call" | custom-call | flops 3000000000 | bytes 1000 | tf_op jit(solution)/shard_map/outward_panel/pallas_call | solution.py:159
  56.3 0.0 collective-permute-done.2.t3
  56.3 0.1 collective-permute-start.3
  56.4 0.0 collective-permute-done.1.t2
  56.4 7.7 %forward.1 = (bf16[2048,128]{1,0:T(8,128)(2,1)S(1)}, bf16[256,128]{1,0:T(8,128)(2,1)S(1)}, bf16[2304,128]{1,0:T(8,128)(2,1)}, f32[128,896]{1,0:T(8,128)S(1)}, f3...) custom-call(bf16[32,4096]{1,0:T(8,128)(2,1)S(1)} %reshape.20.t0, bf16[32,4096]{1,0:T(8,128)(2,1)S(1)} %collective-permute-done.t1, ...), custom_call_target="tpu_custom_call" | custom-call | flops 8000000000 | bytes 1000 | tf_op jit(solution)/shard_map/forward/pallas_call | solution.py:234
  64.1 0.8 copy-done.3
  64.9 0.0 collective-permute-done.3.c1
  64.9 0.7 copy-done.7
  65.7 0.0 reduce-scatter.2.cloned.1.call-update
  65.7 0.1 collective-permute-start.6
  65.8 1.0 copy-done.4
  66.8 0.9 copy-done.6
  67.8 0.9 copy-done.8
  68.7 6.1 %deltas.1 = (bf16[256,512]{1,0:T(8,128)(2,1)S(1)}, bf16[128,4096]{1,0:T(8,128)(2,1)S(1)}, bf16[256,896]{1,0:T(8,128)(2,1)S(1)}, bf16[256,896]{1,0:T(8,128)(2,1)S(1)}) custom-call(bf16[32,4096]{1,0:T(8,128)(2,1)S(1)} %reshape.21.c0, bf16[32,4096]{1,0:T(8,128)(2,1)S(1)} %copy-done.8, bf16[32,4096]{1,0:T(8,128)(2,1)S(1)} %copy-done.6, ...), custom_call_target="tpu_custom_call" | custom-call | flops 200000000 | bytes 1000 | tf_op jit(solution)/shard_map/deltas/pallas_call | solution.py:363
  74.9 0.8 collective-permute-start.8
  75.6 0.1 collective-permute-start.7
  75.7 2.5 %collective-permute-done.7.d_oth = bf16[256,512]{1,0:T(8,128)(2,1)S(1)} collective-permute-done((bf16[256,512]{1,0:T(8,128)(2,1)S(1)}, bf16[256,512]{1,0:T(8,128)(2,1)S(1)}, u32[]{:S(2)}, u32[]{:S(2)}) %collective-permute-start.7) | collective-permute-done | bytes 262176 | tf_op jit(solution)/shard_map/ppermute | solution.py:461
  78.2 0.0 collective-permute-done.6.sib_oth
  78.2 4.2 %gate_grads.1 = (bf16[224,512]{1,0:T(8,128)(2,1)S(1)}, bf16[224,512]{1,0:T(8,128)(2,1)}, bf16[224,512]{1,0:T(8,128)(2,1)}, bf16[224,512]{1,0:T(8,128)(2,1)S(1)}) custom-call(s32[3,224]{1,0:T(4,128)S(1)} %copy-done.9, bf16[2048,128]{1,0:T(8,128)(2,1)S(1)} %get-tuple-element.45.xt_own, bf16[2304,128]{1,0:T(8,128)(2,1)S(1)} %collective-permute-done.6.sib_oth, ...), custom_call_target="tpu_custom_call" | custom-call | flops 200000000 | bytes 1000 | tf_op jit(solution)/shard_map/gate_grads/pallas_call | solution.py:437
  82.4 9.1 %input_parts.1 = bf16[4,32,4096]{2,1,0:T(8,128)(2,1)} custom-call(bf16[256,896]{1,0:T(8,128)(2,1)S(1)} %get-tuple-element.49.gdx, bf16[256,896]{1,0:T(8,128)(2,1)S(1)} %get-tuple-element.50.udx, bf16[2048,896]{1,0:T(8,128)(2,1)} %copy-done.1, bf16[2048,896]{1,0:T(8,128)(2,1)} %copy-done.2), custom_call_target="tpu_custom_call" | custom-call | flops 200000000 | bytes 1000 | tf_op jit(solution)/shard_map/input_parts/pallas_call | solution.py:396
  91.6 5.5 %all-to-all-start.1 = ((bf16[4,32,4096]{2,1,0:T(8,128)(2,1)}), bf16[4,32,4096]{2,1,0:T(8,128)(2,1)}, u32[]{:S(2)}, u32[]{:S(2)}) async-start(bf16[4,32,4096]{2,1,0:T(8,128)(2,1)} %input_parts.1), calls=%async_computation.2 | async-start | bytes 2097152 | tf_op jit(solution)/shard_map/all_to_all | solution.py:477
  97.1 1.5 collective-permute-start.9
  98.6 2.7 %collective-permute-start.10 = (bf16[224,512]{1,0:T(8,128)(2,1)}, bf16[224,512]{1,0:T(8,128)(2,1)S(1)}, u32[]{:S(2)}, u32[]{:S(2)}) collective-permute-start(bf16[224,512]{1,0:T(8,128)(2,1)} %get-tuple-element.56), channel_id=1, source_target_pairs={{128,0},{160,32},{192,64},{224,96},{0,128},{32,160},{64,192},{96,2... | collective-permute-start | bytes 688136 | tf_op jit(solution)/shard_map/ppermute | solution.py:456
  101.4 0.5 collective-permute-start.11
  101.8 0.0 collective-permute-done.8.cot_oth
  101.8 5.8 %down_grads.1 = (bf16[224,512]{1,0:T(8,128)(2,1)S(1)}, bf16[224,512]{1,0:T(8,128)(2,1)S(1)}, bf16[224,512]{1,0:T(8,128)(2,1)S(1)}, bf16[224,512]{1,0:T(8,128)(2,1)S(1)}) custom-call(s32[3,224]{1,0:T(4,128)S(1)} %copy-done.9, bf16[128,4096]{1,0:T(8,128)(2,1)S(1)} %get-tuple-element.51.cot_own, bf16[128,4096]{1,0:T(8,128)(2,1)} %collective-permute-done.8.cot_oth, ...), custom_call_target="tpu_custom_call" | custom-call | flops 200000000 | bytes 1000 | tf_op jit(solution)/shard_map/down_grads/pallas_call | solution.py:290
  107.6 0.4 collective-permute-start.12
  108.0 4.0 %collective-permute-start.13 = (bf16[224,512]{1,0:T(8,128)(2,1)S(1)}, bf16[224,512]{1,0:T(8,128)(2,1)}, u32[]{:S(2)}, u32[]{:S(2)}) collective-permute-start(bf16[224,512]{1,0:T(8,128)(2,1)S(1)} %get-tuple-element.61), channel_id=1, source_target_pairs={{128,0},{160,32},{192,64},{224,96},{0,128},{32,160},{64,192},{96,2... | collective-permute-start | bytes 688136 | tf_op jit(solution)/shard_map/ppermute | solution.py:456
  111.9 0.5 collective-permute-start.14
  112.4 0.0 collective-permute-done.10
  112.4 2.1 %collective-permute-done.11 = bf16[224,512]{1,0:T(8,128)(2,1)S(1)} collective-permute-done((bf16[224,512]{1,0:T(8,128)(2,1)S(1)}, bf16[224,512]{1,0:T(8,128)(2,1)S(1)}, u32[]{:S(2)}, u32[]{:S(2)}) %collective-permute-start.11) | collective-permute-done | bytes 229408 | tf_op jit(solution)/shard_map/ppermute | solution.py:456
  114.6 3.5 %up_grads.1 = (bf16[224,512]{1,0:T(8,128)(2,1)S(1)}, bf16[224,512]{1,0:T(8,128)(2,1)S(1)}, bf16[224,512]{1,0:T(8,128)(2,1)S(1)}, bf16[224,512]{1,0:T(8,128)(2,1)S(1)}) custom-call(s32[3,224]{1,0:T(4,128)S(1)} %copy-done.9, bf16[2048,128]{1,0:T(8,128)(2,1)S(1)} %get-tuple-element.45.xt_own, bf16[2304,128]{1,0:T(8,128)(2,1)S(1)} %collective-permute-done.6.sib_oth, ...), custom_call_target="tpu_custom_call" | custom-call | flops 200000000 | bytes 1000 | tf_op jit(solution)/shard_map/up_grads/pallas_call | solution.py:437
  118.1 4.0 %collective-permute-done.13 = bf16[224,512]{1,0:T(8,128)(2,1)} collective-permute-done((bf16[224,512]{1,0:T(8,128)(2,1)S(1)}, bf16[224,512]{1,0:T(8,128)(2,1)}, u32[]{:S(2)}, u32[]{:S(2)}) %collective-permute-start.13) | collective-permute-done | bytes 229408 | tf_op jit(solution)/shard_map/ppermute | solution.py:456
  122.1 2.3 %collective-permute-done.14 = bf16[224,512]{1,0:T(8,128)(2,1)} collective-permute-done((bf16[224,512]{1,0:T(8,128)(2,1)S(1)}, bf16[224,512]{1,0:T(8,128)(2,1)}, u32[]{:S(2)}, u32[]{:S(2)}) %collective-permute-start.14) | collective-permute-done | bytes 229408 | tf_op jit(solution)/shard_map/ppermute | solution.py:456
  124.5 1.5 reduce_sum.24
  126.0 0.1 reshape.22
  126.1 0.0 reduce-scatter.2.cloned.1.call-done
  126.1 1.1 reshape_reduce_scatter.3
  127.2 1.0 pad_maximum_fusion
  128.2 3.5 %all-to-all-start.2 = ((bf16[8,8,4096]{2,1,0:T(8,128)(2,1)}), bf16[8,8,4096]{2,1,0:T(8,128)(2,1)S(1)}, u32[]{:S(2)}, u32[]{:S(2)}) async-start(bf16[8,8,4096]{2,1,0:T(8,128)(2,1)} %pad_maximum_fusion), calls=%async_computation.3 | async-start | bytes 1048576 | tf_op jit(solution)/shard_map/all_to_all | solution.py:473
  131.7 0.8 multiply_convert_fusion.2
  132.6 0.0 collective-permute-start.15
  132.6 1.9 %collective-permute-start.16 = (bf16[224,512]{1,0:T(8,128)(2,1)S(1)}, bf16[224,512]{1,0:T(8,128)(2,1)S(1)}, u32[]{:S(2)}, u32[]{:S(2)}) collective-permute-start(bf16[224,512]{1,0:T(8,128)(2,1)S(1)} %get-tuple-element.65), channel_id=1, source_target_pairs={{128,0},{160,32},{192,64},{224,96},{0,128},{32,160},{64,192},{96,2... | collective-permute-start | bytes 688136 | tf_op jit(solution)/shard_map/ppermute | solution.py:456
  134.5 2.8 %collective-permute-start.17 = (bf16[224,512]{1,0:T(8,128)(2,1)S(1)}, bf16[224,512]{1,0:T(8,128)(2,1)S(1)}, u32[]{:S(2)}, u32[]{:S(2)}) collective-permute-start(bf16[224,512]{1,0:T(8,128)(2,1)S(1)} %get-tuple-element.66), channel_id=1, source_target_pairs={{192,0},{224,32},{128,64},{160,96},{64,128},{96,160},{0,192},{32,2... | collective-permute-start | bytes 688136 | tf_op jit(solution)/shard_map/ppermute | solution.py:456
  137.3 1.9 %multiply_convert_fusion = bf16[224,512]{1,0:T(8,128)(2,1)} fusion(bf16[224,512]{1,0:T(8,128)(2,1)} %collective-permute-done.14, bf16[224,512]{1,0:T(8,128)(2,1)} %collective-permute-done.13, bf16[224,512]{1,0:T(8,128)(2,1)S(1)} %copy-done.15, bf16[224,512]{1,0:T(8,128)(2,1)S(1)} %get-tuple-element.54), kind=kLoop, calls=%fused_computation.1 | loop fusion | flops 1032192 | bytes 1146880 | tf_op jit(solution)/shard_map/convert_element_type | solution.py:494
  139.1 1.8 %collective-permute-done.15 = bf16[224,512]{1,0:T(8,128)(2,1)S(1)} collective-permute-done((bf16[224,512]{1,0:T(8,128)(2,1)S(1)}, bf16[224,512]{1,0:T(8,128)(2,1)S(1)}, u32[]{:S(2)}, u32[]{:S(2)}) %collective-permute-start.15) | collective-permute-done | bytes 229408 | tf_op jit(solution)/shard_map/ppermute | solution.py:456
  141.0 2.5 %collective-permute-done.16 = bf16[224,512]{1,0:T(8,128)(2,1)S(1)} collective-permute-done((bf16[224,512]{1,0:T(8,128)(2,1)S(1)}, bf16[224,512]{1,0:T(8,128)(2,1)S(1)}, u32[]{:S(2)}, u32[]{:S(2)}) %collective-permute-start.16) | collective-permute-done | bytes 229408 | tf_op jit(solution)/shard_map/ppermute | solution.py:456
  143.4 2.4 %collective-permute-done.17 = bf16[224,512]{1,0:T(8,128)(2,1)S(1)} collective-permute-done((bf16[224,512]{1,0:T(8,128)(2,1)S(1)}, bf16[224,512]{1,0:T(8,128)(2,1)S(1)}, u32[]{:S(2)}, u32[]{:S(2)}) %collective-permute-start.17) | collective-permute-done | bytes 229408 | tf_op jit(solution)/shard_map/ppermute | solution.py:456
  145.8 0.8 multiply_convert_fusion.1
  146.6 1.4 all-to-all-done.2
  148.0 0.1 reduce_sum.25
  148.1 0.7 fusion.1
  (38 shorter events, 0.1 us)
Async XLA Ops:
  7.2 32.1 %copy-start.9 = (s32[3,224]{1,0:T(4,128)S(1)}, s32[3,224]{1,0:T(4,128)}, u32[]{:S(2)}) copy-start(s32[3,224]{1,0:T(4,128)} %idx.7) | copy-start | bytes 8068
  7.2 118.9 %reduce-scatter.2.cloned.1.call-start = ((), (), s32[]{:S(2)}) async-start(), calls=%async_computation.4 | async-start | bytes 1310720 | tf_op jit(solution)/shard_map/reduce_scatter | solution.py:511
  34.1 22.1 %collective-permute-start.2 = (bf16[32,4096]{1,0:T(8,128)(2,1)S(1)}, bf16[32,4096]{1,0:T(8,128)(2,1)S(1)}, u32[]{:S(2)}, u32[]{:S(2)}) collective-permute-start(bf16[32,4096]{1,0:T(8,128)(2,1)S(1)} %reshape.20.t0), channel_id=1, source_target_pairs={{24,0},{25,1},{26,2},{27,3},{28,4},{29,5},{30,6},{31,7},{0,8},{1,9... | collective-permute-start | bytes 786440 | tf_op jit(solution)/shard_map/ppermute | solution.py:451
  35.8 20.6 %collective-permute-start.1 = (bf16[32,4096]{1,0:T(8,128)(2,1)S(1)}, bf16[32,4096]{1,0:T(8,128)(2,1)S(1)}, u32[]{:S(2)}, u32[]{:S(2)}) collective-permute-start(bf16[32,4096]{1,0:T(8,128)(2,1)S(1)} %reshape.20.t0), channel_id=1, source_target_pairs={{16,0},{17,1},{18,2},{19,3},{20,4},{21,5},{22,6},{23,7},{24,8},{25... | collective-permute-start | bytes 786440 | tf_op jit(solution)/shard_map/ppermute | solution.py:451
  36.7 19.6 %collective-permute-start = (bf16[32,4096]{1,0:T(8,128)(2,1)S(1)}, bf16[32,4096]{1,0:T(8,128)(2,1)S(1)}, u32[]{:S(2)}, u32[]{:S(2)}) collective-permute-start(bf16[32,4096]{1,0:T(8,128)(2,1)S(1)} %reshape.20.t0), channel_id=1, source_target_pairs={{8,0},{9,1},{10,2},{11,3},{12,4},{13,5},{14,6},{15,7},{16,8},{17,9... | collective-permute-start | bytes 786440 | tf_op jit(solution)/shard_map/ppermute | solution.py:451
  47.0 9.4 %copy-start.1 = (bf16[2048,896]{1,0:T(8,128)(2,1)}, bf16[2048,896]{1,0:T(8,128)(2,1)S(1)}, u32[]{:S(2)}) copy-start(bf16[2048,896]{1,0:T(8,128)(2,1)S(1)} %get-tuple-element.37.pg) | copy-start | bytes 11010052
  47.0 9.4 %copy-start.2 = (bf16[2048,896]{1,0:T(8,128)(2,1)}, bf16[2048,896]{1,0:T(8,128)(2,1)S(1)}, u32[]{:S(2)}) copy-start(bf16[2048,896]{1,0:T(8,128)(2,1)S(1)} %get-tuple-element.38.pu) | copy-start | bytes 11010052
  47.0 17.9 %collective-permute-start.5 = (bf16[32,4096]{1,0:T(8,128)(2,1)S(1)}, bf16[32,4096]{1,0:T(8,128)(2,1)S(1)}, u32[]{:S(2)}, u32[]{:S(2)}) collective-permute-start(bf16[32,4096]{1,0:T(8,128)(2,1)S(1)} %reshape.21.c0), channel_id=1, source_target_pairs={{24,0},{25,1},{26,2},{27,3},{28,4},{29,5},{30,6},{31,7},{0,8},{1,9... | collective-permute-start | bytes 786440 | tf_op jit(solution)/shard_map/ppermute | solution.py:451
  47.1 17.8 %collective-permute-start.4 = (bf16[32,4096]{1,0:T(8,128)(2,1)S(1)}, bf16[32,4096]{1,0:T(8,128)(2,1)S(1)}, u32[]{:S(2)}, u32[]{:S(2)}) collective-permute-start(bf16[32,4096]{1,0:T(8,128)(2,1)S(1)} %reshape.21.c0), channel_id=1, source_target_pairs={{16,0},{17,1},{18,2},{19,3},{20,4},{21,5},{22,6},{23,7},{24,8},{25... | collective-permute-start | bytes 786440 | tf_op jit(solution)/shard_map/ppermute | solution.py:451
  56.3 7.8 %copy-start = (bf16[256,8192]{1,0:T(8,128)(2,1)}, bf16[256,8192]{1,0:T(8,128)(2,1)S(1)}, u32[]{:S(2)}) copy-start(bf16[256,8192]{1,0:T(8,128)(2,1)S(1)} %outward_panel.1.pd.pd_far) | copy-start | bytes 12582916
  56.3 8.6 %collective-permute-start.3 = (bf16[32,4096]{1,0:T(8,128)(2,1)S(1)}, bf16[32,4096]{1,0:T(8,128)(2,1)S(1)}, u32[]{:S(2)}, u32[]{:S(2)}) collective-permute-start(bf16[32,4096]{1,0:T(8,128)(2,1)S(1)} %reshape.21.c0), channel_id=1, source_target_pairs={{8,0},{9,1},{10,2},{11,3},{12,4},{13,5},{14,6},{15,7},{16,8},{17,9... | collective-permute-start | bytes 786440 | tf_op jit(solution)/shard_map/ppermute | solution.py:451
  64.1 0.8 copy-start.3
  64.9 0.9 copy-start.5
  64.9 0.8 copy-start.7
  65.7 12.5 %collective-permute-start.6 = (bf16[2304,128]{1,0:T(8,128)(2,1)}, bf16[2304,128]{1,0:T(8,128)(2,1)S(1)}, u32[]{:S(2)}, u32[]{:S(2)}) collective-permute-start(bf16[2304,128]{1,0:T(8,128)(2,1)} %get-tuple-element.46), channel_id=1, source_target_pairs={{32,0},{0,32},{96,64},{64,96},{160,128},{128,160},{224,192},{192,2... | collective-permute-start | bytes 1769480 | tf_op jit(solution)/shard_map/ppermute | solution.py:461
  65.8 1.0 copy-start.4
  66.8 0.9 copy-start.6
  67.8 0.9 copy-start.8
  74.9 27.0 %collective-permute-start.8 = (bf16[128,4096]{1,0:T(8,128)(2,1)S(1)}, bf16[128,4096]{1,0:T(8,128)(2,1)}, u32[]{:S(2)}, u32[]{:S(2)}) collective-permute-start(bf16[128,4096]{1,0:T(8,128)(2,1)S(1)} %get-tuple-element.51.cot_own), channel_id=1, source_target_pairs={{32,0},{0,32},{96,64},{64,96},{160,128},{128,160},{224,192},{192,2... | collective-permute-start | bytes 3145736 | tf_op jit(solution)/shard_map/ppermute | solution.py:461
  75.6 2.6 %collective-permute-start.7 = (bf16[256,512]{1,0:T(8,128)(2,1)S(1)}, bf16[256,512]{1,0:T(8,128)(2,1)S(1)}, u32[]{:S(2)}, u32[]{:S(2)}) collective-permute-start(bf16[256,512]{1,0:T(8,128)(2,1)S(1)} %get-tuple-element.58.d_own), channel_id=1, source_target_pairs={{32,0},{0,32},{96,64},{64,96},{160,128},{128,160},{224,192},{192,2... | collective-permute-start | bytes 786440 | tf_op jit(solution)/shard_map/ppermute | solution.py:461
  91.6 32.9 %all-to-all-start.1 = ((bf16[4,32,4096]{2,1,0:T(8,128)(2,1)}), bf16[4,32,4096]{2,1,0:T(8,128)(2,1)}, u32[]{:S(2)}, u32[]{:S(2)}) async-start(bf16[4,32,4096]{2,1,0:T(8,128)(2,1)} %input_parts.1), calls=%async_computation.2 | async-start | bytes 2097152 | tf_op jit(solution)/shard_map/all_to_all | solution.py:477
  97.1 14.8 %collective-permute-start.9 = (bf16[224,512]{1,0:T(8,128)(2,1)}, bf16[224,512]{1,0:T(8,128)(2,1)S(1)}, u32[]{:S(2)}, u32[]{:S(2)}) collective-permute-start(bf16[224,512]{1,0:T(8,128)(2,1)} %get-tuple-element.55), channel_id=1, source_target_pairs={{64,0},{96,32},{0,64},{32,96},{192,128},{224,160},{128,192},{160,2... | collective-permute-start | bytes 688136 | tf_op jit(solution)/shard_map/ppermute | solution.py:456
  98.6 13.8 %collective-permute-start.10 = (bf16[224,512]{1,0:T(8,128)(2,1)}, bf16[224,512]{1,0:T(8,128)(2,1)S(1)}, u32[]{:S(2)}, u32[]{:S(2)}) collective-permute-start(bf16[224,512]{1,0:T(8,128)(2,1)} %get-tuple-element.56), channel_id=1, source_target_pairs={{128,0},{160,32},{192,64},{224,96},{0,128},{32,160},{64,192},{96,2... | collective-permute-start | bytes 688136 | tf_op jit(solution)/shard_map/ppermute | solution.py:456
  101.4 13.2 %collective-permute-start.11 = (bf16[224,512]{1,0:T(8,128)(2,1)S(1)}, bf16[224,512]{1,0:T(8,128)(2,1)S(1)}, u32[]{:S(2)}, u32[]{:S(2)}) collective-permute-start(bf16[224,512]{1,0:T(8,128)(2,1)S(1)} %get-tuple-element.57), channel_id=1, source_target_pairs={{192,0},{224,32},{128,64},{160,96},{64,128},{96,160},{0,192},{32,2... | collective-permute-start | bytes 688136 | tf_op jit(solution)/shard_map/ppermute | solution.py:456
  107.6 10.5 %collective-permute-start.12 = (bf16[224,512]{1,0:T(8,128)(2,1)S(1)}, bf16[224,512]{1,0:T(8,128)(2,1)S(1)}, u32[]{:S(2)}, u32[]{:S(2)}) collective-permute-start(bf16[224,512]{1,0:T(8,128)(2,1)S(1)} %get-tuple-element.60), channel_id=1, source_target_pairs={{64,0},{96,32},{0,64},{32,96},{192,128},{224,160},{128,192},{160,2... | collective-permute-start | bytes 688136 | tf_op jit(solution)/shard_map/ppermute | solution.py:456
  108.0 14.2 %collective-permute-start.13 = (bf16[224,512]{1,0:T(8,128)(2,1)S(1)}, bf16[224,512]{1,0:T(8,128)(2,1)}, u32[]{:S(2)}, u32[]{:S(2)}) collective-permute-start(bf16[224,512]{1,0:T(8,128)(2,1)S(1)} %get-tuple-element.61), channel_id=1, source_target_pairs={{128,0},{160,32},{192,64},{224,96},{0,128},{32,160},{64,192},{96,2... | collective-permute-start | bytes 688136 | tf_op jit(solution)/shard_map/ppermute | solution.py:456
  111.9 10.2 %copy-start.10 = (bf16[224,512]{1,0:T(8,128)(2,1)}, bf16[224,512]{1,0:T(8,128)(2,1)S(1)}, u32[]{:S(2)}) copy-start(bf16[224,512]{1,0:T(8,128)(2,1)S(1)} %collective-permute-done.9) | copy-start | bytes 688132
  111.9 12.5 %collective-permute-start.14 = (bf16[224,512]{1,0:T(8,128)(2,1)S(1)}, bf16[224,512]{1,0:T(8,128)(2,1)}, u32[]{:S(2)}, u32[]{:S(2)}) collective-permute-start(bf16[224,512]{1,0:T(8,128)(2,1)S(1)} %get-tuple-element.62), channel_id=1, source_target_pairs={{192,0},{224,32},{128,64},{160,96},{64,128},{96,160},{0,192},{32,2... | collective-permute-start | bytes 688136 | tf_op jit(solution)/shard_map/ppermute | solution.py:456
  112.4 9.7 %copy-start.12 = (bf16[224,512]{1,0:T(8,128)(2,1)}, bf16[224,512]{1,0:T(8,128)(2,1)S(1)}, u32[]{:S(2)}) copy-start(bf16[224,512]{1,0:T(8,128)(2,1)S(1)} %collective-permute-done.10) | copy-start | bytes 688132
  114.6 7.6 %copy-start.16 = (bf16[224,512]{1,0:T(8,128)(2,1)}, bf16[224,512]{1,0:T(8,128)(2,1)S(1)}, u32[]{:S(2)}) copy-start(bf16[224,512]{1,0:T(8,128)(2,1)S(1)} %collective-permute-done.11) | copy-start | bytes 688132
  118.1 6.4 %copy-start.14 = (bf16[224,512]{1,0:T(8,128)(2,1)}, bf16[224,512]{1,0:T(8,128)(2,1)S(1)}, u32[]{:S(2)}) copy-start(bf16[224,512]{1,0:T(8,128)(2,1)S(1)} %collective-permute-done.12) | copy-start | bytes 688132
  124.4 7.3 %copy-start.11 = (bf16[224,512]{1,0:T(8,128)(2,1)S(1)}, bf16[224,512]{1,0:T(8,128)(2,1)}, u32[]{:S(2)}) copy-start(bf16[224,512]{1,0:T(8,128)(2,1)} %copy-done.10) | copy-start | bytes 688132
  124.4 7.3 %copy-start.13 = (bf16[224,512]{1,0:T(8,128)(2,1)S(1)}, bf16[224,512]{1,0:T(8,128)(2,1)}, u32[]{:S(2)}) copy-start(bf16[224,512]{1,0:T(8,128)(2,1)} %copy-done.12) | copy-start | bytes 688132
  124.4 7.3 %copy-start.17 = (bf16[224,512]{1,0:T(8,128)(2,1)S(1)}, bf16[224,512]{1,0:T(8,128)(2,1)}, u32[]{:S(2)}) copy-start(bf16[224,512]{1,0:T(8,128)(2,1)} %copy-done.16) | copy-start | bytes 688132
  124.5 12.8 %copy-start.15 = (bf16[224,512]{1,0:T(8,128)(2,1)S(1)}, bf16[224,512]{1,0:T(8,128)(2,1)}, u32[]{:S(2)}) copy-start(bf16[224,512]{1,0:T(8,128)(2,1)} %copy-done.14) | copy-start | bytes 688132
  128.2 19.8 %all-to-all-start.2 = ((bf16[8,8,4096]{2,1,0:T(8,128)(2,1)}), bf16[8,8,4096]{2,1,0:T(8,128)(2,1)S(1)}, u32[]{:S(2)}, u32[]{:S(2)}) async-start(bf16[8,8,4096]{2,1,0:T(8,128)(2,1)} %pad_maximum_fusion), calls=%async_computation.3 | async-start | bytes 1048576 | tf_op jit(solution)/shard_map/all_to_all | solution.py:473
  132.6 8.4 %collective-permute-start.15 = (bf16[224,512]{1,0:T(8,128)(2,1)S(1)}, bf16[224,512]{1,0:T(8,128)(2,1)S(1)}, u32[]{:S(2)}, u32[]{:S(2)}) collective-permute-start(bf16[224,512]{1,0:T(8,128)(2,1)S(1)} %get-tuple-element.64), channel_id=1, source_target_pairs={{64,0},{96,32},{0,64},{32,96},{192,128},{224,160},{128,192},{160,2... | collective-permute-start | bytes 688136 | tf_op jit(solution)/shard_map/ppermute | solution.py:456
  132.6 10.8 %collective-permute-start.16 = (bf16[224,512]{1,0:T(8,128)(2,1)S(1)}, bf16[224,512]{1,0:T(8,128)(2,1)S(1)}, u32[]{:S(2)}, u32[]{:S(2)}) collective-permute-start(bf16[224,512]{1,0:T(8,128)(2,1)S(1)} %get-tuple-element.65), channel_id=1, source_target_pairs={{128,0},{160,32},{192,64},{224,96},{0,128},{32,160},{64,192},{96,2... | collective-permute-start | bytes 688136 | tf_op jit(solution)/shard_map/ppermute | solution.py:456
  134.5 11.3 %collective-permute-start.17 = (bf16[224,512]{1,0:T(8,128)(2,1)S(1)}, bf16[224,512]{1,0:T(8,128)(2,1)S(1)}, u32[]{:S(2)}, u32[]{:S(2)}) collective-permute-start(bf16[224,512]{1,0:T(8,128)(2,1)S(1)} %get-tuple-element.66), channel_id=1, source_target_pairs={{192,0},{224,32},{128,64},{160,96},{64,128},{96,160},{0,192},{32,2... | collective-permute-start | bytes 688136 | tf_op jit(solution)/shard_map/ppermute | solution.py:456
Sparse Core Ops, SparseCore 0:
  65.8 20.8 reduce-scatter.1

commit v4 on v3

--- a/solution.py
+++ b/solution.py
@@ -91,65 +91,78 @@
     return jax.ShapeDtypeStruct(dims, dtype)
 
 
-def unfold(src, qh, swap):
-    rows = slice(qh * 16, qh * 16 + 16)
+def unfold(src, row, swap):
+    rows = pl.ds(pl.multiple_of(row, 16), 16)
     halves = [jnp.concatenate([src[rows, k * 128:k * 128 + 128] for k in TILE_ROWS[c]], axis=0) for c in range(2)]
     return mm(swap, jnp.concatenate(halves, axis=1)).astype(BF)
 
 
-def inward_panels_kernel(idx, g_ref, u_ref, pg, pu, scr):
-    j = pl.program_id(0)
-    pg[...] = jnp.zeros_like(pg)
-    pu[...] = jnp.zeros_like(pu)
+def inward_panels_kernel(idx, gate, up, pg, pu, held, tiles, sems):
+    fetches = [pltpu.make_async_copy(src, held.at[m], sems.at[m]) for m, src in enumerate((gate, up))]
+    for fetch in fetches:
+        fetch.start()
     swap = swap_matrix()
-    for m, (src, dst) in enumerate(((g_ref, pg), (u_ref, pu))):
-        for qh in range(2):
-            tiles = scr.at[2 * m + qh]
-            tiles[...] = unfold(src, qh, swap)
+    for m, dst in enumerate((pg, pu)):
+        dst[...] = jnp.zeros_like(dst)
+        fetches[m].wait()
+
+        def column(j, carry):
+            lanes = pl.ds(pl.multiple_of(j * 128, 128), 128)
+            for half in range(2):
+                tiles[half, :, :] = unfold(held.at[m], j * KEEP + half * 16, swap)
+                for q in range(16):
+                    i = idx[m, j * KEEP + half * 16 + q]
+                    for c in range(2):
+                        dst[pl.ds(pl.multiple_of(i * 32 + c * 16, 16), 16), lanes] = tiles[
+                            half, q * 16:q * 16 + 16, c * 128:c * 128 + 128
+                        ]
+            return carry
+
+        lax.fori_loop(0, COLS, column, 0)
+
+
+def outward_panel_kernel(idx, down, pd, held, tiles, sem):
+    fetch = pltpu.make_async_copy(down, held, sem)
+    fetch.start()
+    swap = swap_matrix()
+    pd[...] = jnp.zeros_like(pd)
+    fetch.wait()
+
+    def column(j, carry):
+        for half in range(2):
+            tiles[half, :, :] = unfold(held, j * KEEP + half * 16, swap)
             for q in range(16):
-                i = idx[m, j * KEEP + qh * 16 + q]
+                i = idx[2, j * KEEP + half * 16 + q]
                 for c in range(2):
-                    dst[pl.ds(pl.multiple_of(i * 32 + c * 16, 16), 16), :] = tiles[
-                        q * 16:q * 16 + 16, c * 128:c * 128 + 128
+                    rows = pl.ds(pl.multiple_of(j * 32 + c * 16, 16), 16)
+                    pd[rows, pl.ds(pl.multiple_of(i * 128, 128), 128)] = tiles[
+                        half, q * 16:q * 16 + 16, c * 128:c * 128 + 128
                     ]
-
-
-def outward_panel_kernel(idx, d_ref, pd, scr):
-    j = pl.program_id(0)
-    pd[...] = jnp.zeros_like(pd)
-
-    @pl.when(j < COLS)
-    def _():
-        swap = swap_matrix()
-        for qh in range(2):
-            tiles = scr.at[qh]
-            tiles[...] = unfold(d_ref, qh, swap)
-            for q in range(16):
-                i = idx[2, j * KEEP + qh * 16 + q]
-                for c in range(2):
-                    pd[c * 16:c * 16 + 16, pl.ds(pl.multiple_of(i * 128, 128), 128)] = tiles[
-                        q * 16:q * 16 + 16, c * 128:c * 128 + 128
-                    ]
+        return carry
+
+    lax.fori_loop(0, COLS, column, 0)
 
 
 def hbm(value):
     return pltpu.with_memory_space_constraint(value, pltpu.HBM)
 
 
+def far(n):
+    return [pl.BlockSpec(memory_space=pl.ANY)] * n
+
+
 def inward_panels(idx, gate, up):
-    blocks = pl.BlockSpec((KEEP, D), lambda j, s: (j, 0))
-    panel = pl.BlockSpec((FEAT, 128), lambda j, s: (0, j))
     return pl.pallas_call(
         inward_panels_kernel,
-        grid_spec=pltpu.PrefetchScalarGridSpec(
-            num_scalar_prefetch=1,
-            grid=(COLS,),
-            in_specs=[blocks, blocks],
-            out_specs=[panel, panel],
-            scratch_shapes=[pltpu.VMEM((4, 256, 256), BF)],
-        ),
+        in_specs=smem(1) + far(2),
+        out_specs=vm(2),
         out_shape=[pltpu.VMEM((FEAT, WIDE), BF), pltpu.VMEM((FEAT, WIDE), BF)],
-        compiler_params=params(10),
+        scratch_shapes=[
+            pltpu.VMEM((2, SLOT, D), BF),
+            pltpu.VMEM((2, 256, 256), BF),
+            pltpu.SemaphoreType.DMA((2,)),
+        ],
+        compiler_params=params(14),
         cost_estimate=cost(6),
         name="inward_panels",
     )(idx, hbm(gate), hbm(up))
@@ -158,14 +171,10 @@
 def outward_panel(idx, down):
     return pl.pallas_call(
         outward_panel_kernel,
-        grid_spec=pltpu.PrefetchScalarGridSpec(
-            num_scalar_prefetch=1,
-            grid=(COLS + 1,),
-            in_specs=[pl.BlockSpec((KEEP, D), lambda j, s: (jnp.minimum(j, COLS - 1), 0))],
-            out_specs=pl.BlockSpec((KEEP, 2 * D), lambda j, s: (j, 0)),
-            scratch_shapes=[pltpu.VMEM((2, 256, 256), BF)],
-        ),
+        in_specs=smem(1) + far(1),
+        out_specs=vm(1)[0],
         out_shape=pltpu.VMEM((256, 2 * D), BF),
+        scratch_shapes=[pltpu.VMEM((SLOT, D), BF), pltpu.VMEM((2, 256, 256), BF), pltpu.SemaphoreType.DMA],
         compiler_params=params(10),
         cost_estimate=cost(3),
         name="outward_panel",
@@ -300,8 +309,12 @@
 
 
 def delta_kernel(c0, c1, c2, c3, pd_far, gl2, ul2, own, cot, gdx, udx, cx, pd, sem):
-    fetch = pltpu.make_async_copy(pd_far, pd, sem)
-    fetch.start()
+    def fetch(n):
+        lanes = pl.ds(n * 1024, 1024)
+        return pltpu.make_async_copy(pd_far.at[:, lanes], pd.at[:, lanes], sem.at[n])
+
+    for n in range(8):
+        fetch(n).start()
     at = cols_of(512)
     hjoin = one_hot(split_index(rows_of(256), 128), (at >> 7) * 128 + (at & 63))
     low = low_half((32, 128))
@@ -320,13 +333,11 @@
             cx[top, second] = jnp.where(low, rolled, zero).astype(BF)
             cx[bottom, second] = jnp.where(low, zero, c).astype(BF)
 
-    fetch.wait()
-
-    def product(n, acc):
-        lanes = pl.ds(pl.multiple_of(n * 1024, 1024), 1024)
-        return acc + mm_nt(cx[:, lanes], pd[:, lanes])
-
-    hd = lax.fori_loop(0, 8, product, jnp.zeros((256, 256), F32))
+    hd = jnp.zeros((256, 256), F32)
+    for n in range(8):
+        lanes = slice(n * 1024, n * 1024 + 1024)
+        fetch(n).wait()
+        hd = hd + mm_nt(cx[:, lanes], pd[:, lanes])
     high = hd.astype(BF)
     rest = (hd - high.astype(F32)).astype(BF)
     low = low_half((TOK, 128))
@@ -368,7 +379,7 @@
         scratch_shapes=[
             pltpu.VMEM((256, 2 * D), BF),
             pltpu.VMEM((256, 2 * D), BF),
-            pltpu.SemaphoreType.DMA,
+            pltpu.SemaphoreType.DMA((8,)),
         ],
         compiler_params=params(18),
         cost_estimate=cost(0.2),
@@ -376,33 +387,60 @@
     )(*pieces, hbm(pd), gl2, ul2)
 
 
-def back_kernel(gdx, udx, pg, pu, parts):
+def back_kernel(gdx, udx, pg, pu, out_parts, parts, fjoin):
     y = place()[2]
-    fjoin = one_hot(split_index(rows_of(256), 64), cols_of(256))
     n = pl.program_id(0)
+
+    @pl.when(n == 0)
+    def _():
+        fjoin[...] = one_hot(split_index(rows_of(256), 64), cols_of(256))
+
+    parts[:, :32, :] = out_parts[...]
     acc = (mm_nt(gdx[...], pg[...]) + mm_nt(udx[...], pu[...])).astype(BF)
-    for c in range(2):
+    for c in range(4):
         cols = slice(c * 128, c * 128 + 128)
         pair = jnp.concatenate([acc[:TOK, cols], acc[TOK:, cols]], axis=1)
-        whole = mm(pair, fjoin).astype(BF)
-        lanes = pl.ds(pl.multiple_of(n * 512 + c * 256, 256), 256)
+        whole = mm(pair, fjoin[...]).astype(BF)
         for r in range(NY):
-            parts[lax.rem(y + r, NY), :, lanes] = whole[r * 32:r * 32 + 32, :]
-
-
-def input_parts(gdx, udx, pg, pu):
+            parts[lax.rem(y + r, NY), 32:, c * 256:c * 256 + 256] = whole[r * 32:r * 32 + 32, :]
+
+
+def input_parts(gdx, udx, pg, pu, out_parts):
     whole = pl.BlockSpec((256, WIDE), lambda n: (0, 0))
-    panel = pl.BlockSpec((256, WIDE), lambda n: (n, 0))
+    panel = pl.BlockSpec((512, WIDE), lambda n: (n, 0))
     return pl.pallas_call(
         back_kernel,
-        grid=(FEAT // 256,),
-        in_specs=[whole, whole, panel, panel],
-        out_specs=pl.BlockSpec((NY, 32, D), lambda n: (0, 0, 0)),
-        out_shape=shape(NY, 32, D),
+        grid=(FEAT // 512,),
+        in_specs=[whole, whole, panel, panel, pl.BlockSpec((NY, 32, 1024), lambda n: (0, 0, n))],
+        out_specs=pl.BlockSpec((NY, 64, 1024), lambda n: (0, 0, n)),
+        out_shape=shape(NY, 64, D),
+        scratch_shapes=[pltpu.VMEM((256, 256), BF)],
+        compiler_params=params(14),
+        cost_estimate=cost(0.2),
+        name="input_parts",
+    )(gdx, udx, hbm(pg), hbm(pu), out_parts)
+
+
+def merge_kernel(got, both):
+    for n in range(0, D, 512):
+        lanes = slice(n, n + 512)
+        total = sum(got[r, :, lanes].astype(F32) for r in range(1, NY)) + got[0, :, lanes].astype(F32)
+        for z in range(NZ):
+            both[z, :, lanes] = jnp.concatenate(
+                [total[z * 4:z * 4 + 4], total[32 + z * 4:36 + z * 4]], axis=0
+            ).astype(BF)
+
+
+def merge_y(got):
+    return pl.pallas_call(
+        merge_kernel,
+        in_specs=vm(1),
+        out_specs=vm(1)[0],
+        out_shape=shape(NZ, 8, D),
         compiler_params=params(10),
         cost_estimate=cost(0.2),
-        name="input_parts",
-    )(gdx, udx, hbm(pg), hbm(pu))
+        name="merge_y",
+    )(got)
 
 
 def inward_kernel(m, idx, xt_own, sib_oth, d_own, d_oth, w0, w1, w2, w3, part, tiles):
@@ -507,24 +545,19 @@
     cot = [cot_z] + [from_y(cot_z, s) for s in range(1, NY)]
 
     xt_own, ht_own, sib, gl2, ul2, out_parts = forward(tok, pg, pu, pd)
-    sib_oth = from_core(sib)
-    out_y = lax.psum_scatter(
-        after(out_parts, *cot), "fsdp", scatter_dimension=0, axis_index_groups=y_groups()
-    )
+    sib_oth = from_core(after(sib, *cot))
     own, cot_own, gdx, udx = deltas(cot, pd, gl2, ul2)
     oth, cot_oth = from_core(own), from_core(cot_own)
     gate_wire = inward_grads(0, block_index, xt_own, sib_oth, own, oth)
     gate_got = exchange_x(gate_wire)
-    in_parts = input_parts(after(gdx, gate_wire[0]), udx, pg, pu)
-    in_got = over_y(in_parts)
-    down_wire = down_grads(block_index, cot_own, cot_oth, after(ht_own, in_parts), sib_oth)
+    parts = input_parts(after(gdx, gate_wire[0]), udx, pg, pu, out_parts)
+    parts_got = over_y(parts)
+    down_wire = down_grads(block_index, cot_own, cot_oth, after(ht_own, parts), sib_oth)
     down_got = exchange_x(down_wire)
     up_wire = inward_grads(1, block_index, xt_own, sib_oth, after(own, down_wire[0], *gate_got[1:]), oth)
     up_got = exchange_x(up_wire)
-    in_y = after(in_got, up_wire[0], *down_got[1:]).astype(F32).sum(axis=0).astype(BF)
+    both = merge_y(after(parts_got, up_wire[0], *down_got[1:]))
     gate_grad, up_grad, down_grad = (mean_of(g) for g in (gate_got, up_got, down_got))
-
-    both = jnp.concatenate([part.reshape(NZ, rows, D) for part in (out_y, in_y)], axis=1)
     total = over_z(both).astype(F32).sum(axis=0).astype(BF)
     return (total[:rows], total[rows:], gate_grad, up_grad, down_grad)
 

time: 157 us -> 132 us (0.84)
  between operations: 14.4 us -> 1 us
  Pallas kernels: 50 us -> 42.4 us
  waiting for transfers between devices: 19 us -> 13.8 us
  local copies, waits for them, and re-layouts: 6.7 us -> 9.89 us
    unnamed x36 -> x62, local copies, waits for them, and re-layouts: 4.5 us -> 8.85 us
    pallas_call x3 -> x4, Pallas kernels: 22.6 us -> 18.3 us  [the longest x1 7.13 us: inward_panels(): pl.pallas_call(inward_panels_kernel, in_specs=smem(1) + far(2), out_specs...]
    ppermute x9, waiting for transfers between devices: 15.1 us -> 12.6 us  [from_x(): return lax.ppermute(value, 'dp', pairs)]
  transfers between devices with their start and end apart: 21 -> 20, of which waited for: 8 -> 7; matrix products, arithmetic and copies ran while one was open for 3% -> 4% of each run, Pallas kernels for 32% -> 24%
where the time goes in v4:
time: 132 us; the launch traced here: 131 us
  Pallas kernels  42.4 us (32%)
  starting transfers between devices  32.6 us (25%)
  blocking collectives  25.8 us (20%)
  waiting for transfers between devices  13.8 us (10%)
  local copies, waits for them, and re-layouts  9.89 us (7%)
  other arithmetic  5.49 us (4%)
    all_to_all x1, blocking collectives, over_z(): lax.all_to_all(value, 'fsdp', 0, 0, axis_index_groups=z_groups(), tiled=T...  25.8 us
    ppermute x9, starting transfers between devices, from_x(): return lax.ppermute(value, 'dp', pairs)  14.2 us
    ppermute x9, waiting for transfers between devices, from_x(): return lax.ppermute(value, 'dp', pairs)  12.6 us
    unnamed x62, local copies, waits for them, and re-layouts  8.85 us
    ppermute x6, starting transfers between devices, from_y(): return lax.ppermute(value, 'fsdp', pairs)  8.57 us
    pallas_call x1, Pallas kernels, inward_panels(): pl.pallas_call(inward_panels_kernel, in_specs=smem(1) + far(2), out_specs...  7.13 us
    pallas_call x2, Pallas kernels, inward_grads(): pl.pallas_call(functools.partial(inward_kernel, m), in_specs=smem(1) + vm...  7.08 us
    pallas_call x1, Pallas kernels, forward(): pl.pallas_call(forward_kernel, in_specs=vm(7), out_specs=vm(6), out_shape...  6.74 us
  transfers between devices with their start and end apart: 20, of which 7 were waited for; matrix products, arithmetic and copies ran while one was open for 4% of the time, Pallas kernels for 24%

profile of v4, /device:TPU:8, one launch (start us, length us, event | category | flops | bytes accessed | tf_op | source)
XLA Modules:
  0.0 130.9 jit_solution(10904176129186391329)
XLA Ops:
  0.6 0.8 pad_maximum_fusion
  1.5 25.8 %all_to_all.15 = bf16[8,8,4096]{2,1,0:T(8,128)(2,1)S(1)} all-to-all(bf16[8,8,4096]{2,1,0:T(8,128)(2,1)S(1)} %broadcast_in_dim.2), channel_id=1, replica_groups={{0,1,2,3,4,5,6,7},{8,9,10,11,12,13,14,15},{16,17,18,19,20,21,22,23},{24..., dimensions={0} | all-to-all | bytes 1048576 | tf_op jit(solution)/shard_map/all_to_all | solution.py:511
  27.3 0.2 fusion
  27.5 0.1 reshape.18.t0
  27.6 1.7 %collective-permute-start.5 = (bf16[32,4096]{1,0:T(8,128)(2,1)S(1)}, bf16[32,4096]{1,0:T(8,128)(2,1)S(1)}, u32[]{:S(2)}, u32[]{:S(2)}) collective-permute-start(bf16[32,4096]{1,0:T(8,128)(2,1)S(1)} %reshape.18.t0), channel_id=1, source_target_pairs={{24,0},{25,1},{26,2},{27,3},{28,4},{29,5},{30,6},{31,7},{0,8},{1,9... | collective-permute-start | bytes 786440 | tf_op jit(solution)/shard_map/ppermute | solution.py:489
  29.2 0.9 collective-permute-start.4
  30.2 2.4 %collective-permute-start.3 = (bf16[32,4096]{1,0:T(8,128)(2,1)S(1)}, bf16[32,4096]{1,0:T(8,128)(2,1)S(1)}, u32[]{:S(2)}, u32[]{:S(2)}) collective-permute-start(bf16[32,4096]{1,0:T(8,128)(2,1)S(1)} %reshape.18.t0), channel_id=1, source_target_pairs={{8,0},{9,1},{10,2},{11,3},{12,4},{13,5},{14,6},{15,7},{16,8},{17,9... | collective-permute-start | bytes 786440 | tf_op jit(solution)/shard_map/ppermute | solution.py:489
  32.6 0.1 reshape.17.c0
  32.7 7.1 %inward_panels.1 = (bf16[2048,896]{1,0:T(8,128)(2,1)S(1)}, bf16[2048,896]{1,0:T(8,128)(2,1)S(1)}) custom-call(s32[3,224]{1,0:T(4,128)S(1)} %copy-done.14, bf16[224,4096]{1,0:T(8,128)(2,1)} %gate.1, bf16[224,4096]{1,0:T(8,128)(2,1)} %up.1), custom_call_target="tpu_custom_call" | custom-call | flops 6000000000 | bytes 1000 | tf_op jit(solution)/shard_map/inward_panels/pallas_call | solution.py:155
  39.8 0.1 collective-permute-start.2
  39.9 3.4 %collective-permute-start.1 = (bf16[32,4096]{1,0:T(8,128)(2,1)S(1)}, bf16[32,4096]{1,0:T(8,128)(2,1)S(1)}, u32[]{:S(2)}, u32[]{:S(2)}) collective-permute-start(bf16[32,4096]{1,0:T(8,128)(2,1)S(1)} %reshape.17.c0), channel_id=1, source_target_pairs={{16,0},{17,1},{18,2},{19,3},{20,4},{21,5},{22,6},{23,7},{24,8},{25... | collective-permute-start | bytes 786440 | tf_op jit(solution)/shard_map/ppermute | solution.py:489
  43.3 4.0 %outward_panel.1.pd.pd_far = bf16[256,8192]{1,0:T(8,128)(2,1)S(1)} custom-call(s32[3,224]{1,0:T(4,128)S(1)} %copy-done.14, bf16[224,4096]{1,0:T(8,128)(2,1)} %down.1), custom_call_target="tpu_custom_call" | custom-call | flops 3000000000 | bytes 1000 | tf_op jit(solution)/shard_map/outward_panel/pallas_call | solution.py:172
  47.3 0.0 collective-permute-done.5.t3
  47.3 0.1 collective-permute-start
  47.4 0.0 collective-permute-done.4.t2
  47.4 0.0 collective-permute-done.3.t1
  47.5 6.7 %forward.1 = (bf16[2048,128]{1,0:T(8,128)(2,1)S(1)}, bf16[256,128]{1,0:T(8,128)(2,1)S(1)}, bf16[2304,128]{1,0:T(8,128)(2,1)S(1)}, f32[128,896]{1,0:T(8,128)S(1)}...) custom-call(bf16[32,4096]{1,0:T(8,128)(2,1)S(1)} %reshape.18.t0, ...), custom_call_target="tpu_custom_call" | custom-call | flops 8000000000 | bytes 1000 | tf_op jit(solution)/shard_map/forward/pallas_call | solution.py:243
  54.2 0.0 collective-permute-done.1.c2
  54.2 0.0 collective-permute-done.c1
  54.3 0.3 collective-permute-start.6
  54.5 5.1 %deltas.1 = (bf16[256,512]{1,0:T(8,128)(2,1)S(1)}, bf16[128,4096]{1,0:T(8,128)(2,1)S(1)}, bf16[256,896]{1,0:T(8,128)(2,1)S(1)}, bf16[256,896]{1,0:T(8,128)(2,1)S(1)}) custom-call(bf16[32,4096]{1,0:T(8,128)(2,1)S(1)} %reshape.17.c0, bf16[32,4096]{1,0:T(8,128)(2,1)S(1)} %collective-permute-done.c1, bf16[32,4096]{1,0:T(8,128)(2,1)S(1)} %collective-permute-done.1.c2, ...), custom_call_target="tpu_custom_call" | custom-call | flops 200000000 | bytes 1000 | tf_op jit(solution)/shard_map/deltas/pallas_call | solution.py:374
  59.7 0.6 collective-permute-start.7
  60.3 1.2 collective-permute-done.7.d_oth
  61.4 0.0 collective-permute-done.6.sib_oth
  61.4 3.5 %gate_grads.1 = (bf16[224,512]{1,0:T(8,128)(2,1)S(1)}, bf16[224,512]{1,0:T(8,128)(2,1)S(1)}, bf16[224,512]{1,0:T(8,128)(2,1)S(1)}, bf16[224,512]{1,0:T(8,128)(2,1)S(1)}) custom-call(s32[3,224]{1,0:T(4,128)S(1)} %copy-done.14, bf16[2048,128]{1,0:T(8,128)(2,1)S(1)} %get-tuple-element.43.xt_own, bf16[2304,128]{1,0:T(8,128)(2,1)S(1)} %collective-permute-done.6.sib_oth, ...), custom_call_target="tpu_custom_call" | custom-call | flops 200000000 | bytes 1000 | tf_op jit(solution)/shard_map/gate_grads/pallas_call | solution.py:475
  65.0 0.7 copy-done.8
  65.7 0.7 copy-done.15
  66.4 0.7 copy-done.18
  67.1 0.7 copy-done.23
  67.7 6.1 %input_parts.1 = bf16[4,64,4096]{2,1,0:T(8,128)(2,1)S(1)} custom-call(bf16[256,896]{1,0:T(8,128)(2,1)S(1)} %get-tuple-element.48.gdx, bf16[256,896]{1,0:T(8,128)(2,1)S(1)} %get-tuple-element.49.udx, bf16[2048,896]{1,0:T(8,128)(2,1)} %copy-done.2, bf16[2048,896]{1,0:T(8,128)(2,1)} %copy-done.3, bf16[4,32,4096]{2,1,0:T(8,128)(2,1)S(1)} %get-tuple-element.50.out_parts), custom_call_target="tpu_custom_call" | custom-call | flops 200000000 | bytes 1000 | tf_op jit(solution)/shard_map/input_parts/pallas_call | solution.py:411
  73.8 1.3 %copy-done = bf16[4,64,4096]{2,1,0:T(8,128)(2,1)} copy-done((bf16[4,64,4096]{2,1,0:T(8,128)(2,1)}, bf16[4,64,4096]{2,1,0:T(8,128)(2,1)S(1)}, u32[]{:S(2)}) %copy-start) | copy-done | bytes 2097176
  75.2 5.3 %all-to-all-start.1 = ((bf16[4,64,4096]{2,1,0:T(8,128)(2,1)}), bf16[4,64,4096]{2,1,0:T(8,128)(2,1)S(1)}, u32[]{:S(2)}, u32[]{:S(2)}) async-start(bf16[4,64,4096]{2,1,0:T(8,128)(2,1)} %copy-done), calls=%async_computation.1 | async-start | bytes 4194304 | tf_op jit(solution)/shard_map/all_to_all | solution.py:515
  80.5 0.0 collective-permute-start.8
  80.5 1.5 %collective-permute-start.9 = (bf16[224,512]{1,0:T(8,128)(2,1)}, bf16[224,512]{1,0:T(8,128)(2,1)S(1)}, u32[]{:S(2)}, u32[]{:S(2)}) collective-permute-start(bf16[224,512]{1,0:T(8,128)(2,1)} %copy-done.23), channel_id=1, source_target_pairs={{64,0},{96,32},{0,64},{32,96},{192,128},{224,160},{128,192},{160,2... | collective-permute-start | bytes 688136 | tf_op jit(solution)/shard_map/ppermute | solution.py:494
  82.0 2.7 %collective-permute-start.10 = (bf16[224,512]{1,0:T(8,128)(2,1)}, bf16[224,512]{1,0:T(8,128)(2,1)S(1)}, u32[]{:S(2)}, u32[]{:S(2)}) collective-permute-start(bf16[224,512]{1,0:T(8,128)(2,1)} %copy-done.18), channel_id=1, source_target_pairs={{128,0},{160,32},{192,64},{224,96},{0,128},{32,160},{64,192},{96,2... | collective-permute-start | bytes 688136 | tf_op jit(solution)/shard_map/ppermute | solution.py:494
  84.7 0.5 collective-permute-start.11
  85.2 0.0 collective-permute-done.8.cot_oth
  85.2 1.2 copy-done.7
  86.4 5.1 %down_grads.1 = (bf16[224,512]{1,0:T(8,128)(2,1)S(1)}, bf16[224,512]{1,0:T(8,128)(2,1)S(1)}, bf16[224,512]{1,0:T(8,128)(2,1)S(1)}, bf16[224,512]{1,0:T(8,128)(2,1)S(1)}) custom-call(s32[3,224]{1,0:T(4,128)S(1)} %copy-done.14, bf16[128,4096]{1,0:T(8,128)(2,1)S(1)} %copy-done.7, bf16[128,4096]{1,0:T(8,128)(2,1)S(1)} %collective-permute-done.8.cot_oth, ...), custom_call_target="tpu_custom_call" | custom-call | flops 200000000 | bytes 1000 | tf_op jit(solution)/shard_map/down_grads/pallas_call | solution.py:299
  91.6 0.3 collective-permute-start.12
  91.9 4.0 %collective-permute-start.13 = (bf16[224,512]{1,0:T(8,128)(2,1)S(1)}, bf16[224,512]{1,0:T(8,128)(2,1)S(1)}, u32[]{:S(2)}, u32[]{:S(2)}) collective-permute-start(bf16[224,512]{1,0:T(8,128)(2,1)S(1)} %get-tuple-element.61), channel_id=1, source_target_pairs={{128,0},{160,32},{192,64},{224,96},{0,128},{32,160},{64,192},{96,2... | collective-permute-start | bytes 688136 | tf_op jit(solution)/shard_map/ppermute | solution.py:494
  95.9 0.5 collective-permute-start.14
  96.4 2.1 %collective-permute-done.11 = bf16[224,512]{1,0:T(8,128)(2,1)S(1)} collective-permute-done((bf16[224,512]{1,0:T(8,128)(2,1)}, bf16[224,512]{1,0:T(8,128)(2,1)S(1)}, u32[]{:S(2)}, u32[]{:S(2)}) %collective-permute-start.11) | collective-permute-done | bytes 229408 | tf_op jit(solution)/shard_map/ppermute | solution.py:494
  98.5 3.5 %up_grads.1 = (bf16[224,512]{1,0:T(8,128)(2,1)S(1)}, bf16[224,512]{1,0:T(8,128)(2,1)S(1)}, bf16[224,512]{1,0:T(8,128)(2,1)S(1)}, bf16[224,512]{1,0:T(8,128)(2,1)S(1)}) custom-call(s32[3,224]{1,0:T(4,128)S(1)} %copy-done.14, bf16[2048,128]{1,0:T(8,128)(2,1)S(1)} %get-tuple-element.43.xt_own, bf16[2304,128]{1,0:T(8,128)(2,1)S(1)} %collective-permute-done.6.sib_oth, ...), custom_call_target="tpu_custom_call" | custom-call | flops 200000000 | bytes 1000 | tf_op jit(solution)/shard_map/up_grads/pallas_call | solution.py:475
  102.1 0.7 copy-done.12
  102.8 0.7 copy-done.16
  103.5 0.7 copy-done.19
  104.2 0.7 copy-done.21
  104.9 1.2 collective-permute-done.13
  106.1 0.7 copy-done.29
  106.8 2.0 %collective-permute-done.14 = bf16[224,512]{1,0:T(8,128)(2,1)} collective-permute-done((bf16[224,512]{1,0:T(8,128)(2,1)S(1)}, bf16[224,512]{1,0:T(8,128)(2,1)}, u32[]{:S(2)}, u32[]{:S(2)}) %collective-permute-start.14) | collective-permute-done | bytes 229408 | tf_op jit(solution)/shard_map/ppermute | solution.py:494
  108.7 1.1 merge_y.1
  109.9 3.6 %all-to-all-start.2 = ((bf16[8,8,4096]{2,1,0:T(8,128)(2,1)}), bf16[8,8,4096]{2,1,0:T(8,128)(2,1)S(1)}, u32[]{:S(2)}, u32[]{:S(2)}) async-start(bf16[8,8,4096]{2,1,0:T(8,128)(2,1)} %merge_y.1), calls=%async_computation.2 | async-start | bytes 1048576 | tf_op jit(solution)/shard_map/all_to_all | solution.py:511
  113.5 2.0 %multiply_convert_fusion.2 = bf16[224,512]{1,0:T(8,128)(2,1)} fusion(bf16[224,512]{1,0:T(8,128)(2,1)} %copy-done.28, bf16[224,512]{1,0:T(8,128)(2,1)} %copy-done.25, bf16[224,512]{1,0:T(8,128)(2,1)} %copy-done.24, bf16[224,512]{1,0:T(8,128)(2,1)S(1)} %copy-done.9), kind=kLoop, calls=%fused_computation.2 | loop fusion | flops 1032192 | bytes 1146880 | tf_op jit(solution)/shard_map/convert_element_type | solution.py:532
  115.5 0.0 collective-permute-start.15
  115.6 1.9 %collective-permute-start.16 = (bf16[224,512]{1,0:T(8,128)(2,1)S(1)}, bf16[224,512]{1,0:T(8,128)(2,1)S(1)}, u32[]{:S(2)}, u32[]{:S(2)}) collective-permute-start(bf16[224,512]{1,0:T(8,128)(2,1)S(1)} %copy-done.20), channel_id=1, source_target_pairs={{128,0},{160,32},{192,64},{224,96},{0,128},{32,160},{64,192},{96,2... | collective-permute-start | bytes 688136 | tf_op jit(solution)/shard_map/ppermute | solution.py:494
  117.5 2.8 %collective-permute-start.17 = (bf16[224,512]{1,0:T(8,128)(2,1)S(1)}, bf16[224,512]{1,0:T(8,128)(2,1)S(1)}, u32[]{:S(2)}, u32[]{:S(2)}) collective-permute-start(bf16[224,512]{1,0:T(8,128)(2,1)S(1)} %copy-done.17), channel_id=1, source_target_pairs={{192,0},{224,32},{128,64},{160,96},{64,128},{96,160},{0,192},{32,2... | collective-permute-start | bytes 688136 | tf_op jit(solution)/shard_map/ppermute | solution.py:494
  120.3 1.8 %multiply_convert_fusion = bf16[224,512]{1,0:T(8,128)(2,1)} fusion(bf16[224,512]{1,0:T(8,128)(2,1)} %collective-permute-done.14, bf16[224,512]{1,0:T(8,128)(2,1)S(1)} %copy-done.30, bf16[224,512]{1,0:T(8,128)(2,1)S(1)} %copy-done.27, bf16[224,512]{1,0:T(8,128)(2,1)S(1)} %copy-done.11), kind=kLoop, calls=%fused_computation | loop fusion | flops 1032192 | bytes 1146880 | tf_op jit(solution)/shard_map/convert_element_type | solution.py:532
  122.0 2.1 %collective-permute-done.15 = bf16[224,512]{1,0:T(8,128)(2,1)S(1)} collective-permute-done((bf16[224,512]{1,0:T(8,128)(2,1)S(1)}, bf16[224,512]{1,0:T(8,128)(2,1)S(1)}, u32[]{:S(2)}, u32[]{:S(2)}) %collective-permute-start.15) | collective-permute-done | bytes 229408 | tf_op jit(solution)/shard_map/ppermute | solution.py:494
  124.1 2.7 %collective-permute-done.16 = bf16[224,512]{1,0:T(8,128)(2,1)S(1)} collective-permute-done((bf16[224,512]{1,0:T(8,128)(2,1)S(1)}, bf16[224,512]{1,0:T(8,128)(2,1)S(1)}, u32[]{:S(2)}, u32[]{:S(2)}) %collective-permute-start.16) | collective-permute-done | bytes 229408 | tf_op jit(solution)/shard_map/ppermute | solution.py:494
  126.8 2.6 %collective-permute-done.17 = bf16[224,512]{1,0:T(8,128)(2,1)S(1)} collective-permute-done((bf16[224,512]{1,0:T(8,128)(2,1)S(1)}, bf16[224,512]{1,0:T(8,128)(2,1)S(1)}, u32[]{:S(2)}, u32[]{:S(2)}) %collective-permute-start.17) | collective-permute-done | bytes 229408 | tf_op jit(solution)/shard_map/ppermute | solution.py:494
  129.3 0.8 multiply_convert_fusion.1
  130.2 0.1 reduce_sum.12
  130.2 0.7 fusion.1
  (58 shorter events, 0.1 us)
Async XLA Ops:
  0.6 32.0 %copy-start.14 = (s32[3,224]{1,0:T(4,128)S(1)}, s32[3,224]{1,0:T(4,128)}, u32[]{:S(2)}) copy-start(s32[3,224]{1,0:T(4,128)} %idx.7) | copy-start | bytes 8068
  27.6 19.7 %collective-permute-start.5 = (bf16[32,4096]{1,0:T(8,128)(2,1)S(1)}, bf16[32,4096]{1,0:T(8,128)(2,1)S(1)}, u32[]{:S(2)}, u32[]{:S(2)}) collective-permute-start(bf16[32,4096]{1,0:T(8,128)(2,1)S(1)} %reshape.18.t0), channel_id=1, source_target_pairs={{24,0},{25,1},{26,2},{27,3},{28,4},{29,5},{30,6},{31,7},{0,8},{1,9... | collective-permute-start | bytes 786440 | tf_op jit(solution)/shard_map/ppermute | solution.py:489
  29.2 18.2 %collective-permute-start.4 = (bf16[32,4096]{1,0:T(8,128)(2,1)S(1)}, bf16[32,4096]{1,0:T(8,128)(2,1)S(1)}, u32[]{:S(2)}, u32[]{:S(2)}) collective-permute-start(bf16[32,4096]{1,0:T(8,128)(2,1)S(1)} %reshape.18.t0), channel_id=1, source_target_pairs={{16,0},{17,1},{18,2},{19,3},{20,4},{21,5},{22,6},{23,7},{24,8},{25... | collective-permute-start | bytes 786440 | tf_op jit(solution)/shard_map/ppermute | solution.py:489
  30.2 17.3 %collective-permute-start.3 = (bf16[32,4096]{1,0:T(8,128)(2,1)S(1)}, bf16[32,4096]{1,0:T(8,128)(2,1)S(1)}, u32[]{:S(2)}, u32[]{:S(2)}) collective-permute-start(bf16[32,4096]{1,0:T(8,128)(2,1)S(1)} %reshape.18.t0), channel_id=1, source_target_pairs={{8,0},{9,1},{10,2},{11,3},{12,4},{13,5},{14,6},{15,7},{16,8},{17,9... | collective-permute-start | bytes 786440 | tf_op jit(solution)/shard_map/ppermute | solution.py:489
  39.8 7.6 %copy-start.2 = (bf16[2048,896]{1,0:T(8,128)(2,1)}, bf16[2048,896]{1,0:T(8,128)(2,1)S(1)}, u32[]{:S(2)}) copy-start(bf16[2048,896]{1,0:T(8,128)(2,1)S(1)} %get-tuple-element.37.pg) | copy-start | bytes 11010052
  39.8 7.6 %copy-start.3 = (bf16[2048,896]{1,0:T(8,128)(2,1)}, bf16[2048,896]{1,0:T(8,128)(2,1)S(1)}, u32[]{:S(2)}) copy-start(bf16[2048,896]{1,0:T(8,128)(2,1)S(1)} %get-tuple-element.39.pu) | copy-start | bytes 11010052
  39.8 14.4 %collective-permute-start.2 = (bf16[32,4096]{1,0:T(8,128)(2,1)S(1)}, bf16[32,4096]{1,0:T(8,128)(2,1)S(1)}, u32[]{:S(2)}, u32[]{:S(2)}) collective-permute-start(bf16[32,4096]{1,0:T(8,128)(2,1)S(1)} %reshape.17.c0), channel_id=1, source_target_pairs={{24,0},{25,1},{26,2},{27,3},{28,4},{29,5},{30,6},{31,7},{0,8},{1,9... | collective-permute-start | bytes 786440 | tf_op jit(solution)/shard_map/ppermute | solution.py:489
  39.9 14.3 %collective-permute-start.1 = (bf16[32,4096]{1,0:T(8,128)(2,1)S(1)}, bf16[32,4096]{1,0:T(8,128)(2,1)S(1)}, u32[]{:S(2)}, u32[]{:S(2)}) collective-permute-start(bf16[32,4096]{1,0:T(8,128)(2,1)S(1)} %reshape.17.c0), channel_id=1, source_target_pairs={{16,0},{17,1},{18,2},{19,3},{20,4},{21,5},{22,6},{23,7},{24,8},{25... | collective-permute-start | bytes 786440 | tf_op jit(solution)/shard_map/ppermute | solution.py:489
  47.3 6.9 %copy-start.1 = (bf16[256,8192]{1,0:T(8,128)(2,1)}, bf16[256,8192]{1,0:T(8,128)(2,1)S(1)}, u32[]{:S(2)}) copy-start(bf16[256,8192]{1,0:T(8,128)(2,1)S(1)} %outward_panel.1.pd.pd_far) | copy-start | bytes 12582916
  47.3 6.9 %collective-permute-start = (bf16[32,4096]{1,0:T(8,128)(2,1)S(1)}, bf16[32,4096]{1,0:T(8,128)(2,1)S(1)}, u32[]{:S(2)}, u32[]{:S(2)}) collective-permute-start(bf16[32,4096]{1,0:T(8,128)(2,1)S(1)} %reshape.17.c0), channel_id=1, source_target_pairs={{8,0},{9,1},{10,2},{11,3},{12,4},{13,5},{14,6},{15,7},{16,8},{17,9... | collective-permute-start | bytes 786440 | tf_op jit(solution)/shard_map/ppermute | solution.py:489
  54.3 7.2 %collective-permute-start.6 = (bf16[2304,128]{1,0:T(8,128)(2,1)S(1)}, bf16[2304,128]{1,0:T(8,128)(2,1)S(1)}, u32[]{:S(2)}, u32[]{:S(2)}) collective-permute-start(bf16[2304,128]{1,0:T(8,128)(2,1)S(1)} %get-tuple-element.45), channel_id=1, source_target_pairs={{32,0},{0,32},{96,64},{64,96},{160,128},{128,160},{224,192},{192,2... | collective-permute-start | bytes 1769480 | tf_op jit(solution)/shard_map/ppermute | solution.py:499
  59.7 8.1 %copy-start.6 = (bf16[128,4096]{1,0:T(8,128)(2,1)}, bf16[128,4096]{1,0:T(8,128)(2,1)S(1)}, u32[]{:S(2)}) copy-start(bf16[128,4096]{1,0:T(8,128)(2,1)S(1)} %get-tuple-element.51.cot_own) | copy-start | bytes 3145732
  59.7 1.7 %collective-permute-start.7 = (bf16[256,512]{1,0:T(8,128)(2,1)S(1)}, bf16[256,512]{1,0:T(8,128)(2,1)S(1)}, u32[]{:S(2)}, u32[]{:S(2)}) collective-permute-start(bf16[256,512]{1,0:T(8,128)(2,1)S(1)} %get-tuple-element.58.d_own), channel_id=1, source_target_pairs={{32,0},{0,32},{96,64},{64,96},{160,128},{128,160},{224,192},{192,2... | collective-permute-start | bytes 786440 | tf_op jit(solution)/shard_map/ppermute | solution.py:499
  61.4 6.3 %copy-start.4 = (bf16[256,512]{1,0:T(8,128)(2,1)}, bf16[256,512]{1,0:T(8,128)(2,1)S(1)}, u32[]{:S(2)}) copy-start(bf16[256,512]{1,0:T(8,128)(2,1)S(1)} %collective-permute-done.7.d_oth) | copy-start | bytes 786436
  65.0 0.7 copy-start.8
  65.7 0.7 copy-start.15
  66.4 0.7 copy-start.18
  67.1 0.7 copy-start.23
  73.8 1.3 %copy-start = (bf16[4,64,4096]{2,1,0:T(8,128)(2,1)}, bf16[4,64,4096]{2,1,0:T(8,128)(2,1)S(1)}, u32[]{:S(2)}) copy-start(bf16[4,64,4096]{2,1,0:T(8,128)(2,1)S(1)} %input_parts.1) | copy-start | bytes 6291460
  75.2 33.6 %all-to-all-start.1 = ((bf16[4,64,4096]{2,1,0:T(8,128)(2,1)}), bf16[4,64,4096]{2,1,0:T(8,128)(2,1)S(1)}, u32[]{:S(2)}, u32[]{:S(2)}) async-start(bf16[4,64,4096]{2,1,0:T(8,128)(2,1)} %copy-done), calls=%async_computation.1 | async-start | bytes 4194304 | tf_op jit(solution)/shard_map/all_to_all | solution.py:515
  80.5 18.0 %copy-start.5 = (bf16[256,512]{1,0:T(8,128)(2,1)S(1)}, bf16[256,512]{1,0:T(8,128)(2,1)}, u32[]{:S(2)}) copy-start(bf16[256,512]{1,0:T(8,128)(2,1)} %copy-done.4) | copy-start | bytes 786436
  80.5 4.7 %collective-permute-start.8 = (bf16[128,4096]{1,0:T(8,128)(2,1)}, bf16[128,4096]{1,0:T(8,128)(2,1)S(1)}, u32[]{:S(2)}, u32[]{:S(2)}) collective-permute-start(bf16[128,4096]{1,0:T(8,128)(2,1)} %copy-done.6), channel_id=1, source_target_pairs={{32,0},{0,32},{96,64},{64,96},{160,128},{128,160},{224,192},{192,2... | collective-permute-start | bytes 3145736 | tf_op jit(solution)/shard_map/ppermute | solution.py:499
  80.5 15.4 %collective-permute-start.9 = (bf16[224,512]{1,0:T(8,128)(2,1)}, bf16[224,512]{1,0:T(8,128)(2,1)S(1)}, u32[]{:S(2)}, u32[]{:S(2)}) collective-permute-start(bf16[224,512]{1,0:T(8,128)(2,1)} %copy-done.23), channel_id=1, source_target_pairs={{64,0},{96,32},{0,64},{32,96},{192,128},{224,160},{128,192},{160,2... | collective-permute-start | bytes 688136 | tf_op jit(solution)/shard_map/ppermute | solution.py:494
  82.0 14.4 %collective-permute-start.10 = (bf16[224,512]{1,0:T(8,128)(2,1)}, bf16[224,512]{1,0:T(8,128)(2,1)S(1)}, u32[]{:S(2)}, u32[]{:S(2)}) collective-permute-start(bf16[224,512]{1,0:T(8,128)(2,1)} %copy-done.18), channel_id=1, source_target_pairs={{128,0},{160,32},{192,64},{224,96},{0,128},{32,160},{64,192},{96,2... | collective-permute-start | bytes 688136 | tf_op jit(solution)/shard_map/ppermute | solution.py:494
  84.7 13.8 %collective-permute-start.11 = (bf16[224,512]{1,0:T(8,128)(2,1)}, bf16[224,512]{1,0:T(8,128)(2,1)S(1)}, u32[]{:S(2)}, u32[]{:S(2)}) collective-permute-start(bf16[224,512]{1,0:T(8,128)(2,1)} %copy-done.15), channel_id=1, source_target_pairs={{192,0},{224,32},{128,64},{160,96},{64,128},{96,160},{0,192},{32,2... | collective-permute-start | bytes 688136 | tf_op jit(solution)/shard_map/ppermute | solution.py:494
  85.2 1.2 copy-start.7
  91.6 14.5 %copy-start.10 = (bf16[224,512]{1,0:T(8,128)(2,1)}, bf16[224,512]{1,0:T(8,128)(2,1)S(1)}, u32[]{:S(2)}) copy-start(bf16[224,512]{1,0:T(8,128)(2,1)S(1)} %get-tuple-element.54) | copy-start | bytes 688132
  91.6 13.3 %collective-permute-start.12 = (bf16[224,512]{1,0:T(8,128)(2,1)S(1)}, bf16[224,512]{1,0:T(8,128)(2,1)S(1)}, u32[]{:S(2)}, u32[]{:S(2)}) collective-permute-start(bf16[224,512]{1,0:T(8,128)(2,1)S(1)} %get-tuple-element.60), channel_id=1, source_target_pairs={{64,0},{96,32},{0,64},{32,96},{192,128},{224,160},{128,192},{160,2... | collective-permute-start | bytes 688136 | tf_op jit(solution)/shard_map/ppermute | solution.py:494
  91.9 14.1 %collective-permute-start.13 = (bf16[224,512]{1,0:T(8,128)(2,1)S(1)}, bf16[224,512]{1,0:T(8,128)(2,1)S(1)}, u32[]{:S(2)}, u32[]{:S(2)}) collective-permute-start(bf16[224,512]{1,0:T(8,128)(2,1)S(1)} %get-tuple-element.61), channel_id=1, source_target_pairs={{128,0},{160,32},{192,64},{224,96},{0,128},{32,160},{64,192},{96,2... | collective-permute-start | bytes 688136 | tf_op jit(solution)/shard_map/ppermute | solution.py:494
  95.9 10.2 %copy-start.24 = (bf16[224,512]{1,0:T(8,128)(2,1)}, bf16[224,512]{1,0:T(8,128)(2,1)S(1)}, u32[]{:S(2)}) copy-start(bf16[224,512]{1,0:T(8,128)(2,1)S(1)} %collective-permute-done.9) | copy-start | bytes 688132
  95.9 12.8 %collective-permute-start.14 = (bf16[224,512]{1,0:T(8,128)(2,1)S(1)}, bf16[224,512]{1,0:T(8,128)(2,1)}, u32[]{:S(2)}, u32[]{:S(2)}) collective-permute-start(bf16[224,512]{1,0:T(8,128)(2,1)S(1)} %get-tuple-element.62), channel_id=1, source_target_pairs={{192,0},{224,32},{128,64},{160,96},{64,128},{96,160},{0,192},{32,2... | collective-permute-start | bytes 688136 | tf_op jit(solution)/shard_map/ppermute | solution.py:494
  96.4 9.7 %copy-start.25 = (bf16[224,512]{1,0:T(8,128)(2,1)}, bf16[224,512]{1,0:T(8,128)(2,1)S(1)}, u32[]{:S(2)}) copy-start(bf16[224,512]{1,0:T(8,128)(2,1)S(1)} %collective-permute-done.10) | copy-start | bytes 688132
  98.5 7.6 %copy-start.28 = (bf16[224,512]{1,0:T(8,128)(2,1)}, bf16[224,512]{1,0:T(8,128)(2,1)S(1)}, u32[]{:S(2)}) copy-start(bf16[224,512]{1,0:T(8,128)(2,1)S(1)} %collective-permute-done.11) | copy-start | bytes 688132
  102.1 0.7 copy-start.12
  102.8 0.7 copy-start.16
  103.4 0.7 copy-start.19
  104.2 0.7 copy-start.21
  104.8 8.7 %copy-start.9 = (bf16[224,512]{1,0:T(8,128)(2,1)S(1)}, bf16[224,512]{1,0:T(8,128)(2,1)}, u32[]{:S(2)}) copy-start(bf16[224,512]{1,0:T(8,128)(2,1)} %copy-done.8) | copy-start | bytes 688132
  104.9 1.2 copy-start.26
  106.1 0.7 copy-start.29
  108.7 8.8 %copy-start.17 = (bf16[224,512]{1,0:T(8,128)(2,1)S(1)}, bf16[224,512]{1,0:T(8,128)(2,1)}, u32[]{:S(2)}) copy-start(bf16[224,512]{1,0:T(8,128)(2,1)} %copy-done.16) | copy-start | bytes 688132
  108.7 11.5 %copy-start.11 = (bf16[224,512]{1,0:T(8,128)(2,1)S(1)}, bf16[224,512]{1,0:T(8,128)(2,1)}, u32[]{:S(2)}) copy-start(bf16[224,512]{1,0:T(8,128)(2,1)} %copy-done.10) | copy-start | bytes 688132
  109.9 5.7 %copy-start.22 = (bf16[224,512]{1,0:T(8,128)(2,1)S(1)}, bf16[224,512]{1,0:T(8,128)(2,1)}, u32[]{:S(2)}) copy-start(bf16[224,512]{1,0:T(8,128)(2,1)} %copy-done.21) | copy-start | bytes 688132
  109.9 5.7 %copy-start.20 = (bf16[224,512]{1,0:T(8,128)(2,1)S(1)}, bf16[224,512]{1,0:T(8,128)(2,1)}, u32[]{:S(2)}) copy-start(bf16[224,512]{1,0:T(8,128)(2,1)} %copy-done.19) | copy-start | bytes 688132
  109.9 10.4 %copy-start.27 = (bf16[224,512]{1,0:T(8,128)(2,1)S(1)}, bf16[224,512]{1,0:T(8,128)(2,1)}, u32[]{:S(2)}) copy-start(bf16[224,512]{1,0:T(8,128)(2,1)} %copy-done.26) | copy-start | bytes 688132
  109.9 10.4 %copy-start.30 = (bf16[224,512]{1,0:T(8,128)(2,1)S(1)}, bf16[224,512]{1,0:T(8,128)(2,1)}, u32[]{:S(2)}) copy-start(bf16[224,512]{1,0:T(8,128)(2,1)} %copy-done.29) | copy-start | bytes 688132
  109.9 19.5 %copy-start.13 = (bf16[224,512]{1,0:T(8,128)(2,1)S(1)}, bf16[224,512]{1,0:T(8,128)(2,1)}, u32[]{:S(2)}) copy-start(bf16[224,512]{1,0:T(8,128)(2,1)} %copy-done.12) | copy-start | bytes 688132
  109.9 20.3 %all-to-all-start.2 = ((bf16[8,8,4096]{2,1,0:T(8,128)(2,1)}), bf16[8,8,4096]{2,1,0:T(8,128)(2,1)S(1)}, u32[]{:S(2)}, u32[]{:S(2)}) async-start(bf16[8,8,4096]{2,1,0:T(8,128)(2,1)} %merge_y.1), calls=%async_computation.2 | async-start | bytes 1048576 | tf_op jit(solution)/shard_map/all_to_all | solution.py:511
  115.5 8.5 %collective-permute-start.15 = (bf16[224,512]{1,0:T(8,128)(2,1)S(1)}, bf16[224,512]{1,0:T(8,128)(2,1)S(1)}, u32[]{:S(2)}, u32[]{:S(2)}) collective-permute-start(bf16[224,512]{1,0:T(8,128)(2,1)S(1)} %copy-done.22), channel_id=1, source_target_pairs={{64,0},{96,32},{0,64},{32,96},{192,128},{224,160},{128,192},{160,2... | collective-permute-start | bytes 688136 | tf_op jit(solution)/shard_map/ppermute | solution.py:494
  115.6 11.2 %collective-permute-start.16 = (bf16[224,512]{1,0:T(8,128)(2,1)S(1)}, bf16[224,512]{1,0:T(8,128)(2,1)S(1)}, u32[]{:S(2)}, u32[]{:S(2)}) collective-permute-start(bf16[224,512]{1,0:T(8,128)(2,1)S(1)} %copy-done.20), channel_id=1, source_target_pairs={{128,0},{160,32},{192,64},{224,96},{0,128},{32,160},{64,192},{96,2... | collective-permute-start | bytes 688136 | tf_op jit(solution)/shard_map/ppermute | solution.py:494
  117.5 11.8 %collective-permute-start.17 = (bf16[224,512]{1,0:T(8,128)(2,1)S(1)}, bf16[224,512]{1,0:T(8,128)(2,1)S(1)}, u32[]{:S(2)}, u32[]{:S(2)}) collective-permute-start(bf16[224,512]{1,0:T(8,128)(2,1)S(1)} %copy-done.17), channel_id=1, source_target_pairs={{192,0},{224,32},{128,64},{160,96},{64,128},{96,160},{0,192},{32,2... | collective-permute-start | bytes 688136 | tf_op jit(solution)/shard_map/ppermute | solution.py:494

commit v5 on v4

--- a/solution.py
+++ b/solution.py
@@ -1,5 +1,3 @@
-import functools
-
 import jax
 import jax.numpy as jnp
 from jax import lax
@@ -300,7 +298,7 @@
         down_kernel,
         in_specs=smem(1) + vm(4),
         out_specs=vm(4),
-        out_shape=[shape(SLOT, 512)] * 4,
+        out_shape=[pltpu.HBM((SLOT, 512), BF)] * 4,
         scratch_shapes=[pltpu.VMEM((256, D), BF), pltpu.VMEM((256, D), BF), pltpu.VMEM((256, 256), BF)],
         compiler_params=params(14),
         cost_estimate=cost(0.2),
@@ -375,7 +373,7 @@
         delta_kernel,
         in_specs=vm(4) + [pl.BlockSpec(memory_space=pl.ANY)] + vm(2),
         out_specs=vm(4),
-        out_shape=[shape(256, 512), shape(TOK, D)] + [pltpu.VMEM((256, WIDE), BF)] * 2,
+        out_shape=[shape(256, 512), pltpu.HBM((TOK, D), BF)] + [pltpu.VMEM((256, WIDE), BF)] * 2,
         scratch_shapes=[
             pltpu.VMEM((256, 2 * D), BF),
             pltpu.VMEM((256, 2 * D), BF),
@@ -413,7 +411,7 @@
         grid=(FEAT // 512,),
         in_specs=[whole, whole, panel, panel, pl.BlockSpec((NY, 32, 1024), lambda n: (0, 0, n))],
         out_specs=pl.BlockSpec((NY, 64, 1024), lambda n: (0, 0, n)),
-        out_shape=shape(NY, 64, D),
+        out_shape=pltpu.HBM((NY, 64, D), BF),
         scratch_shapes=[pltpu.VMEM((256, 256), BF)],
         compiler_params=params(14),
         cost_estimate=cost(0.2),
@@ -443,44 +441,45 @@
     )(got)
 
 
-def inward_kernel(m, idx, xt_own, sib_oth, d_own, d_oth, w0, w1, w2, w3, part, tiles):
+def inward_kernel(idx, xt_own, sib_oth, d_own, d_oth, w0, w1, w2, w3, part, tiles):
     wswap = wire_swap(place()[1])
     low = low_half((16, 128))
-    delta = jnp.concatenate([d[m * TOK:m * TOK + TOK, :] for d in (d_own, d_oth)], axis=0)
-
-    def product(n, carry):
-        rows = pl.ds(pl.multiple_of(n * 256, 256), 256)
-        tokens = jnp.concatenate([xt_own[rows, :], sib_oth[rows, :]], axis=1)
-        part[rows, :] = mm(tokens, delta).astype(BF)
-        return carry
-
-    lax.fori_loop(0, 8, product, 0)
-    for j in range(COLS):
-        odd = j % 2
-        lanes = slice((j // 2) * 128, (j // 2) * 128 + 128)
-        for q in range(KEEP):
-            i = idx[m, j * KEEP + q]
-            first = part[pl.ds(pl.multiple_of(i * 16, 16), 16), lanes].astype(F32)
-            second = part[pl.ds(pl.multiple_of(1024 + i * 16, 16), 16), lanes].astype(F32)
-            if odd:
-                first = pltpu.roll(first, 64, 1)
-            else:
-                second = pltpu.roll(second, 64, 1)
-            tile = jnp.where(low, first, second).astype(BF)
-            tiles[(q % 16) * 16:(q % 16) * 16 + 16, (q // 16) * 128:(q // 16) * 128 + 128] = tile
-        emit(wswap, tiles, (w0, w1, w2, w3), j * KEEP)
-
-
-def inward_grads(m, idx, xt_own, sib_oth, d_own, d_oth):
-    return pl.pallas_call(
-        functools.partial(inward_kernel, m),
+    for m in range(2):
+        delta = jnp.concatenate([d[m * TOK:m * TOK + TOK, :] for d in (d_own, d_oth)], axis=0)
+
+        def product(n, carry):
+            rows = pl.ds(pl.multiple_of(n * 256, 256), 256)
+            tokens = jnp.concatenate([xt_own[rows, :], sib_oth[rows, :]], axis=1)
+            part[rows, :] = mm(tokens, delta).astype(BF)
+            return carry
+
+        lax.fori_loop(0, 8, product, 0)
+        for j in range(COLS):
+            odd = j % 2
+            lanes = slice((j // 2) * 128, (j // 2) * 128 + 128)
+            for q in range(KEEP):
+                i = idx[m, j * KEEP + q]
+                first = part[pl.ds(pl.multiple_of(i * 16, 16), 16), lanes].astype(F32)
+                second = part[pl.ds(pl.multiple_of(1024 + i * 16, 16), 16), lanes].astype(F32)
+                if odd:
+                    first = pltpu.roll(first, 64, 1)
+                else:
+                    second = pltpu.roll(second, 64, 1)
+                tile = jnp.where(low, first, second).astype(BF)
+                tiles[(q % 16) * 16:(q % 16) * 16 + 16, (q // 16) * 128:(q // 16) * 128 + 128] = tile
+            emit(wswap, tiles, (w0, w1, w2, w3), m * SLOT + j * KEEP)
+
+
+def inward_grads(idx, xt_own, sib_oth, d_own, d_oth):
+    return pl.pallas_call(
+        inward_kernel,
         in_specs=smem(1) + vm(4),
         out_specs=vm(4),
-        out_shape=[shape(SLOT, 512)] * 4,
+        out_shape=[pltpu.HBM((2 * SLOT, 512), BF)] * 4,
         scratch_shapes=[pltpu.VMEM((FEAT, 512), BF), pltpu.VMEM((256, 256), BF)],
         compiler_params=params(14),
         cost_estimate=cost(0.2),
-        name=("gate_grads", "up_grads")[m],
+        name="inward_grads",
     )(idx, xt_own, sib_oth, d_own, d_oth)
 
 
@@ -527,9 +526,27 @@
     return [parts[0]] + [from_x(parts[d], d) for d in range(1, NX)]
 
 
-def mean_of(parts):
+def mean_of(*parts):
     total = sum((p.astype(F32) for p in parts[1:]), parts[0].astype(F32))
     return (total * (1.0 / (NX * NC))).astype(BF)
+
+
+def inward_mean_kernel(a, b, c, d, gate, up):
+    for n, dst in enumerate((gate, up)):
+        rows = slice(n * SLOT, n * SLOT + SLOT)
+        dst[...] = mean_of(*(p[rows, :] for p in (a, b, c, d)))
+
+
+def inward_mean(*parts):
+    return pl.pallas_call(
+        inward_mean_kernel,
+        in_specs=vm(4),
+        out_specs=vm(2),
+        out_shape=[shape(SLOT, 512)] * 2,
+        compiler_params=params(10),
+        cost_estimate=cost(20),
+        name="inward_mean",
+    )(*parts)
 
 
 def body(tokens, cotangent, gate_blocks, up_blocks, down_blocks, block_index):
@@ -548,17 +565,16 @@
     sib_oth = from_core(after(sib, *cot))
     own, cot_own, gdx, udx = deltas(cot, pd, gl2, ul2)
     oth, cot_oth = from_core(own), from_core(cot_own)
-    gate_wire = inward_grads(0, block_index, xt_own, sib_oth, own, oth)
-    gate_got = exchange_x(gate_wire)
-    parts = input_parts(after(gdx, gate_wire[0]), udx, pg, pu, out_parts)
-    parts_got = over_y(parts)
+    parts = input_parts(gdx, udx, pg, pu, out_parts)
+    parts_got = over_y(after(parts, cot_oth, sib_oth))
     down_wire = down_grads(block_index, cot_own, cot_oth, after(ht_own, parts), sib_oth)
     down_got = exchange_x(down_wire)
-    up_wire = inward_grads(1, block_index, xt_own, sib_oth, after(own, down_wire[0], *gate_got[1:]), oth)
-    up_got = exchange_x(up_wire)
-    both = merge_y(after(parts_got, up_wire[0], *down_got[1:]))
-    gate_grad, up_grad, down_grad = (mean_of(g) for g in (gate_got, up_got, down_got))
-    total = over_z(both).astype(F32).sum(axis=0).astype(BF)
+    wire = inward_grads(block_index, xt_own, sib_oth, after(own, down_wire[0]), oth)
+    got = exchange_x(wire)
+    down_grad = mean_of(*down_got)
+    both = merge_y(after(parts_got, wire[0], down_grad))
+    gate_grad, up_grad = inward_mean(*got)
+    total = after(over_z(both), gate_grad).astype(F32).sum(axis=0).astype(BF)
     return (total[:rows], total[rows:], gate_grad, up_grad, down_grad)
 
 

time: 132 us -> 126 us (0.955)
  starting transfers between devices: 32.6 us -> 27.1 us
  Pallas kernels: 42.4 us -> 46.7 us
  local copies, waits for them, and re-layouts: 9.89 us -> 6.63 us
  other arithmetic: 5.49 us -> 2.67 us
  waiting for transfers between devices: 13.8 us -> 16 us
    ppermute x9 -> x6, starting transfers between devices: 14.2 us -> 9.4 us  [from_x(): return lax.ppermute(value, 'dp', pairs)]
    ppermute x9 -> x6, waiting for transfers between devices: 12.6 us -> 16 us  [from_x(): return lax.ppermute(value, 'dp', pairs)]
    unnamed x62 -> x20, local copies, waits for them, and re-layouts: 8.85 us -> 5.58 us
    convert_element_type x3 -> x1, other arithmetic: 4.6 us -> 1.78 us  [mean_of(): return (total * (1.0 / (NX * NC))).astype(BF)]
    pallas_call x2, Pallas kernels: 7.08 us -> 9.54 us  [the longest x1 7.54 us: inward_grads(): pl.pallas_call(inward_kernel, in_specs=smem(1) + vm(4), out_specs=vm(4),...]
  transfers between devices with their start and end apart: 20 -> 17, of which waited for: 7 -> 4; matrix products, arithmetic and copies ran while one was open for 4% -> 1% of each run, Pallas kernels for 24% -> 33%
where the time goes in v5:
time: 126 us
  Pallas kernels  46.7 us (37%)
  starting transfers between devices  27.1 us (22%)
  blocking collectives  25.8 us (20%)
  waiting for transfers between devices  16 us (13%)
  local copies, waits for them, and re-layouts  6.63 us (5%)
  other arithmetic  2.67 us (2%)
    all_to_all x1, blocking collectives, over_z(): lax.all_to_all(value, 'fsdp', 0, 0, axis_index_groups=z_groups(), tiled=T...  25.8 us
    ppermute x6, waiting for transfers between devices, from_x(): return lax.ppermute(value, 'dp', pairs)  16 us
    ppermute x6, starting transfers between devices, from_x(): return lax.ppermute(value, 'dp', pairs)  9.4 us
    ppermute x6, starting transfers between devices, from_y(): return lax.ppermute(value, 'fsdp', pairs)  8.76 us
    pallas_call x1, Pallas kernels, inward_grads(): pl.pallas_call(inward_kernel, in_specs=smem(1) + vm(4), out_specs=vm(4),...  7.54 us
    pallas_call x1, Pallas kernels, inward_panels(): pl.pallas_call(inward_panels_kernel, in_specs=smem(1) + far(2), out_specs...  7.13 us
    pallas_call x1, Pallas kernels, input_parts(): pl.pallas_call(back_kernel, grid=(FEAT // 512,), in_specs=[whole, whole,...  6.99 us
    pallas_call x1, Pallas kernels, forward(): pl.pallas_call(forward_kernel, in_specs=vm(7), out_specs=vm(6), out_shape...  6.74 us
  transfers between devices with their start and end apart: 17, of which 4 were waited for; matrix products, arithmetic and copies ran while one was open for 1% of the time, Pallas kernels for 33%

profile of v5, /device:TPU:8, one launch (start us, length us, event | category | flops | bytes accessed | tf_op | source)
XLA Modules:
  0.0 125.7 jit_solution(4069530934498359103)
XLA Ops:
  0.6 0.0 copy-start.6
  0.6 0.8 pad_maximum_fusion
  1.5 25.8 %all_to_all.15 = bf16[8,8,4096]{2,1,0:T(8,128)(2,1)S(1)} all-to-all(bf16[8,8,4096]{2,1,0:T(8,128)(2,1)S(1)} %broadcast_in_dim.2), channel_id=1, replica_groups={{0,1,2,3,4,5,6,7},{8,9,10,11,12,13,14,15},{16,17,18,19,20,21,22,23},{24..., dimensions={0} | all-to-all | bytes 1048576 | tf_op jit(solution)/shard_map/all_to_all | solution.py:510
  27.3 0.2 fusion
  27.5 0.1 reshape.18.t0
  27.6 1.7 %collective-permute-start.5 = (bf16[32,4096]{1,0:T(8,128)(2,1)S(1)}, bf16[32,4096]{1,0:T(8,128)(2,1)S(1)}, u32[]{:S(2)}, u32[]{:S(2)}) collective-permute-start(bf16[32,4096]{1,0:T(8,128)(2,1)S(1)} %reshape.18.t0), channel_id=1, source_target_pairs={{24,0},{25,1},{26,2},{27,3},{28,4},{29,5},{30,6},{31,7},{0,8},{1,9... | collective-permute-start | bytes 786440 | tf_op jit(solution)/shard_map/ppermute | solution.py:488
  29.2 0.9 collective-permute-start.4
  30.2 2.4 %collective-permute-start.3 = (bf16[32,4096]{1,0:T(8,128)(2,1)S(1)}, bf16[32,4096]{1,0:T(8,128)(2,1)S(1)}, u32[]{:S(2)}, u32[]{:S(2)}) collective-permute-start(bf16[32,4096]{1,0:T(8,128)(2,1)S(1)} %reshape.18.t0), channel_id=1, source_target_pairs={{8,0},{9,1},{10,2},{11,3},{12,4},{13,5},{14,6},{15,7},{16,8},{17,9... | collective-permute-start | bytes 786440 | tf_op jit(solution)/shard_map/ppermute | solution.py:488
  32.6 0.1 reshape.17.c0
  32.6 0.0 copy-done.6
  32.7 7.1 %inward_panels.1 = (bf16[2048,896]{1,0:T(8,128)(2,1)S(1)}, bf16[2048,896]{1,0:T(8,128)(2,1)S(1)}) custom-call(s32[3,224]{1,0:T(4,128)S(1)} %copy-done.6, bf16[224,4096]{1,0:T(8,128)(2,1)} %gate.1, bf16[224,4096]{1,0:T(8,128)(2,1)} %up.1), custom_call_target="tpu_custom_call" | custom-call | flops 6000000000 | bytes 1000 | tf_op jit(solution)/shard_map/inward_panels/pallas_call | solution.py:153
  39.8 0.0 copy-start.1
  39.8 0.0 copy-start.2
  39.8 0.1 collective-permute-start.2
  39.9 3.4 %collective-permute-start.1 = (bf16[32,4096]{1,0:T(8,128)(2,1)S(1)}, bf16[32,4096]{1,0:T(8,128)(2,1)S(1)}, u32[]{:S(2)}, u32[]{:S(2)}) collective-permute-start(bf16[32,4096]{1,0:T(8,128)(2,1)S(1)} %reshape.17.c0), channel_id=1, source_target_pairs={{16,0},{17,1},{18,2},{19,3},{20,4},{21,5},{22,6},{23,7},{24,8},{25... | collective-permute-start | bytes 786440 | tf_op jit(solution)/shard_map/ppermute | solution.py:488
  43.3 4.0 %outward_panel.1.pd.pd_far = bf16[256,8192]{1,0:T(8,128)(2,1)S(1)} custom-call(s32[3,224]{1,0:T(4,128)S(1)} %copy-done.6, bf16[224,4096]{1,0:T(8,128)(2,1)} %down.1), custom_call_target="tpu_custom_call" | custom-call | flops 3000000000 | bytes 1000 | tf_op jit(solution)/shard_map/outward_panel/pallas_call | solution.py:170
  47.3 0.0 copy-start
  47.3 0.0 collective-permute-done.5.t3
  47.3 0.3 collective-permute-start
  47.6 0.0 collective-permute-done.4.t2
  47.6 0.0 collective-permute-done.3.t1
  47.6 0.0 copy-start.8
  47.6 1.0 copy-done.8
  48.6 0.0 copy-done.1
  48.6 0.0 copy-done.2
  48.6 1.1 copy-done.9
  49.8 6.7 %forward.1 = (bf16[2048,128]{1,0:T(8,128)(2,1)S(1)}, bf16[256,128]{1,0:T(8,128)(2,1)S(1)}, bf16[2304,128]{1,0:T(8,128)(2,1)S(1)}, f32[128,896]{1,0:T(8,128)S(1)}...) custom-call(bf16[32,4096]{1,0:T(8,128)(2,1)S(1)} %reshape.18.t0, bf16[32,4096]{1,0:T(8,128)(2,1)S(1)} %copy-done.9, ...), custom_call_target="tpu_custom_call" | custom-call | flops 8000000000 | bytes 1000 | tf_op jit(solution)/shard_map/forward/pallas_call | solution.py:241
  56.5 0.0 collective-permute-done.2.c3
  56.5 0.0 collective-permute-done.1.c2
  56.5 0.0 collective-permute-done.c1
  56.5 5.2 %deltas.1 = (bf16[256,512]{1,0:T(8,128)(2,1)S(1)}, bf16[128,4096]{1,0:T(8,128)(2,1)}, bf16[256,896]{1,0:T(8,128)(2,1)S(1)}, bf16[256,896]{1,0:T(8,128)(2,1)S(1)}) custom-call(bf16[32,4096]{1,0:T(8,128)(2,1)S(1)} %reshape.17.c0, bf16[32,4096]{1,0:T(8,128)(2,1)S(1)} %collective-permute-done.c1, bf16[32,4096]{1,0:T(8,128)(2,1)S(1)} %collective-permute-done.1.c2, ...), custom_call_target="tpu_custom_call" | custom-call | flops 200000000 | bytes 1000 | tf_op jit(solution)/shard_map/deltas/pallas_call | solution.py:372
  61.7 0.1 collective-permute-start.6
  61.8 0.5 collective-permute-start.7
  62.3 7.0 %input_parts.1 = bf16[4,64,4096]{2,1,0:T(8,128)(2,1)} custom-call(bf16[256,896]{1,0:T(8,128)(2,1)S(1)} %get-tuple-element.41.gdx, bf16[256,896]{1,0:T(8,128)(2,1)S(1)} %get-tuple-element.42.udx, bf16[2048,896]{1,0:T(8,128)(2,1)} %copy-done.1, bf16[2048,896]{1,0:T(8,128)(2,1)} %copy-done.2, bf16[4,32,4096]{2,1,0:T(8,128)(2,1)S(1)} %get-tuple-element.43.out_parts), custom_call_target="tpu_custom_call" | custom-call | flops 200000000 | bytes 1000 | tf_op jit(solution)/shard_map/input_parts/pallas_call | solution.py:409
  69.3 0.0 collective-permute-done.7.sib_oth
  69.3 0.0 collective-permute-done.6.cot_oth
  69.3 1.0 copy-done.4
  70.3 4.9 %all-to-all-start.1 = ((bf16[4,64,4096]{2,1,0:T(8,128)(2,1)}), bf16[4,64,4096]{2,1,0:T(8,128)(2,1)S(1)}, u32[]{:S(2)}, u32[]{:S(2)}) async-start(bf16[4,64,4096]{2,1,0:T(8,128)(2,1)} %input_parts.1), calls=%async_computation.1 | async-start | bytes 4194304 | tf_op jit(solution)/shard_map/all_to_all | solution.py:514
  75.2 0.0 collective-permute-start.8
  75.2 1.2 copy-done.3
  76.4 1.2 copy-done.5
  77.6 6.0 %down_grads.1 = (bf16[224,512]{1,0:T(8,128)(2,1)}, bf16[224,512]{1,0:T(8,128)(2,1)}, bf16[224,512]{1,0:T(8,128)(2,1)}, bf16[224,512]{1,0:T(8,128)(2,1)}) custom-call(s32[3,224]{1,0:T(4,128)S(1)} %copy-done.6, bf16[128,4096]{1,0:T(8,128)(2,1)S(1)} %copy-done.3, bf16[128,4096]{1,0:T(8,128)(2,1)S(1)} %copy-done.5, ...), custom_call_target="tpu_custom_call" | custom-call | flops 200000000 | bytes 1000 | tf_op jit(solution)/shard_map/down_grads/pallas_call | solution.py:297
  83.6 1.5 %collective-permute-start.9 = (bf16[224,512]{1,0:T(8,128)(2,1)}, bf16[224,512]{1,0:T(8,128)(2,1)S(1)}, u32[]{:S(2)}, u32[]{:S(2)}) collective-permute-start(bf16[224,512]{1,0:T(8,128)(2,1)} %get-tuple-element.55), channel_id=1, source_target_pairs={{64,0},{96,32},{0,64},{32,96},{192,128},{224,160},{128,192},{160,2... | collective-permute-start | bytes 688136 | tf_op jit(solution)/shard_map/ppermute | solution.py:493
  85.1 2.7 %collective-permute-start.10 = (bf16[224,512]{1,0:T(8,128)(2,1)}, bf16[224,512]{1,0:T(8,128)(2,1)S(1)}, u32[]{:S(2)}, u32[]{:S(2)}) collective-permute-start(bf16[224,512]{1,0:T(8,128)(2,1)} %get-tuple-element.56), channel_id=1, source_target_pairs={{128,0},{160,32},{192,64},{224,96},{0,128},{32,160},{64,192},{96,2... | collective-permute-start | bytes 688136 | tf_op jit(solution)/shard_map/ppermute | solution.py:493
  87.9 0.5 collective-permute-start.11
  88.3 0.0 collective-permute-done.8.d_oth
  88.3 7.5 %inward_grads.1 = (bf16[448,512]{1,0:T(8,128)(2,1)}, bf16[448,512]{1,0:T(8,128)(2,1)}, bf16[448,512]{1,0:T(8,128)(2,1)}, bf16[448,512]{1,0:T(8,128)(2,1)}) custom-call(s32[3,224]{1,0:T(4,128)S(1)} %copy-done.6, bf16[2048,128]{1,0:T(8,128)(2,1)S(1)} %get-tuple-element.48.xt_own, bf16[2304,128]{1,0:T(8,128)(2,1)S(1)} %collective-permute-done.7.sib_oth, ...), custom_call_target="tpu_custom_call" | custom-call | flops 200000000 | bytes 1000 | tf_op jit(solution)/shard_map/inward_grads/pallas_call | solution.py:474
  95.9 0.3 collective-permute-start.12
  96.2 3.9 %collective-permute-start.13 = (bf16[448,512]{1,0:T(8,128)(2,1)}, bf16[448,512]{1,0:T(8,128)(2,1)S(1)}, u32[]{:S(2)}, u32[]{:S(2)}) collective-permute-start(bf16[448,512]{1,0:T(8,128)(2,1)} %get-tuple-element.60), channel_id=1, source_target_pairs={{128,0},{160,32},{192,64},{224,96},{0,128},{32,160},{64,192},{96,2... | collective-permute-start | bytes 1376264 | tf_op jit(solution)/shard_map/ppermute | solution.py:493
  100.1 0.0 collective-permute-done.9
  100.1 0.5 collective-permute-start.14
  100.6 0.0 collective-permute-done.10
  100.6 1.1 collective-permute-done.11
  101.6 1.8 %multiply_convert_fusion = bf16[224,512]{1,0:T(8,128)(2,1)} fusion(bf16[224,512]{1,0:T(8,128)(2,1)S(1)} %collective-permute-done.11, bf16[224,512]{1,0:T(8,128)(2,1)S(1)} %collective-permute-done.10, bf16[224,512]{1,0:T(8,128)(2,1)S(1)} %collective-permute-done.9, bf16[224,512]{1,0:T(8,128)(2,1)} %get-tuple-element.52), kind=kLoop, calls=%fused_computation | loop fusion | flops 1032192 | bytes 1146880 | tf_op jit(solution)/shard_map/convert_element_type | solution.py:531
  103.4 0.0 all-to-all-done.1.got
  103.4 1.1 merge_y.1
  104.5 3.5 %all-to-all-start.2 = ((bf16[8,8,4096]{2,1,0:T(8,128)(2,1)}), bf16[8,8,4096]{2,1,0:T(8,128)(2,1)S(1)}, u32[]{:S(2)}, u32[]{:S(2)}) async-start(bf16[8,8,4096]{2,1,0:T(8,128)(2,1)} %merge_y.1), calls=%async_computation.2 | async-start | bytes 1048576 | tf_op jit(solution)/shard_map/all_to_all | solution.py:510
  108.0 1.5 %collective-permute-done.12.b = bf16[448,512]{1,0:T(8,128)(2,1)S(1)} collective-permute-done((bf16[448,512]{1,0:T(8,128)(2,1)}, bf16[448,512]{1,0:T(8,128)(2,1)S(1)}, u32[]{:S(2)}, u32[]{:S(2)}) %collective-permute-start.12) | collective-permute-done | bytes 458784 | tf_op jit(solution)/shard_map/ppermute | solution.py:493
  109.5 10.8 %collective-permute-done.13.c = bf16[448,512]{1,0:T(8,128)(2,1)S(1)} collective-permute-done((bf16[448,512]{1,0:T(8,128)(2,1)}, bf16[448,512]{1,0:T(8,128)(2,1)S(1)}, u32[]{:S(2)}, u32[]{:S(2)}) %collective-permute-start.13) | collective-permute-done | bytes 458784 | tf_op jit(solution)/shard_map/ppermute | solution.py:493
  120.3 2.7 %collective-permute-done.14.d = bf16[448,512]{1,0:T(8,128)(2,1)} collective-permute-done((bf16[448,512]{1,0:T(8,128)(2,1)}, bf16[448,512]{1,0:T(8,128)(2,1)}, u32[]{:S(2)}, u32[]{:S(2)}) %collective-permute-start.14) | collective-permute-done | bytes 458784 | tf_op jit(solution)/shard_map/ppermute | solution.py:493
  123.0 2.0 %inward_mean.1 = (bf16[224,512]{1,0:T(8,128)(2,1)}, bf16[224,512]{1,0:T(8,128)(2,1)}) custom-call(bf16[448,512]{1,0:T(8,128)(2,1)S(1)} %copy-done.7, bf16[448,512]{1,0:T(8,128)(2,1)S(1)} %collective-permute-done.12.b, bf16[448,512]{1,0:T(8,128)(2,1)S(1)} %collective-permute-done.13.c, bf16[448,512]{1,0:T(8,128)(2,1)} %collective-permute-done.14.d), custom_call_target="tpu_custom_call" | custom-call | flops 20000000000 | bytes 1000 | tf_op jit(solution)/shard_map/inward_mean/pallas_call | solution.py:541
  125.0 0.0 all-to-all-done.2
  125.0 0.1 reduce_sum.12
  125.1 0.7 fusion.1
  (8 shorter events, 0.0 us)
Async XLA Ops:
  0.6 32.0 %copy-start.6 = (s32[3,224]{1,0:T(4,128)S(1)}, s32[3,224]{1,0:T(4,128)}, u32[]{:S(2)}) copy-start(s32[3,224]{1,0:T(4,128)} %idx.5) | copy-start | bytes 8068
  27.6 19.7 %collective-permute-start.5 = (bf16[32,4096]{1,0:T(8,128)(2,1)S(1)}, bf16[32,4096]{1,0:T(8,128)(2,1)S(1)}, u32[]{:S(2)}, u32[]{:S(2)}) collective-permute-start(bf16[32,4096]{1,0:T(8,128)(2,1)S(1)} %reshape.18.t0), channel_id=1, source_target_pairs={{24,0},{25,1},{26,2},{27,3},{28,4},{29,5},{30,6},{31,7},{0,8},{1,9... | collective-permute-start | bytes 786440 | tf_op jit(solution)/shard_map/ppermute | solution.py:488
  29.2 18.4 %collective-permute-start.4 = (bf16[32,4096]{1,0:T(8,128)(2,1)S(1)}, bf16[32,4096]{1,0:T(8,128)(2,1)S(1)}, u32[]{:S(2)}, u32[]{:S(2)}) collective-permute-start(bf16[32,4096]{1,0:T(8,128)(2,1)S(1)} %reshape.18.t0), channel_id=1, source_target_pairs={{16,0},{17,1},{18,2},{19,3},{20,4},{21,5},{22,6},{23,7},{24,8},{25... | collective-permute-start | bytes 786440 | tf_op jit(solution)/shard_map/ppermute | solution.py:488
  30.2 17.4 %collective-permute-start.3 = (bf16[32,4096]{1,0:T(8,128)(2,1)S(1)}, bf16[32,4096]{1,0:T(8,128)(2,1)S(1)}, u32[]{:S(2)}, u32[]{:S(2)}) collective-permute-start(bf16[32,4096]{1,0:T(8,128)(2,1)S(1)} %reshape.18.t0), channel_id=1, source_target_pairs={{8,0},{9,1},{10,2},{11,3},{12,4},{13,5},{14,6},{15,7},{16,8},{17,9... | collective-permute-start | bytes 786440 | tf_op jit(solution)/shard_map/ppermute | solution.py:488
  39.8 8.8 %copy-start.1 = (bf16[2048,896]{1,0:T(8,128)(2,1)}, bf16[2048,896]{1,0:T(8,128)(2,1)S(1)}, u32[]{:S(2)}) copy-start(bf16[2048,896]{1,0:T(8,128)(2,1)S(1)} %get-tuple-element.36.pg) | copy-start | bytes 11010052
  39.8 8.8 %copy-start.2 = (bf16[2048,896]{1,0:T(8,128)(2,1)}, bf16[2048,896]{1,0:T(8,128)(2,1)S(1)}, u32[]{:S(2)}) copy-start(bf16[2048,896]{1,0:T(8,128)(2,1)S(1)} %get-tuple-element.38.pu) | copy-start | bytes 11010052
  39.8 16.7 %collective-permute-start.2 = (bf16[32,4096]{1,0:T(8,128)(2,1)S(1)}, bf16[32,4096]{1,0:T(8,128)(2,1)S(1)}, u32[]{:S(2)}, u32[]{:S(2)}) collective-permute-start(bf16[32,4096]{1,0:T(8,128)(2,1)S(1)} %reshape.17.c0), channel_id=1, source_target_pairs={{24,0},{25,1},{26,2},{27,3},{28,4},{29,5},{30,6},{31,7},{0,8},{1,9... | collective-permute-start | bytes 786440 | tf_op jit(solution)/shard_map/ppermute | solution.py:488
  39.9 16.6 %collective-permute-start.1 = (bf16[32,4096]{1,0:T(8,128)(2,1)S(1)}, bf16[32,4096]{1,0:T(8,128)(2,1)S(1)}, u32[]{:S(2)}, u32[]{:S(2)}) collective-permute-start(bf16[32,4096]{1,0:T(8,128)(2,1)S(1)} %reshape.17.c0), channel_id=1, source_target_pairs={{16,0},{17,1},{18,2},{19,3},{20,4},{21,5},{22,6},{23,7},{24,8},{25... | collective-permute-start | bytes 786440 | tf_op jit(solution)/shard_map/ppermute | solution.py:488
  47.3 9.2 %copy-start = (bf16[256,8192]{1,0:T(8,128)(2,1)}, bf16[256,8192]{1,0:T(8,128)(2,1)S(1)}, u32[]{:S(2)}) copy-start(bf16[256,8192]{1,0:T(8,128)(2,1)S(1)} %outward_panel.1.pd.pd_far) | copy-start | bytes 12582916
  47.3 9.2 %collective-permute-start = (bf16[32,4096]{1,0:T(8,128)(2,1)S(1)}, bf16[32,4096]{1,0:T(8,128)(2,1)S(1)}, u32[]{:S(2)}, u32[]{:S(2)}) collective-permute-start(bf16[32,4096]{1,0:T(8,128)(2,1)S(1)} %reshape.17.c0), channel_id=1, source_target_pairs={{8,0},{9,1},{10,2},{11,3},{12,4},{13,5},{14,6},{15,7},{16,8},{17,9... | collective-permute-start | bytes 786440 | tf_op jit(solution)/shard_map/ppermute | solution.py:488
  47.6 1.0 copy-start.8
  48.6 1.2 copy-start.9
  61.7 7.6 %collective-permute-start.6 = (bf16[128,4096]{1,0:T(8,128)(2,1)}, bf16[128,4096]{1,0:T(8,128)(2,1)S(1)}, u32[]{:S(2)}, u32[]{:S(2)}) collective-permute-start(bf16[128,4096]{1,0:T(8,128)(2,1)} %get-tuple-element.44.cot_own), channel_id=1, source_target_pairs={{32,0},{0,32},{96,64},{64,96},{160,128},{128,160},{224,192},{192,2... | collective-permute-start | bytes 3145736 | tf_op jit(solution)/shard_map/ppermute | solution.py:498
  61.8 7.5 %collective-permute-start.7 = (bf16[2304,128]{1,0:T(8,128)(2,1)S(1)}, bf16[2304,128]{1,0:T(8,128)(2,1)S(1)}, u32[]{:S(2)}, u32[]{:S(2)}) collective-permute-start(bf16[2304,128]{1,0:T(8,128)(2,1)S(1)} %get-tuple-element.46), channel_id=1, source_target_pairs={{32,0},{0,32},{96,64},{64,96},{160,128},{128,160},{224,192},{192,2... | collective-permute-start | bytes 1769480 | tf_op jit(solution)/shard_map/ppermute | solution.py:498
  69.3 1.0 copy-start.4
  70.3 33.1 %all-to-all-start.1 = ((bf16[4,64,4096]{2,1,0:T(8,128)(2,1)}), bf16[4,64,4096]{2,1,0:T(8,128)(2,1)S(1)}, u32[]{:S(2)}, u32[]{:S(2)}) async-start(bf16[4,64,4096]{2,1,0:T(8,128)(2,1)} %input_parts.1), calls=%async_computation.1 | async-start | bytes 4194304 | tf_op jit(solution)/shard_map/all_to_all | solution.py:514
  75.2 13.2 %collective-permute-start.8 = (bf16[256,512]{1,0:T(8,128)(2,1)S(1)}, bf16[256,512]{1,0:T(8,128)(2,1)S(1)}, u32[]{:S(2)}, u32[]{:S(2)}) collective-permute-start(bf16[256,512]{1,0:T(8,128)(2,1)S(1)} %get-tuple-element.53.d_own), channel_id=1, source_target_pairs={{32,0},{0,32},{96,64},{64,96},{160,128},{128,160},{224,192},{192,2... | collective-permute-start | bytes 786440 | tf_op jit(solution)/shard_map/ppermute | solution.py:498
  75.2 1.2 copy-start.3
  76.4 1.2 copy-start.5
  83.6 16.5 %collective-permute-start.9 = (bf16[224,512]{1,0:T(8,128)(2,1)}, bf16[224,512]{1,0:T(8,128)(2,1)S(1)}, u32[]{:S(2)}, u32[]{:S(2)}) collective-permute-start(bf16[224,512]{1,0:T(8,128)(2,1)} %get-tuple-element.55), channel_id=1, source_target_pairs={{64,0},{96,32},{0,64},{32,96},{192,128},{224,160},{128,192},{160,2... | collective-permute-start | bytes 688136 | tf_op jit(solution)/shard_map/ppermute | solution.py:493
  85.1 15.5 %collective-permute-start.10 = (bf16[224,512]{1,0:T(8,128)(2,1)}, bf16[224,512]{1,0:T(8,128)(2,1)S(1)}, u32[]{:S(2)}, u32[]{:S(2)}) collective-permute-start(bf16[224,512]{1,0:T(8,128)(2,1)} %get-tuple-element.56), channel_id=1, source_target_pairs={{128,0},{160,32},{192,64},{224,96},{0,128},{32,160},{64,192},{96,2... | collective-permute-start | bytes 688136 | tf_op jit(solution)/shard_map/ppermute | solution.py:493
  87.9 13.8 %collective-permute-start.11 = (bf16[224,512]{1,0:T(8,128)(2,1)}, bf16[224,512]{1,0:T(8,128)(2,1)S(1)}, u32[]{:S(2)}, u32[]{:S(2)}) collective-permute-start(bf16[224,512]{1,0:T(8,128)(2,1)} %get-tuple-element.57), channel_id=1, source_target_pairs={{192,0},{224,32},{128,64},{160,96},{64,128},{96,160},{0,192},{32,2... | collective-permute-start | bytes 688136 | tf_op jit(solution)/shard_map/ppermute | solution.py:493
  95.9 13.6 %collective-permute-start.12 = (bf16[448,512]{1,0:T(8,128)(2,1)}, bf16[448,512]{1,0:T(8,128)(2,1)S(1)}, u32[]{:S(2)}, u32[]{:S(2)}) collective-permute-start(bf16[448,512]{1,0:T(8,128)(2,1)} %get-tuple-element.59), channel_id=1, source_target_pairs={{64,0},{96,32},{0,64},{32,96},{192,128},{224,160},{128,192},{160,2... | collective-permute-start | bytes 1376264 | tf_op jit(solution)/shard_map/ppermute | solution.py:493
  96.2 24.2 %collective-permute-start.13 = (bf16[448,512]{1,0:T(8,128)(2,1)}, bf16[448,512]{1,0:T(8,128)(2,1)S(1)}, u32[]{:S(2)}, u32[]{:S(2)}) collective-permute-start(bf16[448,512]{1,0:T(8,128)(2,1)} %get-tuple-element.60), channel_id=1, source_target_pairs={{128,0},{160,32},{192,64},{224,96},{0,128},{32,160},{64,192},{96,2... | collective-permute-start | bytes 1376264 | tf_op jit(solution)/shard_map/ppermute | solution.py:493
  100.1 22.9 %collective-permute-start.14 = (bf16[448,512]{1,0:T(8,128)(2,1)}, bf16[448,512]{1,0:T(8,128)(2,1)}, u32[]{:S(2)}, u32[]{:S(2)}) collective-permute-start(bf16[448,512]{1,0:T(8,128)(2,1)} %get-tuple-element.61), channel_id=1, source_target_pairs={{192,0},{224,32},{128,64},{160,96},{64,128},{96,160},{0,192},{32,2... | collective-permute-start | bytes 1376264 | tf_op jit(solution)/shard_map/ppermute | solution.py:493
  103.4 19.6 %copy-start.7 = (bf16[448,512]{1,0:T(8,128)(2,1)S(1)}, bf16[448,512]{1,0:T(8,128)(2,1)}, u32[]{:S(2)}) copy-start(bf16[448,512]{1,0:T(8,128)(2,1)} %get-tuple-element.54.a) | copy-start | bytes 1376260
  104.5 20.5 %all-to-all-start.2 = ((bf16[8,8,4096]{2,1,0:T(8,128)(2,1)}), bf16[8,8,4096]{2,1,0:T(8,128)(2,1)S(1)}, u32[]{:S(2)}, u32[]{:S(2)}) async-start(bf16[8,8,4096]{2,1,0:T(8,128)(2,1)} %merge_y.1), calls=%async_computation.2 | async-start | bytes 1048576 | tf_op jit(solution)/shard_map/all_to_all | solution.py:510

commit v6 on v5

--- a/solution.py
+++ b/solution.py
@@ -268,18 +268,20 @@
                 ]
 
 
-def down_kernel(idx, cot_own, cot_oth, ht_own, sib_oth, w0, w1, w2, w3, both, part, tiles):
+def down_kernel(idx, cots, ht_own, sib_oth, w0, w1, w2, w3, both, part, tiles, sems):
     wswap = wire_swap(place()[1])
-    both[:TOK, :] = cot_own[...]
-    both[TOK:, :] = cot_oth[...]
-
-    def product(n, carry):
-        lanes = pl.ds(pl.multiple_of(n * 512, 512), 512)
-        hidden = jnp.concatenate([ht_own[...], sib_oth[FEAT:, :]], axis=1)
+    def fetch(n):
+        lanes = pl.ds(n * 1024, 1024)
+        return pltpu.make_async_copy(cots.at[:, lanes], both.at[:, lanes], sems.at[n])
+
+    for n in range(4):
+        fetch(n).start()
+    hidden = jnp.concatenate([ht_own[...], sib_oth[FEAT:, :]], axis=1)
+    for n in range(8):
+        if n % 2 == 0:
+            fetch(n // 2).wait()
+        lanes = slice(n * 512, n * 512 + 512)
         part[:, lanes] = mm(hidden, both[:, lanes]).astype(BF)
-        return carry
-
-    lax.fori_loop(0, 8, product, 0)
     side = lax.broadcasted_iota(jnp.int32, (16, 128), 1) // 64
     for j in range(COLS):
         for q in range(KEEP):
@@ -289,37 +291,62 @@
             near = part[pl.ds(pl.multiple_of(odd * 128 + j * 16, 16), 16), lanes].astype(F32)
             far = part[pl.ds(pl.multiple_of((1 - odd) * 128 + j * 16, 16), 16), lanes].astype(F32)
             tile = jnp.where(side == odd, near, pltpu.roll(far, 64, 1)).astype(BF)
-            tiles[(q % 16) * 16:(q % 16) * 16 + 16, (q // 16) * 128:(q // 16) * 128 + 128] = tile
-        emit(wswap, tiles, (w0, w1, w2, w3), j * KEEP)
-
-
-def down_grads(idx, cot_own, cot_oth, ht_own, sib_oth):
+            tiles[j, (q % 16) * 16:(q % 16) * 16 + 16, (q // 16) * 128:(q // 16) * 128 + 128] = tile
+        emit(wswap, tiles.at[j], (w0, w1, w2, w3), j * KEEP)
+
+
+def down_grads(idx, cots, ht_own, sib_oth):
     return pl.pallas_call(
         down_kernel,
-        in_specs=smem(1) + vm(4),
+        in_specs=smem(1) + far(1) + vm(2),
         out_specs=vm(4),
         out_shape=[pltpu.HBM((SLOT, 512), BF)] * 4,
-        scratch_shapes=[pltpu.VMEM((256, D), BF), pltpu.VMEM((256, D), BF), pltpu.VMEM((256, 256), BF)],
+        scratch_shapes=[
+            pltpu.VMEM((256, D), BF),
+            pltpu.VMEM((256, D), BF),
+            pltpu.VMEM((COLS, 256, 256), BF),
+            pltpu.SemaphoreType.DMA((4,)),
+        ],
         compiler_params=params(14),
         cost_estimate=cost(0.2),
         name="down_grads",
-    )(idx, cot_own, cot_oth, ht_own, sib_oth)
-
-
-def delta_kernel(c0, c1, c2, c3, pd_far, gl2, ul2, own, cot, gdx, udx, cx, pd, sem):
+    )(idx, cots, ht_own, sib_oth)
+
+
+def back_kernel(c0, c1, c2, c3, d0, d1, d2, d3, pd_far, gl2, ul2, pg_far, pu_far, out_parts,
+                own, parts, cots, cx, pd, pg, pu, gdx, udx, ins, sem, panel_sems, part_sems, cot_sems):
+    y = place()[2]
+    share = pltpu.make_async_copy(out_parts, parts.at[:, :32, :], part_sems.at[4])
+    share.start()
+    bundle = [
+        pltpu.make_async_copy(piece, cots.at[pl.ds(n * 32, 32), :], cot_sems.at[n])
+        for n, piece in enumerate((c0, c1, c2, c3, d0, d1, d2, d3))
+    ]
+
+    def fetch_panel(n):
+        rows = pl.ds(n * 512, 512)
+        return [
+            pltpu.make_async_copy(far_ref.at[rows, :], near.at[rows, :], panel_sems.at[m, n])
+            for m, (far_ref, near) in enumerate(((pg_far, pg), (pu_far, pu)))
+        ]
+
     def fetch(n):
         lanes = pl.ds(n * 1024, 1024)
         return pltpu.make_async_copy(pd_far.at[:, lanes], pd.at[:, lanes], sem.at[n])
 
     for n in range(8):
         fetch(n).start()
+    for n in range(4):
+        for copy in fetch_panel(n):
+            copy.start()
+    for copy in bundle:
+        copy.start()
     at = cols_of(512)
     hjoin = one_hot(split_index(rows_of(256), 128), (at >> 7) * 128 + (at & 63))
     low = low_half((32, 128))
     for n, piece in enumerate((c0, c1, c2, c3)):
         top = slice(n * 32, n * 32 + 32)
         bottom = slice(TOK + n * 32, TOK + n * 32 + 32)
-        cot[top, :] = piece[...]
         for m in range(32):
             c = piece[:, m * 128:m * 128 + 128].astype(F32)
             rolled = pltpu.roll(c, 64, 1)
@@ -368,55 +395,50 @@
             before = (gd, ud)
 
 
-def deltas(pieces, pd, gl2, ul2):
-    return pl.pallas_call(
-        delta_kernel,
-        in_specs=vm(4) + [pl.BlockSpec(memory_space=pl.ANY)] + vm(2),
-        out_specs=vm(4),
-        out_shape=[shape(256, 512), pltpu.HBM((TOK, D), BF)] + [pltpu.VMEM((256, WIDE), BF)] * 2,
+    fjoin = one_hot(split_index(rows_of(256), 64), cols_of(256))
+    sends = []
+    for n in range(4):
+        for copy in fetch_panel(n):
+            copy.wait()
+        rows = slice(n * 512, n * 512 + 512)
+        acc = (mm_nt(gdx[...], pg[rows, :]) + mm_nt(udx[...], pu[rows, :])).astype(BF)
+        for c in range(4):
+            cols = slice(c * 128, c * 128 + 128)
+            pair = jnp.concatenate([acc[:TOK, cols], acc[TOK:, cols]], axis=1)
+            whole = mm(pair, fjoin).astype(BF)
+            lanes = slice(n * 1024 + c * 256, n * 1024 + c * 256 + 256)
+            for r in range(NY):
+                ins[lax.rem(y + r, NY), :, lanes] = whole[r * 32:r * 32 + 32, :]
+        lanes = pl.ds(n * 1024, 1024)
+        sends.append(pltpu.make_async_copy(ins.at[:, :, lanes], parts.at[:, 32:, lanes], part_sems.at[n]))
+        sends[-1].start()
+    for copy in sends + bundle + [share]:
+        copy.wait()
+
+
+def backward(pieces, others, pd, gl2, ul2, pg, pu, out_parts):
+    return pl.pallas_call(
+        back_kernel,
+        in_specs=vm(4) + far(5) + vm(2) + far(3),
+        out_specs=vm(1) + far(2),
+        out_shape=[shape(256, 512), pltpu.HBM((NY, 64, D), BF), pltpu.HBM((256, D), BF)],
         scratch_shapes=[
             pltpu.VMEM((256, 2 * D), BF),
             pltpu.VMEM((256, 2 * D), BF),
+            pltpu.VMEM((FEAT, WIDE), BF),
+            pltpu.VMEM((FEAT, WIDE), BF),
+            pltpu.VMEM((256, WIDE), BF),
+            pltpu.VMEM((256, WIDE), BF),
+            pltpu.VMEM((NY, 32, D), BF),
+            pltpu.SemaphoreType.DMA((8,)),
+            pltpu.SemaphoreType.DMA((2, 4)),
+            pltpu.SemaphoreType.DMA((5,)),
             pltpu.SemaphoreType.DMA((8,)),
         ],
-        compiler_params=params(18),
-        cost_estimate=cost(0.2),
-        name="deltas",
-    )(*pieces, hbm(pd), gl2, ul2)
-
-
-def back_kernel(gdx, udx, pg, pu, out_parts, parts, fjoin):
-    y = place()[2]
-    n = pl.program_id(0)
-
-    @pl.when(n == 0)
-    def _():
-        fjoin[...] = one_hot(split_index(rows_of(256), 64), cols_of(256))
-
-    parts[:, :32, :] = out_parts[...]
-    acc = (mm_nt(gdx[...], pg[...]) + mm_nt(udx[...], pu[...])).astype(BF)
-    for c in range(4):
-        cols = slice(c * 128, c * 128 + 128)
-        pair = jnp.concatenate([acc[:TOK, cols], acc[TOK:, cols]], axis=1)
-        whole = mm(pair, fjoin[...]).astype(BF)
-        for r in range(NY):
-            parts[lax.rem(y + r, NY), 32:, c * 256:c * 256 + 256] = whole[r * 32:r * 32 + 32, :]
-
-
-def input_parts(gdx, udx, pg, pu, out_parts):
-    whole = pl.BlockSpec((256, WIDE), lambda n: (0, 0))
-    panel = pl.BlockSpec((512, WIDE), lambda n: (n, 0))
-    return pl.pallas_call(
-        back_kernel,
-        grid=(FEAT // 512,),
-        in_specs=[whole, whole, panel, panel, pl.BlockSpec((NY, 32, 1024), lambda n: (0, 0, n))],
-        out_specs=pl.BlockSpec((NY, 64, 1024), lambda n: (0, 0, n)),
-        out_shape=pltpu.HBM((NY, 64, D), BF),
-        scratch_shapes=[pltpu.VMEM((256, 256), BF)],
-        compiler_params=params(14),
-        cost_estimate=cost(0.2),
-        name="input_parts",
-    )(gdx, udx, hbm(pg), hbm(pu), out_parts)
+        compiler_params=params(26),
+        cost_estimate=cost(9),
+        name="backward",
+    )(*pieces, *others, hbm(pd), gl2, ul2, hbm(pg), hbm(pu), out_parts)
 
 
 def merge_kernel(got, both):
@@ -466,8 +488,8 @@
                 else:
                     second = pltpu.roll(second, 64, 1)
                 tile = jnp.where(low, first, second).astype(BF)
-                tiles[(q % 16) * 16:(q % 16) * 16 + 16, (q // 16) * 128:(q // 16) * 128 + 128] = tile
-            emit(wswap, tiles, (w0, w1, w2, w3), m * SLOT + j * KEEP)
+                tiles[j, (q % 16) * 16:(q % 16) * 16 + 16, (q // 16) * 128:(q // 16) * 128 + 128] = tile
+            emit(wswap, tiles.at[j], (w0, w1, w2, w3), m * SLOT + j * KEEP)
 
 
 def inward_grads(idx, xt_own, sib_oth, d_own, d_oth):
@@ -476,7 +498,7 @@
         in_specs=smem(1) + vm(4),
         out_specs=vm(4),
         out_shape=[pltpu.HBM((2 * SLOT, 512), BF)] * 4,
-        scratch_shapes=[pltpu.VMEM((FEAT, 512), BF), pltpu.VMEM((256, 256), BF)],
+        scratch_shapes=[pltpu.VMEM((FEAT, 512), BF), pltpu.VMEM((COLS, 256, 256), BF)],
         compiler_params=params(14),
         cost_estimate=cost(0.2),
         name="inward_grads",
@@ -555,7 +577,7 @@
     tok_z = ring[:, :rows].reshape(NZ * rows, D)
     cot_z = ring[:, rows:].reshape(NZ * rows, D)
     tok = [tok_z] + [from_y(tok_z, s) for s in range(1, NY)]
-    idx = after(block_index, tok_z)
+    idx = after(block_index, tok_z, cot_z)
     pg, pu = inward_panels(idx, gate_blocks, up_blocks)
     cot_z = after(cot_z, pg)
     pd = outward_panel(idx, down_blocks)
@@ -563,11 +585,11 @@
 
     xt_own, ht_own, sib, gl2, ul2, out_parts = forward(tok, pg, pu, pd)
     sib_oth = from_core(after(sib, *cot))
-    own, cot_own, gdx, udx = deltas(cot, pd, gl2, ul2)
-    oth, cot_oth = from_core(own), from_core(cot_own)
-    parts = input_parts(gdx, udx, pg, pu, out_parts)
-    parts_got = over_y(after(parts, cot_oth, sib_oth))
-    down_wire = down_grads(block_index, cot_own, cot_oth, after(ht_own, parts), sib_oth)
+    cot_oth = [from_core(after(c, ht_own)) for c in cot]
+    own, parts, cots = backward(cot, cot_oth, pd, after(gl2, sib_oth), ul2, pg, pu, out_parts)
+    oth = from_core(own)
+    parts_got = over_y(parts)
+    down_wire = down_grads(block_index, hbm(cots), after(ht_own, parts), sib_oth)
     down_got = exchange_x(down_wire)
     wire = inward_grads(block_index, xt_own, sib_oth, after(own, down_wire[0]), oth)
     got = exchange_x(wire)

time: 126 us -> 125 us (level)
  local copies, waits for them, and re-layouts: 6.63 us -> 1.07 us
  waiting for transfers between devices: 16 us -> 18.4 us
    unnamed x20 -> x10, local copies, waits for them, and re-layouts: 5.58 us -> 0.02 us
    ppermute x3 -> x6, waiting for transfers between devices: 0.01 us -> 2.38 us  [from_core(): return lax.ppermute(value, 'dp', pairs)]
    pallas_call x3 -> x2, Pallas kernels: 18.2 us -> 19.2 us  [the longest x1 13 us: backward(): pl.pallas_call(back_kernel, in_specs=vm(4) + far(5) + vm(2) + far(3), out...]
  transfers between devices with their start and end apart: 17 -> 20, of which waited for: 4 -> 9; matrix products, arithmetic and copies ran while one was open for 1% -> 1% of each run, Pallas kernels for 33% -> 28%
where the time goes in v6:
time: 125 us; the launch traced here: 124 us
  Pallas kernels  47.6 us (38%)
  starting transfers between devices  28.1 us (22%)
  blocking collectives  25.8 us (21%)
  waiting for transfers between devices  18.4 us (15%)
  other arithmetic  2.65 us (2%)
    all_to_all x1, blocking collectives, over_z(): lax.all_to_all(value, 'fsdp', 0, 0, axis_index_groups=z_groups(), tiled=T...  25.8 us
    ppermute x6, waiting for transfers between devices, from_x(): return lax.ppermute(value, 'dp', pairs)  16 us
    pallas_call x1, Pallas kernels, backward(): pl.pallas_call(back_kernel, in_specs=vm(4) + far(5) + vm(2) + far(3), out...  13 us
    ppermute x6, starting transfers between devices, from_x(): return lax.ppermute(value, 'dp', pairs)  9.48 us
    ppermute x6, starting transfers between devices, from_y(): return lax.ppermute(value, 'fsdp', pairs)  8.58 us
    pallas_call x1, Pallas kernels, inward_grads(): pl.pallas_call(inward_kernel, in_specs=smem(1) + vm(4), out_specs=vm(4),...  7.58 us
    pallas_call x1, Pallas kernels, inward_panels(): pl.pallas_call(inward_panels_kernel, in_specs=smem(1) + far(2), out_specs...  7.11 us
    pallas_call x1, Pallas kernels, forward(): pl.pallas_call(forward_kernel, in_specs=vm(7), out_specs=vm(6), out_shape...  6.65 us
  transfers between devices with their start and end apart: 20, of which 9 were waited for; matrix products, arithmetic and copies ran while one was open for 1% of the time, Pallas kernels for 28%

profile of v6, /device:TPU:8, one launch (start us, length us, event | category | flops | bytes accessed | tf_op | source)
XLA Modules:
  0.0 124.5 jit_solution(17665357125094707352)
XLA Ops:
  0.6 0.0 copy-start
  0.6 0.8 pad_maximum_fusion
  1.5 25.8 %all_to_all.15 = bf16[8,8,4096]{2,1,0:T(8,128)(2,1)S(1)} all-to-all(bf16[8,8,4096]{2,1,0:T(8,128)(2,1)S(1)} %broadcast_in_dim.2), channel_id=1, replica_groups={{0,1,2,3,4,5,6,7},{8,9,10,11,12,13,14,15},{16,17,18,19,20,21,22,23},{24..., dimensions={0} | all-to-all | bytes 1048576 | tf_op jit(solution)/shard_map/all_to_all | solution.py:532
  27.3 0.2 fusion
  27.5 0.1 reshape.18.t0
  27.6 1.7 %collective-permute-start.5 = (bf16[32,4096]{1,0:T(8,128)(2,1)S(1)}, bf16[32,4096]{1,0:T(8,128)(2,1)S(1)}, u32[]{:S(2)}, u32[]{:S(2)}) collective-permute-start(bf16[32,4096]{1,0:T(8,128)(2,1)S(1)} %reshape.18.t0), channel_id=1, source_target_pairs={{24,0},{25,1},{26,2},{27,3},{28,4},{29,5},{30,6},{31,7},{0,8},{1,9... | collective-permute-start | bytes 786440 | tf_op jit(solution)/shard_map/ppermute | solution.py:510
  29.2 0.9 collective-permute-start.4
  30.2 2.4 %collective-permute-start.3 = (bf16[32,4096]{1,0:T(8,128)(2,1)S(1)}, bf16[32,4096]{1,0:T(8,128)(2,1)S(1)}, u32[]{:S(2)}, u32[]{:S(2)}) collective-permute-start(bf16[32,4096]{1,0:T(8,128)(2,1)S(1)} %reshape.18.t0), channel_id=1, source_target_pairs={{8,0},{9,1},{10,2},{11,3},{12,4},{13,5},{14,6},{15,7},{16,8},{17,9... | collective-permute-start | bytes 786440 | tf_op jit(solution)/shard_map/ppermute | solution.py:510
  32.6 0.1 reshape.17.c0
  32.6 0.0 copy-done
  32.7 7.1 %inward_panels.1 = (bf16[2048,896]{1,0:T(8,128)(2,1)S(1)}, bf16[2048,896]{1,0:T(8,128)(2,1)S(1)}) custom-call(s32[3,224]{1,0:T(4,128)S(1)} %copy-done, bf16[224,4096]{1,0:T(8,128)(2,1)} %gate.1, bf16[224,4096]{1,0:T(8,128)(2,1)} %up.1), custom_call_target="tpu_custom_call" | custom-call | flops 6000000000 | bytes 1000 | tf_op jit(solution)/shard_map/inward_panels/pallas_call | solution.py:153
  39.8 0.0 copy-start.3
  39.8 0.0 copy-start.4
  39.8 0.1 collective-permute-start.2
  39.9 3.4 %collective-permute-start.1 = (bf16[32,4096]{1,0:T(8,128)(2,1)S(1)}, bf16[32,4096]{1,0:T(8,128)(2,1)S(1)}, u32[]{:S(2)}, u32[]{:S(2)}) collective-permute-start(bf16[32,4096]{1,0:T(8,128)(2,1)S(1)} %reshape.17.c0), channel_id=1, source_target_pairs={{16,0},{17,1},{18,2},{19,3},{20,4},{21,5},{22,6},{23,7},{24,8},{25... | collective-permute-start | bytes 786440 | tf_op jit(solution)/shard_map/ppermute | solution.py:510
  43.3 4.0 %outward_panel.1.pd.pd_far = bf16[256,8192]{1,0:T(8,128)(2,1)S(1)} custom-call(s32[3,224]{1,0:T(4,128)S(1)} %copy-done, bf16[224,4096]{1,0:T(8,128)(2,1)} %down.1), custom_call_target="tpu_custom_call" | custom-call | flops 3000000000 | bytes 1000 | tf_op jit(solution)/shard_map/outward_panel/pallas_call | solution.py:170
  47.3 0.0 copy-start.2
  47.3 0.0 collective-permute-done.5.t3
  47.3 0.1 collective-permute-start
  47.4 0.0 collective-permute-done.4.t2
  47.4 0.0 collective-permute-done.3.t1
  47.4 0.0 copy-done.3
  47.4 0.0 copy-done.4
  47.4 6.6 %forward.1 = (bf16[2048,128]{1,0:T(8,128)(2,1)S(1)}, bf16[256,128]{1,0:T(8,128)(2,1)S(1)}, bf16[2304,128]{1,0:T(8,128)(2,1)S(1)}, f32[128,896]{1,0:T(8,128)S(1)}...) custom-call(bf16[32,4096]{1,0:T(8,128)(2,1)S(1)} %reshape.18.t0, ...), custom_call_target="tpu_custom_call" | custom-call | flops 8000000000 | bytes 1000 | tf_op jit(solution)/shard_map/forward/pallas_call | solution.py:241
  54.1 0.0 copy-done.2
  54.1 0.0 collective-permute-done.2.c3
  54.1 0.0 collective-permute-done.1.c2
  54.1 0.0 collective-permute-done.c1
  54.1 0.1 collective-permute-start.10
  54.2 0.5 collective-permute-start.6
  54.7 0.1 collective-permute-start.7
  54.8 0.4 collective-permute-start.8
  55.2 0.1 collective-permute-start.9
  55.3 0.9 collective-permute-done.10.sib_oth
  56.2 0.4 collective-permute-done.6.d0
  56.6 0.4 collective-permute-done.7.d1
  57.0 0.4 collective-permute-done.8.d2
  57.3 0.4 collective-permute-done.9.d3
  57.7 13.0 %backward.1 = (bf16[256,512]{1,0:T(8,128)(2,1)S(1)}, bf16[4,64,4096]{2,1,0:T(8,128)(2,1)}, bf16[256,4096]{1,0:T(8,128)(2,1)}) custom-call(bf16[32,4096]{1,0:T(8,128)(2,1)S(1)} %reshape.17.c0, bf16[32,4096]{1,0:T(8,128)(2,1)S(1)} %collective-permute-done.c1, bf16[32,4096]{1,0:T(8,128)(2,1)S(1)} %collective-permute-done.1.c2, ...), custom_call_target="tpu_custom_call" | custom-call | flops 8999999488 | bytes 1000 | tf_op jit(solution)/shard_map/backward/pallas_call | solution.py:420
  70.7 5.3 %all-to-all-start.1 = ((bf16[4,64,4096]{2,1,0:T(8,128)(2,1)}), bf16[4,64,4096]{2,1,0:T(8,128)(2,1)S(1)}, u32[]{:S(2)}, u32[]{:S(2)}) async-start(bf16[4,64,4096]{2,1,0:T(8,128)(2,1)} %get-tuple-element.53), calls=%async_computation.1 | async-start | bytes 4194304 | tf_op jit(solution)/shard_map/all_to_all | solution.py:536
  76.1 0.0 collective-permute-start.11
  76.1 6.2 %down_grads.1 = (bf16[224,512]{1,0:T(8,128)(2,1)}, bf16[224,512]{1,0:T(8,128)(2,1)}, bf16[224,512]{1,0:T(8,128)(2,1)}, bf16[224,512]{1,0:T(8,128)(2,1)}) custom-call(s32[3,224]{1,0:T(4,128)S(1)} %copy-done, bf16[256,4096]{1,0:T(8,128)(2,1)} %get-tuple-element.56.cots, bf16[256,128]{1,0:T(8,128)(2,1)S(1)} %get-tuple-element.57.ht_own, ...), custom_call_target="tpu_custom_call" | custom-call | flops 200000000 | bytes 1000 | tf_op jit(solution)/shard_map/down_grads/pallas_call | solution.py:299
  82.3 1.6 %collective-permute-start.12 = (bf16[224,512]{1,0:T(8,128)(2,1)}, bf16[224,512]{1,0:T(8,128)(2,1)S(1)}, u32[]{:S(2)}, u32[]{:S(2)}) collective-permute-start(bf16[224,512]{1,0:T(8,128)(2,1)} %get-tuple-element.61), channel_id=1, source_target_pairs={{64,0},{96,32},{0,64},{32,96},{192,128},{224,160},{128,192},{160,2... | collective-permute-start | bytes 688136 | tf_op jit(solution)/shard_map/ppermute | solution.py:515
  83.9 2.7 %collective-permute-start.13 = (bf16[224,512]{1,0:T(8,128)(2,1)}, bf16[224,512]{1,0:T(8,128)(2,1)S(1)}, u32[]{:S(2)}, u32[]{:S(2)}) collective-permute-start(bf16[224,512]{1,0:T(8,128)(2,1)} %get-tuple-element.62), channel_id=1, source_target_pairs={{128,0},{160,32},{192,64},{224,96},{0,128},{32,160},{64,192},{96,2... | collective-permute-start | bytes 688136 | tf_op jit(solution)/shard_map/ppermute | solution.py:515
  86.6 0.5 collective-permute-start.14
  87.1 0.0 collective-permute-done.11.d_oth
  87.1 7.6 %inward_grads.1 = (bf16[448,512]{1,0:T(8,128)(2,1)}, bf16[448,512]{1,0:T(8,128)(2,1)}, bf16[448,512]{1,0:T(8,128)(2,1)}, bf16[448,512]{1,0:T(8,128)(2,1)}) custom-call(s32[3,224]{1,0:T(4,128)S(1)} %copy-done, bf16[2048,128]{1,0:T(8,128)(2,1)S(1)} %get-tuple-element.54.xt_own, bf16[2304,128]{1,0:T(8,128)(2,1)S(1)} %collective-permute-done.10.sib_oth, ...), custom_call_target="tpu_custom_call" | custom-call | flops 200000000 | bytes 1000 | tf_op jit(solution)/shard_map/inward_grads/pallas_call | solution.py:496
  94.7 0.3 collective-permute-start.15
  94.9 4.0 %collective-permute-start.16 = (bf16[448,512]{1,0:T(8,128)(2,1)}, bf16[448,512]{1,0:T(8,128)(2,1)S(1)}, u32[]{:S(2)}, u32[]{:S(2)}) collective-permute-start(bf16[448,512]{1,0:T(8,128)(2,1)} %get-tuple-element.66), channel_id=1, source_target_pairs={{128,0},{160,32},{192,64},{224,96},{0,128},{32,160},{64,192},{96,2... | collective-permute-start | bytes 1376264 | tf_op jit(solution)/shard_map/ppermute | solution.py:515
  98.9 0.0 collective-permute-done.12
  98.9 0.5 collective-permute-start.17
  99.4 0.0 collective-permute-done.13
  99.4 1.0 collective-permute-done.14
  100.4 1.8 %multiply_convert_fusion = bf16[224,512]{1,0:T(8,128)(2,1)} fusion(bf16[224,512]{1,0:T(8,128)(2,1)S(1)} %collective-permute-done.14, bf16[224,512]{1,0:T(8,128)(2,1)S(1)} %collective-permute-done.13, bf16[224,512]{1,0:T(8,128)(2,1)S(1)} %collective-permute-done.12, bf16[224,512]{1,0:T(8,128)(2,1)} %get-tuple-element.58), kind=kLoop, calls=%fused_computation | loop fusion | flops 1032192 | bytes 1146880 | tf_op jit(solution)/shard_map/convert_element_type | solution.py:553
  102.1 0.0 all-to-all-done.1.got
  102.1 1.1 merge_y.1
  103.3 3.5 %all-to-all-start.2 = ((bf16[8,8,4096]{2,1,0:T(8,128)(2,1)}), bf16[8,8,4096]{2,1,0:T(8,128)(2,1)S(1)}, u32[]{:S(2)}, u32[]{:S(2)}) async-start(bf16[8,8,4096]{2,1,0:T(8,128)(2,1)} %merge_y.1), calls=%async_computation.2 | async-start | bytes 1048576 | tf_op jit(solution)/shard_map/all_to_all | solution.py:532
  106.8 1.5 %collective-permute-done.15.b = bf16[448,512]{1,0:T(8,128)(2,1)S(1)} collective-permute-done((bf16[448,512]{1,0:T(8,128)(2,1)}, bf16[448,512]{1,0:T(8,128)(2,1)S(1)}, u32[]{:S(2)}, u32[]{:S(2)}) %collective-permute-start.15) | collective-permute-done | bytes 458784 | tf_op jit(solution)/shard_map/ppermute | solution.py:515
  108.3 10.8 %collective-permute-done.16.c = bf16[448,512]{1,0:T(8,128)(2,1)S(1)} collective-permute-done((bf16[448,512]{1,0:T(8,128)(2,1)}, bf16[448,512]{1,0:T(8,128)(2,1)S(1)}, u32[]{:S(2)}, u32[]{:S(2)}) %collective-permute-start.16) | collective-permute-done | bytes 458784 | tf_op jit(solution)/shard_map/ppermute | solution.py:515
  119.1 2.7 %collective-permute-done.17.d = bf16[448,512]{1,0:T(8,128)(2,1)} collective-permute-done((bf16[448,512]{1,0:T(8,128)(2,1)}, bf16[448,512]{1,0:T(8,128)(2,1)}, u32[]{:S(2)}, u32[]{:S(2)}) %collective-permute-start.17) | collective-permute-done | bytes 458784 | tf_op jit(solution)/shard_map/ppermute | solution.py:515
  121.8 2.0 %inward_mean.1 = (bf16[224,512]{1,0:T(8,128)(2,1)}, bf16[224,512]{1,0:T(8,128)(2,1)}) custom-call(bf16[448,512]{1,0:T(8,128)(2,1)S(1)} %copy-done.1, bf16[448,512]{1,0:T(8,128)(2,1)S(1)} %collective-permute-done.15.b, bf16[448,512]{1,0:T(8,128)(2,1)S(1)} %collective-permute-done.16.c, bf16[448,512]{1,0:T(8,128)(2,1)} %collective-permute-done.17.d), custom_call_target="tpu_custom_call" | custom-call | flops 20000000000 | bytes 1000 | tf_op jit(solution)/shard_map/inward_mean/pallas_call | solution.py:563
  123.7 0.0 all-to-all-done.2
  123.7 0.1 reduce_sum.12
  123.8 0.7 fusion.1
  (3 shorter events, 0.0 us)
Async XLA Ops:
  0.6 32.0 %copy-start = (s32[3,224]{1,0:T(4,128)S(1)}, s32[3,224]{1,0:T(4,128)}, u32[]{:S(2)}) copy-start(s32[3,224]{1,0:T(4,128)} %idx.5) | copy-start | bytes 8068
  27.6 19.7 %collective-permute-start.5 = (bf16[32,4096]{1,0:T(8,128)(2,1)S(1)}, bf16[32,4096]{1,0:T(8,128)(2,1)S(1)}, u32[]{:S(2)}, u32[]{:S(2)}) collective-permute-start(bf16[32,4096]{1,0:T(8,128)(2,1)S(1)} %reshape.18.t0), channel_id=1, source_target_pairs={{24,0},{25,1},{26,2},{27,3},{28,4},{29,5},{30,6},{31,7},{0,8},{1,9... | collective-permute-start | bytes 786440 | tf_op jit(solution)/shard_map/ppermute | solution.py:510
  29.2 18.2 %collective-permute-start.4 = (bf16[32,4096]{1,0:T(8,128)(2,1)S(1)}, bf16[32,4096]{1,0:T(8,128)(2,1)S(1)}, u32[]{:S(2)}, u32[]{:S(2)}) collective-permute-start(bf16[32,4096]{1,0:T(8,128)(2,1)S(1)} %reshape.18.t0), channel_id=1, source_target_pairs={{16,0},{17,1},{18,2},{19,3},{20,4},{21,5},{22,6},{23,7},{24,8},{25... | collective-permute-start | bytes 786440 | tf_op jit(solution)/shard_map/ppermute | solution.py:510
  30.2 17.2 %collective-permute-start.3 = (bf16[32,4096]{1,0:T(8,128)(2,1)S(1)}, bf16[32,4096]{1,0:T(8,128)(2,1)S(1)}, u32[]{:S(2)}, u32[]{:S(2)}) collective-permute-start(bf16[32,4096]{1,0:T(8,128)(2,1)S(1)} %reshape.18.t0), channel_id=1, source_target_pairs={{8,0},{9,1},{10,2},{11,3},{12,4},{13,5},{14,6},{15,7},{16,8},{17,9... | collective-permute-start | bytes 786440 | tf_op jit(solution)/shard_map/ppermute | solution.py:510
  39.8 7.6 %copy-start.3 = (bf16[2048,896]{1,0:T(8,128)(2,1)}, bf16[2048,896]{1,0:T(8,128)(2,1)S(1)}, u32[]{:S(2)}) copy-start(bf16[2048,896]{1,0:T(8,128)(2,1)S(1)} %get-tuple-element.39.pg.pg_far) | copy-start | bytes 11010052
  39.8 7.6 %copy-start.4 = (bf16[2048,896]{1,0:T(8,128)(2,1)}, bf16[2048,896]{1,0:T(8,128)(2,1)S(1)}, u32[]{:S(2)}) copy-start(bf16[2048,896]{1,0:T(8,128)(2,1)S(1)} %get-tuple-element.41.pu.pu_far) | copy-start | bytes 11010052
  39.8 14.3 %collective-permute-start.2 = (bf16[32,4096]{1,0:T(8,128)(2,1)S(1)}, bf16[32,4096]{1,0:T(8,128)(2,1)S(1)}, u32[]{:S(2)}, u32[]{:S(2)}) collective-permute-start(bf16[32,4096]{1,0:T(8,128)(2,1)S(1)} %reshape.17.c0), channel_id=1, source_target_pairs={{24,0},{25,1},{26,2},{27,3},{28,4},{29,5},{30,6},{31,7},{0,8},{1,9... | collective-permute-start | bytes 786440 | tf_op jit(solution)/shard_map/ppermute | solution.py:510
  39.9 14.2 %collective-permute-start.1 = (bf16[32,4096]{1,0:T(8,128)(2,1)S(1)}, bf16[32,4096]{1,0:T(8,128)(2,1)S(1)}, u32[]{:S(2)}, u32[]{:S(2)}) collective-permute-start(bf16[32,4096]{1,0:T(8,128)(2,1)S(1)} %reshape.17.c0), channel_id=1, source_target_pairs={{16,0},{17,1},{18,2},{19,3},{20,4},{21,5},{22,6},{23,7},{24,8},{25... | collective-permute-start | bytes 786440 | tf_op jit(solution)/shard_map/ppermute | solution.py:510
  47.3 6.8 %copy-start.2 = (bf16[256,8192]{1,0:T(8,128)(2,1)}, bf16[256,8192]{1,0:T(8,128)(2,1)S(1)}, u32[]{:S(2)}) copy-start(bf16[256,8192]{1,0:T(8,128)(2,1)S(1)} %outward_panel.1.pd.pd_far) | copy-start | bytes 12582916
  47.3 6.8 %collective-permute-start = (bf16[32,4096]{1,0:T(8,128)(2,1)S(1)}, bf16[32,4096]{1,0:T(8,128)(2,1)S(1)}, u32[]{:S(2)}, u32[]{:S(2)}) collective-permute-start(bf16[32,4096]{1,0:T(8,128)(2,1)S(1)} %reshape.17.c0), channel_id=1, source_target_pairs={{8,0},{9,1},{10,2},{11,3},{12,4},{13,5},{14,6},{15,7},{16,8},{17,9... | collective-permute-start | bytes 786440 | tf_op jit(solution)/shard_map/ppermute | solution.py:510
  54.1 2.1 %collective-permute-start.10 = (bf16[2304,128]{1,0:T(8,128)(2,1)S(1)}, bf16[2304,128]{1,0:T(8,128)(2,1)S(1)}, u32[]{:S(2)}, u32[]{:S(2)}) collective-permute-start(bf16[2304,128]{1,0:T(8,128)(2,1)S(1)} %get-tuple-element.49), channel_id=1, source_target_pairs={{32,0},{0,32},{96,64},{64,96},{160,128},{128,160},{224,192},{192,2... | collective-permute-start | bytes 1769480 | tf_op jit(solution)/shard_map/ppermute | solution.py:520
  54.2 2.4 %collective-permute-start.6 = (bf16[32,4096]{1,0:T(8,128)(2,1)S(1)}, bf16[32,4096]{1,0:T(8,128)(2,1)S(1)}, u32[]{:S(2)}, u32[]{:S(2)}) collective-permute-start(bf16[32,4096]{1,0:T(8,128)(2,1)S(1)} %reshape.17.c0), channel_id=1, source_target_pairs={{32,0},{0,32},{96,64},{64,96},{160,128},{128,160},{224,192},{192,2... | collective-permute-start | bytes 786440 | tf_op jit(solution)/shard_map/ppermute | solution.py:520
  54.7 2.2 %collective-permute-start.7 = (bf16[32,4096]{1,0:T(8,128)(2,1)S(1)}, bf16[32,4096]{1,0:T(8,128)(2,1)S(1)}, u32[]{:S(2)}, u32[]{:S(2)}) collective-permute-start(bf16[32,4096]{1,0:T(8,128)(2,1)S(1)} %collective-permute-done.c1), channel_id=1, source_target_pairs={{32,0},{0,32},{96,64},{64,96},{160,128},{128,160},{224,192},{192,2... | collective-permute-start | bytes 786440 | tf_op jit(solution)/shard_map/ppermute | solution.py:520
  54.8 2.5 %collective-permute-start.8 = (bf16[32,4096]{1,0:T(8,128)(2,1)S(1)}, bf16[32,4096]{1,0:T(8,128)(2,1)S(1)}, u32[]{:S(2)}, u32[]{:S(2)}) collective-permute-start(bf16[32,4096]{1,0:T(8,128)(2,1)S(1)} %collective-permute-done.1.c2), channel_id=1, source_target_pairs={{32,0},{0,32},{96,64},{64,96},{160,128},{128,160},{224,192},{192,2... | collective-permute-start | bytes 786440 | tf_op jit(solution)/shard_map/ppermute | solution.py:520
  55.2 2.5 %collective-permute-start.9 = (bf16[32,4096]{1,0:T(8,128)(2,1)S(1)}, bf16[32,4096]{1,0:T(8,128)(2,1)S(1)}, u32[]{:S(2)}, u32[]{:S(2)}) collective-permute-start(bf16[32,4096]{1,0:T(8,128)(2,1)S(1)} %collective-permute-done.2.c3), channel_id=1, source_target_pairs={{32,0},{0,32},{96,64},{64,96},{160,128},{128,160},{224,192},{192,2... | collective-permute-start | bytes 786440 | tf_op jit(solution)/shard_map/ppermute | solution.py:520
  70.7 31.4 %all-to-all-start.1 = ((bf16[4,64,4096]{2,1,0:T(8,128)(2,1)}), bf16[4,64,4096]{2,1,0:T(8,128)(2,1)S(1)}, u32[]{:S(2)}, u32[]{:S(2)}) async-start(bf16[4,64,4096]{2,1,0:T(8,128)(2,1)} %get-tuple-element.53), calls=%async_computation.1 | async-start | bytes 4194304 | tf_op jit(solution)/shard_map/all_to_all | solution.py:536
  76.1 11.0 %collective-permute-start.11 = (bf16[256,512]{1,0:T(8,128)(2,1)S(1)}, bf16[256,512]{1,0:T(8,128)(2,1)S(1)}, u32[]{:S(2)}, u32[]{:S(2)}) collective-permute-start(bf16[256,512]{1,0:T(8,128)(2,1)S(1)} %get-tuple-element.59.d_own), channel_id=1, source_target_pairs={{32,0},{0,32},{96,64},{64,96},{160,128},{128,160},{224,192},{192,2... | collective-permute-start | bytes 786440 | tf_op jit(solution)/shard_map/ppermute | solution.py:520
  82.3 16.6 %collective-permute-start.12 = (bf16[224,512]{1,0:T(8,128)(2,1)}, bf16[224,512]{1,0:T(8,128)(2,1)S(1)}, u32[]{:S(2)}, u32[]{:S(2)}) collective-permute-start(bf16[224,512]{1,0:T(8,128)(2,1)} %get-tuple-element.61), channel_id=1, source_target_pairs={{64,0},{96,32},{0,64},{32,96},{192,128},{224,160},{128,192},{160,2... | collective-permute-start | bytes 688136 | tf_op jit(solution)/shard_map/ppermute | solution.py:515
  83.9 15.5 %collective-permute-start.13 = (bf16[224,512]{1,0:T(8,128)(2,1)}, bf16[224,512]{1,0:T(8,128)(2,1)S(1)}, u32[]{:S(2)}, u32[]{:S(2)}) collective-permute-start(bf16[224,512]{1,0:T(8,128)(2,1)} %get-tuple-element.62), channel_id=1, source_target_pairs={{128,0},{160,32},{192,64},{224,96},{0,128},{32,160},{64,192},{96,2... | collective-permute-start | bytes 688136 | tf_op jit(solution)/shard_map/ppermute | solution.py:515
  86.6 13.8 %collective-permute-start.14 = (bf16[224,512]{1,0:T(8,128)(2,1)}, bf16[224,512]{1,0:T(8,128)(2,1)S(1)}, u32[]{:S(2)}, u32[]{:S(2)}) collective-permute-start(bf16[224,512]{1,0:T(8,128)(2,1)} %get-tuple-element.63), channel_id=1, source_target_pairs={{192,0},{224,32},{128,64},{160,96},{64,128},{96,160},{0,192},{32,2... | collective-permute-start | bytes 688136 | tf_op jit(solution)/shard_map/ppermute | solution.py:515
  94.7 13.6 %collective-permute-start.15 = (bf16[448,512]{1,0:T(8,128)(2,1)}, bf16[448,512]{1,0:T(8,128)(2,1)S(1)}, u32[]{:S(2)}, u32[]{:S(2)}) collective-permute-start(bf16[448,512]{1,0:T(8,128)(2,1)} %get-tuple-element.65), channel_id=1, source_target_pairs={{64,0},{96,32},{0,64},{32,96},{192,128},{224,160},{128,192},{160,2... | collective-permute-start | bytes 1376264 | tf_op jit(solution)/shard_map/ppermute | solution.py:515
  94.9 24.2 %collective-permute-start.16 = (bf16[448,512]{1,0:T(8,128)(2,1)}, bf16[448,512]{1,0:T(8,128)(2,1)S(1)}, u32[]{:S(2)}, u32[]{:S(2)}) collective-permute-start(bf16[448,512]{1,0:T(8,128)(2,1)} %get-tuple-element.66), channel_id=1, source_target_pairs={{128,0},{160,32},{192,64},{224,96},{0,128},{32,160},{64,192},{96,2... | collective-permute-start | bytes 1376264 | tf_op jit(solution)/shard_map/ppermute | solution.py:515
  98.9 22.9 %collective-permute-start.17 = (bf16[448,512]{1,0:T(8,128)(2,1)}, bf16[448,512]{1,0:T(8,128)(2,1)}, u32[]{:S(2)}, u32[]{:S(2)}) collective-permute-start(bf16[448,512]{1,0:T(8,128)(2,1)} %get-tuple-element.67), channel_id=1, source_target_pairs={{192,0},{224,32},{128,64},{160,96},{64,128},{96,160},{0,192},{32,2... | collective-permute-start | bytes 1376264 | tf_op jit(solution)/shard_map/ppermute | solution.py:515
  102.1 19.6 %copy-start.1 = (bf16[448,512]{1,0:T(8,128)(2,1)S(1)}, bf16[448,512]{1,0:T(8,128)(2,1)}, u32[]{:S(2)}) copy-start(bf16[448,512]{1,0:T(8,128)(2,1)} %get-tuple-element.60.a) | copy-start | bytes 1376260
  103.3 20.4 %all-to-all-start.2 = ((bf16[8,8,4096]{2,1,0:T(8,128)(2,1)}), bf16[8,8,4096]{2,1,0:T(8,128)(2,1)S(1)}, u32[]{:S(2)}, u32[]{:S(2)}) async-start(bf16[8,8,4096]{2,1,0:T(8,128)(2,1)} %merge_y.1), calls=%async_computation.2 | async-start | bytes 1048576 | tf_op jit(solution)/shard_map/all_to_all | solution.py:532

commit v7 on v6

--- a/solution.py
+++ b/solution.py
@@ -63,6 +63,10 @@
 
 def mm_nt(a, b):
     return lax.dot_general(a, b, (((1,), (1,)), ((), ())), preferred_element_type=F32)
+
+
+def mm_tn(a, b):
+    return lax.dot_general(a, b, (((0,), (0,)), ((), ())), preferred_element_type=F32)
 
 
 def low_half(shape):
@@ -313,63 +317,39 @@
     )(idx, cots, ht_own, sib_oth)
 
 
-def back_kernel(c0, c1, c2, c3, d0, d1, d2, d3, pd_far, gl2, ul2, pg_far, pu_far, out_parts,
-                own, parts, cots, cx, pd, pg, pu, gdx, udx, ins, sem, panel_sems, part_sems, cot_sems):
+def back_kernel(c0, c1, c2, c3, d0, d1, d2, d3, pd, gl2, ul2, pg, pu, out_parts,
+                own, parts, cots, cxt, gdt, udt, ins, part_sems, cot_sems):
     y = place()[2]
+    at = cols_of(512)
+    hjoin = one_hot(split_index(rows_of(256), 128), (at >> 7) * 128 + (at & 63))
+    fjoin = one_hot(split_index(rows_of(256), 64), cols_of(256))
     share = pltpu.make_async_copy(out_parts, parts.at[:, :32, :], part_sems.at[4])
     share.start()
     bundle = [
         pltpu.make_async_copy(piece, cots.at[pl.ds(n * 32, 32), :], cot_sems.at[n])
         for n, piece in enumerate((c0, c1, c2, c3, d0, d1, d2, d3))
     ]
-
-    def fetch_panel(n):
-        rows = pl.ds(n * 512, 512)
-        return [
-            pltpu.make_async_copy(far_ref.at[rows, :], near.at[rows, :], panel_sems.at[m, n])
-            for m, (far_ref, near) in enumerate(((pg_far, pg), (pu_far, pu)))
-        ]
-
-    def fetch(n):
-        lanes = pl.ds(n * 1024, 1024)
-        return pltpu.make_async_copy(pd_far.at[:, lanes], pd.at[:, lanes], sem.at[n])
-
-    for n in range(8):
-        fetch(n).start()
-    for n in range(4):
-        for copy in fetch_panel(n):
-            copy.start()
     for copy in bundle:
         copy.start()
-    at = cols_of(512)
-    hjoin = one_hot(split_index(rows_of(256), 128), (at >> 7) * 128 + (at & 63))
-    low = low_half((32, 128))
-    for n, piece in enumerate((c0, c1, c2, c3)):
-        top = slice(n * 32, n * 32 + 32)
-        bottom = slice(TOK + n * 32, TOK + n * 32 + 32)
-        for m in range(32):
-            c = piece[:, m * 128:m * 128 + 128].astype(F32)
-            rolled = pltpu.roll(c, 64, 1)
-            zero = jnp.zeros_like(c)
-            first = slice(2 * m * 128, 2 * m * 128 + 128)
-            second = slice(2 * m * 128 + 128, 2 * m * 128 + 256)
-            cx[top, first] = jnp.where(low, c, zero).astype(BF)
-            cx[bottom, first] = jnp.where(low, zero, rolled).astype(BF)
-            cx[top, second] = jnp.where(low, rolled, zero).astype(BF)
-            cx[bottom, second] = jnp.where(low, zero, c).astype(BF)
-
-    hd = jnp.zeros((256, 256), F32)
-    for n in range(8):
-        lanes = slice(n * 1024, n * 1024 + 1024)
-        fetch(n).wait()
-        hd = hd + mm_nt(cx[:, lanes], pd[:, lanes])
+    zero = jnp.zeros((64, TOK), BF)
+    for m in range(32):
+        lanes = slice(m * 128, m * 128 + 128)
+        turned = jnp.concatenate([c[:, lanes] for c in (c0, c1, c2, c3)], axis=0).T
+        for e in range(2):
+            row = (2 * m + e) * 128
+            half = turned[e * 64:e * 64 + 64, :]
+            cxt[row:row + 64, :TOK] = half
+            cxt[row:row + 64, TOK:] = zero
+            cxt[row + 64:row + 128, :TOK] = zero
+            cxt[row + 64:row + 128, TOK:] = half
+    hd = mm(pd[...], cxt[...])
     high = hd.astype(BF)
     rest = (hd - high.astype(F32)).astype(BF)
     low = low_half((TOK, 128))
     for g in range(2):
-        cols = slice(g * 128, g * 128 + 128)
+        rows = slice(g * 128, g * 128 + 128)
         joined = sum(
-            mm(jnp.concatenate([part[:TOK, cols], part[TOK:, cols]], axis=1), hjoin) for part in (high, rest)
+            mm_tn(jnp.concatenate([part[rows, :TOK], part[rows, TOK:]], axis=0), hjoin) for part in (high, rest)
         )
         before = None
         for jl in range(4):
@@ -382,9 +362,13 @@
             sig = 1.0 / (1.0 + jnp.exp(-gl))
             gd = delta * ul * sig * (1.0 + gl * (1.0 - sig))
             ud = delta * gl * sig
-            for dst, val in ((gdx, gd), (udx, ud)):
-                dst[:TOK, lanes] = jnp.where(low, val, 0.0).astype(BF)
-                dst[TOK:, lanes] = jnp.where(low, 0.0, val).astype(BF)
+            for dst, val in ((gdt, gd), (udt, ud)):
+                turned = val.astype(BF).T
+                row = j * 128
+                dst[row:row + 64, :TOK] = turned[:64, :]
+                dst[row:row + 64, TOK:] = zero
+                dst[row + 64:row + 128, :TOK] = zero
+                dst[row + 64:row + 128, TOK:] = turned[64:, :]
             pair = slice((j // 2) * 128, (j // 2) * 128 + 128)
             if j % 2:
                 own[:TOK, pair] = jnp.where(low, before[0], gd).astype(BF)
@@ -393,19 +377,14 @@
                 own[:TOK, pair] = jnp.where(low, gd, 0.0).astype(BF)
                 own[TOK:, pair] = jnp.where(low, ud, 0.0).astype(BF)
             before = (gd, ud)
-
-
-    fjoin = one_hot(split_index(rows_of(256), 64), cols_of(256))
     sends = []
     for n in range(4):
-        for copy in fetch_panel(n):
-            copy.wait()
         rows = slice(n * 512, n * 512 + 512)
-        acc = (mm_nt(gdx[...], pg[rows, :]) + mm_nt(udx[...], pu[rows, :])).astype(BF)
+        acc = (mm(pg[rows, :], gdt[...]) + mm(pu[rows, :], udt[...])).astype(BF)
         for c in range(4):
-            cols = slice(c * 128, c * 128 + 128)
-            pair = jnp.concatenate([acc[:TOK, cols], acc[TOK:, cols]], axis=1)
-            whole = mm(pair, fjoin).astype(BF)
+            rows = slice(c * 128, c * 128 + 128)
+            pair = jnp.concatenate([acc[rows, :TOK], acc[rows, TOK:]], axis=0)
+            whole = mm_tn(pair, fjoin).astype(BF)
             lanes = slice(n * 1024 + c * 256, n * 1024 + c * 256 + 256)
             for r in range(NY):
                 ins[lax.rem(y + r, NY), :, lanes] = whole[r * 32:r * 32 + 32, :]
@@ -419,26 +398,21 @@
 def backward(pieces, others, pd, gl2, ul2, pg, pu, out_parts):
     return pl.pallas_call(
         back_kernel,
-        in_specs=vm(4) + far(5) + vm(2) + far(3),
+        in_specs=vm(4) + far(4) + vm(5) + far(1),
         out_specs=vm(1) + far(2),
         out_shape=[shape(256, 512), pltpu.HBM((NY, 64, D), BF), pltpu.HBM((256, D), BF)],
         scratch_shapes=[
-            pltpu.VMEM((256, 2 * D), BF),
-            pltpu.VMEM((256, 2 * D), BF),
-            pltpu.VMEM((FEAT, WIDE), BF),
-            pltpu.VMEM((FEAT, WIDE), BF),
-            pltpu.VMEM((256, WIDE), BF),
-            pltpu.VMEM((256, WIDE), BF),
+            pltpu.VMEM((2 * D, 256), BF),
+            pltpu.VMEM((WIDE, 256), BF),
+            pltpu.VMEM((WIDE, 256), BF),
             pltpu.VMEM((NY, 32, D), BF),
-            pltpu.SemaphoreType.DMA((8,)),
-            pltpu.SemaphoreType.DMA((2, 4)),
             pltpu.SemaphoreType.DMA((5,)),
             pltpu.SemaphoreType.DMA((8,)),
         ],
         compiler_params=params(26),
         cost_estimate=cost(9),
         name="backward",
-    )(*pieces, *others, hbm(pd), gl2, ul2, hbm(pg), hbm(pu), out_parts)
+    )(*pieces, *others, pd, gl2, ul2, pg, pu, out_parts)
 
 
 def merge_kernel(got, both):
@@ -469,13 +443,10 @@
     for m in range(2):
         delta = jnp.concatenate([d[m * TOK:m * TOK + TOK, :] for d in (d_own, d_oth)], axis=0)
 
-        def product(n, carry):
-            rows = pl.ds(pl.multiple_of(n * 256, 256), 256)
+        for n in range(8):
+            rows = slice(n * 256, n * 256 + 256)
             tokens = jnp.concatenate([xt_own[rows, :], sib_oth[rows, :]], axis=1)
             part[rows, :] = mm(tokens, delta).astype(BF)
-            return carry
-
-        lax.fori_loop(0, 8, product, 0)
         for j in range(COLS):
             odd = j % 2
             lanes = slice((j // 2) * 128, (j // 2) * 128 + 128)

time: 125 us -> 121 us (0.968)
  Pallas kernels: 47.6 us -> 41.5 us
  waiting for transfers between devices: 18.4 us -> 21 us
    pallas_call x1, Pallas kernels: 13 us -> 9.47 us  [backward(): pl.pallas_call(back_kernel, in_specs=vm(4) + far(4) + vm(5) + far(1), out...]
    pallas_call x1, Pallas kernels: 7.58 us -> 4.99 us  [inward_grads(): pl.pallas_call(inward_kernel, in_specs=smem(1) + vm(4), out_specs=vm(4),...]
    all_to_all x1, waiting for transfers between devices: 0.01 us -> 1.6 us  [over_z(): lax.all_to_all(value, 'fsdp', 0, 0, axis_index_groups=z_groups(), tiled=T...]
  transfers between devices with their start and end apart: 20 -> 20, of which waited for: 9 -> 10; matrix products, arithmetic and copies ran while one was open for 1% -> 2% of each run, Pallas kernels for 28% -> 27%
where the time goes in v7:
time: 121 us
  Pallas kernels  41.5 us (34%)
  starting transfers between devices  28.1 us (23%)
  blocking collectives  25.8 us (21%)
  waiting for transfers between devices  21 us (17%)
  other arithmetic  2.65 us (2%)
    all_to_all x1, blocking collectives, over_z(): lax.all_to_all(value, 'fsdp', 0, 0, axis_index_groups=z_groups(), tiled=T...  25.8 us
    ppermute x6, waiting for transfers between devices, from_x(): return lax.ppermute(value, 'dp', pairs)  17 us
    ppermute x6, starting transfers between devices, from_x(): return lax.ppermute(value, 'dp', pairs)  9.48 us
    pallas_call x1, Pallas kernels, backward(): pl.pallas_call(back_kernel, in_specs=vm(4) + far(4) + vm(5) + far(1), out...  9.47 us
    ppermute x6, starting transfers between devices, from_y(): return lax.ppermute(value, 'fsdp', pairs)  8.57 us
    pallas_call x1, Pallas kernels, inward_panels(): pl.pallas_call(inward_panels_kernel, in_specs=smem(1) + far(2), out_specs...  7.12 us
    pallas_call x1, Pallas kernels, forward(): pl.pallas_call(forward_kernel, in_specs=vm(7), out_specs=vm(6), out_shape...  6.65 us
    pallas_call x1, Pallas kernels, down_grads(): pl.pallas_call(down_kernel, in_specs=smem(1) + far(1) + vm(2), out_specs=...  6.22 us
  transfers between devices with their start and end apart: 20, of which 10 were waited for; matrix products, arithmetic and copies ran while one was open for 2% of the time, Pallas kernels for 27%

profile of v7, /device:TPU:8, one launch (start us, length us, event | category | flops | bytes accessed | tf_op | source)
XLA Modules:
  0.0 120.9 jit_solution(11261653804504855510)
XLA Ops:
  0.6 0.0 copy-start
  0.6 0.8 pad_maximum_fusion
  1.5 25.8 %all_to_all.15 = bf16[8,8,4096]{2,1,0:T(8,128)(2,1)S(1)} all-to-all(bf16[8,8,4096]{2,1,0:T(8,128)(2,1)S(1)} %broadcast_in_dim.2), channel_id=1, replica_groups={{0,1,2,3,4,5,6,7},{8,9,10,11,12,13,14,15},{16,17,18,19,20,21,22,23},{24..., dimensions={0} | all-to-all | bytes 1048576 | tf_op jit(solution)/shard_map/all_to_all | solution.py:503
  27.3 0.2 fusion
  27.5 0.1 reshape.18.t0
  27.6 1.7 %collective-permute-start.5 = (bf16[32,4096]{1,0:T(8,128)(2,1)S(1)}, bf16[32,4096]{1,0:T(8,128)(2,1)S(1)}, u32[]{:S(2)}, u32[]{:S(2)}) collective-permute-start(bf16[32,4096]{1,0:T(8,128)(2,1)S(1)} %reshape.18.t0), channel_id=1, source_target_pairs={{24,0},{25,1},{26,2},{27,3},{28,4},{29,5},{30,6},{31,7},{0,8},{1,9... | collective-permute-start | bytes 786440 | tf_op jit(solution)/shard_map/ppermute | solution.py:481
  29.2 0.9 collective-permute-start.4
  30.2 2.4 %collective-permute-start.3 = (bf16[32,4096]{1,0:T(8,128)(2,1)S(1)}, bf16[32,4096]{1,0:T(8,128)(2,1)S(1)}, u32[]{:S(2)}, u32[]{:S(2)}) collective-permute-start(bf16[32,4096]{1,0:T(8,128)(2,1)S(1)} %reshape.18.t0), channel_id=1, source_target_pairs={{8,0},{9,1},{10,2},{11,3},{12,4},{13,5},{14,6},{15,7},{16,8},{17,9... | collective-permute-start | bytes 786440 | tf_op jit(solution)/shard_map/ppermute | solution.py:481
  32.6 0.1 reshape.17.c0
  32.6 0.0 copy-done
  32.7 7.1 %inward_panels.1 = (bf16[2048,896]{1,0:T(8,128)(2,1)S(1)}, bf16[2048,896]{1,0:T(8,128)(2,1)S(1)}) custom-call(s32[3,224]{1,0:T(4,128)S(1)} %copy-done, bf16[224,4096]{1,0:T(8,128)(2,1)} %gate.1, bf16[224,4096]{1,0:T(8,128)(2,1)} %up.1), custom_call_target="tpu_custom_call" | custom-call | flops 6000000000 | bytes 1000 | tf_op jit(solution)/shard_map/inward_panels/pallas_call | solution.py:157
  39.8 0.1 collective-permute-start.2
  39.9 3.4 %collective-permute-start.1 = (bf16[32,4096]{1,0:T(8,128)(2,1)S(1)}, bf16[32,4096]{1,0:T(8,128)(2,1)S(1)}, u32[]{:S(2)}, u32[]{:S(2)}) collective-permute-start(bf16[32,4096]{1,0:T(8,128)(2,1)S(1)} %reshape.17.c0), channel_id=1, source_target_pairs={{16,0},{17,1},{18,2},{19,3},{20,4},{21,5},{22,6},{23,7},{24,8},{25... | collective-permute-start | bytes 786440 | tf_op jit(solution)/shard_map/ppermute | solution.py:481
  43.3 4.0 %outward_panel.1.pd = bf16[256,8192]{1,0:T(8,128)(2,1)S(1)} custom-call(s32[3,224]{1,0:T(4,128)S(1)} %copy-done, bf16[224,4096]{1,0:T(8,128)(2,1)} %down.1), custom_call_target="tpu_custom_call" | custom-call | flops 3000000000 | bytes 1000 | tf_op jit(solution)/shard_map/outward_panel/pallas_call | solution.py:174
  47.3 0.0 collective-permute-done.5.t3
  47.3 0.1 collective-permute-start
  47.4 0.0 collective-permute-done.4.t2
  47.4 0.0 collective-permute-done.3.t1
  47.4 6.6 %forward.1 = (bf16[2048,128]{1,0:T(8,128)(2,1)S(1)}, bf16[256,128]{1,0:T(8,128)(2,1)S(1)}, bf16[2304,128]{1,0:T(8,128)(2,1)S(1)}, f32[128,896]{1,0:T(8,128)S(1)}...) custom-call(bf16[32,4096]{1,0:T(8,128)(2,1)S(1)} %reshape.18.t0, ...), custom_call_target="tpu_custom_call" | custom-call | flops 8000000000 | bytes 1000 | tf_op jit(solution)/shard_map/forward/pallas_call | solution.py:245
  54.0 0.0 collective-permute-done.2.c3
  54.0 0.0 collective-permute-done.1.c2
  54.1 0.0 collective-permute-done.c1
  54.1 0.1 collective-permute-start.10
  54.2 0.5 collective-permute-start.6
  54.7 0.1 collective-permute-start.7
  54.8 0.4 collective-permute-start.8
  55.2 0.1 collective-permute-start.9
  55.3 0.9 collective-permute-done.10.sib_oth
  56.2 0.4 collective-permute-done.6.d0
  56.5 0.4 collective-permute-done.7.d1
  56.9 0.4 collective-permute-done.8.d2
  57.3 0.4 collective-permute-done.9.d3
  57.7 9.5 %backward.1 = (bf16[256,512]{1,0:T(8,128)(2,1)S(1)}, bf16[4,64,4096]{2,1,0:T(8,128)(2,1)}, bf16[256,4096]{1,0:T(8,128)(2,1)}) custom-call(bf16[32,4096]{1,0:T(8,128)(2,1)S(1)} %reshape.17.c0, bf16[32,4096]{1,0:T(8,128)(2,1)S(1)} %collective-permute-done.c1, bf16[32,4096]{1,0:T(8,128)(2,1)S(1)} %collective-permute-done.1.c2, ...), custom_call_target="tpu_custom_call" | custom-call | flops 8999999488 | bytes 1000 | tf_op jit(solution)/shard_map/backward/pallas_call | solution.py:399
  67.1 5.3 %all-to-all-start.1 = ((bf16[4,64,4096]{2,1,0:T(8,128)(2,1)}), bf16[4,64,4096]{2,1,0:T(8,128)(2,1)S(1)}, u32[]{:S(2)}, u32[]{:S(2)}) async-start(bf16[4,64,4096]{2,1,0:T(8,128)(2,1)} %get-tuple-element.53), calls=%async_computation.1 | async-start | bytes 4194304 | tf_op jit(solution)/shard_map/all_to_all | solution.py:507
  72.5 0.0 collective-permute-start.11
  72.5 6.2 %down_grads.1 = (bf16[224,512]{1,0:T(8,128)(2,1)}, bf16[224,512]{1,0:T(8,128)(2,1)}, bf16[224,512]{1,0:T(8,128)(2,1)}, bf16[224,512]{1,0:T(8,128)(2,1)}) custom-call(s32[3,224]{1,0:T(4,128)S(1)} %copy-done, bf16[256,4096]{1,0:T(8,128)(2,1)} %get-tuple-element.56.cots, bf16[256,128]{1,0:T(8,128)(2,1)S(1)} %get-tuple-element.57.ht_own, ...), custom_call_target="tpu_custom_call" | custom-call | flops 200000000 | bytes 1000 | tf_op jit(solution)/shard_map/down_grads/pallas_call | solution.py:303
  78.7 1.6 %collective-permute-start.12 = (bf16[224,512]{1,0:T(8,128)(2,1)}, bf16[224,512]{1,0:T(8,128)(2,1)S(1)}, u32[]{:S(2)}, u32[]{:S(2)}) collective-permute-start(bf16[224,512]{1,0:T(8,128)(2,1)} %get-tuple-element.61), channel_id=1, source_target_pairs={{64,0},{96,32},{0,64},{32,96},{192,128},{224,160},{128,192},{160,2... | collective-permute-start | bytes 688136 | tf_op jit(solution)/shard_map/ppermute | solution.py:486
  80.3 2.7 %collective-permute-start.13 = (bf16[224,512]{1,0:T(8,128)(2,1)}, bf16[224,512]{1,0:T(8,128)(2,1)S(1)}, u32[]{:S(2)}, u32[]{:S(2)}) collective-permute-start(bf16[224,512]{1,0:T(8,128)(2,1)} %get-tuple-element.62), channel_id=1, source_target_pairs={{128,0},{160,32},{192,64},{224,96},{0,128},{32,160},{64,192},{96,2... | collective-permute-start | bytes 688136 | tf_op jit(solution)/shard_map/ppermute | solution.py:486
  83.0 0.5 collective-permute-start.14
  83.5 0.0 collective-permute-done.11.d_oth
  83.5 5.0 %inward_grads.1 = (bf16[448,512]{1,0:T(8,128)(2,1)}, bf16[448,512]{1,0:T(8,128)(2,1)}, bf16[448,512]{1,0:T(8,128)(2,1)}, bf16[448,512]{1,0:T(8,128)(2,1)}) custom-call(s32[3,224]{1,0:T(4,128)S(1)} %copy-done, bf16[2048,128]{1,0:T(8,128)(2,1)S(1)} %get-tuple-element.54.xt_own, bf16[2304,128]{1,0:T(8,128)(2,1)S(1)} %collective-permute-done.10.sib_oth, ...), custom_call_target="tpu_custom_call" | custom-call | flops 200000000 | bytes 1000 | tf_op jit(solution)/shard_map/inward_grads/pallas_call | solution.py:467
  88.5 0.3 collective-permute-start.15
  88.8 3.9 %collective-permute-start.16 = (bf16[448,512]{1,0:T(8,128)(2,1)}, bf16[448,512]{1,0:T(8,128)(2,1)S(1)}, u32[]{:S(2)}, u32[]{:S(2)}) collective-permute-start(bf16[448,512]{1,0:T(8,128)(2,1)} %get-tuple-element.66), channel_id=1, source_target_pairs={{128,0},{160,32},{192,64},{224,96},{0,128},{32,160},{64,192},{96,2... | collective-permute-start | bytes 1376264 | tf_op jit(solution)/shard_map/ppermute | solution.py:486
  92.7 0.0 collective-permute-done.12
  92.7 0.5 collective-permute-start.17
  93.2 1.4 %collective-permute-done.13 = bf16[224,512]{1,0:T(8,128)(2,1)S(1)} collective-permute-done((bf16[224,512]{1,0:T(8,128)(2,1)}, bf16[224,512]{1,0:T(8,128)(2,1)S(1)}, u32[]{:S(2)}, u32[]{:S(2)}) %collective-permute-start.13) | collective-permute-done | bytes 229408 | tf_op jit(solution)/shard_map/ppermute | solution.py:486
  94.6 3.1 %collective-permute-done.14 = bf16[224,512]{1,0:T(8,128)(2,1)S(1)} collective-permute-done((bf16[224,512]{1,0:T(8,128)(2,1)}, bf16[224,512]{1,0:T(8,128)(2,1)S(1)}, u32[]{:S(2)}, u32[]{:S(2)}) %collective-permute-start.14) | collective-permute-done | bytes 229408 | tf_op jit(solution)/shard_map/ppermute | solution.py:486
  97.7 1.8 %multiply_convert_fusion = bf16[224,512]{1,0:T(8,128)(2,1)} fusion(bf16[224,512]{1,0:T(8,128)(2,1)S(1)} %collective-permute-done.14, bf16[224,512]{1,0:T(8,128)(2,1)S(1)} %collective-permute-done.13, bf16[224,512]{1,0:T(8,128)(2,1)S(1)} %collective-permute-done.12, bf16[224,512]{1,0:T(8,128)(2,1)} %get-tuple-element.58), kind=kLoop, calls=%fused_computation | loop fusion | flops 1032192 | bytes 1146880 | tf_op jit(solution)/shard_map/convert_element_type | solution.py:524
  99.5 0.0 copy-start.1
  99.5 0.0 all-to-all-done.1.got
  99.5 1.1 merge_y.1
  100.6 3.5 %all-to-all-start.2 = ((bf16[8,8,4096]{2,1,0:T(8,128)(2,1)}), bf16[8,8,4096]{2,1,0:T(8,128)(2,1)S(1)}, u32[]{:S(2)}, u32[]{:S(2)}) async-start(bf16[8,8,4096]{2,1,0:T(8,128)(2,1)} %merge_y.1), calls=%async_computation.2 | async-start | bytes 1048576 | tf_op jit(solution)/shard_map/all_to_all | solution.py:503
  104.1 0.0 collective-permute-done.15.b
  104.1 9.8 %collective-permute-done.16.c = bf16[448,512]{1,0:T(8,128)(2,1)S(1)} collective-permute-done((bf16[448,512]{1,0:T(8,128)(2,1)}, bf16[448,512]{1,0:T(8,128)(2,1)S(1)}, u32[]{:S(2)}, u32[]{:S(2)}) %collective-permute-start.16) | collective-permute-done | bytes 458784 | tf_op jit(solution)/shard_map/ppermute | solution.py:486
  113.9 2.6 %collective-permute-done.17.d = bf16[448,512]{1,0:T(8,128)(2,1)} collective-permute-done((bf16[448,512]{1,0:T(8,128)(2,1)}, bf16[448,512]{1,0:T(8,128)(2,1)}, u32[]{:S(2)}, u32[]{:S(2)}) %collective-permute-start.17) | collective-permute-done | bytes 458784 | tf_op jit(solution)/shard_map/ppermute | solution.py:486
  116.6 0.0 copy-done.1
  116.6 2.0 %inward_mean.1 = (bf16[224,512]{1,0:T(8,128)(2,1)}, bf16[224,512]{1,0:T(8,128)(2,1)}) custom-call(bf16[448,512]{1,0:T(8,128)(2,1)S(1)} %copy-done.1, bf16[448,512]{1,0:T(8,128)(2,1)S(1)} %collective-permute-done.15.b, bf16[448,512]{1,0:T(8,128)(2,1)S(1)} %collective-permute-done.16.c, bf16[448,512]{1,0:T(8,128)(2,1)} %collective-permute-done.17.d), custom_call_target="tpu_custom_call" | custom-call | flops 20000000000 | bytes 1000 | tf_op jit(solution)/shard_map/inward_mean/pallas_call | solution.py:534
  118.5 1.6 %all-to-all-done.2 = bf16[8,8,4096]{2,1,0:T(8,128)(2,1)S(1)} async-done(((bf16[8,8,4096]{2,1,0:T(8,128)(2,1)}), bf16[8,8,4096]{2,1,0:T(8,128)(2,1)S(1)}, u32[]{:S(2)}, u32[]{:S(2)}) %all-to-all-start.2) | async-done | bytes 524320 | tf_op jit(solution)/shard_map/all_to_all | solution.py:503
  120.1 0.1 reduce_sum.12
  120.2 0.7 fusion.1
  (1 shorter events, 0.0 us)
Async XLA Ops:
  0.6 32.0 %copy-start = (s32[3,224]{1,0:T(4,128)S(1)}, s32[3,224]{1,0:T(4,128)}, u32[]{:S(2)}) copy-start(s32[3,224]{1,0:T(4,128)} %idx.5) | copy-start | bytes 8068
  27.6 19.7 %collective-permute-start.5 = (bf16[32,4096]{1,0:T(8,128)(2,1)S(1)}, bf16[32,4096]{1,0:T(8,128)(2,1)S(1)}, u32[]{:S(2)}, u32[]{:S(2)}) collective-permute-start(bf16[32,4096]{1,0:T(8,128)(2,1)S(1)} %reshape.18.t0), channel_id=1, source_target_pairs={{24,0},{25,1},{26,2},{27,3},{28,4},{29,5},{30,6},{31,7},{0,8},{1,9... | collective-permute-start | bytes 786440 | tf_op jit(solution)/shard_map/ppermute | solution.py:481
  29.2 18.1 %collective-permute-start.4 = (bf16[32,4096]{1,0:T(8,128)(2,1)S(1)}, bf16[32,4096]{1,0:T(8,128)(2,1)S(1)}, u32[]{:S(2)}, u32[]{:S(2)}) collective-permute-start(bf16[32,4096]{1,0:T(8,128)(2,1)S(1)} %reshape.18.t0), channel_id=1, source_target_pairs={{16,0},{17,1},{18,2},{19,3},{20,4},{21,5},{22,6},{23,7},{24,8},{25... | collective-permute-start | bytes 786440 | tf_op jit(solution)/shard_map/ppermute | solution.py:481
  30.2 17.2 %collective-permute-start.3 = (bf16[32,4096]{1,0:T(8,128)(2,1)S(1)}, bf16[32,4096]{1,0:T(8,128)(2,1)S(1)}, u32[]{:S(2)}, u32[]{:S(2)}) collective-permute-start(bf16[32,4096]{1,0:T(8,128)(2,1)S(1)} %reshape.18.t0), channel_id=1, source_target_pairs={{8,0},{9,1},{10,2},{11,3},{12,4},{13,5},{14,6},{15,7},{16,8},{17,9... | collective-permute-start | bytes 786440 | tf_op jit(solution)/shard_map/ppermute | solution.py:481
  39.8 14.3 %collective-permute-start.2 = (bf16[32,4096]{1,0:T(8,128)(2,1)S(1)}, bf16[32,4096]{1,0:T(8,128)(2,1)S(1)}, u32[]{:S(2)}, u32[]{:S(2)}) collective-permute-start(bf16[32,4096]{1,0:T(8,128)(2,1)S(1)} %reshape.17.c0), channel_id=1, source_target_pairs={{24,0},{25,1},{26,2},{27,3},{28,4},{29,5},{30,6},{31,7},{0,8},{1,9... | collective-permute-start | bytes 786440 | tf_op jit(solution)/shard_map/ppermute | solution.py:481
  39.9 14.2 %collective-permute-start.1 = (bf16[32,4096]{1,0:T(8,128)(2,1)S(1)}, bf16[32,4096]{1,0:T(8,128)(2,1)S(1)}, u32[]{:S(2)}, u32[]{:S(2)}) collective-permute-start(bf16[32,4096]{1,0:T(8,128)(2,1)S(1)} %reshape.17.c0), channel_id=1, source_target_pairs={{16,0},{17,1},{18,2},{19,3},{20,4},{21,5},{22,6},{23,7},{24,8},{25... | collective-permute-start | bytes 786440 | tf_op jit(solution)/shard_map/ppermute | solution.py:481
  47.3 6.8 %collective-permute-start = (bf16[32,4096]{1,0:T(8,128)(2,1)S(1)}, bf16[32,4096]{1,0:T(8,128)(2,1)S(1)}, u32[]{:S(2)}, u32[]{:S(2)}) collective-permute-start(bf16[32,4096]{1,0:T(8,128)(2,1)S(1)} %reshape.17.c0), channel_id=1, source_target_pairs={{8,0},{9,1},{10,2},{11,3},{12,4},{13,5},{14,6},{15,7},{16,8},{17,9... | collective-permute-start | bytes 786440 | tf_op jit(solution)/shard_map/ppermute | solution.py:481
  54.1 2.1 %collective-permute-start.10 = (bf16[2304,128]{1,0:T(8,128)(2,1)S(1)}, bf16[2304,128]{1,0:T(8,128)(2,1)S(1)}, u32[]{:S(2)}, u32[]{:S(2)}) collective-permute-start(bf16[2304,128]{1,0:T(8,128)(2,1)S(1)} %get-tuple-element.49), channel_id=1, source_target_pairs={{32,0},{0,32},{96,64},{64,96},{160,128},{128,160},{224,192},{192,2... | collective-permute-start | bytes 1769480 | tf_op jit(solution)/shard_map/ppermute | solution.py:491
  54.2 2.4 %collective-permute-start.6 = (bf16[32,4096]{1,0:T(8,128)(2,1)S(1)}, bf16[32,4096]{1,0:T(8,128)(2,1)S(1)}, u32[]{:S(2)}, u32[]{:S(2)}) collective-permute-start(bf16[32,4096]{1,0:T(8,128)(2,1)S(1)} %reshape.17.c0), channel_id=1, source_target_pairs={{32,0},{0,32},{96,64},{64,96},{160,128},{128,160},{224,192},{192,2... | collective-permute-start | bytes 786440 | tf_op jit(solution)/shard_map/ppermute | solution.py:491
  54.7 2.2 %collective-permute-start.7 = (bf16[32,4096]{1,0:T(8,128)(2,1)S(1)}, bf16[32,4096]{1,0:T(8,128)(2,1)S(1)}, u32[]{:S(2)}, u32[]{:S(2)}) collective-permute-start(bf16[32,4096]{1,0:T(8,128)(2,1)S(1)} %collective-permute-done.c1), channel_id=1, source_target_pairs={{32,0},{0,32},{96,64},{64,96},{160,128},{128,160},{224,192},{192,2... | collective-permute-start | bytes 786440 | tf_op jit(solution)/shard_map/ppermute | solution.py:491
  54.8 2.5 %collective-permute-start.8 = (bf16[32,4096]{1,0:T(8,128)(2,1)S(1)}, bf16[32,4096]{1,0:T(8,128)(2,1)S(1)}, u32[]{:S(2)}, u32[]{:S(2)}) collective-permute-start(bf16[32,4096]{1,0:T(8,128)(2,1)S(1)} %collective-permute-done.1.c2), channel_id=1, source_target_pairs={{32,0},{0,32},{96,64},{64,96},{160,128},{128,160},{224,192},{192,2... | collective-permute-start | bytes 786440 | tf_op jit(solution)/shard_map/ppermute | solution.py:491
  55.2 2.5 %collective-permute-start.9 = (bf16[32,4096]{1,0:T(8,128)(2,1)S(1)}, bf16[32,4096]{1,0:T(8,128)(2,1)S(1)}, u32[]{:S(2)}, u32[]{:S(2)}) collective-permute-start(bf16[32,4096]{1,0:T(8,128)(2,1)S(1)} %collective-permute-done.2.c3), channel_id=1, source_target_pairs={{32,0},{0,32},{96,64},{64,96},{160,128},{128,160},{224,192},{192,2... | collective-permute-start | bytes 786440 | tf_op jit(solution)/shard_map/ppermute | solution.py:491
  67.1 32.3 %all-to-all-start.1 = ((bf16[4,64,4096]{2,1,0:T(8,128)(2,1)}), bf16[4,64,4096]{2,1,0:T(8,128)(2,1)S(1)}, u32[]{:S(2)}, u32[]{:S(2)}) async-start(bf16[4,64,4096]{2,1,0:T(8,128)(2,1)} %get-tuple-element.53), calls=%async_computation.1 | async-start | bytes 4194304 | tf_op jit(solution)/shard_map/all_to_all | solution.py:507
  72.5 11.0 %collective-permute-start.11 = (bf16[256,512]{1,0:T(8,128)(2,1)S(1)}, bf16[256,512]{1,0:T(8,128)(2,1)S(1)}, u32[]{:S(2)}, u32[]{:S(2)}) collective-permute-start(bf16[256,512]{1,0:T(8,128)(2,1)S(1)} %get-tuple-element.59.d_own), channel_id=1, source_target_pairs={{32,0},{0,32},{96,64},{64,96},{160,128},{128,160},{224,192},{192,2... | collective-permute-start | bytes 786440 | tf_op jit(solution)/shard_map/ppermute | solution.py:491
  78.7 14.0 %collective-permute-start.12 = (bf16[224,512]{1,0:T(8,128)(2,1)}, bf16[224,512]{1,0:T(8,128)(2,1)S(1)}, u32[]{:S(2)}, u32[]{:S(2)}) collective-permute-start(bf16[224,512]{1,0:T(8,128)(2,1)} %get-tuple-element.61), channel_id=1, source_target_pairs={{64,0},{96,32},{0,64},{32,96},{192,128},{224,160},{128,192},{160,2... | collective-permute-start | bytes 688136 | tf_op jit(solution)/shard_map/ppermute | solution.py:486
  80.3 14.3 %collective-permute-start.13 = (bf16[224,512]{1,0:T(8,128)(2,1)}, bf16[224,512]{1,0:T(8,128)(2,1)S(1)}, u32[]{:S(2)}, u32[]{:S(2)}) collective-permute-start(bf16[224,512]{1,0:T(8,128)(2,1)} %get-tuple-element.62), channel_id=1, source_target_pairs={{128,0},{160,32},{192,64},{224,96},{0,128},{32,160},{64,192},{96,2... | collective-permute-start | bytes 688136 | tf_op jit(solution)/shard_map/ppermute | solution.py:486
  83.0 14.7 %collective-permute-start.14 = (bf16[224,512]{1,0:T(8,128)(2,1)}, bf16[224,512]{1,0:T(8,128)(2,1)S(1)}, u32[]{:S(2)}, u32[]{:S(2)}) collective-permute-start(bf16[224,512]{1,0:T(8,128)(2,1)} %get-tuple-element.63), channel_id=1, source_target_pairs={{192,0},{224,32},{128,64},{160,96},{64,128},{96,160},{0,192},{32,2... | collective-permute-start | bytes 688136 | tf_op jit(solution)/shard_map/ppermute | solution.py:486
  88.5 15.6 %collective-permute-start.15 = (bf16[448,512]{1,0:T(8,128)(2,1)}, bf16[448,512]{1,0:T(8,128)(2,1)S(1)}, u32[]{:S(2)}, u32[]{:S(2)}) collective-permute-start(bf16[448,512]{1,0:T(8,128)(2,1)} %get-tuple-element.65), channel_id=1, source_target_pairs={{64,0},{96,32},{0,64},{32,96},{192,128},{224,160},{128,192},{160,2... | collective-permute-start | bytes 1376264 | tf_op jit(solution)/shard_map/ppermute | solution.py:486
  88.8 25.2 %collective-permute-start.16 = (bf16[448,512]{1,0:T(8,128)(2,1)}, bf16[448,512]{1,0:T(8,128)(2,1)S(1)}, u32[]{:S(2)}, u32[]{:S(2)}) collective-permute-start(bf16[448,512]{1,0:T(8,128)(2,1)} %get-tuple-element.66), channel_id=1, source_target_pairs={{128,0},{160,32},{192,64},{224,96},{0,128},{32,160},{64,192},{96,2... | collective-permute-start | bytes 1376264 | tf_op jit(solution)/shard_map/ppermute | solution.py:486
  92.7 23.9 %collective-permute-start.17 = (bf16[448,512]{1,0:T(8,128)(2,1)}, bf16[448,512]{1,0:T(8,128)(2,1)}, u32[]{:S(2)}, u32[]{:S(2)}) collective-permute-start(bf16[448,512]{1,0:T(8,128)(2,1)} %get-tuple-element.67), channel_id=1, source_target_pairs={{192,0},{224,32},{128,64},{160,96},{64,128},{96,160},{0,192},{32,2... | collective-permute-start | bytes 1376264 | tf_op jit(solution)/shard_map/ppermute | solution.py:486
  99.5 17.1 %copy-start.1 = (bf16[448,512]{1,0:T(8,128)(2,1)S(1)}, bf16[448,512]{1,0:T(8,128)(2,1)}, u32[]{:S(2)}) copy-start(bf16[448,512]{1,0:T(8,128)(2,1)} %get-tuple-element.60.a) | copy-start | bytes 1376260
  100.6 19.5 %all-to-all-start.2 = ((bf16[8,8,4096]{2,1,0:T(8,128)(2,1)}), bf16[8,8,4096]{2,1,0:T(8,128)(2,1)S(1)}, u32[]{:S(2)}, u32[]{:S(2)}) async-start(bf16[8,8,4096]{2,1,0:T(8,128)(2,1)} %merge_y.1), calls=%async_computation.2 | async-start | bytes 1048576 | tf_op jit(solution)/shard_map/all_to_all | solution.py:503

commit v8 on v7

--- a/solution.py
+++ b/solution.py
@@ -381,13 +381,16 @@
     for n in range(4):
         rows = slice(n * 512, n * 512 + 512)
         acc = (mm(pg[rows, :], gdt[...]) + mm(pu[rows, :], udt[...])).astype(BF)
+        turned = acc.T
+        pairs = [
+            jnp.concatenate([turned[p * TOK:p * TOK + TOK, c * 128:c * 128 + 128] for p in range(2)], axis=1)
+            for c in range(4)
+        ]
+        whole = mm(jnp.concatenate(pairs, axis=0), fjoin).astype(BF)
         for c in range(4):
-            rows = slice(c * 128, c * 128 + 128)
-            pair = jnp.concatenate([acc[rows, :TOK], acc[rows, TOK:]], axis=0)
-            whole = mm_tn(pair, fjoin).astype(BF)
             lanes = slice(n * 1024 + c * 256, n * 1024 + c * 256 + 256)
             for r in range(NY):
-                ins[lax.rem(y + r, NY), :, lanes] = whole[r * 32:r * 32 + 32, :]
+                ins[lax.rem(y + r, NY), :, lanes] = whole[c * TOK + r * 32:c * TOK + r * 32 + 32, :]
         lanes = pl.ds(n * 1024, 1024)
         sends.append(pltpu.make_async_copy(ins.at[:, :, lanes], parts.at[:, 32:, lanes], part_sems.at[n]))
         sends[-1].start()

time: 121 us -> 121 us (level)
  no operation moved by 1% of the time
where the time goes in v8:
time: 121 us
  Pallas kernels  41.5 us (34%)
  starting transfers between devices  28.1 us (23%)
  blocking collectives  25.8 us (21%)
  waiting for transfers between devices  21 us (17%)
  other arithmetic  2.65 us (2%)
    all_to_all x1, blocking collectives, over_z(): lax.all_to_all(value, 'fsdp', 0, 0, axis_index_groups=z_groups(), tiled=T...  25.8 us
    ppermute x6, waiting for transfers between devices, from_x(): return lax.ppermute(value, 'dp', pairs)  17 us
    ppermute x6, starting transfers between devices, from_x(): return lax.ppermute(value, 'dp', pairs)  9.48 us
    pallas_call x1, Pallas kernels, backward(): pl.pallas_call(back_kernel, in_specs=vm(4) + far(4) + vm(5) + far(1), out...  9.44 us
    ppermute x6, starting transfers between devices, from_y(): return lax.ppermute(value, 'fsdp', pairs)  8.57 us
    pallas_call x1, Pallas kernels, inward_panels(): pl.pallas_call(inward_panels_kernel, in_specs=smem(1) + far(2), out_specs...  7.11 us
    pallas_call x1, Pallas kernels, forward(): pl.pallas_call(forward_kernel, in_specs=vm(7), out_specs=vm(6), out_shape...  6.65 us
    pallas_call x1, Pallas kernels, down_grads(): pl.pallas_call(down_kernel, in_specs=smem(1) + far(1) + vm(2), out_specs=...  6.22 us
  transfers between devices with their start and end apart: 20, of which 10 were waited for; matrix products, arithmetic and copies ran while one was open for 2% of the time, Pallas kernels for 27%

profile of v8, /device:TPU:8, one launch (start us, length us, event | category | flops | bytes accessed | tf_op | source)
XLA Modules:
  0.0 120.8 jit_solution(13377293443081010137)
XLA Ops:
  0.6 0.0 copy-start
  0.6 0.8 pad_maximum_fusion
  1.5 25.8 %all_to_all.15 = bf16[8,8,4096]{2,1,0:T(8,128)(2,1)S(1)} all-to-all(bf16[8,8,4096]{2,1,0:T(8,128)(2,1)S(1)} %broadcast_in_dim.2), channel_id=1, replica_groups={{0,1,2,3,4,5,6,7},{8,9,10,11,12,13,14,15},{16,17,18,19,20,21,22,23},{24..., dimensions={0} | all-to-all | bytes 1048576 | tf_op jit(solution)/shard_map/all_to_all | solution.py:506
  27.3 0.2 fusion
  27.5 0.1 reshape.18.t0
  27.6 1.7 %collective-permute-start.5 = (bf16[32,4096]{1,0:T(8,128)(2,1)S(1)}, bf16[32,4096]{1,0:T(8,128)(2,1)S(1)}, u32[]{:S(2)}, u32[]{:S(2)}) collective-permute-start(bf16[32,4096]{1,0:T(8,128)(2,1)S(1)} %reshape.18.t0), channel_id=1, source_target_pairs={{24,0},{25,1},{26,2},{27,3},{28,4},{29,5},{30,6},{31,7},{0,8},{1,9... | collective-permute-start | bytes 786440 | tf_op jit(solution)/shard_map/ppermute | solution.py:484
  29.2 0.9 collective-permute-start.4
  30.2 2.4 %collective-permute-start.3 = (bf16[32,4096]{1,0:T(8,128)(2,1)S(1)}, bf16[32,4096]{1,0:T(8,128)(2,1)S(1)}, u32[]{:S(2)}, u32[]{:S(2)}) collective-permute-start(bf16[32,4096]{1,0:T(8,128)(2,1)S(1)} %reshape.18.t0), channel_id=1, source_target_pairs={{8,0},{9,1},{10,2},{11,3},{12,4},{13,5},{14,6},{15,7},{16,8},{17,9... | collective-permute-start | bytes 786440 | tf_op jit(solution)/shard_map/ppermute | solution.py:484
  32.6 0.1 reshape.17.c0
  32.6 0.0 copy-done
  32.7 7.1 %inward_panels.1 = (bf16[2048,896]{1,0:T(8,128)(2,1)S(1)}, bf16[2048,896]{1,0:T(8,128)(2,1)S(1)}) custom-call(s32[3,224]{1,0:T(4,128)S(1)} %copy-done, bf16[224,4096]{1,0:T(8,128)(2,1)} %gate.1, bf16[224,4096]{1,0:T(8,128)(2,1)} %up.1), custom_call_target="tpu_custom_call" | custom-call | flops 6000000000 | bytes 1000 | tf_op jit(solution)/shard_map/inward_panels/pallas_call | solution.py:157
  39.8 0.1 collective-permute-start.2
  39.9 3.4 %collective-permute-start.1 = (bf16[32,4096]{1,0:T(8,128)(2,1)S(1)}, bf16[32,4096]{1,0:T(8,128)(2,1)S(1)}, u32[]{:S(2)}, u32[]{:S(2)}) collective-permute-start(bf16[32,4096]{1,0:T(8,128)(2,1)S(1)} %reshape.17.c0), channel_id=1, source_target_pairs={{16,0},{17,1},{18,2},{19,3},{20,4},{21,5},{22,6},{23,7},{24,8},{25... | collective-permute-start | bytes 786440 | tf_op jit(solution)/shard_map/ppermute | solution.py:484
  43.3 4.0 %outward_panel.1.pd = bf16[256,8192]{1,0:T(8,128)(2,1)S(1)} custom-call(s32[3,224]{1,0:T(4,128)S(1)} %copy-done, bf16[224,4096]{1,0:T(8,128)(2,1)} %down.1), custom_call_target="tpu_custom_call" | custom-call | flops 3000000000 | bytes 1000 | tf_op jit(solution)/shard_map/outward_panel/pallas_call | solution.py:174
  47.3 0.0 collective-permute-done.5.t3
  47.3 0.1 collective-permute-start
  47.4 0.0 collective-permute-done.4.t2
  47.4 0.0 collective-permute-done.3.t1
  47.4 6.6 %forward.1 = (bf16[2048,128]{1,0:T(8,128)(2,1)S(1)}, bf16[256,128]{1,0:T(8,128)(2,1)S(1)}, bf16[2304,128]{1,0:T(8,128)(2,1)S(1)}, f32[128,896]{1,0:T(8,128)S(1)}...) custom-call(bf16[32,4096]{1,0:T(8,128)(2,1)S(1)} %reshape.18.t0, ...), custom_call_target="tpu_custom_call" | custom-call | flops 8000000000 | bytes 1000 | tf_op jit(solution)/shard_map/forward/pallas_call | solution.py:245
  54.0 0.0 collective-permute-done.2.c3
  54.0 0.0 collective-permute-done.1.c2
  54.1 0.0 collective-permute-done.c1
  54.1 0.1 collective-permute-start.10
  54.2 0.5 collective-permute-start.6
  54.7 0.1 collective-permute-start.7
  54.8 0.4 collective-permute-start.8
  55.2 0.1 collective-permute-start.9
  55.3 0.9 collective-permute-done.10.sib_oth
  56.2 0.4 collective-permute-done.6.d0
  56.5 0.4 collective-permute-done.7.d1
  56.9 0.4 collective-permute-done.8.d2
  57.3 0.4 collective-permute-done.9.d3
  57.7 9.4 %backward.1 = (bf16[256,512]{1,0:T(8,128)(2,1)S(1)}, bf16[4,64,4096]{2,1,0:T(8,128)(2,1)}, bf16[256,4096]{1,0:T(8,128)(2,1)}) custom-call(bf16[32,4096]{1,0:T(8,128)(2,1)S(1)} %reshape.17.c0, bf16[32,4096]{1,0:T(8,128)(2,1)S(1)} %collective-permute-done.c1, bf16[32,4096]{1,0:T(8,128)(2,1)S(1)} %collective-permute-done.1.c2, ...), custom_call_target="tpu_custom_call" | custom-call | flops 8999999488 | bytes 1000 | tf_op jit(solution)/shard_map/backward/pallas_call | solution.py:402
  67.1 5.3 %all-to-all-start.1 = ((bf16[4,64,4096]{2,1,0:T(8,128)(2,1)}), bf16[4,64,4096]{2,1,0:T(8,128)(2,1)S(1)}, u32[]{:S(2)}, u32[]{:S(2)}) async-start(bf16[4,64,4096]{2,1,0:T(8,128)(2,1)} %get-tuple-element.53), calls=%async_computation.1 | async-start | bytes 4194304 | tf_op jit(solution)/shard_map/all_to_all | solution.py:510
  72.4 0.0 collective-permute-start.11
  72.5 6.2 %down_grads.1 = (bf16[224,512]{1,0:T(8,128)(2,1)}, bf16[224,512]{1,0:T(8,128)(2,1)}, bf16[224,512]{1,0:T(8,128)(2,1)}, bf16[224,512]{1,0:T(8,128)(2,1)}) custom-call(s32[3,224]{1,0:T(4,128)S(1)} %copy-done, bf16[256,4096]{1,0:T(8,128)(2,1)} %get-tuple-element.56.cots, bf16[256,128]{1,0:T(8,128)(2,1)S(1)} %get-tuple-element.57.ht_own, ...), custom_call_target="tpu_custom_call" | custom-call | flops 200000000 | bytes 1000 | tf_op jit(solution)/shard_map/down_grads/pallas_call | solution.py:303
  78.7 1.6 %collective-permute-start.12 = (bf16[224,512]{1,0:T(8,128)(2,1)}, bf16[224,512]{1,0:T(8,128)(2,1)S(1)}, u32[]{:S(2)}, u32[]{:S(2)}) collective-permute-start(bf16[224,512]{1,0:T(8,128)(2,1)} %get-tuple-element.61), channel_id=1, source_target_pairs={{64,0},{96,32},{0,64},{32,96},{192,128},{224,160},{128,192},{160,2... | collective-permute-start | bytes 688136 | tf_op jit(solution)/shard_map/ppermute | solution.py:489
  80.3 2.7 %collective-permute-start.13 = (bf16[224,512]{1,0:T(8,128)(2,1)}, bf16[224,512]{1,0:T(8,128)(2,1)S(1)}, u32[]{:S(2)}, u32[]{:S(2)}) collective-permute-start(bf16[224,512]{1,0:T(8,128)(2,1)} %get-tuple-element.62), channel_id=1, source_target_pairs={{128,0},{160,32},{192,64},{224,96},{0,128},{32,160},{64,192},{96,2... | collective-permute-start | bytes 688136 | tf_op jit(solution)/shard_map/ppermute | solution.py:489
  83.0 0.5 collective-permute-start.14
  83.5 0.0 collective-permute-done.11.d_oth
  83.5 5.0 %inward_grads.1 = (bf16[448,512]{1,0:T(8,128)(2,1)}, bf16[448,512]{1,0:T(8,128)(2,1)}, bf16[448,512]{1,0:T(8,128)(2,1)}, bf16[448,512]{1,0:T(8,128)(2,1)}) custom-call(s32[3,224]{1,0:T(4,128)S(1)} %copy-done, bf16[2048,128]{1,0:T(8,128)(2,1)S(1)} %get-tuple-element.54.xt_own, bf16[2304,128]{1,0:T(8,128)(2,1)S(1)} %collective-permute-done.10.sib_oth, ...), custom_call_target="tpu_custom_call" | custom-call | flops 200000000 | bytes 1000 | tf_op jit(solution)/shard_map/inward_grads/pallas_call | solution.py:470
  88.5 0.3 collective-permute-start.15
  88.7 3.9 %collective-permute-start.16 = (bf16[448,512]{1,0:T(8,128)(2,1)}, bf16[448,512]{1,0:T(8,128)(2,1)S(1)}, u32[]{:S(2)}, u32[]{:S(2)}) collective-permute-start(bf16[448,512]{1,0:T(8,128)(2,1)} %get-tuple-element.66), channel_id=1, source_target_pairs={{128,0},{160,32},{192,64},{224,96},{0,128},{32,160},{64,192},{96,2... | collective-permute-start | bytes 1376264 | tf_op jit(solution)/shard_map/ppermute | solution.py:489
  92.7 0.0 collective-permute-done.12
  92.7 0.5 collective-permute-start.17
  93.2 1.4 %collective-permute-done.13 = bf16[224,512]{1,0:T(8,128)(2,1)S(1)} collective-permute-done((bf16[224,512]{1,0:T(8,128)(2,1)}, bf16[224,512]{1,0:T(8,128)(2,1)S(1)}, u32[]{:S(2)}, u32[]{:S(2)}) %collective-permute-start.13) | collective-permute-done | bytes 229408 | tf_op jit(solution)/shard_map/ppermute | solution.py:489
  94.5 3.2 %collective-permute-done.14 = bf16[224,512]{1,0:T(8,128)(2,1)S(1)} collective-permute-done((bf16[224,512]{1,0:T(8,128)(2,1)}, bf16[224,512]{1,0:T(8,128)(2,1)S(1)}, u32[]{:S(2)}, u32[]{:S(2)}) %collective-permute-start.14) | collective-permute-done | bytes 229408 | tf_op jit(solution)/shard_map/ppermute | solution.py:489
  97.7 1.8 %multiply_convert_fusion = bf16[224,512]{1,0:T(8,128)(2,1)} fusion(bf16[224,512]{1,0:T(8,128)(2,1)S(1)} %collective-permute-done.14, bf16[224,512]{1,0:T(8,128)(2,1)S(1)} %collective-permute-done.13, bf16[224,512]{1,0:T(8,128)(2,1)S(1)} %collective-permute-done.12, bf16[224,512]{1,0:T(8,128)(2,1)} %get-tuple-element.58), kind=kLoop, calls=%fused_computation | loop fusion | flops 1032192 | bytes 1146880 | tf_op jit(solution)/shard_map/convert_element_type | solution.py:527
  99.5 0.0 copy-start.1
  99.5 0.0 all-to-all-done.1.got
  99.5 1.1 merge_y.1
  100.6 3.5 %all-to-all-start.2 = ((bf16[8,8,4096]{2,1,0:T(8,128)(2,1)}), bf16[8,8,4096]{2,1,0:T(8,128)(2,1)S(1)}, u32[]{:S(2)}, u32[]{:S(2)}) async-start(bf16[8,8,4096]{2,1,0:T(8,128)(2,1)} %merge_y.1), calls=%async_computation.2 | async-start | bytes 1048576 | tf_op jit(solution)/shard_map/all_to_all | solution.py:506
  104.1 0.0 collective-permute-done.15.b
  104.1 9.8 %collective-permute-done.16.c = bf16[448,512]{1,0:T(8,128)(2,1)S(1)} collective-permute-done((bf16[448,512]{1,0:T(8,128)(2,1)}, bf16[448,512]{1,0:T(8,128)(2,1)S(1)}, u32[]{:S(2)}, u32[]{:S(2)}) %collective-permute-start.16) | collective-permute-done | bytes 458784 | tf_op jit(solution)/shard_map/ppermute | solution.py:489
  113.9 2.6 %collective-permute-done.17.d = bf16[448,512]{1,0:T(8,128)(2,1)} collective-permute-done((bf16[448,512]{1,0:T(8,128)(2,1)}, bf16[448,512]{1,0:T(8,128)(2,1)}, u32[]{:S(2)}, u32[]{:S(2)}) %collective-permute-start.17) | collective-permute-done | bytes 458784 | tf_op jit(solution)/shard_map/ppermute | solution.py:489
  116.6 0.0 copy-done.1
  116.6 2.0 %inward_mean.1 = (bf16[224,512]{1,0:T(8,128)(2,1)}, bf16[224,512]{1,0:T(8,128)(2,1)}) custom-call(bf16[448,512]{1,0:T(8,128)(2,1)S(1)} %copy-done.1, bf16[448,512]{1,0:T(8,128)(2,1)S(1)} %collective-permute-done.15.b, bf16[448,512]{1,0:T(8,128)(2,1)S(1)} %collective-permute-done.16.c, bf16[448,512]{1,0:T(8,128)(2,1)} %collective-permute-done.17.d), custom_call_target="tpu_custom_call" | custom-call | flops 20000000000 | bytes 1000 | tf_op jit(solution)/shard_map/inward_mean/pallas_call | solution.py:537
  118.5 1.6 %all-to-all-done.2 = bf16[8,8,4096]{2,1,0:T(8,128)(2,1)S(1)} async-done(((bf16[8,8,4096]{2,1,0:T(8,128)(2,1)}), bf16[8,8,4096]{2,1,0:T(8,128)(2,1)S(1)}, u32[]{:S(2)}, u32[]{:S(2)}) %all-to-all-start.2) | async-done | bytes 524320 | tf_op jit(solution)/shard_map/all_to_all | solution.py:506
  120.1 0.1 reduce_sum.12
  120.2 0.7 fusion.1
  (1 shorter events, 0.0 us)
Async XLA Ops:
  0.6 32.0 %copy-start = (s32[3,224]{1,0:T(4,128)S(1)}, s32[3,224]{1,0:T(4,128)}, u32[]{:S(2)}) copy-start(s32[3,224]{1,0:T(4,128)} %idx.5) | copy-start | bytes 8068
  27.6 19.7 %collective-permute-start.5 = (bf16[32,4096]{1,0:T(8,128)(2,1)S(1)}, bf16[32,4096]{1,0:T(8,128)(2,1)S(1)}, u32[]{:S(2)}, u32[]{:S(2)}) collective-permute-start(bf16[32,4096]{1,0:T(8,128)(2,1)S(1)} %reshape.18.t0), channel_id=1, source_target_pairs={{24,0},{25,1},{26,2},{27,3},{28,4},{29,5},{30,6},{31,7},{0,8},{1,9... | collective-permute-start | bytes 786440 | tf_op jit(solution)/shard_map/ppermute | solution.py:484
  29.2 18.1 %collective-permute-start.4 = (bf16[32,4096]{1,0:T(8,128)(2,1)S(1)}, bf16[32,4096]{1,0:T(8,128)(2,1)S(1)}, u32[]{:S(2)}, u32[]{:S(2)}) collective-permute-start(bf16[32,4096]{1,0:T(8,128)(2,1)S(1)} %reshape.18.t0), channel_id=1, source_target_pairs={{16,0},{17,1},{18,2},{19,3},{20,4},{21,5},{22,6},{23,7},{24,8},{25... | collective-permute-start | bytes 786440 | tf_op jit(solution)/shard_map/ppermute | solution.py:484
  30.2 17.2 %collective-permute-start.3 = (bf16[32,4096]{1,0:T(8,128)(2,1)S(1)}, bf16[32,4096]{1,0:T(8,128)(2,1)S(1)}, u32[]{:S(2)}, u32[]{:S(2)}) collective-permute-start(bf16[32,4096]{1,0:T(8,128)(2,1)S(1)} %reshape.18.t0), channel_id=1, source_target_pairs={{8,0},{9,1},{10,2},{11,3},{12,4},{13,5},{14,6},{15,7},{16,8},{17,9... | collective-permute-start | bytes 786440 | tf_op jit(solution)/shard_map/ppermute | solution.py:484
  39.8 14.3 %collective-permute-start.2 = (bf16[32,4096]{1,0:T(8,128)(2,1)S(1)}, bf16[32,4096]{1,0:T(8,128)(2,1)S(1)}, u32[]{:S(2)}, u32[]{:S(2)}) collective-permute-start(bf16[32,4096]{1,0:T(8,128)(2,1)S(1)} %reshape.17.c0), channel_id=1, source_target_pairs={{24,0},{25,1},{26,2},{27,3},{28,4},{29,5},{30,6},{31,7},{0,8},{1,9... | collective-permute-start | bytes 786440 | tf_op jit(solution)/shard_map/ppermute | solution.py:484
  39.9 14.2 %collective-permute-start.1 = (bf16[32,4096]{1,0:T(8,128)(2,1)S(1)}, bf16[32,4096]{1,0:T(8,128)(2,1)S(1)}, u32[]{:S(2)}, u32[]{:S(2)}) collective-permute-start(bf16[32,4096]{1,0:T(8,128)(2,1)S(1)} %reshape.17.c0), channel_id=1, source_target_pairs={{16,0},{17,1},{18,2},{19,3},{20,4},{21,5},{22,6},{23,7},{24,8},{25... | collective-permute-start | bytes 786440 | tf_op jit(solution)/shard_map/ppermute | solution.py:484
  47.3 6.8 %collective-permute-start = (bf16[32,4096]{1,0:T(8,128)(2,1)S(1)}, bf16[32,4096]{1,0:T(8,128)(2,1)S(1)}, u32[]{:S(2)}, u32[]{:S(2)}) collective-permute-start(bf16[32,4096]{1,0:T(8,128)(2,1)S(1)} %reshape.17.c0), channel_id=1, source_target_pairs={{8,0},{9,1},{10,2},{11,3},{12,4},{13,5},{14,6},{15,7},{16,8},{17,9... | collective-permute-start | bytes 786440 | tf_op jit(solution)/shard_map/ppermute | solution.py:484
  54.1 2.1 %collective-permute-start.10 = (bf16[2304,128]{1,0:T(8,128)(2,1)S(1)}, bf16[2304,128]{1,0:T(8,128)(2,1)S(1)}, u32[]{:S(2)}, u32[]{:S(2)}) collective-permute-start(bf16[2304,128]{1,0:T(8,128)(2,1)S(1)} %get-tuple-element.49), channel_id=1, source_target_pairs={{32,0},{0,32},{96,64},{64,96},{160,128},{128,160},{224,192},{192,2... | collective-permute-start | bytes 1769480 | tf_op jit(solution)/shard_map/ppermute | solution.py:494
  54.2 2.4 %collective-permute-start.6 = (bf16[32,4096]{1,0:T(8,128)(2,1)S(1)}, bf16[32,4096]{1,0:T(8,128)(2,1)S(1)}, u32[]{:S(2)}, u32[]{:S(2)}) collective-permute-start(bf16[32,4096]{1,0:T(8,128)(2,1)S(1)} %reshape.17.c0), channel_id=1, source_target_pairs={{32,0},{0,32},{96,64},{64,96},{160,128},{128,160},{224,192},{192,2... | collective-permute-start | bytes 786440 | tf_op jit(solution)/shard_map/ppermute | solution.py:494
  54.7 2.2 %collective-permute-start.7 = (bf16[32,4096]{1,0:T(8,128)(2,1)S(1)}, bf16[32,4096]{1,0:T(8,128)(2,1)S(1)}, u32[]{:S(2)}, u32[]{:S(2)}) collective-permute-start(bf16[32,4096]{1,0:T(8,128)(2,1)S(1)} %collective-permute-done.c1), channel_id=1, source_target_pairs={{32,0},{0,32},{96,64},{64,96},{160,128},{128,160},{224,192},{192,2... | collective-permute-start | bytes 786440 | tf_op jit(solution)/shard_map/ppermute | solution.py:494
  54.8 2.5 %collective-permute-start.8 = (bf16[32,4096]{1,0:T(8,128)(2,1)S(1)}, bf16[32,4096]{1,0:T(8,128)(2,1)S(1)}, u32[]{:S(2)}, u32[]{:S(2)}) collective-permute-start(bf16[32,4096]{1,0:T(8,128)(2,1)S(1)} %collective-permute-done.1.c2), channel_id=1, source_target_pairs={{32,0},{0,32},{96,64},{64,96},{160,128},{128,160},{224,192},{192,2... | collective-permute-start | bytes 786440 | tf_op jit(solution)/shard_map/ppermute | solution.py:494
  55.2 2.5 %collective-permute-start.9 = (bf16[32,4096]{1,0:T(8,128)(2,1)S(1)}, bf16[32,4096]{1,0:T(8,128)(2,1)S(1)}, u32[]{:S(2)}, u32[]{:S(2)}) collective-permute-start(bf16[32,4096]{1,0:T(8,128)(2,1)S(1)} %collective-permute-done.2.c3), channel_id=1, source_target_pairs={{32,0},{0,32},{96,64},{64,96},{160,128},{128,160},{224,192},{192,2... | collective-permute-start | bytes 786440 | tf_op jit(solution)/shard_map/ppermute | solution.py:494
  67.1 32.4 %all-to-all-start.1 = ((bf16[4,64,4096]{2,1,0:T(8,128)(2,1)}), bf16[4,64,4096]{2,1,0:T(8,128)(2,1)S(1)}, u32[]{:S(2)}, u32[]{:S(2)}) async-start(bf16[4,64,4096]{2,1,0:T(8,128)(2,1)} %get-tuple-element.53), calls=%async_computation.1 | async-start | bytes 4194304 | tf_op jit(solution)/shard_map/all_to_all | solution.py:510
  72.4 11.0 %collective-permute-start.11 = (bf16[256,512]{1,0:T(8,128)(2,1)S(1)}, bf16[256,512]{1,0:T(8,128)(2,1)S(1)}, u32[]{:S(2)}, u32[]{:S(2)}) collective-permute-start(bf16[256,512]{1,0:T(8,128)(2,1)S(1)} %get-tuple-element.59.d_own), channel_id=1, source_target_pairs={{32,0},{0,32},{96,64},{64,96},{160,128},{128,160},{224,192},{192,2... | collective-permute-start | bytes 786440 | tf_op jit(solution)/shard_map/ppermute | solution.py:494
  78.7 14.0 %collective-permute-start.12 = (bf16[224,512]{1,0:T(8,128)(2,1)}, bf16[224,512]{1,0:T(8,128)(2,1)S(1)}, u32[]{:S(2)}, u32[]{:S(2)}) collective-permute-start(bf16[224,512]{1,0:T(8,128)(2,1)} %get-tuple-element.61), channel_id=1, source_target_pairs={{64,0},{96,32},{0,64},{32,96},{192,128},{224,160},{128,192},{160,2... | collective-permute-start | bytes 688136 | tf_op jit(solution)/shard_map/ppermute | solution.py:489
  80.3 14.3 %collective-permute-start.13 = (bf16[224,512]{1,0:T(8,128)(2,1)}, bf16[224,512]{1,0:T(8,128)(2,1)S(1)}, u32[]{:S(2)}, u32[]{:S(2)}) collective-permute-start(bf16[224,512]{1,0:T(8,128)(2,1)} %get-tuple-element.62), channel_id=1, source_target_pairs={{128,0},{160,32},{192,64},{224,96},{0,128},{32,160},{64,192},{96,2... | collective-permute-start | bytes 688136 | tf_op jit(solution)/shard_map/ppermute | solution.py:489
  83.0 14.7 %collective-permute-start.14 = (bf16[224,512]{1,0:T(8,128)(2,1)}, bf16[224,512]{1,0:T(8,128)(2,1)S(1)}, u32[]{:S(2)}, u32[]{:S(2)}) collective-permute-start(bf16[224,512]{1,0:T(8,128)(2,1)} %get-tuple-element.63), channel_id=1, source_target_pairs={{192,0},{224,32},{128,64},{160,96},{64,128},{96,160},{0,192},{32,2... | collective-permute-start | bytes 688136 | tf_op jit(solution)/shard_map/ppermute | solution.py:489
  88.5 15.6 %collective-permute-start.15 = (bf16[448,512]{1,0:T(8,128)(2,1)}, bf16[448,512]{1,0:T(8,128)(2,1)S(1)}, u32[]{:S(2)}, u32[]{:S(2)}) collective-permute-start(bf16[448,512]{1,0:T(8,128)(2,1)} %get-tuple-element.65), channel_id=1, source_target_pairs={{64,0},{96,32},{0,64},{32,96},{192,128},{224,160},{128,192},{160,2... | collective-permute-start | bytes 1376264 | tf_op jit(solution)/shard_map/ppermute | solution.py:489
  88.7 25.2 %collective-permute-start.16 = (bf16[448,512]{1,0:T(8,128)(2,1)}, bf16[448,512]{1,0:T(8,128)(2,1)S(1)}, u32[]{:S(2)}, u32[]{:S(2)}) collective-permute-start(bf16[448,512]{1,0:T(8,128)(2,1)} %get-tuple-element.66), channel_id=1, source_target_pairs={{128,0},{160,32},{192,64},{224,96},{0,128},{32,160},{64,192},{96,2... | collective-permute-start | bytes 1376264 | tf_op jit(solution)/shard_map/ppermute | solution.py:489
  92.7 23.9 %collective-permute-start.17 = (bf16[448,512]{1,0:T(8,128)(2,1)}, bf16[448,512]{1,0:T(8,128)(2,1)}, u32[]{:S(2)}, u32[]{:S(2)}) collective-permute-start(bf16[448,512]{1,0:T(8,128)(2,1)} %get-tuple-element.67), channel_id=1, source_target_pairs={{192,0},{224,32},{128,64},{160,96},{64,128},{96,160},{0,192},{32,2... | collective-permute-start | bytes 1376264 | tf_op jit(solution)/shard_map/ppermute | solution.py:489
  99.5 17.1 %copy-start.1 = (bf16[448,512]{1,0:T(8,128)(2,1)S(1)}, bf16[448,512]{1,0:T(8,128)(2,1)}, u32[]{:S(2)}) copy-start(bf16[448,512]{1,0:T(8,128)(2,1)} %get-tuple-element.60.a) | copy-start | bytes 1376260
  100.6 19.5 %all-to-all-start.2 = ((bf16[8,8,4096]{2,1,0:T(8,128)(2,1)}), bf16[8,8,4096]{2,1,0:T(8,128)(2,1)S(1)}, u32[]{:S(2)}, u32[]{:S(2)}) async-start(bf16[8,8,4096]{2,1,0:T(8,128)(2,1)} %merge_y.1), calls=%async_computation.2 | async-start | bytes 1048576 | tf_op jit(solution)/shard_map/all_to_all | solution.py:506

commit v9 on v8

--- a/solution.py
+++ b/solution.py
@@ -378,20 +378,20 @@
                 own[TOK:, pair] = jnp.where(low, ud, 0.0).astype(BF)
             before = (gd, ud)
     sends = []
-    for n in range(4):
-        rows = slice(n * 512, n * 512 + 512)
+    for n in range(2):
+        rows = slice(n * 1024, n * 1024 + 1024)
         acc = (mm(pg[rows, :], gdt[...]) + mm(pu[rows, :], udt[...])).astype(BF)
         turned = acc.T
         pairs = [
             jnp.concatenate([turned[p * TOK:p * TOK + TOK, c * 128:c * 128 + 128] for p in range(2)], axis=1)
-            for c in range(4)
+            for c in range(8)
         ]
         whole = mm(jnp.concatenate(pairs, axis=0), fjoin).astype(BF)
-        for c in range(4):
-            lanes = slice(n * 1024 + c * 256, n * 1024 + c * 256 + 256)
+        for c in range(8):
+            lanes = slice(n * 2048 + c * 256, n * 2048 + c * 256 + 256)
             for r in range(NY):
                 ins[lax.rem(y + r, NY), :, lanes] = whole[c * TOK + r * 32:c * TOK + r * 32 + 32, :]
-        lanes = pl.ds(n * 1024, 1024)
+        lanes = pl.ds(n * 2048, 2048)
         sends.append(pltpu.make_async_copy(ins.at[:, :, lanes], parts.at[:, 32:, lanes], part_sems.at[n]))
         sends[-1].start()
     for copy in sends + bundle + [share]:

time: 121 us -> 120 us (level)
  no operation moved by 1% of the time
where the time goes in v9:
time: 120 us
  Pallas kernels  40.4 us (34%)
  starting transfers between devices  28.1 us (23%)
  blocking collectives  25.8 us (22%)
  waiting for transfers between devices  21 us (18%)
  other arithmetic  2.65 us (2%)
    all_to_all x1, blocking collectives, over_z(): lax.all_to_all(value, 'fsdp', 0, 0, axis_index_groups=z_groups(), tiled=T...  25.8 us
    ppermute x6, waiting for transfers between devices, from_x(): return lax.ppermute(value, 'dp', pairs)  17 us
    ppermute x6, starting transfers between devices, from_x(): return lax.ppermute(value, 'dp', pairs)  9.48 us
    ppermute x6, starting transfers between devices, from_y(): return lax.ppermute(value, 'fsdp', pairs)  8.57 us
    pallas_call x1, Pallas kernels, backward(): pl.pallas_call(back_kernel, in_specs=vm(4) + far(4) + vm(5) + far(1), out...  8.34 us
    pallas_call x1, Pallas kernels, inward_panels(): pl.pallas_call(inward_panels_kernel, in_specs=smem(1) + far(2), out_specs...  7.12 us
    pallas_call x1, Pallas kernels, forward(): pl.pallas_call(forward_kernel, in_specs=vm(7), out_specs=vm(6), out_shape...  6.65 us
    pallas_call x1, Pallas kernels, down_grads(): pl.pallas_call(down_kernel, in_specs=smem(1) + far(1) + vm(2), out_specs=...  6.22 us
  transfers between devices with their start and end apart: 20, of which 10 were waited for; matrix products, arithmetic and copies ran while one was open for 2% of the time, Pallas kernels for 27%

profile of v9, /device:TPU:8, one launch (start us, length us, event | category | flops | bytes accessed | tf_op | source)
XLA Modules:
  0.0 119.8 jit_solution(8017612423293478816)
XLA Ops:
  0.6 0.0 copy-start
  0.6 0.8 pad_maximum_fusion
  1.5 25.8 %all_to_all.15 = bf16[8,8,4096]{2,1,0:T(8,128)(2,1)S(1)} all-to-all(bf16[8,8,4096]{2,1,0:T(8,128)(2,1)S(1)} %broadcast_in_dim.2), channel_id=1, replica_groups={{0,1,2,3,4,5,6,7},{8,9,10,11,12,13,14,15},{16,17,18,19,20,21,22,23},{24..., dimensions={0} | all-to-all | bytes 1048576 | tf_op jit(solution)/shard_map/all_to_all | solution.py:506
  27.3 0.2 fusion
  27.5 0.1 reshape.18.t0
  27.6 1.7 %collective-permute-start.5 = (bf16[32,4096]{1,0:T(8,128)(2,1)S(1)}, bf16[32,4096]{1,0:T(8,128)(2,1)S(1)}, u32[]{:S(2)}, u32[]{:S(2)}) collective-permute-start(bf16[32,4096]{1,0:T(8,128)(2,1)S(1)} %reshape.18.t0), channel_id=1, source_target_pairs={{24,0},{25,1},{26,2},{27,3},{28,4},{29,5},{30,6},{31,7},{0,8},{1,9... | collective-permute-start | bytes 786440 | tf_op jit(solution)/shard_map/ppermute | solution.py:484
  29.2 0.9 collective-permute-start.4
  30.2 2.4 %collective-permute-start.3 = (bf16[32,4096]{1,0:T(8,128)(2,1)S(1)}, bf16[32,4096]{1,0:T(8,128)(2,1)S(1)}, u32[]{:S(2)}, u32[]{:S(2)}) collective-permute-start(bf16[32,4096]{1,0:T(8,128)(2,1)S(1)} %reshape.18.t0), channel_id=1, source_target_pairs={{8,0},{9,1},{10,2},{11,3},{12,4},{13,5},{14,6},{15,7},{16,8},{17,9... | collective-permute-start | bytes 786440 | tf_op jit(solution)/shard_map/ppermute | solution.py:484
  32.6 0.1 reshape.17.c0
  32.6 0.0 copy-done
  32.7 7.1 %inward_panels.1 = (bf16[2048,896]{1,0:T(8,128)(2,1)S(1)}, bf16[2048,896]{1,0:T(8,128)(2,1)S(1)}) custom-call(s32[3,224]{1,0:T(4,128)S(1)} %copy-done, bf16[224,4096]{1,0:T(8,128)(2,1)} %gate.1, bf16[224,4096]{1,0:T(8,128)(2,1)} %up.1), custom_call_target="tpu_custom_call" | custom-call | flops 6000000000 | bytes 1000 | tf_op jit(solution)/shard_map/inward_panels/pallas_call | solution.py:157
  39.8 0.1 collective-permute-start.2
  39.9 3.4 %collective-permute-start.1 = (bf16[32,4096]{1,0:T(8,128)(2,1)S(1)}, bf16[32,4096]{1,0:T(8,128)(2,1)S(1)}, u32[]{:S(2)}, u32[]{:S(2)}) collective-permute-start(bf16[32,4096]{1,0:T(8,128)(2,1)S(1)} %reshape.17.c0), channel_id=1, source_target_pairs={{16,0},{17,1},{18,2},{19,3},{20,4},{21,5},{22,6},{23,7},{24,8},{25... | collective-permute-start | bytes 786440 | tf_op jit(solution)/shard_map/ppermute | solution.py:484
  43.3 4.0 %outward_panel.1.pd = bf16[256,8192]{1,0:T(8,128)(2,1)S(1)} custom-call(s32[3,224]{1,0:T(4,128)S(1)} %copy-done, bf16[224,4096]{1,0:T(8,128)(2,1)} %down.1), custom_call_target="tpu_custom_call" | custom-call | flops 3000000000 | bytes 1000 | tf_op jit(solution)/shard_map/outward_panel/pallas_call | solution.py:174
  47.3 0.0 collective-permute-done.5.t3
  47.3 0.1 collective-permute-start
  47.4 0.0 collective-permute-done.4.t2
  47.4 0.0 collective-permute-done.3.t1
  47.4 6.6 %forward.1 = (bf16[2048,128]{1,0:T(8,128)(2,1)S(1)}, bf16[256,128]{1,0:T(8,128)(2,1)S(1)}, bf16[2304,128]{1,0:T(8,128)(2,1)S(1)}, f32[128,896]{1,0:T(8,128)S(1)}...) custom-call(bf16[32,4096]{1,0:T(8,128)(2,1)S(1)} %reshape.18.t0, ...), custom_call_target="tpu_custom_call" | custom-call | flops 8000000000 | bytes 1000 | tf_op jit(solution)/shard_map/forward/pallas_call | solution.py:245
  54.1 0.0 collective-permute-done.2.c3
  54.1 0.0 collective-permute-done.1.c2
  54.1 0.0 collective-permute-done.c1
  54.1 0.1 collective-permute-start.10
  54.2 0.5 collective-permute-start.6
  54.7 0.1 collective-permute-start.7
  54.8 0.4 collective-permute-start.8
  55.2 0.1 collective-permute-start.9
  55.3 0.9 collective-permute-done.10.sib_oth
  56.2 0.4 collective-permute-done.6.d0
  56.5 0.4 collective-permute-done.7.d1
  56.9 0.4 collective-permute-done.8.d2
  57.3 0.4 collective-permute-done.9.d3
  57.7 8.3 %backward.1 = (bf16[256,512]{1,0:T(8,128)(2,1)S(1)}, bf16[4,64,4096]{2,1,0:T(8,128)(2,1)}, bf16[256,4096]{1,0:T(8,128)(2,1)}) custom-call(bf16[32,4096]{1,0:T(8,128)(2,1)S(1)} %reshape.17.c0, bf16[32,4096]{1,0:T(8,128)(2,1)S(1)} %collective-permute-done.c1, bf16[32,4096]{1,0:T(8,128)(2,1)S(1)} %collective-permute-done.1.c2, ...), custom_call_target="tpu_custom_call" | custom-call | flops 8999999488 | bytes 1000 | tf_op jit(solution)/shard_map/backward/pallas_call | solution.py:402
  66.0 5.3 %all-to-all-start.1 = ((bf16[4,64,4096]{2,1,0:T(8,128)(2,1)}), bf16[4,64,4096]{2,1,0:T(8,128)(2,1)S(1)}, u32[]{:S(2)}, u32[]{:S(2)}) async-start(bf16[4,64,4096]{2,1,0:T(8,128)(2,1)} %get-tuple-element.53), calls=%async_computation.1 | async-start | bytes 4194304 | tf_op jit(solution)/shard_map/all_to_all | solution.py:510
  71.4 0.0 collective-permute-start.11
  71.4 6.2 %down_grads.1 = (bf16[224,512]{1,0:T(8,128)(2,1)}, bf16[224,512]{1,0:T(8,128)(2,1)}, bf16[224,512]{1,0:T(8,128)(2,1)}, bf16[224,512]{1,0:T(8,128)(2,1)}) custom-call(s32[3,224]{1,0:T(4,128)S(1)} %copy-done, bf16[256,4096]{1,0:T(8,128)(2,1)} %get-tuple-element.56.cots, bf16[256,128]{1,0:T(8,128)(2,1)S(1)} %get-tuple-element.57.ht_own, ...), custom_call_target="tpu_custom_call" | custom-call | flops 200000000 | bytes 1000 | tf_op jit(solution)/shard_map/down_grads/pallas_call | solution.py:303
  77.6 1.6 %collective-permute-start.12 = (bf16[224,512]{1,0:T(8,128)(2,1)}, bf16[224,512]{1,0:T(8,128)(2,1)S(1)}, u32[]{:S(2)}, u32[]{:S(2)}) collective-permute-start(bf16[224,512]{1,0:T(8,128)(2,1)} %get-tuple-element.61), channel_id=1, source_target_pairs={{64,0},{96,32},{0,64},{32,96},{192,128},{224,160},{128,192},{160,2... | collective-permute-start | bytes 688136 | tf_op jit(solution)/shard_map/ppermute | solution.py:489
  79.2 2.7 %collective-permute-start.13 = (bf16[224,512]{1,0:T(8,128)(2,1)}, bf16[224,512]{1,0:T(8,128)(2,1)S(1)}, u32[]{:S(2)}, u32[]{:S(2)}) collective-permute-start(bf16[224,512]{1,0:T(8,128)(2,1)} %get-tuple-element.62), channel_id=1, source_target_pairs={{128,0},{160,32},{192,64},{224,96},{0,128},{32,160},{64,192},{96,2... | collective-permute-start | bytes 688136 | tf_op jit(solution)/shard_map/ppermute | solution.py:489
  81.9 0.5 collective-permute-start.14
  82.4 0.0 collective-permute-done.11.d_oth
  82.4 5.0 %inward_grads.1 = (bf16[448,512]{1,0:T(8,128)(2,1)}, bf16[448,512]{1,0:T(8,128)(2,1)}, bf16[448,512]{1,0:T(8,128)(2,1)}, bf16[448,512]{1,0:T(8,128)(2,1)}) custom-call(s32[3,224]{1,0:T(4,128)S(1)} %copy-done, bf16[2048,128]{1,0:T(8,128)(2,1)S(1)} %get-tuple-element.54.xt_own, bf16[2304,128]{1,0:T(8,128)(2,1)S(1)} %collective-permute-done.10.sib_oth, ...), custom_call_target="tpu_custom_call" | custom-call | flops 200000000 | bytes 1000 | tf_op jit(solution)/shard_map/inward_grads/pallas_call | solution.py:470
  87.4 0.3 collective-permute-start.15
  87.6 3.9 %collective-permute-start.16 = (bf16[448,512]{1,0:T(8,128)(2,1)}, bf16[448,512]{1,0:T(8,128)(2,1)S(1)}, u32[]{:S(2)}, u32[]{:S(2)}) collective-permute-start(bf16[448,512]{1,0:T(8,128)(2,1)} %get-tuple-element.66), channel_id=1, source_target_pairs={{128,0},{160,32},{192,64},{224,96},{0,128},{32,160},{64,192},{96,2... | collective-permute-start | bytes 1376264 | tf_op jit(solution)/shard_map/ppermute | solution.py:489
  91.6 0.0 collective-permute-done.12
  91.6 0.5 collective-permute-start.17
  92.1 1.4 %collective-permute-done.13 = bf16[224,512]{1,0:T(8,128)(2,1)S(1)} collective-permute-done((bf16[224,512]{1,0:T(8,128)(2,1)}, bf16[224,512]{1,0:T(8,128)(2,1)S(1)}, u32[]{:S(2)}, u32[]{:S(2)}) %collective-permute-start.13) | collective-permute-done | bytes 229408 | tf_op jit(solution)/shard_map/ppermute | solution.py:489
  93.4 3.2 %collective-permute-done.14 = bf16[224,512]{1,0:T(8,128)(2,1)S(1)} collective-permute-done((bf16[224,512]{1,0:T(8,128)(2,1)}, bf16[224,512]{1,0:T(8,128)(2,1)S(1)}, u32[]{:S(2)}, u32[]{:S(2)}) %collective-permute-start.14) | collective-permute-done | bytes 229408 | tf_op jit(solution)/shard_map/ppermute | solution.py:489
  96.6 1.8 %multiply_convert_fusion = bf16[224,512]{1,0:T(8,128)(2,1)} fusion(bf16[224,512]{1,0:T(8,128)(2,1)S(1)} %collective-permute-done.14, bf16[224,512]{1,0:T(8,128)(2,1)S(1)} %collective-permute-done.13, bf16[224,512]{1,0:T(8,128)(2,1)S(1)} %collective-permute-done.12, bf16[224,512]{1,0:T(8,128)(2,1)} %get-tuple-element.58), kind=kLoop, calls=%fused_computation | loop fusion | flops 1032192 | bytes 1146880 | tf_op jit(solution)/shard_map/convert_element_type | solution.py:527
  98.3 0.0 copy-start.1
  98.4 0.0 all-to-all-done.1.got
  98.4 1.1 merge_y.1
  99.5 3.5 %all-to-all-start.2 = ((bf16[8,8,4096]{2,1,0:T(8,128)(2,1)}), bf16[8,8,4096]{2,1,0:T(8,128)(2,1)S(1)}, u32[]{:S(2)}, u32[]{:S(2)}) async-start(bf16[8,8,4096]{2,1,0:T(8,128)(2,1)} %merge_y.1), calls=%async_computation.2 | async-start | bytes 1048576 | tf_op jit(solution)/shard_map/all_to_all | solution.py:506
  103.0 0.0 collective-permute-done.15.b
  103.0 9.8 %collective-permute-done.16.c = bf16[448,512]{1,0:T(8,128)(2,1)S(1)} collective-permute-done((bf16[448,512]{1,0:T(8,128)(2,1)}, bf16[448,512]{1,0:T(8,128)(2,1)S(1)}, u32[]{:S(2)}, u32[]{:S(2)}) %collective-permute-start.16) | collective-permute-done | bytes 458784 | tf_op jit(solution)/shard_map/ppermute | solution.py:489
  112.8 2.6 %collective-permute-done.17.d = bf16[448,512]{1,0:T(8,128)(2,1)} collective-permute-done((bf16[448,512]{1,0:T(8,128)(2,1)}, bf16[448,512]{1,0:T(8,128)(2,1)}, u32[]{:S(2)}, u32[]{:S(2)}) %collective-permute-start.17) | collective-permute-done | bytes 458784 | tf_op jit(solution)/shard_map/ppermute | solution.py:489
  115.5 0.0 copy-done.1
  115.5 2.0 %inward_mean.1 = (bf16[224,512]{1,0:T(8,128)(2,1)}, bf16[224,512]{1,0:T(8,128)(2,1)}) custom-call(bf16[448,512]{1,0:T(8,128)(2,1)S(1)} %copy-done.1, bf16[448,512]{1,0:T(8,128)(2,1)S(1)} %collective-permute-done.15.b, bf16[448,512]{1,0:T(8,128)(2,1)S(1)} %collective-permute-done.16.c, bf16[448,512]{1,0:T(8,128)(2,1)} %collective-permute-done.17.d), custom_call_target="tpu_custom_call" | custom-call | flops 20000000000 | bytes 1000 | tf_op jit(solution)/shard_map/inward_mean/pallas_call | solution.py:537
  117.4 1.6 %all-to-all-done.2 = bf16[8,8,4096]{2,1,0:T(8,128)(2,1)S(1)} async-done(((bf16[8,8,4096]{2,1,0:T(8,128)(2,1)}), bf16[8,8,4096]{2,1,0:T(8,128)(2,1)S(1)}, u32[]{:S(2)}, u32[]{:S(2)}) %all-to-all-start.2) | async-done | bytes 524320 | tf_op jit(solution)/shard_map/all_to_all | solution.py:506
  119.0 0.1 reduce_sum.12
  119.1 0.7 fusion.1
  (1 shorter events, 0.0 us)
Async XLA Ops:
  0.6 32.0 %copy-start = (s32[3,224]{1,0:T(4,128)S(1)}, s32[3,224]{1,0:T(4,128)}, u32[]{:S(2)}) copy-start(s32[3,224]{1,0:T(4,128)} %idx.5) | copy-start | bytes 8068
  27.6 19.7 %collective-permute-start.5 = (bf16[32,4096]{1,0:T(8,128)(2,1)S(1)}, bf16[32,4096]{1,0:T(8,128)(2,1)S(1)}, u32[]{:S(2)}, u32[]{:S(2)}) collective-permute-start(bf16[32,4096]{1,0:T(8,128)(2,1)S(1)} %reshape.18.t0), channel_id=1, source_target_pairs={{24,0},{25,1},{26,2},{27,3},{28,4},{29,5},{30,6},{31,7},{0,8},{1,9... | collective-permute-start | bytes 786440 | tf_op jit(solution)/shard_map/ppermute | solution.py:484
  29.2 18.1 %collective-permute-start.4 = (bf16[32,4096]{1,0:T(8,128)(2,1)S(1)}, bf16[32,4096]{1,0:T(8,128)(2,1)S(1)}, u32[]{:S(2)}, u32[]{:S(2)}) collective-permute-start(bf16[32,4096]{1,0:T(8,128)(2,1)S(1)} %reshape.18.t0), channel_id=1, source_target_pairs={{16,0},{17,1},{18,2},{19,3},{20,4},{21,5},{22,6},{23,7},{24,8},{25... | collective-permute-start | bytes 786440 | tf_op jit(solution)/shard_map/ppermute | solution.py:484
  30.2 17.2 %collective-permute-start.3 = (bf16[32,4096]{1,0:T(8,128)(2,1)S(1)}, bf16[32,4096]{1,0:T(8,128)(2,1)S(1)}, u32[]{:S(2)}, u32[]{:S(2)}) collective-permute-start(bf16[32,4096]{1,0:T(8,128)(2,1)S(1)} %reshape.18.t0), channel_id=1, source_target_pairs={{8,0},{9,1},{10,2},{11,3},{12,4},{13,5},{14,6},{15,7},{16,8},{17,9... | collective-permute-start | bytes 786440 | tf_op jit(solution)/shard_map/ppermute | solution.py:484
  39.8 14.3 %collective-permute-start.2 = (bf16[32,4096]{1,0:T(8,128)(2,1)S(1)}, bf16[32,4096]{1,0:T(8,128)(2,1)S(1)}, u32[]{:S(2)}, u32[]{:S(2)}) collective-permute-start(bf16[32,4096]{1,0:T(8,128)(2,1)S(1)} %reshape.17.c0), channel_id=1, source_target_pairs={{24,0},{25,1},{26,2},{27,3},{28,4},{29,5},{30,6},{31,7},{0,8},{1,9... | collective-permute-start | bytes 786440 | tf_op jit(solution)/shard_map/ppermute | solution.py:484
  39.9 14.2 %collective-permute-start.1 = (bf16[32,4096]{1,0:T(8,128)(2,1)S(1)}, bf16[32,4096]{1,0:T(8,128)(2,1)S(1)}, u32[]{:S(2)}, u32[]{:S(2)}) collective-permute-start(bf16[32,4096]{1,0:T(8,128)(2,1)S(1)} %reshape.17.c0), channel_id=1, source_target_pairs={{16,0},{17,1},{18,2},{19,3},{20,4},{21,5},{22,6},{23,7},{24,8},{25... | collective-permute-start | bytes 786440 | tf_op jit(solution)/shard_map/ppermute | solution.py:484
  47.3 6.8 %collective-permute-start = (bf16[32,4096]{1,0:T(8,128)(2,1)S(1)}, bf16[32,4096]{1,0:T(8,128)(2,1)S(1)}, u32[]{:S(2)}, u32[]{:S(2)}) collective-permute-start(bf16[32,4096]{1,0:T(8,128)(2,1)S(1)} %reshape.17.c0), channel_id=1, source_target_pairs={{8,0},{9,1},{10,2},{11,3},{12,4},{13,5},{14,6},{15,7},{16,8},{17,9... | collective-permute-start | bytes 786440 | tf_op jit(solution)/shard_map/ppermute | solution.py:484
  54.1 2.1 %collective-permute-start.10 = (bf16[2304,128]{1,0:T(8,128)(2,1)S(1)}, bf16[2304,128]{1,0:T(8,128)(2,1)S(1)}, u32[]{:S(2)}, u32[]{:S(2)}) collective-permute-start(bf16[2304,128]{1,0:T(8,128)(2,1)S(1)} %get-tuple-element.49), channel_id=1, source_target_pairs={{32,0},{0,32},{96,64},{64,96},{160,128},{128,160},{224,192},{192,2... | collective-permute-start | bytes 1769480 | tf_op jit(solution)/shard_map/ppermute | solution.py:494
  54.2 2.4 %collective-permute-start.6 = (bf16[32,4096]{1,0:T(8,128)(2,1)S(1)}, bf16[32,4096]{1,0:T(8,128)(2,1)S(1)}, u32[]{:S(2)}, u32[]{:S(2)}) collective-permute-start(bf16[32,4096]{1,0:T(8,128)(2,1)S(1)} %reshape.17.c0), channel_id=1, source_target_pairs={{32,0},{0,32},{96,64},{64,96},{160,128},{128,160},{224,192},{192,2... | collective-permute-start | bytes 786440 | tf_op jit(solution)/shard_map/ppermute | solution.py:494
  54.7 2.2 %collective-permute-start.7 = (bf16[32,4096]{1,0:T(8,128)(2,1)S(1)}, bf16[32,4096]{1,0:T(8,128)(2,1)S(1)}, u32[]{:S(2)}, u32[]{:S(2)}) collective-permute-start(bf16[32,4096]{1,0:T(8,128)(2,1)S(1)} %collective-permute-done.c1), channel_id=1, source_target_pairs={{32,0},{0,32},{96,64},{64,96},{160,128},{128,160},{224,192},{192,2... | collective-permute-start | bytes 786440 | tf_op jit(solution)/shard_map/ppermute | solution.py:494
  54.8 2.5 %collective-permute-start.8 = (bf16[32,4096]{1,0:T(8,128)(2,1)S(1)}, bf16[32,4096]{1,0:T(8,128)(2,1)S(1)}, u32[]{:S(2)}, u32[]{:S(2)}) collective-permute-start(bf16[32,4096]{1,0:T(8,128)(2,1)S(1)} %collective-permute-done.1.c2), channel_id=1, source_target_pairs={{32,0},{0,32},{96,64},{64,96},{160,128},{128,160},{224,192},{192,2... | collective-permute-start | bytes 786440 | tf_op jit(solution)/shard_map/ppermute | solution.py:494
  55.2 2.5 %collective-permute-start.9 = (bf16[32,4096]{1,0:T(8,128)(2,1)S(1)}, bf16[32,4096]{1,0:T(8,128)(2,1)S(1)}, u32[]{:S(2)}, u32[]{:S(2)}) collective-permute-start(bf16[32,4096]{1,0:T(8,128)(2,1)S(1)} %collective-permute-done.2.c3), channel_id=1, source_target_pairs={{32,0},{0,32},{96,64},{64,96},{160,128},{128,160},{224,192},{192,2... | collective-permute-start | bytes 786440 | tf_op jit(solution)/shard_map/ppermute | solution.py:494
  66.0 32.3 %all-to-all-start.1 = ((bf16[4,64,4096]{2,1,0:T(8,128)(2,1)}), bf16[4,64,4096]{2,1,0:T(8,128)(2,1)S(1)}, u32[]{:S(2)}, u32[]{:S(2)}) async-start(bf16[4,64,4096]{2,1,0:T(8,128)(2,1)} %get-tuple-element.53), calls=%async_computation.1 | async-start | bytes 4194304 | tf_op jit(solution)/shard_map/all_to_all | solution.py:510
  71.4 11.0 %collective-permute-start.11 = (bf16[256,512]{1,0:T(8,128)(2,1)S(1)}, bf16[256,512]{1,0:T(8,128)(2,1)S(1)}, u32[]{:S(2)}, u32[]{:S(2)}) collective-permute-start(bf16[256,512]{1,0:T(8,128)(2,1)S(1)} %get-tuple-element.59.d_own), channel_id=1, source_target_pairs={{32,0},{0,32},{96,64},{64,96},{160,128},{128,160},{224,192},{192,2... | collective-permute-start | bytes 786440 | tf_op jit(solution)/shard_map/ppermute | solution.py:494
  77.6 14.0 %collective-permute-start.12 = (bf16[224,512]{1,0:T(8,128)(2,1)}, bf16[224,512]{1,0:T(8,128)(2,1)S(1)}, u32[]{:S(2)}, u32[]{:S(2)}) collective-permute-start(bf16[224,512]{1,0:T(8,128)(2,1)} %get-tuple-element.61), channel_id=1, source_target_pairs={{64,0},{96,32},{0,64},{32,96},{192,128},{224,160},{128,192},{160,2... | collective-permute-start | bytes 688136 | tf_op jit(solution)/shard_map/ppermute | solution.py:489
  79.2 14.3 %collective-permute-start.13 = (bf16[224,512]{1,0:T(8,128)(2,1)}, bf16[224,512]{1,0:T(8,128)(2,1)S(1)}, u32[]{:S(2)}, u32[]{:S(2)}) collective-permute-start(bf16[224,512]{1,0:T(8,128)(2,1)} %get-tuple-element.62), channel_id=1, source_target_pairs={{128,0},{160,32},{192,64},{224,96},{0,128},{32,160},{64,192},{96,2... | collective-permute-start | bytes 688136 | tf_op jit(solution)/shard_map/ppermute | solution.py:489
  81.9 14.7 %collective-permute-start.14 = (bf16[224,512]{1,0:T(8,128)(2,1)}, bf16[224,512]{1,0:T(8,128)(2,1)S(1)}, u32[]{:S(2)}, u32[]{:S(2)}) collective-permute-start(bf16[224,512]{1,0:T(8,128)(2,1)} %get-tuple-element.63), channel_id=1, source_target_pairs={{192,0},{224,32},{128,64},{160,96},{64,128},{96,160},{0,192},{32,2... | collective-permute-start | bytes 688136 | tf_op jit(solution)/shard_map/ppermute | solution.py:489
  87.4 15.6 %collective-permute-start.15 = (bf16[448,512]{1,0:T(8,128)(2,1)}, bf16[448,512]{1,0:T(8,128)(2,1)S(1)}, u32[]{:S(2)}, u32[]{:S(2)}) collective-permute-start(bf16[448,512]{1,0:T(8,128)(2,1)} %get-tuple-element.65), channel_id=1, source_target_pairs={{64,0},{96,32},{0,64},{32,96},{192,128},{224,160},{128,192},{160,2... | collective-permute-start | bytes 1376264 | tf_op jit(solution)/shard_map/ppermute | solution.py:489
  87.6 25.2 %collective-permute-start.16 = (bf16[448,512]{1,0:T(8,128)(2,1)}, bf16[448,512]{1,0:T(8,128)(2,1)S(1)}, u32[]{:S(2)}, u32[]{:S(2)}) collective-permute-start(bf16[448,512]{1,0:T(8,128)(2,1)} %get-tuple-element.66), channel_id=1, source_target_pairs={{128,0},{160,32},{192,64},{224,96},{0,128},{32,160},{64,192},{96,2... | collective-permute-start | bytes 1376264 | tf_op jit(solution)/shard_map/ppermute | solution.py:489
  91.6 23.9 %collective-permute-start.17 = (bf16[448,512]{1,0:T(8,128)(2,1)}, bf16[448,512]{1,0:T(8,128)(2,1)}, u32[]{:S(2)}, u32[]{:S(2)}) collective-permute-start(bf16[448,512]{1,0:T(8,128)(2,1)} %get-tuple-element.67), channel_id=1, source_target_pairs={{192,0},{224,32},{128,64},{160,96},{64,128},{96,160},{0,192},{32,2... | collective-permute-start | bytes 1376264 | tf_op jit(solution)/shard_map/ppermute | solution.py:489
  98.3 17.1 %copy-start.1 = (bf16[448,512]{1,0:T(8,128)(2,1)S(1)}, bf16[448,512]{1,0:T(8,128)(2,1)}, u32[]{:S(2)}) copy-start(bf16[448,512]{1,0:T(8,128)(2,1)} %get-tuple-element.60.a) | copy-start | bytes 1376260
  99.5 19.5 %all-to-all-start.2 = ((bf16[8,8,4096]{2,1,0:T(8,128)(2,1)}), bf16[8,8,4096]{2,1,0:T(8,128)(2,1)S(1)}, u32[]{:S(2)}, u32[]{:S(2)}) async-start(bf16[8,8,4096]{2,1,0:T(8,128)(2,1)} %merge_y.1), calls=%async_computation.2 | async-start | bytes 1048576 | tf_op jit(solution)/shard_map/all_to_all | solution.py:506
